TPU v7x, 128 devices: a whole 4x4x4 slice. The times are simulated.
128 devices in a mesh: gx: 16 (over z_lo, x, core), gy: 8 (over y, z_hi).
Axes of the slice: x: 4, y: 4, z: 4 (z_hi: 2, z_lo: 2; z = z_hi * 2 + z_lo), core: 2. Of those that a mesh axis runs over, the one named last changes fastest.
Arguments:
- tokens: bfloat16 [4096, 8192], P('gy', 'gx'), may hold values from -6 to 6
- norm_gain: float32 [8192], replicated, may hold values from 0.1 to 1.9
- query_weight: bfloat16 [8192, 8192], P('gy', 'gx')
- kv_weight: bfloat16 [8192, 2048], P('gy')
- out_weight: bfloat16 [8192, 8192], P('gx', 'gy'), may hold values from -0.0625 to 0.0625
- lengths: int32 [8], P('gy'), may hold values from 1 to 512, as said below
Outputs:
- mixed: bfloat16 [4096, 8192], P('gy', 'gx')
Inputs may be any that keep to these rules, and one draw needn't show every extreme that they name: `lengths`: some transcript has all 512 slots valid in every draw.
All inputs are finite; a program needn't handle non-finite values.
Results may differ from a plain program's by a relative error of at most 0.039.
Values may be sent and summed in bfloat16 or wider, within the bound.
No kernel may reach another device: no remote copies, remote signals or barrier semaphores. Data moves between devices by JAX's collectives and lax.ppermute only.
A program may use at most 128 MiB of HBM per device.

v0:
```python
import jax
import jax.numpy as jnp
from jax import lax
from jax.sharding import PartitionSpec as P

QUERY_HEADS = 64
KEY_VALUE_HEADS = 8
HEAD_SIZE = 128
TRANSCRIPT_SLOTS = 512


rope_base = 500000.0
norm_eps = 1e-05


def apply_rope(vectors, positions):
    half_dim = vectors.shape[-1] // 2
    steps_up = jnp.arange(0, half_dim, dtype=jnp.float32) * (2.0 / vectors.shape[-1])
    inverse = jnp.power(jnp.float32(rope_base), -steps_up)
    angles = positions.astype(jnp.float32)[:, None] * inverse[None, :]
    cosine = jnp.cos(angles)[:, None, :]
    sine_part = jnp.sin(angles)[:, None, :]
    low_half = vectors[..., :half_dim]
    high_half = vectors[..., half_dim:]
    return jnp.concatenate(
        [low_half * cosine - high_half * sine_part, high_half * cosine + low_half * sine_part],
        axis=-1,
    )


def local(tokens, norm_gain, query_weight, kv_weight, out_weight, lengths):
    tok_rows = tokens.shape[0]
    query_cols = query_weight.shape[1]
    resident_heads = query_cols // HEAD_SIZE
    whole = lax.all_gather(tokens, "gx", axis=1, tiled=True)
    wide_rows = whole.astype(jnp.float32)
    square_mean = jnp.mean(wide_rows * wide_rows, axis=-1, keepdims=True)
    normed = (wide_rows * lax.rsqrt(square_mean + norm_eps) * norm_gain[None, :]).astype(
        jnp.bfloat16
    )
    key_value_group = lax.axis_index("gx") * resident_heads // (QUERY_HEADS // KEY_VALUE_HEADS)
    kv_cols = lax.dynamic_slice_in_dim(kv_weight, key_value_group * 2 * HEAD_SIZE, 2 * HEAD_SIZE, 1)
    spread = lax.all_to_all(normed, "gy", split_axis=1, concat_axis=0, tiled=True)
    both_weights = jnp.concatenate([query_weight, kv_cols], axis=1)
    summed = lax.psum_scatter(
        jnp.dot(spread, both_weights, preferred_element_type=jnp.float32).astype(jnp.bfloat16),
        "gy",
        scatter_dimension=0,
        tiled=True,
    ).astype(jnp.float32)
    projected = summed[:, :query_cols]
    key_value_projected = summed[:, query_cols:]
    positions = jnp.arange(tok_rows, dtype=jnp.int32) % TRANSCRIPT_SLOTS
    query_rows = apply_rope(
        projected.reshape(tok_rows, resident_heads, HEAD_SIZE), positions
    ).astype(jnp.bfloat16)
    key_row_stack = apply_rope(key_value_projected[:, None, :HEAD_SIZE], positions)[:, 0, :].astype(
        jnp.bfloat16
    )
    value_row_stack = key_value_projected[:, HEAD_SIZE:].astype(jnp.bfloat16)
    seq_local = tok_rows // TRANSCRIPT_SLOTS
    query_blocks = query_rows.reshape(seq_local, TRANSCRIPT_SLOTS, resident_heads, HEAD_SIZE)
    key_blocks = key_row_stack.reshape(seq_local, TRANSCRIPT_SLOTS, HEAD_SIZE)
    value_blocks = value_row_stack.reshape(seq_local, TRANSCRIPT_SLOTS, HEAD_SIZE)
    scores = jnp.einsum(
        "sqhd,skd->shqk", query_blocks, key_blocks, preferred_element_type=jnp.float32
    ) / jnp.sqrt(jnp.float32(HEAD_SIZE))
    slot_q = jnp.arange(TRANSCRIPT_SLOTS, dtype=jnp.int32)[:, None]
    slot_k = jnp.arange(TRANSCRIPT_SLOTS, dtype=jnp.int32)[None, :]
    allowed_mask = (slot_k[None] <= slot_q[None]) & (slot_k[None] < lengths[:, None, None])
    scores = jnp.where(allowed_mask[:, None], scores, -jnp.inf)
    top_score = jnp.max(scores, axis=-1, keepdims=True)
    expd = jnp.exp(scores - top_score)
    probs = (expd / jnp.sum(expd, axis=-1, keepdims=True)).astype(jnp.bfloat16)
    attended_output = jnp.einsum(
        "shqk,skd->sqhd", probs, value_blocks, preferred_element_type=jnp.float32
    )
    attended_output = attended_output.astype(jnp.bfloat16).reshape(tok_rows, query_cols)
    partial_value = jnp.dot(
        attended_output,
        lax.all_gather(out_weight, "gy", axis=1, tiled=True),
        preferred_element_type=jnp.float32,
    )
    mixed_sum = lax.psum_scatter(
        partial_value.astype(jnp.bfloat16), "gx", scatter_dimension=1, tiled=True
    ).astype(jnp.float32)
    return (tokens.astype(jnp.float32) + mixed_sum).astype(jnp.bfloat16)


def solution(mesh):
    placed = (P("gy", "gx"), P(), P("gy", "gx"), P("gy", None), P("gx", "gy"), P("gy"))
    return jax.shard_map(
        local, mesh=mesh, in_specs=placed, out_specs=P("gy", "gx"), check_vma=False
    )
```

profile of v0, /device:TPU:3, one launch (start us, length us, event | category | flops | bytes accessed | tf_op | source)
XLA Modules:
  0.0 512.2 jit_solution(16827151807470660880)
XLA Ops:
  6.5 2.0 copy.21
  8.6 55.2 %all-gather.3.cloned.1.call-done = bf16[512,8192]{0,1:T(8,128)(2,1)} async-done(((bf16[512,512]{0,1:T(8,128)(2,1)}), bf16[512,8192]{0,1:T(8,128)(2,1)}) %all-gather.3.cloned.1.call-update) | async-done | bytes 8388624 | tf_op jit(solution)/shard_map/all_gather | solution.py:35
  63.9 5.3 %fusion = f32[512]{0:T(512)S(1)} fusion(bf16[512,8192]{0,1:T(8,128)(2,1)} %all-gather.3.cloned.1.call-done), kind=kLoop, calls=%fused_computation.2 | loop fusion | flops 12582400 | bytes 8390656 | tf_op jit(solution)/shard_map/reduce_sum | solution.py:37
  69.6 4.3 fusion.2
  74.0 6.6 %all-to-all-start = ((bf16[512,8,1024]{0,2,1:T(8,128)(2,1)}), bf16[512,8,1024]{0,2,1:T(8,128)(2,1)}, u32[]{:S(2)}, u32[]{:S(2)}) async-start(bf16[512,8,1024]{0,2,1:T(8,128)(2,1)} %bitcast.46), calls=%async_computation | async-start | bytes 16777216 | tf_op jit(solution)/shard_map/all_to_all | solution.py:43
  80.6 1.1 constant_dynamic-slice_fusion
  81.7 114.2 %all-to-all-done = bf16[512,8,1024]{0,2,1:T(8,128)(2,1)} async-done(((bf16[512,8,1024]{0,2,1:T(8,128)(2,1)}), bf16[512,8,1024]{0,2,1:T(8,128)(2,1)}, u32[]{:S(2)}, u32[]{:S(2)}) %all-to-all-start) | async-done | bytes 8388640 | tf_op jit(solution)/shard_map/all_to_all | solution.py:43
  195.9 11.5 %copy.22 = bf16[8,512,1024]{2,1,0:T(8,128)(2,1)} copy(bf16[8,512,1024]{1,2,0:T(8,128)(2,1)} %bitcast.1) | data formatting | bytes 16777216 | tf_op jit(solution)/shard_map/all_to_all | solution.py:43
  207.4 12.0 %convolution_convert_fusion.1 = bf16[4096,768]{0,1:T(8,128)(2,1)} fusion(bf16[4096,1024]{1,0:T(8,128)(2,1)} %bitcast.47, bf16[1024,256]{1,0:T(8,128)(2,1)S(1)} %constant_dynamic-slice_fusion, bf16[1024,512]{1,0:T(8,128)(2,1)S(1)} %copy-done.4), kind=kOutput, calls=%fused_computation.6 | convolution fusion | flops 6448742400 | bytes 16252928 | tf_op jit(solution)/shard_map/dot_general | solution.py:46
  219.5 0.7 all-gather.5.cloned.1.call-update
  221.2 1.8 multiply_cosine_fusion
  223.0 95.8 %reduce-scatter.3.cloned.1.call-done = bf16[512,768]{0,1:T(8,128)(2,1)} async-done(((bf16[4096,768]{0,1:T(8,128)(2,1)}), bf16[512,768]{0,1:T(8,128)(2,1)}) %reduce-scatter.3.cloned.1.call-update) | async-done | bytes 786448 | tf_op jit(solution)/shard_map/reduce_scatter | solution.py:45
  318.7 1.2 slice.36
  320.0 0.9 fusion.37
  321.2 1.4 copy.32
  322.9 0.6 fusion.24
  323.4 1.2 subtract_convert_fusion
  324.7 1.2 fusion.4
  325.8 0.9 fusion.3
  326.8 1.5 fusion.11
  328.3 100.7 %all-gather.5.cloned.1.call-done = bf16[512,8192]{1,0:T(8,128)(2,1)} async-done(((bf16[512,1024]{1,0:T(8,128)(2,1)}), bf16[512,8192]{1,0:T(8,128)(2,1)}) %all-gather.5.cloned.1.call-update) | async-done | bytes 8388624 | tf_op jit(solution)/shard_map/all_gather | solution.py:81
  429.0 10.1 %convolution_convert_fusion = bf16[512,8192]{1,0:T(8,128)(2,1)} fusion(bf16[512,512]{0,1:T(8,128)(2,1)S(1)} %bitcast.49, bf16[512,8192]{1,0:T(8,128)(2,1)} %all-gather.5.cloned.1.call-done), kind=kOutput, calls=%fused_computation.5 | convolution fusion | flops 4299161600 | bytes 17301504 | tf_op jit(solution)/shard_map/dot_general | solution.py:79
  439.1 64.7 %reduce-scatter.5.cloned.1.call-done = bf16[512,512]{1,0:T(8,128)(2,1)} async-done(((bf16[512,8192]{1,0:T(8,128)(2,1)}), bf16[512,512]{1,0:T(8,128)(2,1)}) %reduce-scatter.5.cloned.1.call-update) | async-done | bytes 524304 | tf_op jit(solution)/shard_map/reduce_scatter | solution.py:84
  503.7 2.0 add_convert_fusion
  (25 shorter events, 1.5 us)
Async XLA Ops:
  6.5 57.3 %all-gather.3.cloned.1.call-start = ((), (), s32[]{:S(2)}) async-start(), calls=%async_computation.3 | async-start | bytes 8912896 | tf_op jit(solution)/shard_map/all_gather | solution.py:35
  8.6 60.6 %copy-start.3 = (f32[8192]{0:T(1024)S(1)}, f32[8192]{0:T(1024)}, u32[]{:S(2)}) copy-start(f32[8192]{0:T(1024)} %param.7) | copy-start | bytes 98308
  63.9 5.8 %copy-start = (bf16[512,8192]{0,1:T(8,128)(2,1)S(1)}, bf16[512,8192]{0,1:T(8,128)(2,1)}, u32[]{:S(2)}) copy-start(bf16[512,8192]{0,1:T(8,128)(2,1)} %all-gather.3.cloned.1.call-done) | copy-start | bytes 25165828
  74.0 121.9 %all-to-all-start = ((bf16[512,8,1024]{0,2,1:T(8,128)(2,1)}), bf16[512,8,1024]{0,2,1:T(8,128)(2,1)}, u32[]{:S(2)}, u32[]{:S(2)}) async-start(bf16[512,8,1024]{0,2,1:T(8,128)(2,1)} %bitcast.46), calls=%async_computation | async-start | bytes 16777216 | tf_op jit(solution)/shard_map/all_to_all | solution.py:43
  80.6 238.2 %reduce-scatter.3.cloned.1.call-start = ((), (), s32[]{:S(2)}) async-start(), calls=%async_computation.4 | async-start | bytes 7077888 | tf_op jit(solution)/shard_map/reduce_scatter | solution.py:45
  195.9 11.5 %copy-start.4 = (bf16[1024,512]{1,0:T(8,128)(2,1)S(1)}, bf16[1024,512]{1,0:T(8,128)(2,1)}, u32[]{:S(2)}) copy-start(bf16[1024,512]{1,0:T(8,128)(2,1)} %param.8) | copy-start | bytes 3145732
  219.4 209.5 %all-gather.5.cloned.1.call-start = ((), (), s32[]{:S(2)}) async-start(), calls=%async_computation.5 | async-start | bytes 9437184 | tf_op jit(solution)/shard_map/all_gather | solution.py:81
  220.2 283.6 %reduce-scatter.5.cloned.1.call-start = ((), (), s32[]{:S(2)}) async-start(), calls=%async_computation.6 | async-start | bytes 8912896 | tf_op jit(solution)/shard_map/reduce_scatter | solution.py:84
  318.7 3.9 copy-start.1
  439.0 64.7 %copy-start.2 = (bf16[512,512]{1,0:T(8,128)(2,1)S(1)}, bf16[512,512]{1,0:T(8,128)(2,1)}, u32[]{:S(2)}) copy-start(bf16[512,512]{1,0:T(8,128)(2,1)} %param.6) | copy-start | bytes 1572868
Sparse Core Ops, SparseCore 0:
  9.1 54.7 all-gather.2
  219.5 99.1 reduce-scatter.2
  321.4 107.5 all-gather.4
  439.2 64.4 reduce-scatter.4
where the time goes:
time: 521 us; the launch traced here: 512 us
  waiting for transfers between devices  431 us (83%)
  matrix products  24.7 us (5%)
  local copies, waits for them, and re-layouts  19 us (4%)
  other arithmetic  16.5 us (3%)
  between operations  13.9 us (3%)
  starting transfers between devices  6.89 us (1%)
    all_to_all x1, waiting for transfers between devices, local(): lax.all_to_all(normed, 'gy', split_axis=1, concat_axis=0, tiled=True)  114 us
    all_gather x1, waiting for transfers between devices, local(): lax.all_gather(out_weight, 'gy', axis=1, tiled=True)  101 us
    reduce_scatter x1, waiting for transfers between devices, local(): lax.psum_scatter(jnp.dot(spread, both_weights, preferred_element_type=jnp...  95.8 us
    reduce_scatter x1, waiting for transfers between devices, local(): lax.psum_scatter(partial_value.astype(jnp.bfloat16), 'gx', scatter_dimens...  64.7 us
    all_gather x1, waiting for transfers between devices, local(): whole = lax.all_gather(tokens, 'gx', axis=1, tiled=True)  55.2 us
    dot_general x1, matrix products, local(): jnp.dot(spread, both_weights, preferred_element_type=jnp.float32)  12 us
    all_to_all x1, local copies, waits for them, and re-layouts, local(): lax.all_to_all(normed, 'gy', split_axis=1, concat_axis=0, tiled=True)  11.5 us
  transfers between devices with their start and end apart: 5, of which 5 were waited for; matrix products, arithmetic and copies ran while one was open for 2% of the time, Pallas kernels for 0%

commit v1 on v0

v1 whole, which is shorter than its diff:
```python
import jax
import jax.numpy as jnp
from jax import lax
from jax.sharding import Mesh, PartitionSpec as P

HEAD_SIZE = 128
SLOTS = 512
HALF = 256
AXES = ("zl", "x", "core", "y", "zh")
SIZES = (2, 4, 2, 4, 2)

rope_base = 500000.0
norm_eps = 1e-05


def coords(i):
    out = {}
    for name, size in zip(AXES[::-1], SIZES[::-1]):
        i, out[name] = divmod(i, size)
    return out


def index(c):
    i = 0
    for name, size in zip(AXES, SIZES):
        i = i * size + c[name] % size
    return i


def pairs(change):
    out = []
    for i in range(128):
        c = coords(i)
        out.append((i, index({**c, **change(c)})))
    return out


def send(value, change):
    return lax.ppermute(value, AXES, pairs(change))


def core_swap(value):
    return send(value, lambda c: dict(core=1 - c["core"]))


def zh_swap(value):
    return send(value, lambda c: dict(zh=1 - c["zh"]))


def y_shift(value, k):
    return send(value, lambda c: dict(y=c["y"] + k))


def to_slice(flip):
    def change(c):
        return dict(
            y=2 * c["zl"] + c["x"] // 2,
            zl=c["y"] // 2,
            x=(c["y"] % 2) * 2 + c["x"] % 2,
            core=c["core"] ^ flip,
        )

    return change


def rope_tables(positions):
    half_dim = HEAD_SIZE // 2
    steps_up = jnp.arange(0, half_dim, dtype=jnp.float32) * (2.0 / HEAD_SIZE)
    inverse = jnp.power(jnp.float32(rope_base), -steps_up)
    angles = positions.astype(jnp.float32)[:, None] * inverse[None, :]
    return jnp.cos(angles)[:, None, :], jnp.sin(angles)[:, None, :]


def apply_rope(vectors, tables):
    cosine, sine = tables
    half_dim = HEAD_SIZE // 2
    low = vectors[..., :half_dim]
    high = vectors[..., half_dim:]
    return jnp.concatenate([low * cosine - high * sine, high * cosine + low * sine], axis=-1)


def half_of(value, which, dim=0):
    size = value.shape[dim] // 2
    return lax.dynamic_slice_in_dim(value, which * size, size, dim)


def ordered(first, own, other, dim=0):
    return jnp.where(
        first, jnp.concatenate([own, other], dim), jnp.concatenate([other, own], dim)
    )


def dot(a, b):
    return jnp.dot(a, b, preferred_element_type=jnp.float32)


def local(tokens, norm_gain, query_weight, kv_weight, out_weight, lengths):
    core = lax.axis_index("core")
    chip = lax.axis_index(("zl", "x"))
    y = lax.axis_index("y")
    zh = lax.axis_index("zh")
    is_first = core == 0

    gain = lax.dynamic_slice_in_dim(norm_gain, (chip * 2 + core) * 512, 512, 0)
    wide = tokens.astype(jnp.float32)
    gained = (wide * gain[None, :]).astype(jnp.bfloat16)
    mine = send(half_of(gained, core), to_slice(0))
    theirs = send(half_of(gained, 1 - core), to_slice(1))
    block = ordered(is_first, mine, theirs, 1)
    gathered = lax.all_gather(block, ("zl", "x"), axis=0, tiled=False)
    gathered = gathered.reshape(4, 2, HALF, 1024)
    squares = lax.psum(jnp.sum(wide * wide, axis=-1), ("zl", "x", "core"))

    kv_own = lax.dynamic_slice_in_dim(kv_weight, chip * 256 + core * 128, 128, 1)
    near = jnp.concatenate([query_weight, kv_own], axis=1)
    far = zh_swap(near)
    near_other = core_swap(near)
    far_other = core_swap(far)

    def whole(own, other):
        kv = ordered(is_first, own[:, 512:], other[:, 512:], 1)
        return jnp.concatenate([own[:, :512], other[:, :512], kv], axis=1)

    near_whole = whole(near, near_other)
    far_whole = whole(far, far_other)

    out_far = zh_swap(out_weight)
    pair = ordered(zh == 0, out_weight[:, None], out_far[:, None], 1)
    up = y_shift(pair, 1)
    down = y_shift(pair, -1)
    across_a = y_shift(up[:256], 1)
    across_b = y_shift(down[256:], -1)
    across = jnp.concatenate([across_a, across_b], 0)
    own_rows = jnp.zeros((4, 512, 2, 1024), jnp.bfloat16)
    for k, part in ((0, pair), (3, up), (1, down), (2, across)):
        own_rows = lax.dynamic_update_slice(own_rows, part[None], ((y + k) % 4, 0, 0, 0))
    other_rows = core_swap(own_rows)

    rows_near = lax.dynamic_index_in_dim(gathered, zh, 1, keepdims=False).reshape(1024, 1024)
    rows_far = lax.dynamic_index_in_dim(gathered, 1 - zh, 1, keepdims=False).reshape(1024, 1024)
    projected = (dot(rows_near, near_whole) + dot(rows_far, far_whole)).astype(jnp.bfloat16)
    summed = lax.psum_scatter(
        projected.reshape(4, HALF, 1280), "y", scatter_dimension=0, tiled=False
    ).astype(jnp.float32)
    scale = half_of(lax.rsqrt(squares / 8192.0 + norm_eps), core)
    summed = summed * scale[:, None]

    own_slots = core * HALF + jnp.arange(HALF, dtype=jnp.int32)
    tables = rope_tables(own_slots)
    queries = apply_rope(summed[:, :1024].reshape(HALF, 8, HEAD_SIZE), tables).astype(jnp.bfloat16)
    key_own = apply_rope(summed[:, None, 1024:1152], tables)[:, 0].astype(jnp.bfloat16)
    kv_rows = jnp.concatenate([key_own, summed[:, 1152:].astype(jnp.bfloat16)], axis=1)
    kv_all = jnp.concatenate([kv_rows, core_swap(kv_rows)], axis=0)
    keys, values = kv_all[:, :HEAD_SIZE], kv_all[:, HEAD_SIZE:]
    slot_k = jnp.concatenate([own_slots, (1 - core) * HALF + jnp.arange(HALF, dtype=jnp.int32)])
    scores = jnp.einsum(
        "qhd,kd->hqk", queries, keys, preferred_element_type=jnp.float32
    ) / jnp.sqrt(jnp.float32(HEAD_SIZE))
    allowed = (slot_k[None, :] <= own_slots[:, None]) & (slot_k[None, :] < lengths[0])
    scores = jnp.where(allowed[None], scores, -jnp.inf)
    expd = jnp.exp(scores - jnp.max(scores, axis=-1, keepdims=True))
    probs = (expd / jnp.sum(expd, axis=-1, keepdims=True)).astype(jnp.bfloat16)
    attended = jnp.einsum("hqk,kd->qhd", probs, values, preferred_element_type=jnp.float32)
    attended = attended.astype(jnp.bfloat16).reshape(HALF, 1024)

    partial = jnp.einsum(
        "qr,yrzc->yzqc", attended[:, :512], own_rows, preferred_element_type=jnp.float32
    ) + jnp.einsum(
        "qr,yrzc->yzqc", attended[:, 512:], other_rows, preferred_element_type=jnp.float32
    )
    partial = partial.astype(jnp.bfloat16).reshape(8, HALF, 1024)
    mixed = lax.psum_scatter(partial, ("zl", "x"), scatter_dimension=0, tiled=False)
    keep = half_of(mixed, core, 1)
    got = core_swap(half_of(mixed, 1 - core, 1))
    return (wide + ordered(is_first, keep, got, 0).astype(jnp.float32)).astype(jnp.bfloat16)


def solution(mesh):
    split = Mesh(mesh.devices.reshape(SIZES), AXES)
    gx, gy = ("zl", "x", "core"), ("y", "zh")
    placed = (P(gy, gx), P(), P(gy, gx), P(gy, None), P(gx, gy), P(gy))
    return jax.shard_map(
        local, mesh=split, in_specs=placed, out_specs=P(gy, gx), check_vma=False
    )
```

time: 521 us -> 304 us (0.58)
  waiting for transfers between devices: 431 us -> 124 us
  blocking collectives: 0 us -> 69.1 us
  starting transfers between devices: 6.89 us -> 23.4 us
  local copies, waits for them, and re-layouts: 19 us -> 31.7 us
    all_gather x2 -> x1, waiting for transfers between devices: 156 us -> 0.01 us  [local(): gathered = lax.all_gather(block, ('zl', 'x'), axis=0, tiled=False)]
    all_to_all x1 -> x0, waiting for transfers between devices: 114 us -> none  [local(): lax.all_to_all(normed, 'gy', split_axis=1, concat_axis=0, tiled=True)]
    reduce_scatter x2, waiting for transfers between devices: 160 us -> 54.6 us  [the longest x1 54.6 us: local(): lax.psum_scatter(partial, ('zl', 'x'), scatter_dimension=0, tiled=False)]
    ppermute x0 -> x13, waiting for transfers between devices: none -> 69.5 us  [send(): return lax.ppermute(value, AXES, pairs(change))]
    psum x0 -> x1, blocking collectives: none -> 69.1 us  [local(): squares = lax.psum(jnp.sum(wide * wide, axis=-1), ('zl', 'x', 'core'))]
    ppermute x0 -> x13, starting transfers between devices: none -> 23.1 us  [send(): return lax.ppermute(value, AXES, pairs(change))]
    all_to_all x1 -> x0, local copies, waits for them, and re-layouts: 11.5 us -> none  [local(): lax.all_to_all(normed, 'gy', split_axis=1, concat_axis=0, tiled=True)]
    slice x2 -> x11, local copies, waits for them, and re-layouts: 2.13 us -> 12.2 us  [the longest x3 5.85 us: whole(): return jnp.concatenate([own[:, :512], other[:, :512], kv], axis=1)]
  transfers between devices with their start and end apart: 5 -> 16, of which waited for: 5 -> 8; matrix products, arithmetic and copies ran while one was open for 2% -> 16% of each run, Pallas kernels for 0% -> 0%
where the time goes in v1:
time: 304 us; the launch traced here: 300 us
  waiting for transfers between devices  124 us (41%)
  blocking collectives  69.1 us (23%)
  local copies, waits for them, and re-layouts  31.7 us (10%)
  starting transfers between devices  23.4 us (8%)
  matrix products  20.6 us (7%)
  other arithmetic  17.2 us (6%)
  between operations  14.1 us (5%)
    ppermute x13, waiting for transfers between devices, send(): return lax.ppermute(value, AXES, pairs(change))  69.5 us
    psum x1, blocking collectives, local(): squares = lax.psum(jnp.sum(wide * wide, axis=-1), ('zl', 'x', 'core'))  69.1 us
    reduce_scatter x1, waiting for transfers between devices, local(): lax.psum_scatter(partial, ('zl', 'x'), scatter_dimension=0, tiled=False)  54.6 us
    ppermute x13, starting transfers between devices, send(): return lax.ppermute(value, AXES, pairs(change))  23.1 us
    dot_general x1, matrix products, local(): jnp.einsum('qr,yrzc->yzqc', attended[:, :512], own_rows, preferred_elemen...  7.8 us
  transfers between devices with their start and end apart: 16, of which 8 were waited for; matrix products, arithmetic and copies ran while one was open for 16% of the time, Pallas kernels for 0%

profile of v1, /device:TPU:3, one launch (start us, length us, event | category | flops | bytes accessed | tf_op | source)
XLA Modules:
  0.0 300.2 jit_solution(5668835281005079977)
XLA Ops:
  12.9 3.7 %collective-permute-start = (bf16[512,1024]{0,1:T(8,128)(2,1)S(1)}, bf16[512,1024]{0,1:T(8,128)(2,1)S(1)}, u32[]{:S(2)}, u32[]{:S(2)}) collective-permute-start(bf16[512,1024]{0,1:T(8,128)(2,1)S(1)} %copy.51), channel_id=1, source_target_pairs={{0,1},{1,0},{2,3},{3,2},{4,5},{5,4},{6,7},{7,6},{8,9},{9,8},{10,11... | collective-permute-start | bytes 3145736 | tf_op jit(solution)/shard_map/ppermute | solution.py:39
  18.8 32.3 %collective-permute-done = bf16[512,1024]{0,1:T(8,128)(2,1)S(1)} collective-permute-done((bf16[512,1024]{0,1:T(8,128)(2,1)S(1)}, bf16[512,1024]{0,1:T(8,128)(2,1)S(1)}, u32[]{:S(2)}, u32[]{:S(2)}) %collective-permute-start) | collective-permute-done | bytes 1048608 | tf_op jit(solution)/shard_map/ppermute | solution.py:39
  53.7 6.0 %collective-permute-start.1 = (bf16[512,2,1024]{0,2,1:T(8,128)(2,1)}, bf16[512,2,1024]{0,2,1:T(8,128)(2,1)S(1)}, u32[]{:S(2)}, u32[]{:S(2)}) collective-permute-start(bf16[512,2,1024]{0,2,1:T(8,128)(2,1)} %maximum_select_fusion.1), channel_id=1, source_target_pairs={{0,2},{1,3},{2,4},{3,5},{4,6},{5,7},{6,0},{7,1},{8,10},{9,11},{10,... | collective-permute-start | bytes 6291464 | tf_op jit(solution)/shard_map/ppermute | solution.py:39
  59.7 3.5 %collective-permute-start.2 = (bf16[512,2,1024]{0,2,1:T(8,128)(2,1)}, bf16[512,2,1024]{0,2,1:T(8,128)(2,1)}, u32[]{:S(2)}, u32[]{:S(2)}) collective-permute-start(bf16[512,2,1024]{0,2,1:T(8,128)(2,1)} %maximum_select_fusion.1), channel_id=1, source_target_pairs={{0,6},{1,7},{2,0},{3,1},{4,2},{5,3},{6,4},{7,5},{8,14},{9,15},{10,... | collective-permute-start | bytes 6291464 | tf_op jit(solution)/shard_map/ppermute | solution.py:39
  63.3 16.0 %collective-permute-done.8 = bf16[1024,640]{1,0:T(8,128)(2,1)} collective-permute-done((bf16[1024,640]{1,0:T(8,128)(2,1)}, bf16[1024,640]{1,0:T(8,128)(2,1)}, u32[]{:S(2)}, u32[]{:S(2)}) %collective-permute-start.8) | collective-permute-done | bytes 1310752 | tf_op jit(solution)/shard_map/ppermute | solution.py:39
  80.2 4.0 %broadcast_in_dim.26 = bf16[4,512,2,1024]{1,3,2,0:T(8,128)(2,1)} broadcast(bf16[]{:T(256)} %constant.69.clone.1), dimensions={} | broadcast | bytes 8388610 | tf_op jit(solution)/shard_map/broadcast_in_dim | solution.py:134
  89.1 2.3 slice.81
  93.3 2.3 slice.82
  96.6 12.9 %collective-permute-done.1 = bf16[512,2,1024]{0,2,1:T(8,128)(2,1)S(1)} collective-permute-done((bf16[512,2,1024]{0,2,1:T(8,128)(2,1)}, bf16[512,2,1024]{0,2,1:T(8,128)(2,1)S(1)}, u32[]{:S(2)}, u32[]{:S(2)}) %collective-permute-start.1) | collective-permute-done | bytes 2097184 | tf_op jit(solution)/shard_map/ppermute | solution.py:39
  110.5 2.3 slice.78
  112.8 2.7 collective-permute-start.4
  117.0 3.0 %bitcast_dynamic-update-slice_fusion = bf16[4,512,2,1024]{1,3,2,0:T(8,128)(2,1)} fusion(bf16[4,512,2,1024]{1,3,2,0:T(8,128)(2,1)} %bitcast_dynamic-update-slice_fusion.1, s32[]{:T(128)S(6)} %select_n.125, bf16[512,2,1024]{0,2,1:T(8,128)(2,1)} %collective-permute-done.2), kind=kLoop, calls=%fused_computation.23 | loop fusion | bytes 4194308 | tf_op jit(solution)/shard_map/dynamic_update_slice | solution.py:136
  120.0 2.8 constant_dynamic-slice_fusion.2
  122.8 2.9 fusion.2
  125.7 2.9 add_convert_fusion.1
  128.7 2.6 copy.54
  131.5 4.9 %collective-permute-done.3 = bf16[256,2,1024]{0,2,1:T(8,128)(2,1)} collective-permute-done((bf16[256,2,1024]{0,2,1:T(8,128)(2,1)}, bf16[256,2,1024]{0,2,1:T(8,128)(2,1)}, u32[]{:S(2)}, u32[]{:S(2)}) %collective-permute-start.3) | collective-permute-done | bytes 1048608 | tf_op jit(solution)/shard_map/ppermute | solution.py:39
  137.6 3.0 %fusion.14 = bf16[4,512,2,1024]{1,3,2,0:T(8,128)(2,1)} fusion(bf16[4,512,2,1024]{1,3,2,0:T(8,128)(2,1)} %bitcast_dynamic-update-slice_fusion, s32[]{:T(128)S(6)} %select_n.127, bf16[256,2,1024]{0,2,1:T(8,128)(2,1)} %collective-permute-done.4, bf16[256,2,1024]{0,2,1:T(8,128)(2,1)} %collective-permute-done.3), kind=kLoop, calls=%fused_computation.22 | loop fusion | flops 4194304 | bytes 4194308 | tf_op jit(solution)/shard_map/dynamic_update_slice | solution.py:136
  142.2 69.1 %psum.7 = f32[512]{0:T(512)S(1)} all-reduce(f32[512]{0:T(512)S(1)} %get-tuple-element.13), channel_id=1, replica_groups=mesh['zl'=2,'x'=4,'core'=2,'y'=4,'zh'=2] {'zl','x','core'}, use_global_device_ids=true, to_apply=%region_2.3 | all-reduce | flops 512 | bytes 4096 | tf_op jit(solution)/shard_map/psum | solution.py:112
  214.5 2.6 collective-permute-start.10
  219.0 1.8 fusion.43
  221.4 5.7 %fusion.27 = f32[4,2,1024,256]{3,2,1,0:T(8,128)S(1)} fusion(bf16[4,512,2,1024]{1,3,2,0:T(8,128)(2,1)} %collective-permute-done.11, bf16[256,1024]{0,1:T(8,128)(2,1)S(1)} %bitcast.80), kind=kOutput, calls=%fused_computation.50 | convolution fusion | flops 2147483648 | bytes 17039360 | tf_op jit(solution)/shard_map/qr,yrzc->yzqc/dot_general | solution.py:168
  227.1 7.8 %add_convert_fusion = bf16[4,2,1024,256]{3,2,1,0:T(8,128)(2,1)} fusion(f32[4,2,1024,256]{3,2,1,0:T(8,128)S(1)} %fusion.27, bf16[4,512,2,1024]{1,3,2,0:T(8,128)(2,1)} %fusion.14, bf16[256,1024]{0,1:T(8,128)(2,1)S(1)} %bitcast.81), kind=kOutput, calls=%fused_computation.1 | convolution fusion | flops 2151677952 | bytes 21233664 | tf_op jit(solution)/shard_map/qr,yrzc->yzqc/dot_general | solution.py:166
  234.9 54.6 %reduce-scatter.5.cloned.1.call-done = bf16[1,256,1024]{1,2,0:T(8,128)(2,1)} async-done(((bf16[8,256,1024]{1,2,0:T(8,128)(2,1)}), bf16[1,256,1024]{1,2,0:T(8,128)(2,1)}) %reduce-scatter.5.cloned.1.call-update) | async-done | bytes 524304 | tf_op jit(solution)/shard_map/reduce_scatter | solution.py:172
  (90 shorter events, 34.5 us)
Async XLA Ops:
  6.5 5.8 %copy-start.3 = (bf16[512,1024]{1,0:T(8,128)(2,1)S(1)}, bf16[512,1024]{1,0:T(8,128)(2,1)}, u32[]{:S(2)}) copy-start(bf16[512,1024]{1,0:T(8,128)(2,1)} %param.10) | copy-start | bytes 3145732
  6.5 11.1 %copy-start.4 = (bf16[1024,512]{1,0:T(8,128)(2,1)S(1)}, bf16[1024,512]{1,0:T(8,128)(2,1)}, u32[]{:S(2)}) copy-start(bf16[1024,512]{1,0:T(8,128)(2,1)} %param.8) | copy-start | bytes 3145732
  6.5 113.4 %all-gather.2.cloned.1.call-start = ((), (), s32[]{:S(2)}) async-start(), calls=%async_computation.2 | async-start | bytes 4718592 | tf_op jit(solution)/shard_map/all_gather | solution.py:110
  8.8 1.4 collective-permute-start.5
  9.5 1.9 collective-permute-start.6
  12.3 200.5 %reduce-scatter.3.cloned.1.call-start = ((), (), s32[]{:S(2)}) async-start(), calls=%async_computation.3 | async-start | bytes 3276800 | tf_op jit(solution)/shard_map/reduce_scatter | solution.py:142
  12.9 38.1 %collective-permute-start = (bf16[512,1024]{0,1:T(8,128)(2,1)S(1)}, bf16[512,1024]{0,1:T(8,128)(2,1)S(1)}, u32[]{:S(2)}, u32[]{:S(2)}) collective-permute-start(bf16[512,1024]{0,1:T(8,128)(2,1)S(1)} %copy.51), channel_id=1, source_target_pairs={{0,1},{1,0},{2,3},{3,2},{4,5},{5,4},{6,7},{7,6},{8,9},{9,8},{10,11... | collective-permute-start | bytes 3145736 | tf_op jit(solution)/shard_map/ppermute | solution.py:39
  18.8 60.5 %collective-permute-start.8 = (bf16[1024,640]{1,0:T(8,128)(2,1)}, bf16[1024,640]{1,0:T(8,128)(2,1)}, u32[]{:S(2)}, u32[]{:S(2)}) collective-permute-start(bf16[1024,640]{1,0:T(8,128)(2,1)} %pad_maximum_fusion), channel_id=1, source_target_pairs={{0,1},{1,0},{2,3},{3,2},{4,5},{5,4},{6,7},{7,6},{8,9},{9,8},{10,11... | collective-permute-start | bytes 3932168 | tf_op jit(solution)/shard_map/ppermute | solution.py:39
  53.7 55.7 %collective-permute-start.1 = (bf16[512,2,1024]{0,2,1:T(8,128)(2,1)}, bf16[512,2,1024]{0,2,1:T(8,128)(2,1)S(1)}, u32[]{:S(2)}, u32[]{:S(2)}) collective-permute-start(bf16[512,2,1024]{0,2,1:T(8,128)(2,1)} %maximum_select_fusion.1), channel_id=1, source_target_pairs={{0,2},{1,3},{2,4},{3,5},{4,6},{5,7},{6,0},{7,1},{8,10},{9,11},{10,... | collective-permute-start | bytes 6291464 | tf_op jit(solution)/shard_map/ppermute | solution.py:39
  59.7 50.8 %collective-permute-start.2 = (bf16[512,2,1024]{0,2,1:T(8,128)(2,1)}, bf16[512,2,1024]{0,2,1:T(8,128)(2,1)}, u32[]{:S(2)}, u32[]{:S(2)}) collective-permute-start(bf16[512,2,1024]{0,2,1:T(8,128)(2,1)} %maximum_select_fusion.1), channel_id=1, source_target_pairs={{0,6},{1,7},{2,0},{3,1},{4,2},{5,3},{6,4},{7,5},{8,14},{9,15},{10,... | collective-permute-start | bytes 6291464 | tf_op jit(solution)/shard_map/ppermute | solution.py:39
  63.3 22.6 %collective-permute-start.7 = (bf16[1024,640]{1,0:T(8,128)(2,1)}, bf16[1024,640]{1,0:T(8,128)(2,1)}, u32[]{:S(2)}, u32[]{:S(2)}) collective-permute-start(bf16[1024,640]{1,0:T(8,128)(2,1)} %pad_maximum_fusion), channel_id=1, source_target_pairs={{0,8},{1,9},{2,10},{3,11},{4,12},{5,13},{6,14},{7,15},{8,0},{9,1},... | collective-permute-start | bytes 3932168 | tf_op jit(solution)/shard_map/ppermute | solution.py:39
  79.3 13.1 %collective-permute-start.9 = (bf16[1024,640]{1,0:T(8,128)(2,1)}, bf16[1024,640]{1,0:T(8,128)(2,1)}, u32[]{:S(2)}, u32[]{:S(2)}) collective-permute-start(bf16[1024,640]{1,0:T(8,128)(2,1)} %collective-permute-done.8), channel_id=1, source_target_pairs={{0,8},{1,9},{2,10},{3,11},{4,12},{5,13},{6,14},{7,15},{8,0},{9,1},... | collective-permute-start | bytes 3932168 | tf_op jit(solution)/shard_map/ppermute | solution.py:39
  80.2 4.0 %copy-start.1 = (bf16[512,1024]{0,1:T(8,128)(2,1)S(1)}, bf16[512,1024]{0,1:T(8,128)(2,1)}, u32[]{:S(2)}) copy-start(bf16[512,1024]{0,1:T(8,128)(2,1)} %copy-done) | copy-start | bytes 3145732
  110.5 25.9 %collective-permute-start.3 = (bf16[256,2,1024]{0,2,1:T(8,128)(2,1)}, bf16[256,2,1024]{0,2,1:T(8,128)(2,1)}, u32[]{:S(2)}, u32[]{:S(2)}) collective-permute-start(bf16[256,2,1024]{0,2,1:T(8,128)(2,1)} %slice.77), channel_id=1, source_target_pairs={{0,2},{1,3},{2,4},{3,5},{4,6},{5,7},{6,0},{7,1},{8,10},{9,11},{10,... | collective-permute-start | bytes 3145736 | tf_op jit(solution)/shard_map/ppermute | solution.py:39
  112.8 24.8 %collective-permute-start.4 = (bf16[256,2,1024]{0,2,1:T(8,128)(2,1)}, bf16[256,2,1024]{0,2,1:T(8,128)(2,1)}, u32[]{:S(2)}, u32[]{:S(2)}) collective-permute-start(bf16[256,2,1024]{0,2,1:T(8,128)(2,1)} %slice.78), channel_id=1, source_target_pairs={{0,6},{1,7},{2,0},{3,1},{4,2},{5,3},{6,4},{7,5},{8,14},{9,15},{10,... | collective-permute-start | bytes 3145736 | tf_op jit(solution)/shard_map/ppermute | solution.py:39
  120.0 2.8 copy-start.8
  122.8 2.9 copy-start.6
  122.8 2.9 copy-start.7
  122.8 2.9 copy-start.9
  131.3 158.3 %reduce-scatter.5.cloned.1.call-start = ((), (), s32[]{:S(2)}) async-start(), calls=%async_computation.4 | async-start | bytes 4718592 | tf_op jit(solution)/shard_map/reduce_scatter | solution.py:172
  140.6 80.7 %collective-permute-start.11 = (bf16[4,512,2,1024]{1,3,2,0:T(8,128)(2,1)}, bf16[4,512,2,1024]{1,3,2,0:T(8,128)(2,1)}, u32[]{:S(2)}, u32[]{:S(2)}) collective-permute-start(bf16[4,512,2,1024]{1,3,2,0:T(8,128)(2,1)} %fusion.14), channel_id=1, source_target_pairs={{0,8},{1,9},{2,10},{3,11},{4,12},{5,13},{6,14},{7,15},{8,0},{9,1},... | collective-permute-start | bytes 25165832 | tf_op jit(solution)/shard_map/ppermute | solution.py:39
  214.5 3.7 %collective-permute-start.10 = (bf16[256,256]{0,1:T(8,128)(2,1)S(1)}, bf16[256,256]{0,1:T(8,128)(2,1)S(1)}, u32[]{:S(2)}, u32[]{:S(2)}) collective-permute-start(bf16[256,256]{0,1:T(8,128)(2,1)S(1)} %pad_maximum_fusion.2), channel_id=1, source_target_pairs={{0,8},{1,9},{2,10},{3,11},{4,12},{5,13},{6,14},{7,15},{8,0},{9,1},... | collective-permute-start | bytes 393224 | tf_op jit(solution)/shard_map/ppermute | solution.py:39
  234.9 57.7 %copy-start.2 = (bf16[512,512]{1,0:T(8,128)(2,1)S(1)}, bf16[512,512]{1,0:T(8,128)(2,1)}, u32[]{:S(2)}) copy-start(bf16[512,512]{1,0:T(8,128)(2,1)} %param.6) | copy-start | bytes 1572868
  290.7 1.9 collective-permute-start.12
  (2 other events, 3.8 us)
Sparse Core Ops, SparseCore 0:
  12.5 68.2 all-gather.1
  131.4 72.4 reduce-scatter.2
  235.1 54.4 reduce-scatter.4

commit v2 on v1

--- a/solution.py
+++ b/solution.py
@@ -45,6 +45,18 @@
 
 def zh_swap(value):
     return send(value, lambda c: dict(zh=1 - c["zh"]))
+
+
+def zl_swap(value):
+    return send(value, lambda c: dict(zl=1 - c["zl"]))
+
+
+def x_shift(value, k):
+    return send(value, lambda c: dict(x=c["x"] + k))
+
+
+def after(value, other):
+    return lax.optimization_barrier((value, other))[0]
 
 
 def y_shift(value, k):
@@ -97,9 +109,15 @@
 def local(tokens, norm_gain, query_weight, kv_weight, out_weight, lengths):
     core = lax.axis_index("core")
     chip = lax.axis_index(("zl", "x"))
+    zl = lax.axis_index("zl")
+    x = lax.axis_index("x")
     y = lax.axis_index("y")
     zh = lax.axis_index("zh")
     is_first = core == 0
+
+    kv_own = lax.dynamic_slice_in_dim(kv_weight, chip * 256 + core * 128, 128, 1)
+    near = jnp.concatenate([query_weight, kv_own], axis=1)
+    far = zh_swap(near)
 
     gain = lax.dynamic_slice_in_dim(norm_gain, (chip * 2 + core) * 512, 512, 0)
     wide = tokens.astype(jnp.float32)
@@ -107,13 +125,34 @@
     mine = send(half_of(gained, core), to_slice(0))
     theirs = send(half_of(gained, 1 - core), to_slice(1))
     block = ordered(is_first, mine, theirs, 1)
-    gathered = lax.all_gather(block, ("zl", "x"), axis=0, tiled=False)
+
+    beside = zl_swap(block)
+    left = x_shift(block, 1)
+    right = x_shift(block, -1)
+    squares = lax.psum(after(jnp.sum(wide * wide, axis=-1), block), ("zl", "x", "core"))
+    left, right, beside, squares = lax.optimization_barrier((left, right, beside, squares))
+    beside_left = x_shift(beside, 1)
+    beside_right = x_shift(beside, -1)
+    opposite = jnp.concatenate([x_shift(left[:128], 1), x_shift(right[128:], -1)], 0)
+    beside_opposite = jnp.concatenate(
+        [x_shift(beside_left[:128], 1), x_shift(beside_right[128:], -1)], 0
+    )
+    gathered = jnp.zeros((2, 4, HALF, 1024), jnp.bfloat16)
+    for dz, dx, part in (
+        (0, 0, block),
+        (0, 3, left),
+        (0, 1, right),
+        (1, 0, beside),
+        (0, 2, opposite),
+        (1, 3, beside_left),
+        (1, 1, beside_right),
+        (1, 2, beside_opposite),
+    ):
+        gathered = lax.dynamic_update_slice(
+            gathered, part[None, None], (zl ^ dz, (x + dx) % 4, 0, 0)
+        )
     gathered = gathered.reshape(4, 2, HALF, 1024)
-    squares = lax.psum(jnp.sum(wide * wide, axis=-1), ("zl", "x", "core"))
-
-    kv_own = lax.dynamic_slice_in_dim(kv_weight, chip * 256 + core * 128, 128, 1)
-    near = jnp.concatenate([query_weight, kv_own], axis=1)
-    far = zh_swap(near)
+
     near_other = core_swap(near)
     far_other = core_swap(far)
 
@@ -124,17 +163,16 @@
     near_whole = whole(near, near_other)
     far_whole = whole(far, far_other)
 
-    out_far = zh_swap(out_weight)
-    pair = ordered(zh == 0, out_weight[:, None], out_far[:, None], 1)
-    up = y_shift(pair, 1)
-    down = y_shift(pair, -1)
-    across_a = y_shift(up[:256], 1)
-    across_b = y_shift(down[256:], -1)
-    across = jnp.concatenate([across_a, across_b], 0)
-    own_rows = jnp.zeros((4, 512, 2, 1024), jnp.bfloat16)
-    for k, part in ((0, pair), (3, up), (1, down), (2, across)):
-        own_rows = lax.dynamic_update_slice(own_rows, part[None], ((y + k) % 4, 0, 0, 0))
-    other_rows = core_swap(own_rows)
+    out_near = lax.all_gather(out_weight, "y", axis=0, tiled=False)
+    far_own = zh_swap(after(out_weight, far))
+    up = y_shift(far_own, 1)
+    down = y_shift(far_own, -1)
+    across = jnp.concatenate([y_shift(up[:256], 1), y_shift(down[256:], -1)], 0)
+    out_far = jnp.zeros((4, 512, 1024), jnp.bfloat16)
+    for k, part in ((0, far_own), (3, up), (1, down), (2, across)):
+        out_far = lax.dynamic_update_slice(out_far, part[None], ((y + k) % 4, 0, 0))
+    out_near_other = core_swap(out_near)
+    out_far_other = core_swap(out_far)
 
     rows_near = lax.dynamic_index_in_dim(gathered, zh, 1, keepdims=False).reshape(1024, 1024)
     rows_far = lax.dynamic_index_in_dim(gathered, 1 - zh, 1, keepdims=False).reshape(1024, 1024)
@@ -163,12 +201,16 @@
     attended = jnp.einsum("hqk,kd->qhd", probs, values, preferred_element_type=jnp.float32)
     attended = attended.astype(jnp.bfloat16).reshape(HALF, 1024)
 
-    partial = jnp.einsum(
-        "qr,yrzc->yzqc", attended[:, :512], own_rows, preferred_element_type=jnp.float32
-    ) + jnp.einsum(
-        "qr,yrzc->yzqc", attended[:, 512:], other_rows, preferred_element_type=jnp.float32
-    )
-    partial = partial.astype(jnp.bfloat16).reshape(8, HALF, 1024)
+    def columns(own, other):
+        return jnp.einsum(
+            "qr,yrc->yqc", attended[:, :512], own, preferred_element_type=jnp.float32
+        ) + jnp.einsum(
+            "qr,yrc->yqc", attended[:, 512:], other, preferred_element_type=jnp.float32
+        )
+
+    near_part = columns(out_near, out_near_other).astype(jnp.bfloat16)[:, None]
+    far_part = columns(out_far, out_far_other).astype(jnp.bfloat16)[:, None]
+    partial = ordered(zh == 0, near_part, far_part, 1).reshape(8, HALF, 1024)
     mixed = lax.psum_scatter(partial, ("zl", "x"), scatter_dimension=0, tiled=False)
     keep = half_of(mixed, core, 1)
     got = core_swap(half_of(mixed, 1 - core, 1))

time: 304 us -> 280 us (0.921)
  blocking collectives: 69.1 us -> 24.6 us
  starting transfers between devices: 23.4 us -> 54.3 us
  local copies, waits for them, and re-layouts: 31.7 us -> 24.1 us
  other arithmetic: 17.2 us -> 11.4 us
    psum x1, blocking collectives: 69.1 us -> 24.6 us  [local(): lax.psum(after(jnp.sum(wide * wide, axis=-1), block), ('zl', 'x', 'core'))]
    ppermute x13 -> x23, starting transfers between devices: 23.1 us -> 54.3 us  [send(): return lax.ppermute(value, AXES, pairs(change))]
    slice x3 -> x4, local copies, waits for them, and re-layouts: 5.85 us -> 0.9 us  [whole(): return jnp.concatenate([own[:, :512], other[:, :512], kv], axis=1)]
    ppermute x13 -> x23, waiting for transfers between devices: 69.5 us -> 74.1 us  [send(): return lax.ppermute(value, AXES, pairs(change))]
    dynamic_update_slice x2 -> x4, other arithmetic: 4.78 us -> 1.3 us  [the longest x1 1.06 us: local(): out_far = lax.dynamic_update_slice(out_far, part[None], ((y + k) % 4, 0, 0))]
    dot_general x2 -> x4, matrix products: 13.5 us -> 12 us  [the longest x2 7.1 us: columns(): jnp.einsum('qr,yrc->yqc', attended[:, 512:], other, preferred_element_typ...]
  transfers between devices with their start and end apart: 16 -> 26, of which waited for: 8 -> 11; matrix products, arithmetic and copies ran while one was open for 16% -> 16% of each run, Pallas kernels for 0% -> 0%
where the time goes in v2:
time: 280 us; the launch traced here: 276 us
  waiting for transfers between devices  127 us (45%)
  starting transfers between devices  54.3 us (19%)
  blocking collectives  24.6 us (9%)
  local copies, waits for them, and re-layouts  24.1 us (9%)
  matrix products  20.5 us (7%)
  between operations  14.3 us (5%)
  other arithmetic  11.4 us (4%)
    ppermute x23, waiting for transfers between devices, send(): return lax.ppermute(value, AXES, pairs(change))  74.1 us
    ppermute x23, starting transfers between devices, send(): return lax.ppermute(value, AXES, pairs(change))  54.3 us
    reduce_scatter x1, waiting for transfers between devices, local(): lax.psum_scatter(partial, ('zl', 'x'), scatter_dimension=0, tiled=False)  52 us
    psum x1, blocking collectives, local(): lax.psum(after(jnp.sum(wide * wide, axis=-1), block), ('zl', 'x', 'core'))  24.6 us
    dot_general x2, matrix products, dot(): return jnp.dot(a, b, preferred_element_type=jnp.float32)  7.33 us
    dot_general x2, matrix products, columns(): jnp.einsum('qr,yrc->yqc', attended[:, 512:], other, preferred_element_typ...  7.1 us
  transfers between devices with their start and end apart: 26, of which 11 were waited for; matrix products, arithmetic and copies ran while one was open for 16% of the time, Pallas kernels for 0%

profile of v2, /device:TPU:3, one launch (start us, length us, event | category | flops | bytes accessed | tf_op | source)
XLA Modules:
  0.0 276.1 jit_solution(10451417300669560083)
XLA Ops:
  12.9 16.7 %collective-permute-start.2 = (bf16[256,1024]{1,0:T(8,128)(2,1)}, bf16[256,1024]{1,0:T(8,128)(2,1)}, u32[]{:S(2)}, u32[]{:S(2)}) collective-permute-start(bf16[256,1024]{1,0:T(8,128)(2,1)} %maximum_select_fusion.2), channel_id=1, source_target_pairs={{0,16},{1,17},{2,18},{3,19},{4,20},{5,21},{6,22},{7,23},{8,24},{9,... | collective-permute-start | bytes 1572872 | tf_op jit(solution)/shard_map/ppermute | solution.py:39
  29.7 4.7 %collective-permute-start.4 = (bf16[256,1024]{1,0:T(8,128)(2,1)}, bf16[256,1024]{1,0:T(8,128)(2,1)}, u32[]{:S(2)}, u32[]{:S(2)}) collective-permute-start(bf16[256,1024]{1,0:T(8,128)(2,1)} %maximum_select_fusion.2), channel_id=1, source_target_pairs={{0,64},{1,65},{2,66},{3,67},{4,68},{5,69},{6,70},{7,71},{8,72},{9,... | collective-permute-start | bytes 1572872 | tf_op jit(solution)/shard_map/ppermute | solution.py:39
  37.2 4.6 %collective-permute-start.12 = (bf16[1024,640]{1,0:T(8,128)(2,1)}, bf16[1024,640]{1,0:T(8,128)(2,1)S(1)}, u32[]{:S(2)}, u32[]{:S(2)}) collective-permute-start(bf16[1024,640]{1,0:T(8,128)(2,1)} %pad_maximum_fusion), channel_id=1, source_target_pairs={{0,1},{1,0},{2,3},{3,2},{4,5},{5,4},{6,7},{7,6},{8,9},{9,8},{10,11... | collective-permute-start | bytes 3932168 | tf_op jit(solution)/shard_map/ppermute | solution.py:39
  41.8 24.6 %psum.7 = f32[512]{0:T(512)S(1)} all-reduce(f32[512]{0:T(512)S(1)} %get-tuple-element.11), channel_id=1, replica_groups=mesh['zl'=2,'x'=4,'core'=2,'y'=4,'zh'=2] {'zl','x','core'}, use_global_device_ids=true, to_apply=%region_1.2 | all-reduce | flops 512 | bytes 4096 | tf_op jit(solution)/shard_map/psum | solution.py:132
  69.1 4.3 %collective-permute-start.7 = (bf16[256,1024]{1,0:T(8,128)(2,1)}, bf16[256,1024]{1,0:T(8,128)(2,1)S(1)}, u32[]{:S(2)}, u32[]{:S(2)}) collective-permute-start(bf16[256,1024]{1,0:T(8,128)(2,1)} %collective-permute-done.4), channel_id=1, source_target_pairs={{0,16},{1,17},{2,18},{3,19},{4,20},{5,21},{6,22},{7,23},{8,24},{9,... | collective-permute-start | bytes 1572872 | tf_op jit(solution)/shard_map/ppermute | solution.py:39
  74.5 3.1 %collective-permute-done.5 = bf16[128,1024]{1,0:T(8,128)(2,1)S(1)} collective-permute-done((bf16[128,1024]{1,0:T(8,128)(2,1)S(1)}, bf16[128,1024]{1,0:T(8,128)(2,1)S(1)}, u32[]{:S(2)}, u32[]{:S(2)}) %collective-permute-start.5) | collective-permute-done | bytes 262176 | tf_op jit(solution)/shard_map/ppermute | solution.py:39
  77.6 2.3 collective-permute-start.6
  81.0 10.4 %collective-permute-done.6 = bf16[128,1024]{1,0:T(8,128)(2,1)S(1)} collective-permute-done((bf16[128,1024]{1,0:T(8,128)(2,1)S(1)}, bf16[128,1024]{1,0:T(8,128)(2,1)S(1)}, u32[]{:S(2)}, u32[]{:S(2)}) %collective-permute-start.6) | collective-permute-done | bytes 262176 | tf_op jit(solution)/shard_map/ppermute | solution.py:39
  93.2 2.9 %collective-permute-start.13 = (bf16[1024,640]{1,0:T(8,128)(2,1)S(1)}, bf16[1024,640]{1,0:T(8,128)(2,1)S(1)}, u32[]{:S(2)}, u32[]{:S(2)}) collective-permute-start(bf16[1024,640]{1,0:T(8,128)(2,1)S(1)} %collective-permute-done.12), channel_id=1, source_target_pairs={{0,8},{1,9},{2,10},{3,11},{4,12},{5,13},{6,14},{7,15},{8,0},{9,1},... | collective-permute-start | bytes 3932168 | tf_op jit(solution)/shard_map/ppermute | solution.py:39
  100.6 2.9 %fusion.2 = f32[1024,1280]{1,0:T(8,128)S(1)} fusion(bf16[1024,1024]{1,0:T(8,128)(2,1)S(1)} %bitcast.103, bf16[1024,256]{1,0:T(8,128)(2,1)S(1)} %maximum_select_fusion.3, bf16[1024,512]{1,0:T(8,128)(2,1)S(1)} %slice-done, bf16[1024,512]{1,0:T(8,128)(2,1)S(1)} %copy-done.5), kind=kOutput, calls=%fused_computation.9 | convolution fusion | flops 2692218880 | bytes 9961472 | tf_op jit(solution)/shard_map/dot_general | solution.py:106
  103.8 4.5 %add_convert_fusion = bf16[1024,1280]{1,0:T(8,128)(2,1)} fusion(f32[1024,1280]{1,0:T(8,128)S(1)} %fusion.2, bf16[1024,1024]{1,0:T(8,128)(2,1)S(1)} %bitcast.102, bf16[1024,256]{1,0:T(8,128)(2,1)S(1)} %maximum_select_fusion.4, bf16[1024,512]{1,0:T(8,128)(2,1)S(1)} %slice.100, bf16[1024,512]{1,0:T(8,128)(2,1)S(1)} %slice.99), kind=kOutput, calls=%fused_computation.1 | convolution fusion | flops 2694840320 | bytes 12582912 | tf_op jit(solution)/shard_map/dot_general | solution.py:106
  108.3 4.5 %copy.35 = bf16[4,256,1280]{1,2,0:T(8,128)(2,1)} copy(bf16[4,256,1280]{2,1,0:T(8,128)(2,1)} %bitcast.101) | data formatting | bytes 5242880 | tf_op jit(solution)/shard_map/reshape | solution.py:181
  113.4 4.9 %collective-permute-start.16 = (bf16[512,1024]{0,1:T(8,128)(2,1)S(1)}, bf16[512,1024]{0,1:T(8,128)(2,1)S(1)}, u32[]{:S(2)}, u32[]{:S(2)}) collective-permute-start(bf16[512,1024]{0,1:T(8,128)(2,1)S(1)} %copy.42), channel_id=1, source_target_pairs={{0,1},{1,0},{2,3},{3,2},{4,5},{5,4},{6,7},{7,6},{8,9},{9,8},{10,11... | collective-permute-start | bytes 3145736 | tf_op jit(solution)/shard_map/ppermute | solution.py:39
  119.0 21.3 %collective-permute-done.16 = bf16[512,1024]{0,1:T(8,128)(2,1)S(1)} collective-permute-done((bf16[512,1024]{0,1:T(8,128)(2,1)S(1)}, bf16[512,1024]{0,1:T(8,128)(2,1)S(1)}, u32[]{:S(2)}, u32[]{:S(2)}) %collective-permute-start.16) | collective-permute-done | bytes 1048608 | tf_op jit(solution)/shard_map/ppermute | solution.py:39
  140.3 2.7 collective-permute-start.18
  146.5 23.1 %collective-permute-done.17 = bf16[512,1024]{0,1:T(8,128)(2,1)S(1)} collective-permute-done((bf16[512,1024]{0,1:T(8,128)(2,1)S(1)}, bf16[512,1024]{0,1:T(8,128)(2,1)S(1)}, u32[]{:S(2)}, u32[]{:S(2)}) %collective-permute-start.17) | collective-permute-done | bytes 1048608 | tf_op jit(solution)/shard_map/ppermute | solution.py:39
  169.8 2.7 collective-permute-start.20
  174.6 8.5 %collective-permute-done.19 = bf16[256,1024]{0,1:T(8,128)(2,1)S(1)} collective-permute-done((bf16[256,1024]{0,1:T(8,128)(2,1)S(1)}, bf16[256,1024]{0,1:T(8,128)(2,1)S(1)}, u32[]{:S(2)}, u32[]{:S(2)}) %collective-permute-start.19) | collective-permute-done | bytes 524320 | tf_op jit(solution)/shard_map/ppermute | solution.py:39
  190.6 2.9 %collective-permute-done.14 = bf16[256,256]{0,1:T(8,128)(2,1)S(1)} collective-permute-done((bf16[256,256]{0,1:T(8,128)(2,1)S(1)}, bf16[256,256]{0,1:T(8,128)(2,1)S(1)}, u32[]{:S(2)}, u32[]{:S(2)}) %collective-permute-start.14) | collective-permute-done | bytes 131104 | tf_op jit(solution)/shard_map/ppermute | solution.py:39
  199.7 3.5 %fusion.32 = f32[4,1024,256]{1,2,0:T(8,128)S(1)} fusion(bf16[4,512,1024]{1,2,0:T(8,128)(2,1)} %collective-permute-done.21, bf16[256,1024]{0,1:T(8,128)(2,1)S(1)} %bitcast.105), kind=kOutput, calls=%fused_computation.68 | convolution fusion | flops 1073741824 | bytes 8650752 | tf_op jit(solution)/shard_map/qr,yrc->yqc/dot_general | solution.py:207
  203.2 3.6 %fusion.18 = bf16[4,1,256,1024]{3,2,0,1:T(8,128)(2,1)S(1)} fusion(f32[4,1024,256]{1,2,0:T(8,128)S(1)} %fusion.32, bf16[4,512,1024]{1,2,0:T(8,128)(2,1)} %fusion.23, bf16[256,1024]{0,1:T(8,128)(2,1)S(1)} %bitcast.106), kind=kOutput, calls=%fused_computation.25 | convolution fusion | flops 1075838976 | bytes 10747904 | tf_op jit(solution)/shard_map/qr,yrc->yqc/dot_general | solution.py:205
  206.8 3.6 %fusion.17 = bf16[4,1,256,1024]{3,2,0,1:T(8,128)(2,1)S(1)} fusion(f32[256,4,1024]{2,0,1:T(8,128)S(1)} %fusion.31, bf16[4,512,1024]{2,1,0:T(8,128)(2,1)} %collective-permute-done.15, bf16[256,1024]{0,1:T(8,128)(2,1)S(1)} %bitcast.107), kind=kOutput, calls=%fused_computation.24 | convolution fusion | flops 1075838976 | bytes 10747904 | tf_op jit(solution)/shard_map/qr,yrc->yqc/dot_general | solution.py:207
  211.1 2.4 copy.45
  213.5 52.0 %reduce-scatter.5.cloned.1.call-done = bf16[1,256,1024]{2,1,0:T(8,128)(2,1)} async-done(((bf16[8,256,1024]{2,1,0:T(8,128)(2,1)}), bf16[1,256,1024]{2,1,0:T(8,128)(2,1)}) %reduce-scatter.5.cloned.1.call-update) | async-done | bytes 524304 | tf_op jit(solution)/shard_map/reduce_scatter | solution.py:214
  (125 shorter events, 45.1 us)
Async XLA Ops:
  6.5 180.4 %all-gather.3.cloned.1.call-start = ((), (), s32[]{:S(2)}) async-start(), calls=%async_computation.4 | async-start | bytes 5242880 | tf_op jit(solution)/shard_map/all_gather | solution.py:166
  7.3 179.8 %reduce-scatter.3.cloned.1.call-start = ((), (), s32[]{:S(2)}) async-start(), calls=%async_computation.2 | async-start | bytes 3276800 | tf_op jit(solution)/shard_map/reduce_scatter | solution.py:180
  10.1 1.9 collective-permute-start.1
  12.9 53.5 %collective-permute-start.2 = (bf16[256,1024]{1,0:T(8,128)(2,1)}, bf16[256,1024]{1,0:T(8,128)(2,1)}, u32[]{:S(2)}, u32[]{:S(2)}) collective-permute-start(bf16[256,1024]{1,0:T(8,128)(2,1)} %maximum_select_fusion.2), channel_id=1, source_target_pairs={{0,16},{1,17},{2,18},{3,19},{4,20},{5,21},{6,22},{7,23},{8,24},{9,... | collective-permute-start | bytes 1572872 | tf_op jit(solution)/shard_map/ppermute | solution.py:39
  29.7 36.8 %collective-permute-start.3 = (bf16[256,1024]{1,0:T(8,128)(2,1)}, bf16[256,1024]{1,0:T(8,128)(2,1)S(1)}, u32[]{:S(2)}, u32[]{:S(2)}) collective-permute-start(bf16[256,1024]{1,0:T(8,128)(2,1)} %maximum_select_fusion.2), channel_id=1, source_target_pairs={{0,48},{1,49},{2,50},{3,51},{4,52},{5,53},{6,54},{7,55},{8,56},{9,... | collective-permute-start | bytes 1572872 | tf_op jit(solution)/shard_map/ppermute | solution.py:39
  29.7 36.8 %collective-permute-start.4 = (bf16[256,1024]{1,0:T(8,128)(2,1)}, bf16[256,1024]{1,0:T(8,128)(2,1)}, u32[]{:S(2)}, u32[]{:S(2)}) collective-permute-start(bf16[256,1024]{1,0:T(8,128)(2,1)} %maximum_select_fusion.2), channel_id=1, source_target_pairs={{0,64},{1,65},{2,66},{3,67},{4,68},{5,69},{6,70},{7,71},{8,72},{9,... | collective-permute-start | bytes 1572872 | tf_op jit(solution)/shard_map/ppermute | solution.py:39
  36.6 56.6 %collective-permute-start.11 = (bf16[1024,640]{1,0:T(8,128)(2,1)}, bf16[1024,640]{1,0:T(8,128)(2,1)S(1)}, u32[]{:S(2)}, u32[]{:S(2)}) collective-permute-start(bf16[1024,640]{1,0:T(8,128)(2,1)} %pad_maximum_fusion), channel_id=1, source_target_pairs={{0,8},{1,9},{2,10},{3,11},{4,12},{5,13},{6,14},{7,15},{8,0},{9,1},... | collective-permute-start | bytes 3932168 | tf_op jit(solution)/shard_map/ppermute | solution.py:39
  37.2 56.0 %collective-permute-start.12 = (bf16[1024,640]{1,0:T(8,128)(2,1)}, bf16[1024,640]{1,0:T(8,128)(2,1)S(1)}, u32[]{:S(2)}, u32[]{:S(2)}) collective-permute-start(bf16[1024,640]{1,0:T(8,128)(2,1)} %pad_maximum_fusion), channel_id=1, source_target_pairs={{0,1},{1,0},{2,3},{3,2},{4,5},{5,4},{6,7},{7,6},{8,9},{9,8},{10,11... | collective-permute-start | bytes 3932168 | tf_op jit(solution)/shard_map/ppermute | solution.py:39
  67.5 10.1 %collective-permute-start.5 = (bf16[128,1024]{1,0:T(8,128)(2,1)S(1)}, bf16[128,1024]{1,0:T(8,128)(2,1)S(1)}, u32[]{:S(2)}, u32[]{:S(2)}) collective-permute-start(bf16[128,1024]{1,0:T(8,128)(2,1)S(1)} %slice.72), channel_id=1, source_target_pairs={{0,16},{1,17},{2,18},{3,19},{4,20},{5,21},{6,22},{7,23},{8,24},{9,... | collective-permute-start | bytes 786440 | tf_op jit(solution)/shard_map/ppermute | solution.py:39
  69.1 23.5 %collective-permute-start.7 = (bf16[256,1024]{1,0:T(8,128)(2,1)}, bf16[256,1024]{1,0:T(8,128)(2,1)S(1)}, u32[]{:S(2)}, u32[]{:S(2)}) collective-permute-start(bf16[256,1024]{1,0:T(8,128)(2,1)} %collective-permute-done.4), channel_id=1, source_target_pairs={{0,16},{1,17},{2,18},{3,19},{4,20},{5,21},{6,22},{7,23},{8,24},{9,... | collective-permute-start | bytes 1572872 | tf_op jit(solution)/shard_map/ppermute | solution.py:39
  73.4 18.2 %collective-permute-start.8 = (bf16[256,1024]{1,0:T(8,128)(2,1)}, bf16[256,1024]{1,0:T(8,128)(2,1)S(1)}, u32[]{:S(2)}, u32[]{:S(2)}) collective-permute-start(bf16[256,1024]{1,0:T(8,128)(2,1)} %collective-permute-done.4), channel_id=1, source_target_pairs={{0,48},{1,49},{2,50},{3,51},{4,52},{5,53},{6,54},{7,55},{8,56},{9,... | collective-permute-start | bytes 1572872 | tf_op jit(solution)/shard_map/ppermute | solution.py:39
  77.6 13.9 %collective-permute-start.6 = (bf16[128,1024]{1,0:T(8,128)(2,1)S(1)}, bf16[128,1024]{1,0:T(8,128)(2,1)S(1)}, u32[]{:S(2)}, u32[]{:S(2)}) collective-permute-start(bf16[128,1024]{1,0:T(8,128)(2,1)S(1)} %slice.73), channel_id=1, source_target_pairs={{0,48},{1,49},{2,50},{3,51},{4,52},{5,53},{6,54},{7,55},{8,56},{9,... | collective-permute-start | bytes 786440 | tf_op jit(solution)/shard_map/ppermute | solution.py:39
  91.6 5.8 %collective-permute-start.10 = (bf16[128,1024]{1,0:T(8,128)(2,1)S(1)}, bf16[128,1024]{1,0:T(8,128)(2,1)S(1)}, u32[]{:S(2)}, u32[]{:S(2)}) collective-permute-start(bf16[128,1024]{1,0:T(8,128)(2,1)S(1)} %slice.96), channel_id=1, source_target_pairs={{0,48},{1,49},{2,50},{3,51},{4,52},{5,53},{6,54},{7,55},{8,56},{9,... | collective-permute-start | bytes 786440 | tf_op jit(solution)/shard_map/ppermute | solution.py:39
  92.7 6.4 %collective-permute-start.9 = (bf16[128,1024]{1,0:T(8,128)(2,1)S(1)}, bf16[128,1024]{1,0:T(8,128)(2,1)S(1)}, u32[]{:S(2)}, u32[]{:S(2)}) collective-permute-start(bf16[128,1024]{1,0:T(8,128)(2,1)S(1)} %slice.95), channel_id=1, source_target_pairs={{0,16},{1,17},{2,18},{3,19},{4,20},{5,21},{6,22},{7,23},{8,24},{9,... | collective-permute-start | bytes 786440 | tf_op jit(solution)/shard_map/ppermute | solution.py:39
  93.2 10.3 %collective-permute-start.13 = (bf16[1024,640]{1,0:T(8,128)(2,1)S(1)}, bf16[1024,640]{1,0:T(8,128)(2,1)S(1)}, u32[]{:S(2)}, u32[]{:S(2)}) collective-permute-start(bf16[1024,640]{1,0:T(8,128)(2,1)S(1)} %collective-permute-done.12), channel_id=1, source_target_pairs={{0,8},{1,9},{2,10},{3,11},{4,12},{5,13},{6,14},{7,15},{8,0},{9,1},... | collective-permute-start | bytes 3932168 | tf_op jit(solution)/shard_map/ppermute | solution.py:39
  112.8 152.8 %reduce-scatter.5.cloned.1.call-start = ((), (), s32[]{:S(2)}) async-start(), calls=%async_computation.3 | async-start | bytes 4718592 | tf_op jit(solution)/shard_map/reduce_scatter | solution.py:214
  113.4 26.9 %collective-permute-start.16 = (bf16[512,1024]{0,1:T(8,128)(2,1)S(1)}, bf16[512,1024]{0,1:T(8,128)(2,1)S(1)}, u32[]{:S(2)}, u32[]{:S(2)}) collective-permute-start(bf16[512,1024]{0,1:T(8,128)(2,1)S(1)} %copy.42), channel_id=1, source_target_pairs={{0,1},{1,0},{2,3},{3,2},{4,5},{5,4},{6,7},{7,6},{8,9},{9,8},{10,11... | collective-permute-start | bytes 3145736 | tf_op jit(solution)/shard_map/ppermute | solution.py:39
  140.3 29.3 %collective-permute-start.17 = (bf16[512,1024]{0,1:T(8,128)(2,1)S(1)}, bf16[512,1024]{0,1:T(8,128)(2,1)S(1)}, u32[]{:S(2)}, u32[]{:S(2)}) collective-permute-start(bf16[512,1024]{0,1:T(8,128)(2,1)S(1)} %collective-permute-done.16), channel_id=1, source_target_pairs={{0,2},{1,3},{2,4},{3,5},{4,6},{5,7},{6,0},{7,1},{8,10},{9,11},{10,... | collective-permute-start | bytes 3145736 | tf_op jit(solution)/shard_map/ppermute | solution.py:39
  140.3 29.5 %collective-permute-start.18 = (bf16[512,1024]{0,1:T(8,128)(2,1)S(1)}, bf16[512,1024]{0,1:T(8,128)(2,1)S(1)}, u32[]{:S(2)}, u32[]{:S(2)}) collective-permute-start(bf16[512,1024]{0,1:T(8,128)(2,1)S(1)} %collective-permute-done.16), channel_id=1, source_target_pairs={{0,6},{1,7},{2,0},{3,1},{4,2},{5,3},{6,4},{7,5},{8,14},{9,15},{10,... | collective-permute-start | bytes 3145736 | tf_op jit(solution)/shard_map/ppermute | solution.py:39
  169.7 13.4 %collective-permute-start.19 = (bf16[256,1024]{0,1:T(8,128)(2,1)S(1)}, bf16[256,1024]{0,1:T(8,128)(2,1)S(1)}, u32[]{:S(2)}, u32[]{:S(2)}) collective-permute-start(bf16[256,1024]{0,1:T(8,128)(2,1)S(1)} %slice.114), channel_id=1, source_target_pairs={{0,2},{1,3},{2,4},{3,5},{4,6},{5,7},{6,0},{7,1},{8,10},{9,11},{10,... | collective-permute-start | bytes 1572872 | tf_op jit(solution)/shard_map/ppermute | solution.py:39
  169.8 13.3 %collective-permute-start.20 = (bf16[256,1024]{0,1:T(8,128)(2,1)S(1)}, bf16[256,1024]{0,1:T(8,128)(2,1)S(1)}, u32[]{:S(2)}, u32[]{:S(2)}) collective-permute-start(bf16[256,1024]{0,1:T(8,128)(2,1)S(1)} %slice.115), channel_id=1, source_target_pairs={{0,6},{1,7},{2,0},{3,1},{4,2},{5,3},{6,4},{7,5},{8,14},{9,15},{10,... | collective-permute-start | bytes 1572872 | tf_op jit(solution)/shard_map/ppermute | solution.py:39
  184.1 15.5 %collective-permute-start.21 = (bf16[4,512,1024]{1,2,0:T(8,128)(2,1)}, bf16[4,512,1024]{1,2,0:T(8,128)(2,1)}, u32[]{:S(2)}, u32[]{:S(2)}) collective-permute-start(bf16[4,512,1024]{1,2,0:T(8,128)(2,1)} %fusion.23), channel_id=1, source_target_pairs={{0,8},{1,9},{2,10},{3,11},{4,12},{5,13},{6,14},{7,15},{8,0},{9,1},... | collective-permute-start | bytes 12582920 | tf_op jit(solution)/shard_map/ppermute | solution.py:39
  187.0 19.8 %collective-permute-start.15 = (bf16[4,512,1024]{2,1,0:T(8,128)(2,1)}, bf16[4,512,1024]{2,1,0:T(8,128)(2,1)}, u32[]{:S(2)}, u32[]{:S(2)}) collective-permute-start(bf16[4,512,1024]{2,1,0:T(8,128)(2,1)} %bitcast.98), channel_id=1, source_target_pairs={{0,8},{1,9},{2,10},{3,11},{4,12},{5,13},{6,14},{7,15},{8,0},{9,1},... | collective-permute-start | bytes 12582920 | tf_op jit(solution)/shard_map/ppermute | solution.py:39
  188.7 4.8 %collective-permute-start.14 = (bf16[256,256]{0,1:T(8,128)(2,1)S(1)}, bf16[256,256]{0,1:T(8,128)(2,1)S(1)}, u32[]{:S(2)}, u32[]{:S(2)}) collective-permute-start(bf16[256,256]{0,1:T(8,128)(2,1)S(1)} %pad_maximum_fusion.2), channel_id=1, source_target_pairs={{0,8},{1,9},{2,10},{3,11},{4,12},{5,13},{6,14},{7,15},{8,0},{9,1},... | collective-permute-start | bytes 393224 | tf_op jit(solution)/shard_map/ppermute | solution.py:39
  (13 other events, 148.5 us)
Sparse Core Ops, SparseCore 0:
  9.0 53.0 all-gather.2
  112.9 38.6 reduce-scatter.2
  213.6 51.8 reduce-scatter.4

commit v3 on v2

v3 whole, which is shorter than its diff:
```python
import jax
import jax.numpy as jnp
from jax import lax
from jax.experimental import pallas as pl
from jax.experimental.pallas import tpu as pltpu
from jax.sharding import Mesh, PartitionSpec as P

HEAD_SIZE = 128
SLOTS = 512
HALF = 256
AXES = ("zl", "x", "core", "y", "zh")
SIZES = (2, 4, 2, 4, 2)

rope_base = 500000.0
norm_eps = 1e-05


def coords(i):
    out = {}
    for name, size in zip(AXES[::-1], SIZES[::-1]):
        i, out[name] = divmod(i, size)
    return out


def index(c):
    i = 0
    for name, size in zip(AXES, SIZES):
        i = i * size + c[name] % size
    return i


def pairs(change):
    out = []
    for i in range(128):
        c = coords(i)
        out.append((i, index({**c, **change(c)})))
    return out


def send(value, change):
    return lax.ppermute(value, AXES, pairs(change))


def core_swap(value):
    return send(value, lambda c: dict(core=1 - c["core"]))


def zh_swap(value):
    return send(value, lambda c: dict(zh=1 - c["zh"]))


def zl_swap(value):
    return send(value, lambda c: dict(zl=1 - c["zl"]))


def x_shift(value, k):
    return send(value, lambda c: dict(x=c["x"] + k))


def after(value, other):
    return lax.optimization_barrier((value, other))[0]


def y_shift(value, k):
    return send(value, lambda c: dict(y=c["y"] + k))


def to_slice(flip):
    def change(c):
        return dict(
            y=2 * c["zl"] + c["x"] // 2,
            zl=c["y"] // 2,
            x=(c["y"] % 2) * 2 + c["x"] % 2,
            core=c["core"] ^ flip,
        )

    return change


def to_home(flip):
    def change(c):
        moves = c["x"] % 2 != c["zh"]
        return dict(x=c["x"] ^ moves, zh=c["zh"] ^ moves, core=c["core"] ^ flip)

    return change


def rope_tables(positions):
    half_dim = HEAD_SIZE // 2
    steps_up = jnp.arange(0, half_dim, dtype=jnp.float32) * (2.0 / HEAD_SIZE)
    inverse = jnp.power(jnp.float32(rope_base), -steps_up)
    angles = positions.astype(jnp.float32)[:, None] * inverse[None, :]
    cosine, sine = jnp.cos(angles), jnp.sin(angles)
    return jnp.concatenate([cosine, cosine], 1), jnp.concatenate([-sine, sine], 1)


def rotated(vectors, cosine, sine):
    return vectors * cosine + pltpu.roll(vectors, HEAD_SIZE // 2, 1) * sine


def key_value_kernel(sum_ref, scale_ref, cos_ref, sin_ref, out_ref):
    rows = sum_ref[...].astype(jnp.float32) * scale_ref[...]
    keys = rotated(rows[:, :HEAD_SIZE], cos_ref[...], sin_ref[...])
    out_ref[:, :HEAD_SIZE] = keys.astype(jnp.bfloat16)
    out_ref[:, HEAD_SIZE:] = rows[:, HEAD_SIZE:].astype(jnp.bfloat16)


def key_value_rows(summed, scale, cosine, sine):
    whole = pl.BlockSpec((HALF, HEAD_SIZE), lambda i: (0, 0))
    return pl.pallas_call(
        key_value_kernel,
        grid=(1,),
        in_specs=[
            pl.BlockSpec((HALF, 2 * HEAD_SIZE), lambda i: (0, 4)),
            pl.BlockSpec((HALF, 1), lambda i: (0, 0)),
            whole,
            whole,
        ],
        out_specs=pl.BlockSpec((HALF, 2 * HEAD_SIZE), lambda i: (0, 0)),
        out_shape=jax.ShapeDtypeStruct((HALF, 2 * HEAD_SIZE), jnp.bfloat16),
    )(summed, scale, cosine, sine)


def attention_kernel(sum_ref, scale_ref, cos_ref, sin_ref, bias_ref, own_ref, other_ref, out_ref):
    rows = sum_ref[...].astype(jnp.float32) * scale_ref[...]
    queries = rotated(rows, cos_ref[...], sin_ref[...]).astype(jnp.bfloat16)
    contract = (((1,), (1,)), ((), ()))

    def scores_of(ref, first):
        scores = lax.dot_general(
            queries, ref[:, :HEAD_SIZE], contract, preferred_element_type=jnp.float32
        )
        return scores * (HEAD_SIZE**-0.5) + bias_ref[:, first : first + HALF]

    own, other = scores_of(own_ref, 0), scores_of(other_ref, HALF)
    top = jnp.maximum(
        jnp.max(own, axis=-1, keepdims=True), jnp.max(other, axis=-1, keepdims=True)
    )
    own, other = jnp.exp(own - top), jnp.exp(other - top)
    total = jnp.sum(own, axis=-1, keepdims=True) + jnp.sum(other, axis=-1, keepdims=True)
    mixed = dot(own.astype(jnp.bfloat16), own_ref[:, HEAD_SIZE:]) + dot(
        other.astype(jnp.bfloat16), other_ref[:, HEAD_SIZE:]
    )
    out_ref[...] = (mixed / total).astype(jnp.bfloat16)


def attention(summed, scale, cosine, sine, bias, own, other):
    def fixed(shape):
        return pl.BlockSpec(shape, lambda h: (0, 0))

    return pl.pallas_call(
        attention_kernel,
        grid=(8,),
        in_specs=[
            pl.BlockSpec((HALF, HEAD_SIZE), lambda h: (0, h)),
            fixed((HALF, 1)),
            fixed((HALF, HEAD_SIZE)),
            fixed((HALF, HEAD_SIZE)),
            fixed((HALF, SLOTS)),
            fixed((HALF, 2 * HEAD_SIZE)),
            fixed((HALF, 2 * HEAD_SIZE)),
        ],
        out_specs=pl.BlockSpec((HALF, HEAD_SIZE), lambda h: (0, h)),
        out_shape=jax.ShapeDtypeStruct((HALF, 1024), jnp.bfloat16),
    )(summed, scale, cosine, sine, bias, own, other)


def half_of(value, which, dim=0):
    size = value.shape[dim] // 2
    return lax.dynamic_slice_in_dim(value, which * size, size, dim)


def ordered(first, own, other, dim=0):
    return jnp.where(
        first, jnp.concatenate([own, other], dim), jnp.concatenate([other, own], dim)
    )


def dot(a, b):
    return jnp.dot(a, b, preferred_element_type=jnp.float32)


def local(tokens, norm_gain, query_weight, kv_weight, out_weight, lengths):
    core = lax.axis_index("core")
    chip = lax.axis_index(("zl", "x"))
    zl = lax.axis_index("zl")
    x = lax.axis_index("x")
    y = lax.axis_index("y")
    zh = lax.axis_index("zh")
    is_first = core == 0

    kv_own = lax.dynamic_slice_in_dim(kv_weight, chip * 256 + core * 128, 128, 1)
    near = jnp.concatenate([query_weight, kv_own], axis=1)
    far = zh_swap(near)

    gain = lax.dynamic_slice_in_dim(norm_gain, (chip * 2 + core) * 512, 512, 0)
    wide = tokens.astype(jnp.float32)
    gained = (wide * gain[None, :]).astype(jnp.bfloat16)
    mine = send(half_of(gained, core), to_slice(0))
    theirs = send(half_of(gained, 1 - core), to_slice(1))
    block = ordered(is_first, mine, theirs, 1)

    beside = zl_swap(block)
    left = x_shift(block, 1)
    right = x_shift(block, -1)
    left, right, beside, far = lax.optimization_barrier((left, right, beside, far))
    beside_left = x_shift(beside, 1)
    beside_right = x_shift(beside, -1)
    opposite = jnp.concatenate([x_shift(left[:128], 1), x_shift(right[128:], -1)], 0)
    beside_opposite = jnp.concatenate(
        [x_shift(beside_left[:128], 1), x_shift(beside_right[128:], -1)], 0
    )
    gathered = jnp.zeros((4, HALF, 2048), jnp.bfloat16)
    for dz, dx, part in (
        (0, 0, block),
        (0, 3, left),
        (0, 1, right),
        (1, 0, beside),
        (0, 2, opposite),
        (1, 3, beside_left),
        (1, 1, beside_right),
        (1, 2, beside_opposite),
    ):
        zs, xs = zl ^ dz, (x + dx) % 4
        gathered = lax.dynamic_update_slice(
            gathered, part[None], (zs * 2 + xs // 2, 0, (xs % 2) * 1024)
        )

    near_other = core_swap(near)
    far_other = core_swap(far)

    def whole(own, other):
        kv = ordered(is_first, own[:, 512:], other[:, 512:], 1)
        return jnp.concatenate([own[:, :512], other[:, :512], kv], axis=1)

    weights = ordered(zh == 0, whole(near, near_other), whole(far, far_other), 0)

    out_near = lax.all_gather(out_weight, "y", axis=0, tiled=False)
    out_other = core_swap(out_near)

    projected = dot(gathered.reshape(1024, 2048), weights).astype(jnp.bfloat16)
    summed = lax.psum_scatter(
        projected.reshape(4, HALF, 1280), "y", scatter_dimension=0, tiled=True
    ).reshape(HALF, 1280)

    slice_gain = lax.dynamic_slice_in_dim(norm_gain, y * 2048, 2048, 0)
    plain = gathered.astype(jnp.float32) * (1.0 / slice_gain)
    squares = jnp.sum(plain * plain, axis=-1)
    total = lax.dynamic_index_in_dim(squares, y, 0, keepdims=False)
    for k in (1, 2, 3):
        total += y_shift(lax.dynamic_index_in_dim(squares, (y + k) % 4, 0, keepdims=False), k)
    scale = lax.rsqrt(total / 8192.0 + norm_eps)[:, None]

    own_slots = core * HALF + jnp.arange(HALF, dtype=jnp.int32)
    slot_k = jnp.concatenate([own_slots, (1 - core) * HALF + jnp.arange(HALF, dtype=jnp.int32)])
    allowed = (slot_k[None, :] <= own_slots[:, None]) & (slot_k[None, :] < lengths[0])
    bias = jnp.where(allowed, 0.0, -jnp.inf).astype(jnp.float32)
    cosine, sine = rope_tables(own_slots)

    kv_rows = key_value_rows(summed, scale, cosine, sine)
    attended = attention(summed, scale, cosine, sine, bias, kv_rows, core_swap(kv_rows))

    def columns(rows):
        return (
            jnp.einsum("qr,yrc->yqc", rows[:, :512], out_near, preferred_element_type=jnp.float32)
            + jnp.einsum("qr,yrc->yqc", rows[:, 512:], out_other, preferred_element_type=jnp.float32)
        ).astype(jnp.bfloat16)[:, None]

    partial = ordered(zh == 0, columns(attended), columns(zh_swap(attended)), 1)
    mixed = lax.psum_scatter(
        partial.reshape(8, HALF, 1024), ("zl", "x"), scatter_dimension=0, tiled=True
    ).reshape(HALF, 1024)
    keep = send(half_of(mixed, core, 1), to_home(0))
    got = send(half_of(mixed, 1 - core, 1), to_home(1))
    return (wide + ordered(is_first, keep, got, 0).astype(jnp.float32)).astype(jnp.bfloat16)


def solution(mesh):
    split = Mesh(mesh.devices.reshape(SIZES), AXES)
    gx, gy = ("zl", "x", "core"), ("y", "zh")
    placed = (P(gy, gx), P(), P(gy, gx), P(gy, None), P(gx, gy), P(gy))
    return jax.shard_map(
        local, mesh=split, in_specs=placed, out_specs=P(gy, gx), check_vma=False
    )
```

time: 280 us -> 274 us (0.979)
  blocking collectives: 24.6 us -> 0 us
  matrix products: 20.5 us -> 36.8 us
  waiting for transfers between devices: 127 us -> 113 us
  Pallas kernels: 0 us -> 9.63 us
  other arithmetic: 11.4 us -> 17.8 us
  starting transfers between devices: 54.3 us -> 57.4 us
    ppermute x23 -> x22, waiting for transfers between devices: 74.1 us -> 41.7 us  [send(): return lax.ppermute(value, AXES, pairs(change))]
    psum x1 -> x0, blocking collectives: 24.6 us -> none  [local(): lax.psum(after(jnp.sum(wide * wide, axis=-1), block), ('zl', 'x', 'core'))]
    dot_general x2 -> x1, matrix products: 7.33 us -> 27.3 us  [dot(): return jnp.dot(a, b, preferred_element_type=jnp.float32)]
    reduce_scatter x1, waiting for transfers between devices: 0.02 us -> 19.4 us  [local(): lax.psum_scatter(projected.reshape(4, HALF, 1280), 'y', scatter_dimension...]
    pallas_call x0 -> x2, Pallas kernels: none -> 9.63 us  [the longest x1 7.7 us: attention(): pl.pallas_call(attention_kernel, grid=(8,), in_specs=[pl.BlockSpec((HALF,...]
    reshape x1 -> x0, local copies, waits for them, and re-layouts: 4.49 us -> none  [local(): projected.reshape(4, HALF, 1280)]
    dot_general x6 -> x4, matrix products: 13.2 us -> 9.51 us  [the longest x2 6.97 us: columns(): jnp.einsum('qr,yrc->yqc', rows[:, 512:], out_other, preferred_element_typ...]
    ppermute x23 -> x22, starting transfers between devices: 54.3 us -> 57.3 us  [send(): return lax.ppermute(value, AXES, pairs(change))]
  transfers between devices with their start and end apart: 26 -> 25, of which waited for: 11 -> 13; matrix products, arithmetic and copies ran while one was open for 16% -> 25% of each run, Pallas kernels for 0% -> 4%
where the time goes in v3:
time: 274 us; the launch traced here: 273 us
  waiting for transfers between devices  113 us (41%)
  starting transfers between devices  57.4 us (21%)
  matrix products  36.8 us (13%)
  local copies, waits for them, and re-layouts  23.8 us (9%)
  other arithmetic  17.8 us (6%)
  between operations  14 us (5%)
  Pallas kernels  9.63 us (4%)
    ppermute x22, starting transfers between devices, send(): return lax.ppermute(value, AXES, pairs(change))  57.3 us
    reduce_scatter x1, waiting for transfers between devices, local(): lax.psum_scatter(partial.reshape(8, HALF, 1024), ('zl', 'x'), scatter_dim...  51.3 us
    ppermute x22, waiting for transfers between devices, send(): return lax.ppermute(value, AXES, pairs(change))  41.7 us
    dot_general x1, matrix products, dot(): return jnp.dot(a, b, preferred_element_type=jnp.float32)  27.3 us
    reduce_scatter x1, waiting for transfers between devices, local(): lax.psum_scatter(projected.reshape(4, HALF, 1280), 'y', scatter_dimension...  19.4 us
    pallas_call x1, Pallas kernels, attention(): pl.pallas_call(attention_kernel, grid=(8,), in_specs=[pl.BlockSpec((HALF,...  7.7 us
    dynamic_update_slice x5, local copies, waits for them, and re-layouts, local(): lax.dynamic_update_slice(gathered, part[None], (zs * 2 + xs // 2, 0, xs %...  7.42 us
    dot_general x2, matrix products, columns(): jnp.einsum('qr,yrc->yqc', rows[:, 512:], out_other, preferred_element_typ...  6.97 us
  transfers between devices with their start and end apart: 25, of which 13 were waited for; matrix products, arithmetic and copies ran while one was open for 25% of the time, Pallas kernels for 4%

profile of v3, /device:TPU:3, one launch (start us, length us, event | category | flops | bytes accessed | tf_op | source)
XLA Modules:
  0.0 272.6 jit_solution(10058654168805821578)
XLA Ops:
  9.6 3.7 %collective-permute-start.5 = (bf16[1024,640]{1,0:T(8,128)(2,1)S(1)}, bf16[1024,640]{1,0:T(8,128)(2,1)S(1)}, u32[]{:S(2)}, u32[]{:S(2)}) collective-permute-start(bf16[1024,640]{1,0:T(8,128)(2,1)S(1)} %pad_maximum_fusion), channel_id=1, source_target_pairs={{0,1},{1,0},{2,3},{3,2},{4,5},{5,4},{6,7},{7,6},{8,9},{9,8},{10,11... | collective-permute-start | bytes 3932168 | tf_op jit(solution)/shard_map/ppermute | solution.py:41
  15.0 3.6 %collective-permute-start = (bf16[256,512]{1,0:T(8,128)(2,1)}, bf16[256,512]{1,0:T(8,128)(2,1)}, u32[]{:S(2)}, u32[]{:S(2)}) collective-permute-start(bf16[256,512]{1,0:T(8,128)(2,1)} %get-tuple-element.15), channel_id=1, source_target_pairs={{0,0},{1,1},{2,32},{3,33},{4,64},{5,65},{6,96},{7,97},{8,8},{9,9},... | collective-permute-start | bytes 786440 | tf_op jit(solution)/shard_map/ppermute | solution.py:41
  23.7 13.1 %collective-permute-start.2 = (bf16[256,1024]{1,0:T(8,128)(2,1)}, bf16[256,1024]{1,0:T(8,128)(2,1)}, u32[]{:S(2)}, u32[]{:S(2)}) collective-permute-start(bf16[256,1024]{1,0:T(8,128)(2,1)} %maximum_select_fusion.6), channel_id=1, source_target_pairs={{0,16},{1,17},{2,18},{3,19},{4,20},{5,21},{6,22},{7,23},{8,24},{9,... | collective-permute-start | bytes 1572872 | tf_op jit(solution)/shard_map/ppermute | solution.py:41
  36.8 8.8 %collective-permute-start.4 = (bf16[256,1024]{1,0:T(8,128)(2,1)}, bf16[256,1024]{1,0:T(8,128)(2,1)}, u32[]{:S(2)}, u32[]{:S(2)}) collective-permute-start(bf16[256,1024]{1,0:T(8,128)(2,1)} %maximum_select_fusion.6), channel_id=1, source_target_pairs={{0,64},{1,65},{2,66},{3,67},{4,68},{5,69},{6,70},{7,71},{8,72},{9,... | collective-permute-start | bytes 1572872 | tf_op jit(solution)/shard_map/ppermute | solution.py:41
  45.6 2.5 broadcast_in_dim.49
  51.0 12.4 %collective-permute-done.4 = bf16[256,1024]{1,0:T(8,128)(2,1)} collective-permute-done((bf16[256,1024]{1,0:T(8,128)(2,1)}, bf16[256,1024]{1,0:T(8,128)(2,1)}, u32[]{:S(2)}, u32[]{:S(2)}) %collective-permute-start.4) | collective-permute-done | bytes 524320 | tf_op jit(solution)/shard_map/ppermute | solution.py:41
  67.1 2.4 collective-permute-start.13
  87.2 2.7 collective-permute-done.10
  89.9 2.5 collective-permute-done.11
  94.4 27.3 %fusion.23 = bf16[1024,1280]{1,0:T(8,128)(2,1)} fusion(bf16[1024,2048]{1,0:T(8,128)(2,1)} %bitcast.9, bf16[1024,256]{1,0:T(8,128)(2,1)} %maximum_select_fusion.8, bf16[1024,512]{1,0:T(8,128)(2,1)S(1)} %slice.60, bf16[1024,512]{1,0:T(8,128)(2,1)} %slice.48, bf16[1024,256]{1,0:T(8,128)(2,1)} %maximum_select_fusion.7, bf16[1024,512]{1,0:T(8,128)(2,1)} %slice.58, ...), kind=kOutput, calls=%fused_computation.28 | convolution fusion | flops 5435555840 | bytes 12058625 | tf_op jit(solution)/shard_map/dot_general | solution.py:180
  121.8 2.4 collective-permute-start.18
  127.0 3.3 %multiply_reduce_fusion = f32[4,256]{1,0:T(4,128)S(1)} fusion(bf16[4,256,2048]{2,1,0:T(8,128)(2,1)} %fusion.30, f32[2048]{0:T(1024)S(1)} %dynamic-slice_divide_fusion), kind=kLoop, calls=%fused_computation | loop fusion | flops 8387584 | bytes 4206592 | tf_op jit(solution)/shard_map/reduce_sum | solution.py:248
  131.7 4.1 %collective-permute-start.15 = (f32[256]{0:T(256)S(1)}, f32[256]{0:T(256)S(1)}, u32[]{:S(2)}, u32[]{:S(2)}) collective-permute-start(f32[256]{0:T(256)S(1)} %bitcast.71), channel_id=1, source_target_pairs={{0,4},{1,5},{2,6},{3,7},{4,0},{5,1},{6,2},{7,3},{8,12},{9,13},{10,... | collective-permute-start | bytes 3080 | tf_op jit(solution)/shard_map/ppermute | solution.py:41
  139.5 19.4 %reduce-scatter.3.cloned.1.call-done = bf16[1,256,1280]{2,1,0:T(8,128)(2,1)} async-done(((bf16[4,256,1280]{2,1,0:T(8,128)(2,1)}), bf16[1,256,1280]{2,1,0:T(8,128)(2,1)}) %reduce-scatter.3.cloned.1.call-update) | async-done | bytes 655376 | tf_op jit(solution)/shard_map/reduce_scatter | solution.py:242
  163.2 7.7 %shard_map.65 = bf16[256,1024]{1,0:T(8,128)(2,1)} custom-call(bf16[256,1280]{1,0:T(8,128)(2,1)} %bitcast.66, f32[256,1]{1,0:T(8,128)} %copy.8.scale_ref, f32[256,128]{1,0:T(8,128)} %get-tuple-element.24.cos_ref, f32[256,128]{1,0:T(8,128)} %get-tuple-element.25.sin_ref, f32[256,512]{1,0:T(8,128)} %and_select_fusion.bias_ref, ...), custom_call_target="tpu_custom_call" | custom-call | tf_op jit(solution)/shard_map/pallas_call | solution.py:151
  170.9 2.9 %collective-permute-start.19 = (bf16[256,1024]{1,0:T(8,128)(2,1)}, bf16[256,1024]{1,0:T(8,128)(2,1)S(1)}, u32[]{:S(2)}, u32[]{:S(2)}) collective-permute-start(bf16[256,1024]{1,0:T(8,128)(2,1)} %shard_map.65), channel_id=1, source_target_pairs={{0,1},{1,0},{2,3},{3,2},{4,5},{5,4},{6,7},{7,6},{8,9},{9,8},{10,11... | collective-permute-start | bytes 1572872 | tf_op jit(solution)/shard_map/ppermute | solution.py:41
  173.9 3.5 %fusion.32 = f32[256,4,1024]{2,0,1:T(8,128)S(1)} fusion(bf16[4,512,1024]{2,1,0:T(8,128)(2,1)} %collective-permute-done.18, bf16[256,1024]{1,0:T(8,128)(2,1)} %shard_map.65), kind=kOutput, calls=%fused_computation.56 | convolution fusion | flops 1073741824 | bytes 8650752 | tf_op jit(solution)/shard_map/qr,yrc->yqc/dot_general | solution.py:266
  178.7 7.2 %collective-permute-done.19 = bf16[256,1024]{1,0:T(8,128)(2,1)S(1)} collective-permute-done((bf16[256,1024]{1,0:T(8,128)(2,1)}, bf16[256,1024]{1,0:T(8,128)(2,1)S(1)}, u32[]{:S(2)}, u32[]{:S(2)}) %collective-permute-start.19) | collective-permute-done | bytes 524320 | tf_op jit(solution)/shard_map/ppermute | solution.py:41
  185.9 3.4 %fusion.31 = f32[256,4,1024]{2,0,1:T(8,128)S(1)} fusion(bf16[4,512,1024]{2,1,0:T(8,128)(2,1)} %collective-permute-done.18, bf16[256,1024]{1,0:T(8,128)(2,1)S(1)} %collective-permute-done.19), kind=kOutput, calls=%fused_computation.53 | convolution fusion | flops 1073741824 | bytes 8650752 | tf_op jit(solution)/shard_map/qr,yrc->yqc/dot_general | solution.py:266
  191.3 2.4 copy.9
  193.7 51.3 %reduce-scatter.5.cloned.1.call-done = bf16[1,256,1024]{2,1,0:T(8,128)(2,1)} async-done(((bf16[8,256,1024]{2,1,0:T(8,128)(2,1)}), bf16[1,256,1024]{2,1,0:T(8,128)(2,1)}) %reduce-scatter.5.cloned.1.call-update) | async-done | bytes 524304 | tf_op jit(solution)/shard_map/reduce_scatter | solution.py:270
  246.2 6.7 %collective-permute-start.20 = (bf16[256,512]{1,0:T(8,128)(2,1)S(1)}, bf16[256,512]{1,0:T(8,128)(2,1)S(1)}, u32[]{:S(2)}, u32[]{:S(2)}) collective-permute-start(bf16[256,512]{1,0:T(8,128)(2,1)S(1)} %get-tuple-element.13), channel_id=1, source_target_pairs={{0,0},{1,16},{2,2},{3,18},{4,4},{5,20},{6,6},{7,22},{8,8},{9,24},{... | collective-permute-start | bytes 786440 | tf_op jit(solution)/shard_map/ppermute | solution.py:41
  253.5 5.5 %collective-permute-done.20 = bf16[256,512]{1,0:T(8,128)(2,1)S(1)} collective-permute-done((bf16[256,512]{1,0:T(8,128)(2,1)S(1)}, bf16[256,512]{1,0:T(8,128)(2,1)S(1)}, u32[]{:S(2)}, u32[]{:S(2)}) %collective-permute-start.20) | collective-permute-done | bytes 262176 | tf_op jit(solution)/shard_map/ppermute | solution.py:41
  258.9 6.1 %collective-permute-done.21 = bf16[256,512]{1,0:T(8,128)(2,1)S(1)} collective-permute-done((bf16[256,512]{1,0:T(8,128)(2,1)S(1)}, bf16[256,512]{1,0:T(8,128)(2,1)S(1)}, u32[]{:S(2)}, u32[]{:S(2)}) %collective-permute-start.21) | collective-permute-done | bytes 262176 | tf_op jit(solution)/shard_map/ppermute | solution.py:41
  (91 shorter events, 53.6 us)
Async XLA Ops:
  6.5 115.3 %all-gather.3.cloned.1.call-start = ((), (), s32[]{:S(2)}) async-start(), calls=%async_computation.4 | async-start | bytes 5242880 | tf_op jit(solution)/shard_map/all_gather | solution.py:238
  7.3 151.6 %reduce-scatter.3.cloned.1.call-start = ((), (), s32[]{:S(2)}) async-start(), calls=%async_computation.2 | async-start | bytes 3276800 | tf_op jit(solution)/shard_map/reduce_scatter | solution.py:242
  9.6 53.7 %collective-permute-start.5 = (bf16[1024,640]{1,0:T(8,128)(2,1)S(1)}, bf16[1024,640]{1,0:T(8,128)(2,1)S(1)}, u32[]{:S(2)}, u32[]{:S(2)}) collective-permute-start(bf16[1024,640]{1,0:T(8,128)(2,1)S(1)} %pad_maximum_fusion), channel_id=1, source_target_pairs={{0,1},{1,0},{2,3},{3,2},{4,5},{5,4},{6,7},{7,6},{8,9},{9,8},{10,11... | collective-permute-start | bytes 3932168 | tf_op jit(solution)/shard_map/ppermute | solution.py:41
  15.0 4.6 %collective-permute-start = (bf16[256,512]{1,0:T(8,128)(2,1)}, bf16[256,512]{1,0:T(8,128)(2,1)}, u32[]{:S(2)}, u32[]{:S(2)}) collective-permute-start(bf16[256,512]{1,0:T(8,128)(2,1)} %get-tuple-element.15), channel_id=1, source_target_pairs={{0,0},{1,1},{2,32},{3,33},{4,64},{5,65},{6,96},{7,97},{8,8},{9,9},... | collective-permute-start | bytes 786440 | tf_op jit(solution)/shard_map/ppermute | solution.py:41
  18.6 2.8 %collective-permute-start.1 = (bf16[256,512]{1,0:T(8,128)(2,1)}, bf16[256,512]{1,0:T(8,128)(2,1)}, u32[]{:S(2)}, u32[]{:S(2)}) collective-permute-start(bf16[256,512]{1,0:T(8,128)(2,1)} %get-tuple-element.16), channel_id=1, source_target_pairs={{0,8},{1,9},{2,40},{3,41},{4,72},{5,73},{6,104},{7,105},{8,0},{9,1... | collective-permute-start | bytes 786440 | tf_op jit(solution)/shard_map/ppermute | solution.py:41
  19.6 54.6 %collective-permute-start.12 = (bf16[1024,640]{1,0:T(8,128)(2,1)S(1)}, bf16[1024,640]{1,0:T(8,128)(2,1)}, u32[]{:S(2)}, u32[]{:S(2)}) collective-permute-start(bf16[1024,640]{1,0:T(8,128)(2,1)S(1)} %pad_maximum_fusion), channel_id=1, source_target_pairs={{0,8},{1,9},{2,10},{3,11},{4,12},{5,13},{6,14},{7,15},{8,0},{9,1},... | collective-permute-start | bytes 3932168 | tf_op jit(solution)/shard_map/ppermute | solution.py:41
  23.7 26.6 %collective-permute-start.2 = (bf16[256,1024]{1,0:T(8,128)(2,1)}, bf16[256,1024]{1,0:T(8,128)(2,1)}, u32[]{:S(2)}, u32[]{:S(2)}) collective-permute-start(bf16[256,1024]{1,0:T(8,128)(2,1)} %maximum_select_fusion.6), channel_id=1, source_target_pairs={{0,16},{1,17},{2,18},{3,19},{4,20},{5,21},{6,22},{7,23},{8,24},{9,... | collective-permute-start | bytes 1572872 | tf_op jit(solution)/shard_map/ppermute | solution.py:41
  36.8 14.1 %collective-permute-start.3 = (bf16[256,1024]{1,0:T(8,128)(2,1)}, bf16[256,1024]{1,0:T(8,128)(2,1)}, u32[]{:S(2)}, u32[]{:S(2)}) collective-permute-start(bf16[256,1024]{1,0:T(8,128)(2,1)} %maximum_select_fusion.6), channel_id=1, source_target_pairs={{0,48},{1,49},{2,50},{3,51},{4,52},{5,53},{6,54},{7,55},{8,56},{9,... | collective-permute-start | bytes 1572872 | tf_op jit(solution)/shard_map/ppermute | solution.py:41
  36.8 26.5 %collective-permute-start.4 = (bf16[256,1024]{1,0:T(8,128)(2,1)}, bf16[256,1024]{1,0:T(8,128)(2,1)}, u32[]{:S(2)}, u32[]{:S(2)}) collective-permute-start(bf16[256,1024]{1,0:T(8,128)(2,1)} %maximum_select_fusion.6), channel_id=1, source_target_pairs={{0,64},{1,65},{2,66},{3,67},{4,68},{5,69},{6,70},{7,71},{8,72},{9,... | collective-permute-start | bytes 1572872 | tf_op jit(solution)/shard_map/ppermute | solution.py:41
  63.3 20.2 %collective-permute-start.8 = (bf16[256,1024]{1,0:T(8,128)(2,1)}, bf16[256,1024]{1,0:T(8,128)(2,1)S(1)}, u32[]{:S(2)}, u32[]{:S(2)}) collective-permute-start(bf16[256,1024]{1,0:T(8,128)(2,1)} %collective-permute-done.4), channel_id=1, source_target_pairs={{0,16},{1,17},{2,18},{3,19},{4,20},{5,21},{6,22},{7,23},{8,24},{9,... | collective-permute-start | bytes 1572872 | tf_op jit(solution)/shard_map/ppermute | solution.py:41
  64.5 20.0 %collective-permute-start.9 = (bf16[256,1024]{1,0:T(8,128)(2,1)}, bf16[256,1024]{1,0:T(8,128)(2,1)S(1)}, u32[]{:S(2)}, u32[]{:S(2)}) collective-permute-start(bf16[256,1024]{1,0:T(8,128)(2,1)} %collective-permute-done.4), channel_id=1, source_target_pairs={{0,48},{1,49},{2,50},{3,51},{4,52},{5,53},{6,54},{7,55},{8,56},{9,... | collective-permute-start | bytes 1572872 | tf_op jit(solution)/shard_map/ppermute | solution.py:41
  65.8 16.0 %collective-permute-start.6 = (bf16[128,1024]{1,0:T(8,128)(2,1)S(1)}, bf16[128,1024]{1,0:T(8,128)(2,1)S(1)}, u32[]{:S(2)}, u32[]{:S(2)}) collective-permute-start(bf16[128,1024]{1,0:T(8,128)(2,1)S(1)} %slice.42), channel_id=1, source_target_pairs={{0,16},{1,17},{2,18},{3,19},{4,20},{5,21},{6,22},{7,23},{8,24},{9,... | collective-permute-start | bytes 786440 | tf_op jit(solution)/shard_map/ppermute | solution.py:41
  67.1 26.2 %collective-permute-start.13 = (bf16[1024,640]{1,0:T(8,128)(2,1)S(1)}, bf16[1024,640]{1,0:T(8,128)(2,1)S(1)}, u32[]{:S(2)}, u32[]{:S(2)}) collective-permute-start(bf16[1024,640]{1,0:T(8,128)(2,1)S(1)} %collective-permute-done.5), channel_id=1, source_target_pairs={{0,8},{1,9},{2,10},{3,11},{4,12},{5,13},{6,14},{7,15},{8,0},{9,1},... | collective-permute-start | bytes 3932168 | tf_op jit(solution)/shard_map/ppermute | solution.py:41
  74.2 8.5 %collective-permute-start.7 = (bf16[128,1024]{1,0:T(8,128)(2,1)S(1)}, bf16[128,1024]{1,0:T(8,128)(2,1)S(1)}, u32[]{:S(2)}, u32[]{:S(2)}) collective-permute-start(bf16[128,1024]{1,0:T(8,128)(2,1)S(1)} %slice.43), channel_id=1, source_target_pairs={{0,48},{1,49},{2,50},{3,51},{4,52},{5,53},{6,54},{7,55},{8,56},{9,... | collective-permute-start | bytes 786440 | tf_op jit(solution)/shard_map/ppermute | solution.py:41
  83.5 6.3 %collective-permute-start.10 = (bf16[128,1024]{1,0:T(8,128)(2,1)S(1)}, bf16[128,1024]{1,0:T(8,128)(2,1)S(1)}, u32[]{:S(2)}, u32[]{:S(2)}) collective-permute-start(bf16[128,1024]{1,0:T(8,128)(2,1)S(1)} %slice.56), channel_id=1, source_target_pairs={{0,16},{1,17},{2,18},{3,19},{4,20},{5,21},{6,22},{7,23},{8,24},{9,... | collective-permute-start | bytes 786440 | tf_op jit(solution)/shard_map/ppermute | solution.py:41
  84.6 7.8 %collective-permute-start.11 = (bf16[128,1024]{1,0:T(8,128)(2,1)S(1)}, bf16[128,1024]{1,0:T(8,128)(2,1)S(1)}, u32[]{:S(2)}, u32[]{:S(2)}) collective-permute-start(bf16[128,1024]{1,0:T(8,128)(2,1)S(1)} %slice.57), channel_id=1, source_target_pairs={{0,48},{1,49},{2,50},{3,51},{4,52},{5,53},{6,54},{7,55},{8,56},{9,... | collective-permute-start | bytes 786440 | tf_op jit(solution)/shard_map/ppermute | solution.py:41
  121.7 123.4 %reduce-scatter.5.cloned.1.call-start = ((), (), s32[]{:S(2)}) async-start(), calls=%async_computation.3 | async-start | bytes 4718592 | tf_op jit(solution)/shard_map/reduce_scatter | solution.py:270
  121.8 52.1 %collective-permute-start.18 = (bf16[4,512,1024]{2,1,0:T(8,128)(2,1)}, bf16[4,512,1024]{2,1,0:T(8,128)(2,1)}, u32[]{:S(2)}, u32[]{:S(2)}) collective-permute-start(bf16[4,512,1024]{2,1,0:T(8,128)(2,1)} %bitcast.62), channel_id=1, source_target_pairs={{0,8},{1,9},{2,10},{3,11},{4,12},{5,13},{6,14},{7,15},{8,0},{9,1},... | collective-permute-start | bytes 12582920 | tf_op jit(solution)/shard_map/ppermute | solution.py:41
  130.4 6.5 %collective-permute-start.14 = (f32[256]{0:T(256)S(1)}, f32[256]{0:T(256)S(1)}, u32[]{:S(2)}, u32[]{:S(2)}) collective-permute-start(f32[256]{0:T(256)S(1)} %bitcast.72), channel_id=1, source_target_pairs={{0,2},{1,3},{2,4},{3,5},{4,6},{5,7},{6,0},{7,1},{8,10},{9,11},{10,... | collective-permute-start | bytes 3080 | tf_op jit(solution)/shard_map/ppermute | solution.py:41
  131.7 5.2 %collective-permute-start.15 = (f32[256]{0:T(256)S(1)}, f32[256]{0:T(256)S(1)}, u32[]{:S(2)}, u32[]{:S(2)}) collective-permute-start(f32[256]{0:T(256)S(1)} %bitcast.71), channel_id=1, source_target_pairs={{0,4},{1,5},{2,6},{3,7},{4,0},{5,1},{6,2},{7,3},{8,12},{9,13},{10,... | collective-permute-start | bytes 3080 | tf_op jit(solution)/shard_map/ppermute | solution.py:41
  135.8 2.8 %collective-permute-start.16 = (f32[256]{0:T(256)S(1)}, f32[256]{0:T(256)S(1)}, u32[]{:S(2)}, u32[]{:S(2)}) collective-permute-start(f32[256]{0:T(256)S(1)} %bitcast.70), channel_id=1, source_target_pairs={{0,6},{1,7},{2,0},{3,1},{4,2},{5,3},{6,4},{7,5},{8,14},{9,15},{10,... | collective-permute-start | bytes 3080 | tf_op jit(solution)/shard_map/ppermute | solution.py:41
  170.9 14.9 %collective-permute-start.19 = (bf16[256,1024]{1,0:T(8,128)(2,1)}, bf16[256,1024]{1,0:T(8,128)(2,1)S(1)}, u32[]{:S(2)}, u32[]{:S(2)}) collective-permute-start(bf16[256,1024]{1,0:T(8,128)(2,1)} %shard_map.65), channel_id=1, source_target_pairs={{0,1},{1,0},{2,3},{3,2},{4,5},{5,4},{6,7},{7,6},{8,9},{9,8},{10,11... | collective-permute-start | bytes 1572872 | tf_op jit(solution)/shard_map/ppermute | solution.py:41
  246.2 12.8 %collective-permute-start.20 = (bf16[256,512]{1,0:T(8,128)(2,1)S(1)}, bf16[256,512]{1,0:T(8,128)(2,1)S(1)}, u32[]{:S(2)}, u32[]{:S(2)}) collective-permute-start(bf16[256,512]{1,0:T(8,128)(2,1)S(1)} %get-tuple-element.13), channel_id=1, source_target_pairs={{0,0},{1,16},{2,2},{3,18},{4,4},{5,20},{6,6},{7,22},{8,8},{9,24},{... | collective-permute-start | bytes 786440 | tf_op jit(solution)/shard_map/ppermute | solution.py:41
  252.8 12.2 %collective-permute-start.21 = (bf16[256,512]{1,0:T(8,128)(2,1)S(1)}, bf16[256,512]{1,0:T(8,128)(2,1)S(1)}, u32[]{:S(2)}, u32[]{:S(2)}) collective-permute-start(bf16[256,512]{1,0:T(8,128)(2,1)S(1)} %get-tuple-element.14), channel_id=1, source_target_pairs={{0,8},{1,24},{2,10},{3,26},{4,12},{5,28},{6,14},{7,30},{8,0},{9,16... | collective-permute-start | bytes 786440 | tf_op jit(solution)/shard_map/ppermute | solution.py:41
  (6 other events, 33.8 us)
Sparse Core Ops, SparseCore 0:
  9.0 58.0 all-gather.2
  121.8 36.9 reduce-scatter.2
  193.9 51.1 reduce-scatter.4

commit v4 on v3

--- a/solution.py
+++ b/solution.py
@@ -144,15 +144,15 @@
     out_ref[...] = (mixed / total).astype(jnp.bfloat16)
 
 
-def attention(summed, scale, cosine, sine, bias, own, other):
+def attention(first, summed, scale, cosine, sine, bias, own, other):
     def fixed(shape):
         return pl.BlockSpec(shape, lambda h: (0, 0))
 
     return pl.pallas_call(
         attention_kernel,
-        grid=(8,),
+        grid=(4,),
         in_specs=[
-            pl.BlockSpec((HALF, HEAD_SIZE), lambda h: (0, h)),
+            pl.BlockSpec((HALF, HEAD_SIZE), lambda h: (0, h + first)),
             fixed((HALF, 1)),
             fixed((HALF, HEAD_SIZE)),
             fixed((HALF, HEAD_SIZE)),
@@ -161,8 +161,34 @@
             fixed((HALF, 2 * HEAD_SIZE)),
         ],
         out_specs=pl.BlockSpec((HALF, HEAD_SIZE), lambda h: (0, h)),
-        out_shape=jax.ShapeDtypeStruct((HALF, 1024), jnp.bfloat16),
+        out_shape=jax.ShapeDtypeStruct((HALF, 512), jnp.bfloat16),
     )(summed, scale, cosine, sine, bias, own, other)
+
+
+def columns_kernel(zh_ref, own_a, own_b, far_a, far_b, near_ref, other_ref, out_ref):
+    def put(which, left, right):
+        rows = dot(left[...], near_ref[0]) + dot(right[...], other_ref[0])
+        start = pl.multiple_of(which * HALF, HALF)
+        out_ref[0, pl.ds(start, HALF), :] = rows.astype(jnp.bfloat16)
+
+    put(zh_ref[0], own_a, own_b)
+    put(1 - zh_ref[0], far_a, far_b)
+
+
+def columns(zh, own_a, own_b, far_a, far_b, near, other):
+    rows = pl.BlockSpec((HALF, 512), lambda j, z: (0, 0))
+    block = pl.BlockSpec((1, 512, 1024), lambda j, z: (j, 0, 0))
+    return pl.pallas_call(
+        columns_kernel,
+        grid_spec=pltpu.PrefetchScalarGridSpec(
+            num_scalar_prefetch=1,
+            grid=(4,),
+            in_specs=[rows, rows, rows, rows, block, block],
+            out_specs=pl.BlockSpec((1, SLOTS, 1024), lambda j, z: (j, 0, 0)),
+        ),
+        out_shape=jax.ShapeDtypeStruct((4, SLOTS, 1024), jnp.bfloat16),
+        compiler_params=pltpu.CompilerParams(vmem_limit_bytes=32 * 1024 * 1024),
+    )(zh.reshape(1), own_a, own_b, far_a, far_b, near, other)
 
 
 def half_of(value, which, dim=0):
@@ -189,21 +215,23 @@
     zh = lax.axis_index("zh")
     is_first = core == 0
 
-    kv_own = lax.dynamic_slice_in_dim(kv_weight, chip * 256 + core * 128, 128, 1)
-    near = jnp.concatenate([query_weight, kv_own], axis=1)
-    far = zh_swap(near)
-
     gain = lax.dynamic_slice_in_dim(norm_gain, (chip * 2 + core) * 512, 512, 0)
     wide = tokens.astype(jnp.float32)
     gained = (wide * gain[None, :]).astype(jnp.bfloat16)
-    mine = send(half_of(gained, core), to_slice(0))
-    theirs = send(half_of(gained, 1 - core), to_slice(1))
+    mine_out, theirs_out = half_of(gained, core), half_of(gained, 1 - core)
+    mine = send(mine_out, to_slice(0))
+    theirs = send(theirs_out, to_slice(1))
     block = ordered(is_first, mine, theirs, 1)
+
+    kv_own = lax.dynamic_slice_in_dim(kv_weight, chip * 256 + core * 128, 128, 1)
+    near = after(jnp.concatenate([query_weight, kv_own], axis=1), (mine_out, theirs_out))
+    far_top = zh_swap(near[:512])
 
     beside = zl_swap(block)
     left = x_shift(block, 1)
     right = x_shift(block, -1)
-    left, right, beside, far = lax.optimization_barrier((left, right, beside, far))
+    left, right, beside, far_top = lax.optimization_barrier((left, right, beside, far_top))
+    far_bottom = zh_swap(after(near[512:], beside))
     beside_left = x_shift(beside, 1)
     beside_right = x_shift(beside, -1)
     opposite = jnp.concatenate([x_shift(left[:128], 1), x_shift(right[128:], -1)], 0)
@@ -227,21 +255,34 @@
         )
 
     near_other = core_swap(near)
+    far = jnp.concatenate([far_top, far_bottom], axis=0)
     far_other = core_swap(far)
 
     def whole(own, other):
         kv = ordered(is_first, own[:, 512:], other[:, 512:], 1)
         return jnp.concatenate([own[:, :512], other[:, :512], kv], axis=1)
 
-    weights = ordered(zh == 0, whole(near, near_other), whole(far, far_other), 0)
+    weights = lax.optimization_barrier(
+        ordered(zh == 0, whole(near, near_other), whole(far, far_other), 0)
+    )
 
     out_near = lax.all_gather(out_weight, "y", axis=0, tiled=False)
     out_other = core_swap(out_near)
 
-    projected = dot(gathered.reshape(1024, 2048), weights).astype(jnp.bfloat16)
-    summed = lax.psum_scatter(
-        projected.reshape(4, HALF, 1280), "y", scatter_dimension=0, tiled=True
-    ).reshape(HALF, 1280)
+    def term(k):
+        rows = lax.dynamic_index_in_dim(gathered, (y + k) % 4, 0, keepdims=False)
+        return dot(rows, weights)
+
+    farthest = term(2).astype(jnp.bfloat16)
+    from_below = y_shift(farthest[:128], 1)
+    from_above = y_shift(farthest[128:], -1)
+    upper, lower, kept = lax.optimization_barrier((term(1), term(3), term(0)))
+    upper = jnp.concatenate([upper[:128] + from_below.astype(jnp.float32), upper[128:]], 0)
+    lower = jnp.concatenate([lower[:128], lower[128:] + from_above.astype(jnp.float32)], 0)
+    from_below = y_shift(upper.astype(jnp.bfloat16), 1)
+    from_above = y_shift(lower.astype(jnp.bfloat16), -1)
+    summed = kept + from_below.astype(jnp.float32) + from_above.astype(jnp.float32)
+    summed = summed.astype(jnp.bfloat16)
 
     slice_gain = lax.dynamic_slice_in_dim(norm_gain, y * 2048, 2048, 0)
     plain = gathered.astype(jnp.float32) * (1.0 / slice_gain)
@@ -258,15 +299,13 @@
     cosine, sine = rope_tables(own_slots)
 
     kv_rows = key_value_rows(summed, scale, cosine, sine)
-    attended = attention(summed, scale, cosine, sine, bias, kv_rows, core_swap(kv_rows))
-
-    def columns(rows):
-        return (
-            jnp.einsum("qr,yrc->yqc", rows[:, :512], out_near, preferred_element_type=jnp.float32)
-            + jnp.einsum("qr,yrc->yqc", rows[:, 512:], out_other, preferred_element_type=jnp.float32)
-        ).astype(jnp.bfloat16)[:, None]
-
-    partial = ordered(zh == 0, columns(attended), columns(zh_swap(attended)), 1)
+    kv_other = core_swap(kv_rows)
+    own_a = attention(0, summed, scale, cosine, sine, bias, kv_rows, kv_other)
+    far_a = zh_swap(own_a)
+    own_b = attention(4, summed, scale, cosine, sine, bias, kv_rows, kv_other)
+    far_b = zh_swap(own_b)
+
+    partial = columns(zh, own_a, own_b, far_a, far_b, out_near, out_other)
     mixed = lax.psum_scatter(
         partial.reshape(8, HALF, 1024), ("zl", "x"), scatter_dimension=0, tiled=True
     ).reshape(HALF, 1024)

time: 274 us -> 289 us (1.055)
  other arithmetic: 17.8 us -> 46.8 us
  matrix products: 36.8 us -> 11.4 us
  waiting for transfers between devices: 113 us -> 123 us
  Pallas kernels: 9.63 us -> 17.6 us
  local copies, waits for them, and re-layouts: 23.8 us -> 19.5 us
    select_n x4, other arithmetic: 4.93 us -> 36.4 us  [ordered(): jnp.where(first, jnp.concatenate([own, other], dim), jnp.concatenate([oth...]
    ppermute x22 -> x28, waiting for transfers between devices: 41.7 us -> 69.5 us  [send(): return lax.ppermute(value, AXES, pairs(change))]
    reduce_scatter x1 -> x0, waiting for transfers between devices: 19.4 us -> none  [local(): lax.psum_scatter(projected.reshape(4, HALF, 1280), 'y', scatter_dimension...]
    dot_general x1 -> x4, matrix products: 27.3 us -> 11.4 us  [dot(): return jnp.dot(a, b, preferred_element_type=jnp.float32)]
    dot_general x4 -> x0, matrix products: 9.51 us -> none  [the longest x2 6.97 us: columns(): jnp.einsum('qr,yrc->yqc', rows[:, 512:], out_other, preferred_element_typ...]
    unnamed x10 -> x33, local copies, waits for them, and re-layouts: 0.67 us -> 9.24 us
    pallas_call x1 -> x3, Pallas kernels: 7.7 us -> 15.6 us  [the longest x2 9.37 us: attention(): pl.pallas_call(attention_kernel, grid=(4,), in_specs=[pl.BlockSpec((HALF,...]
    dynamic_update_slice x5, local copies, waits for them, and re-layouts: 7.42 us -> 0.26 us  [local(): lax.dynamic_update_slice(gathered, part[None], (zs * 2 + xs // 2, 0, xs %...]
  transfers between devices with their start and end apart: 25 -> 30, of which waited for: 13 -> 17; matrix products, arithmetic and copies ran while one was open for 25% -> 23% of each run, Pallas kernels for 4% -> 4%
where the time goes in v4:
time: 289 us; the launch traced here: 288 us
  waiting for transfers between devices  123 us (43%)
  starting transfers between devices  55.3 us (19%)
  other arithmetic  46.8 us (16%)
  local copies, waits for them, and re-layouts  19.5 us (7%)
  Pallas kernels  17.6 us (6%)
  between operations  14.7 us (5%)
  matrix products  11.4 us (4%)
    ppermute x28, waiting for transfers between devices, send(): return lax.ppermute(value, AXES, pairs(change))  69.5 us
    ppermute x28, starting transfers between devices, send(): return lax.ppermute(value, AXES, pairs(change))  55.3 us
    reduce_scatter x1, waiting for transfers between devices, local(): lax.psum_scatter(partial.reshape(8, HALF, 1024), ('zl', 'x'), scatter_dim...  53.3 us
    select_n x4, other arithmetic, ordered(): jnp.where(first, jnp.concatenate([own, other], dim), jnp.concatenate([oth...  36.4 us
    dot_general x4, matrix products, dot(): return jnp.dot(a, b, preferred_element_type=jnp.float32)  11.4 us
    pallas_call x2, Pallas kernels, attention(): pl.pallas_call(attention_kernel, grid=(4,), in_specs=[pl.BlockSpec((HALF,...  9.37 us
    unnamed x33, local copies, waits for them, and re-layouts  9.24 us
    pallas_call x1, Pallas kernels, columns(): pl.pallas_call(columns_kernel, grid_spec=pltpu.PrefetchScalarGridSpec(num...  6.28 us
  transfers between devices with their start and end apart: 30, of which 17 were waited for; matrix products, arithmetic and copies ran while one was open for 23% of the time, Pallas kernels for 4%

profile of v4, /device:TPU:3, one launch (start us, length us, event | category | flops | bytes accessed | tf_op | source)
XLA Modules:
  0.0 288.1 jit_solution(11144064561121449884)
XLA Ops:
  13.5 3.6 %collective-permute-start.5 = (bf16[512,640]{1,0:T(8,128)(2,1)}, bf16[512,640]{1,0:T(8,128)(2,1)}, u32[]{:S(2)}, u32[]{:S(2)}) collective-permute-start(bf16[512,640]{1,0:T(8,128)(2,1)} %get-tuple-element.24), channel_id=1, source_target_pairs={{0,1},{1,0},{2,3},{3,2},{4,5},{5,4},{6,7},{7,6},{8,9},{9,8},{10,11... | collective-permute-start | bytes 1966088 | tf_op jit(solution)/shard_map/ppermute | solution.py:41
  17.4 10.8 %collective-permute-start.2 = (bf16[256,1024]{1,0:T(8,128)(2,1)S(1)}, bf16[256,1024]{1,0:T(8,128)(2,1)S(1)}, u32[]{:S(2)}, u32[]{:S(2)}) collective-permute-start(bf16[256,1024]{1,0:T(8,128)(2,1)S(1)} %maximum_select_fusion.2), channel_id=1, source_target_pairs={{0,16},{1,17},{2,18},{3,19},{4,20},{5,21},{6,22},{7,23},{8,24},{9,... | collective-permute-start | bytes 1572872 | tf_op jit(solution)/shard_map/ppermute | solution.py:41
  28.3 3.4 %collective-permute-start.4 = (bf16[256,1024]{1,0:T(8,128)(2,1)S(1)}, bf16[256,1024]{1,0:T(8,128)(2,1)S(1)}, u32[]{:S(2)}, u32[]{:S(2)}) collective-permute-start(bf16[256,1024]{1,0:T(8,128)(2,1)S(1)} %maximum_select_fusion.2), channel_id=1, source_target_pairs={{0,64},{1,65},{2,66},{3,67},{4,68},{5,69},{6,70},{7,71},{8,72},{9,... | collective-permute-start | bytes 1572872 | tf_op jit(solution)/shard_map/ppermute | solution.py:41
  33.8 9.7 %collective-permute-done.5 = bf16[512,640]{1,0:T(8,128)(2,1)} collective-permute-done((bf16[512,640]{1,0:T(8,128)(2,1)}, bf16[512,640]{1,0:T(8,128)(2,1)}, u32[]{:S(2)}, u32[]{:S(2)}) %collective-permute-start.5) | collective-permute-done | bytes 655392 | tf_op jit(solution)/shard_map/ppermute | solution.py:41
  43.6 7.8 %collective-permute-done.4 = bf16[256,1024]{1,0:T(8,128)(2,1)S(1)} collective-permute-done((bf16[256,1024]{1,0:T(8,128)(2,1)S(1)}, bf16[256,1024]{1,0:T(8,128)(2,1)S(1)}, u32[]{:S(2)}, u32[]{:S(2)}) %collective-permute-start.4) | collective-permute-done | bytes 524320 | tf_op jit(solution)/shard_map/ppermute | solution.py:41
  56.1 4.1 %collective-permute-start.8 = (bf16[256,1024]{1,0:T(8,128)(2,1)S(1)}, bf16[256,1024]{1,0:T(8,128)(2,1)S(1)}, u32[]{:S(2)}, u32[]{:S(2)}) collective-permute-start(bf16[256,1024]{1,0:T(8,128)(2,1)S(1)} %copy-done.15), channel_id=1, source_target_pairs={{0,16},{1,17},{2,18},{3,19},{4,20},{5,21},{6,22},{7,23},{8,24},{9,... | collective-permute-start | bytes 1572872 | tf_op jit(solution)/shard_map/ppermute | solution.py:41
  63.1 5.9 %collective-permute-done.13 = bf16[512,640]{1,0:T(8,128)(2,1)} collective-permute-done((bf16[512,640]{1,0:T(8,128)(2,1)}, bf16[512,640]{1,0:T(8,128)(2,1)}, u32[]{:S(2)}, u32[]{:S(2)}) %collective-permute-start.13) | collective-permute-done | bytes 655392 | tf_op jit(solution)/shard_map/ppermute | solution.py:41
  70.4 5.9 %collective-permute-done.6 = bf16[128,1024]{1,0:T(8,128)(2,1)S(1)} collective-permute-done((bf16[128,1024]{1,0:T(8,128)(2,1)S(1)}, bf16[128,1024]{1,0:T(8,128)(2,1)S(1)}, u32[]{:S(2)}, u32[]{:S(2)}) %collective-permute-start.6) | collective-permute-done | bytes 262176 | tf_op jit(solution)/shard_map/ppermute | solution.py:41
  87.2 35.9 %maximum_select_fusion = bf16[2048,1280]{1,0:T(8,128)(2,1)S(1)} fusion(bf16[1024,256]{1,0:T(8,128)(2,1)S(1)} %maximum_select_fusion.4, bf16[1024,512]{1,0:T(8,128)(2,1)S(1)} %slice.87, bf16[1024,512]{1,0:T(8,128)(2,1)S(1)} %slice.86, bf16[1024,256]{1,0:T(8,128)(2,1)S(1)} %maximum_select_fusion.3, bf16[1024,512]{1,0:T(8,128)(2,1)S(1)} %slice.84, ...), kind=kLoop, calls=%fused_computation.1 | loop fusion | flops 65536000 | bytes 10485761 | tf_op jit(solution)/shard_map/jit(_where)/select_n | solution.py:200
  130.0 4.3 %fusion.5 = f32[256,1280]{1,0:T(8,128)S(1)} fusion(bf16[2048,1280]{1,0:T(8,128)(2,1)} %copy-done.6, bf16[4,256,2048]{2,1,0:T(8,128)(2,1)} %copy-done.4, s32[]{:T(128)S(6)} %select_n.263), kind=kOutput, calls=%fused_computation.12 | convolution fusion | flops 1342177280 | bytes 7602180 | tf_op jit(solution)/shard_map/dot_general | solution.py:206
  134.4 4.0 %fusion.7 = f32[256,1280]{1,0:T(8,128)S(1)} fusion(bf16[2048,1280]{1,0:T(8,128)(2,1)} %copy-done.6, bf16[4,256,2048]{2,1,0:T(8,128)(2,1)S(1)} %copy-done.5, s32[]{:T(128)S(6)} %select_n.256), kind=kOutput, calls=%fused_computation.14 | convolution fusion | flops 1342177280 | bytes 7602180 | tf_op jit(solution)/shard_map/dot_general | solution.py:206
  138.5 3.1 %collective-permute-start.17 = (bf16[128,1280]{1,0:T(8,128)(2,1)S(1)}, bf16[128,1280]{1,0:T(8,128)(2,1)S(1)}, u32[]{:S(2)}, u32[]{:S(2)}) collective-permute-start(bf16[128,1280]{1,0:T(8,128)(2,1)S(1)} %get-tuple-element.26), channel_id=1, source_target_pairs={{0,6},{1,7},{2,0},{3,1},{4,2},{5,3},{6,4},{7,5},{8,14},{9,15},{10,... | collective-permute-start | bytes 983048 | tf_op jit(solution)/shard_map/ppermute | solution.py:41
  141.7 3.7 %collective-permute-done.15 = bf16[128,1280]{1,0:T(8,128)(2,1)S(1)} collective-permute-done((bf16[128,1280]{1,0:T(8,128)(2,1)S(1)}, bf16[128,1280]{1,0:T(8,128)(2,1)S(1)}, u32[]{:S(2)}, u32[]{:S(2)}) %collective-permute-start.15) | collective-permute-done | bytes 327712 | tf_op jit(solution)/shard_map/ppermute | solution.py:41
  145.9 2.9 %collective-permute-done.17 = bf16[128,1280]{1,0:T(8,128)(2,1)S(1)} collective-permute-done((bf16[128,1280]{1,0:T(8,128)(2,1)S(1)}, bf16[128,1280]{1,0:T(8,128)(2,1)S(1)}, u32[]{:S(2)}, u32[]{:S(2)}) %collective-permute-start.17) | collective-permute-done | bytes 327712 | tf_op jit(solution)/shard_map/ppermute | solution.py:41
  148.9 3.3 %collective-permute-start.18 = (bf16[256,1280]{1,0:T(8,128)(2,1)S(1)}, bf16[256,1280]{1,0:T(8,128)(2,1)}, u32[]{:S(2)}, u32[]{:S(2)}) collective-permute-start(bf16[256,1280]{1,0:T(8,128)(2,1)S(1)} %pad_maximum_fusion.2), channel_id=1, source_target_pairs={{0,6},{1,7},{2,0},{3,1},{4,2},{5,3},{6,4},{7,5},{8,14},{9,15},{10,... | collective-permute-start | bytes 1966088 | tf_op jit(solution)/shard_map/ppermute | solution.py:41
  155.4 7.2 %collective-permute-done.19 = f32[256]{0:T(256)S(1)} collective-permute-done((f32[256]{0:T(256)S(1)}, f32[256]{0:T(256)S(1)}, u32[]{:S(2)}, u32[]{:S(2)}) %collective-permute-start.19) | collective-permute-done | bytes 1056 | tf_op jit(solution)/shard_map/ppermute | solution.py:41
  174.6 4.7 %shard_map.66.own_b = bf16[256,512]{1,0:T(8,128)(2,1)} custom-call(bf16[256,1280]{1,0:T(8,128)(2,1)} %add_convert_fusion.sum_ref, f32[256,1]{1,0:T(8,128)} %copy.8.scale_ref, f32[256,128]{1,0:T(8,128)} %get-tuple-element.38.cos_ref, f32[256,128]{1,0:T(8,128)} %get-tuple-element.39.sin_ref, f32[256,512]{1,0:T(8,128)} %and_select_fusion.bias_ref, ...), custom_call_target="tpu_custom_call" | custom-call | tf_op jit(solution)/shard_map/pallas_call | solution.py:151
  180.9 4.7 %shard_map.65.own_a = bf16[256,512]{1,0:T(8,128)(2,1)} custom-call(bf16[256,1280]{1,0:T(8,128)(2,1)} %add_convert_fusion.sum_ref, f32[256,1]{1,0:T(8,128)} %copy.8.scale_ref, f32[256,128]{1,0:T(8,128)} %get-tuple-element.38.cos_ref, f32[256,128]{1,0:T(8,128)} %get-tuple-element.39.sin_ref, f32[256,512]{1,0:T(8,128)} %and_select_fusion.bias_ref, ...), custom_call_target="tpu_custom_call" | custom-call | tf_op jit(solution)/shard_map/pallas_call | solution.py:151
  188.5 6.1 %collective-permute-done.23.far_a = bf16[256,512]{1,0:T(8,128)(2,1)S(1)} collective-permute-done((bf16[256,512]{1,0:T(8,128)(2,1)}, bf16[256,512]{1,0:T(8,128)(2,1)S(1)}, u32[]{:S(2)}, u32[]{:S(2)}) %collective-permute-start.23) | collective-permute-done | bytes 262176 | tf_op jit(solution)/shard_map/ppermute | solution.py:41
  198.6 6.3 %shard_map.67 = bf16[4,512,1024]{2,1,0:T(8,128)(2,1)S(1)} custom-call(s32[1]{0:T(128)} %bitcast.zh_ref, bf16[256,512]{1,0:T(8,128)(2,1)S(1)} %copy-done.3, bf16[256,512]{1,0:T(8,128)(2,1)S(1)} %copy-done.2, bf16[256,512]{1,0:T(8,128)(2,1)S(1)} %collective-permute-done.23.far_a, bf16[256,512]{1,0:T(8,128)(2,1)S(1)} %collective-permute-done.24.far_b, ...), custom_call_target="tpu_custom_call" | custom-call | tf_op jit(solution)/shard_map/pallas_call | solution.py:181
  206.9 53.3 %reduce-scatter.2.cloned.1.call-done = bf16[1,256,1024]{2,1,0:T(8,128)(2,1)} async-done(((bf16[8,256,1024]{2,1,0:T(8,128)(2,1)}), bf16[1,256,1024]{2,1,0:T(8,128)(2,1)}) %reduce-scatter.2.cloned.1.call-update) | async-done | bytes 524304 | tf_op jit(solution)/shard_map/reduce_scatter | solution.py:309
  261.3 6.7 %collective-permute-start.26 = (bf16[256,512]{1,0:T(8,128)(2,1)S(1)}, bf16[256,512]{1,0:T(8,128)(2,1)S(1)}, u32[]{:S(2)}, u32[]{:S(2)}) collective-permute-start(bf16[256,512]{1,0:T(8,128)(2,1)S(1)} %get-tuple-element.27), channel_id=1, source_target_pairs={{0,0},{1,16},{2,2},{3,18},{4,4},{5,20},{6,6},{7,22},{8,8},{9,24},{... | collective-permute-start | bytes 786440 | tf_op jit(solution)/shard_map/ppermute | solution.py:41
  268.6 5.5 %collective-permute-done.26 = bf16[256,512]{1,0:T(8,128)(2,1)S(1)} collective-permute-done((bf16[256,512]{1,0:T(8,128)(2,1)S(1)}, bf16[256,512]{1,0:T(8,128)(2,1)S(1)}, u32[]{:S(2)}, u32[]{:S(2)}) %collective-permute-start.26) | collective-permute-done | bytes 262176 | tf_op jit(solution)/shard_map/ppermute | solution.py:41
  274.1 6.1 %collective-permute-done.27 = bf16[256,512]{1,0:T(8,128)(2,1)S(1)} collective-permute-done((bf16[256,512]{1,0:T(8,128)(2,1)S(1)}, bf16[256,512]{1,0:T(8,128)(2,1)S(1)}, u32[]{:S(2)}, u32[]{:S(2)}) %collective-permute-start.27) | collective-permute-done | bytes 262176 | tf_op jit(solution)/shard_map/ppermute | solution.py:41
  (135 shorter events, 64.1 us)
Async XLA Ops:
  6.5 120.5 %all-gather.3.cloned.1.call-start = ((), (), s32[]{:S(2)}) async-start(), calls=%async_computation.2 | async-start | bytes 5242880 | tf_op jit(solution)/shard_map/all_gather | solution.py:269
  8.5 8.7 %collective-permute-start = (bf16[256,512]{1,0:T(8,128)(2,1)S(1)}, bf16[256,512]{1,0:T(8,128)(2,1)S(1)}, u32[]{:S(2)}, u32[]{:S(2)}) collective-permute-start(bf16[256,512]{1,0:T(8,128)(2,1)S(1)} %get-tuple-element.29), channel_id=1, source_target_pairs={{0,0},{1,1},{2,32},{3,33},{4,64},{5,65},{6,96},{7,97},{8,8},{9,9},... | collective-permute-start | bytes 786440 | tf_op jit(solution)/shard_map/ppermute | solution.py:41
  12.2 68.6 %collective-permute-start.12 = (bf16[1024,640]{1,0:T(8,128)(2,1)S(1)}, bf16[1024,640]{1,0:T(8,128)(2,1)}, u32[]{:S(2)}, u32[]{:S(2)}) collective-permute-start(bf16[1024,640]{1,0:T(8,128)(2,1)S(1)} %pad_maximum_fusion), channel_id=1, source_target_pairs={{0,8},{1,9},{2,10},{3,11},{4,12},{5,13},{6,14},{7,15},{8,0},{9,1},... | collective-permute-start | bytes 3932168 | tf_op jit(solution)/shard_map/ppermute | solution.py:41
  13.5 30.0 %collective-permute-start.5 = (bf16[512,640]{1,0:T(8,128)(2,1)}, bf16[512,640]{1,0:T(8,128)(2,1)}, u32[]{:S(2)}, u32[]{:S(2)}) collective-permute-start(bf16[512,640]{1,0:T(8,128)(2,1)} %get-tuple-element.24), channel_id=1, source_target_pairs={{0,1},{1,0},{2,3},{3,2},{4,5},{5,4},{6,7},{7,6},{8,9},{9,8},{10,11... | collective-permute-start | bytes 1966088 | tf_op jit(solution)/shard_map/ppermute | solution.py:41
  17.2 243.1 %reduce-scatter.2.cloned.1.call-start = ((), (), s32[]{:S(2)}) async-start(), calls=%async_computation.1 | async-start | bytes 4718592 | tf_op jit(solution)/shard_map/reduce_scatter | solution.py:309
  17.4 26.1 %collective-permute-start.2 = (bf16[256,1024]{1,0:T(8,128)(2,1)S(1)}, bf16[256,1024]{1,0:T(8,128)(2,1)S(1)}, u32[]{:S(2)}, u32[]{:S(2)}) collective-permute-start(bf16[256,1024]{1,0:T(8,128)(2,1)S(1)} %maximum_select_fusion.2), channel_id=1, source_target_pairs={{0,16},{1,17},{2,18},{3,19},{4,20},{5,21},{6,22},{7,23},{8,24},{9,... | collective-permute-start | bytes 1572872 | tf_op jit(solution)/shard_map/ppermute | solution.py:41
  28.2 15.3 %collective-permute-start.3 = (bf16[256,1024]{1,0:T(8,128)(2,1)S(1)}, bf16[256,1024]{1,0:T(8,128)(2,1)S(1)}, u32[]{:S(2)}, u32[]{:S(2)}) collective-permute-start(bf16[256,1024]{1,0:T(8,128)(2,1)S(1)} %maximum_select_fusion.2), channel_id=1, source_target_pairs={{0,48},{1,49},{2,50},{3,51},{4,52},{5,53},{6,54},{7,55},{8,56},{9,... | collective-permute-start | bytes 1572872 | tf_op jit(solution)/shard_map/ppermute | solution.py:41
  28.3 23.1 %collective-permute-start.4 = (bf16[256,1024]{1,0:T(8,128)(2,1)S(1)}, bf16[256,1024]{1,0:T(8,128)(2,1)S(1)}, u32[]{:S(2)}, u32[]{:S(2)}) collective-permute-start(bf16[256,1024]{1,0:T(8,128)(2,1)S(1)} %maximum_select_fusion.2), channel_id=1, source_target_pairs={{0,64},{1,65},{2,66},{3,67},{4,68},{5,69},{6,70},{7,71},{8,72},{9,... | collective-permute-start | bytes 1572872 | tf_op jit(solution)/shard_map/ppermute | solution.py:41
  51.4 17.6 %collective-permute-start.13 = (bf16[512,640]{1,0:T(8,128)(2,1)}, bf16[512,640]{1,0:T(8,128)(2,1)}, u32[]{:S(2)}, u32[]{:S(2)}) collective-permute-start(bf16[512,640]{1,0:T(8,128)(2,1)} %get-tuple-element.19), channel_id=1, source_target_pairs={{0,1},{1,0},{2,3},{3,2},{4,5},{5,4},{6,7},{7,6},{8,9},{9,8},{10,11... | collective-permute-start | bytes 1966088 | tf_op jit(solution)/shard_map/ppermute | solution.py:41
  56.1 22.6 %collective-permute-start.8 = (bf16[256,1024]{1,0:T(8,128)(2,1)S(1)}, bf16[256,1024]{1,0:T(8,128)(2,1)S(1)}, u32[]{:S(2)}, u32[]{:S(2)}) collective-permute-start(bf16[256,1024]{1,0:T(8,128)(2,1)S(1)} %copy-done.15), channel_id=1, source_target_pairs={{0,16},{1,17},{2,18},{3,19},{4,20},{5,21},{6,22},{7,23},{8,24},{9,... | collective-permute-start | bytes 1572872 | tf_op jit(solution)/shard_map/ppermute | solution.py:41
  60.2 20.3 %collective-permute-start.9 = (bf16[256,1024]{1,0:T(8,128)(2,1)S(1)}, bf16[256,1024]{1,0:T(8,128)(2,1)S(1)}, u32[]{:S(2)}, u32[]{:S(2)}) collective-permute-start(bf16[256,1024]{1,0:T(8,128)(2,1)S(1)} %copy-done.15), channel_id=1, source_target_pairs={{0,48},{1,49},{2,50},{3,51},{4,52},{5,53},{6,54},{7,55},{8,56},{9,... | collective-permute-start | bytes 1572872 | tf_op jit(solution)/shard_map/ppermute | solution.py:41
  60.2 16.1 %collective-permute-start.6 = (bf16[128,1024]{1,0:T(8,128)(2,1)S(1)}, bf16[128,1024]{1,0:T(8,128)(2,1)S(1)}, u32[]{:S(2)}, u32[]{:S(2)}) collective-permute-start(bf16[128,1024]{1,0:T(8,128)(2,1)S(1)} %slice.63), channel_id=1, source_target_pairs={{0,16},{1,17},{2,18},{3,19},{4,20},{5,21},{6,22},{7,23},{8,24},{9,... | collective-permute-start | bytes 786440 | tf_op jit(solution)/shard_map/ppermute | solution.py:41
  69.0 9.7 %collective-permute-start.7 = (bf16[128,1024]{1,0:T(8,128)(2,1)S(1)}, bf16[128,1024]{1,0:T(8,128)(2,1)S(1)}, u32[]{:S(2)}, u32[]{:S(2)}) collective-permute-start(bf16[128,1024]{1,0:T(8,128)(2,1)S(1)} %slice.64), channel_id=1, source_target_pairs={{0,48},{1,49},{2,50},{3,51},{4,52},{5,53},{6,54},{7,55},{8,56},{9,... | collective-permute-start | bytes 786440 | tf_op jit(solution)/shard_map/ppermute | solution.py:41
  76.3 10.5 %collective-permute-start.14 = (bf16[1024,640]{1,0:T(8,128)(2,1)S(1)}, bf16[1024,640]{1,0:T(8,128)(2,1)S(1)}, u32[]{:S(2)}, u32[]{:S(2)}) collective-permute-start(bf16[1024,640]{1,0:T(8,128)(2,1)S(1)} %constant_dynamic-update-slice_fusion), channel_id=1, source_target_pairs={{0,8},{1,9},{2,10},{3,11},{4,12},{5,13},{6,14},{7,15},{8,0},{9,1},... | collective-permute-start | bytes 3932168 | tf_op jit(solution)/shard_map/ppermute | solution.py:41
  127.1 67.5 %collective-permute-start.25 = (bf16[4,512,1024]{2,1,0:T(8,128)(2,1)}, bf16[4,512,1024]{2,1,0:T(8,128)(2,1)}, u32[]{:S(2)}, u32[]{:S(2)}) collective-permute-start(bf16[4,512,1024]{2,1,0:T(8,128)(2,1)} %bitcast.51), channel_id=1, source_target_pairs={{0,8},{1,9},{2,10},{3,11},{4,12},{5,13},{6,14},{7,15},{8,0},{9,1},... | collective-permute-start | bytes 12582920 | tf_op jit(solution)/shard_map/ppermute | solution.py:41
  134.3 11.1 %collective-permute-start.15 = (bf16[128,1280]{1,0:T(8,128)(2,1)S(1)}, bf16[128,1280]{1,0:T(8,128)(2,1)S(1)}, u32[]{:S(2)}, u32[]{:S(2)}) collective-permute-start(bf16[128,1280]{1,0:T(8,128)(2,1)S(1)} %get-tuple-element.25), channel_id=1, source_target_pairs={{0,2},{1,3},{2,4},{3,5},{4,6},{5,7},{6,0},{7,1},{8,10},{9,11},{10,... | collective-permute-start | bytes 983048 | tf_op jit(solution)/shard_map/ppermute | solution.py:41
  138.5 10.3 %collective-permute-start.17 = (bf16[128,1280]{1,0:T(8,128)(2,1)S(1)}, bf16[128,1280]{1,0:T(8,128)(2,1)S(1)}, u32[]{:S(2)}, u32[]{:S(2)}) collective-permute-start(bf16[128,1280]{1,0:T(8,128)(2,1)S(1)} %get-tuple-element.26), channel_id=1, source_target_pairs={{0,6},{1,7},{2,0},{3,1},{4,2},{5,3},{6,4},{7,5},{8,14},{9,15},{10,... | collective-permute-start | bytes 983048 | tf_op jit(solution)/shard_map/ppermute | solution.py:41
  145.5 20.8 %collective-permute-start.16 = (bf16[256,1280]{1,0:T(8,128)(2,1)S(1)}, bf16[256,1280]{1,0:T(8,128)(2,1)S(1)}, u32[]{:S(2)}, u32[]{:S(2)}) collective-permute-start(bf16[256,1280]{1,0:T(8,128)(2,1)S(1)} %pad_maximum_fusion.1), channel_id=1, source_target_pairs={{0,2},{1,3},{2,4},{3,5},{4,6},{5,7},{6,0},{7,1},{8,10},{9,11},{10,... | collective-permute-start | bytes 1966088 | tf_op jit(solution)/shard_map/ppermute | solution.py:41
  148.9 17.4 %collective-permute-start.18 = (bf16[256,1280]{1,0:T(8,128)(2,1)S(1)}, bf16[256,1280]{1,0:T(8,128)(2,1)}, u32[]{:S(2)}, u32[]{:S(2)}) collective-permute-start(bf16[256,1280]{1,0:T(8,128)(2,1)S(1)} %pad_maximum_fusion.2), channel_id=1, source_target_pairs={{0,6},{1,7},{2,0},{3,1},{4,2},{5,3},{6,4},{7,5},{8,14},{9,15},{10,... | collective-permute-start | bytes 1966088 | tf_op jit(solution)/shard_map/ppermute | solution.py:41
  153.4 9.2 %collective-permute-start.19 = (f32[256]{0:T(256)S(1)}, f32[256]{0:T(256)S(1)}, u32[]{:S(2)}, u32[]{:S(2)}) collective-permute-start(f32[256]{0:T(256)S(1)} %bitcast.59), channel_id=1, source_target_pairs={{0,2},{1,3},{2,4},{3,5},{4,6},{5,7},{6,0},{7,1},{8,10},{9,11},{10,... | collective-permute-start | bytes 3080 | tf_op jit(solution)/shard_map/ppermute | solution.py:41
  179.2 9.2 %collective-permute-start.24 = (bf16[256,512]{1,0:T(8,128)(2,1)}, bf16[256,512]{1,0:T(8,128)(2,1)S(1)}, u32[]{:S(2)}, u32[]{:S(2)}) collective-permute-start(bf16[256,512]{1,0:T(8,128)(2,1)} %shard_map.66.own_b), channel_id=1, source_target_pairs={{0,1},{1,0},{2,3},{3,2},{4,5},{5,4},{6,7},{7,6},{8,9},{9,8},{10,11... | collective-permute-start | bytes 786440 | tf_op jit(solution)/shard_map/ppermute | solution.py:41
  185.6 8.9 %collective-permute-start.23 = (bf16[256,512]{1,0:T(8,128)(2,1)}, bf16[256,512]{1,0:T(8,128)(2,1)S(1)}, u32[]{:S(2)}, u32[]{:S(2)}) collective-permute-start(bf16[256,512]{1,0:T(8,128)(2,1)} %shard_map.65.own_a), channel_id=1, source_target_pairs={{0,1},{1,0},{2,3},{3,2},{4,5},{5,4},{6,7},{7,6},{8,9},{9,8},{10,11... | collective-permute-start | bytes 786440 | tf_op jit(solution)/shard_map/ppermute | solution.py:41
  261.3 12.8 %collective-permute-start.26 = (bf16[256,512]{1,0:T(8,128)(2,1)S(1)}, bf16[256,512]{1,0:T(8,128)(2,1)S(1)}, u32[]{:S(2)}, u32[]{:S(2)}) collective-permute-start(bf16[256,512]{1,0:T(8,128)(2,1)S(1)} %get-tuple-element.27), channel_id=1, source_target_pairs={{0,0},{1,16},{2,2},{3,18},{4,4},{5,20},{6,6},{7,22},{8,8},{9,24},{... | collective-permute-start | bytes 786440 | tf_op jit(solution)/shard_map/ppermute | solution.py:41
  268.0 12.2 %collective-permute-start.27 = (bf16[256,512]{1,0:T(8,128)(2,1)S(1)}, bf16[256,512]{1,0:T(8,128)(2,1)S(1)}, u32[]{:S(2)}, u32[]{:S(2)}) collective-permute-start(bf16[256,512]{1,0:T(8,128)(2,1)S(1)} %get-tuple-element.28), channel_id=1, source_target_pairs={{0,8},{1,24},{2,10},{3,26},{4,12},{5,28},{6,14},{7,30},{8,0},{9,16... | collective-permute-start | bytes 786440 | tf_op jit(solution)/shard_map/ppermute | solution.py:41
  (22 other events, 262.8 us)
Sparse Core Ops, SparseCore 0:
  17.3 53.3 all-gather.2
  207.0 53.1 reduce-scatter.1

commit v5 on v3

v5 whole, which is shorter than its diff:
```python
import jax
import jax.numpy as jnp
from jax import lax
from jax.experimental import pallas as pl
from jax.experimental.pallas import tpu as pltpu
from jax.sharding import Mesh, PartitionSpec as P

HEAD_SIZE = 128
SLOTS = 512
HALF = 256
AXES = ("zl", "x", "core", "y", "zh")
SIZES = (2, 4, 2, 4, 2)

rope_base = 500000.0
norm_eps = 1e-05


def coords(i):
    out = {}
    for name, size in zip(AXES[::-1], SIZES[::-1]):
        i, out[name] = divmod(i, size)
    return out


def index(c):
    i = 0
    for name, size in zip(AXES, SIZES):
        i = i * size + c[name] % size
    return i


def pairs(change):
    out = []
    for i in range(128):
        c = coords(i)
        out.append((i, index({**c, **change(c)})))
    return out


def send(value, change):
    return lax.ppermute(value, AXES, pairs(change))


def core_swap(value):
    return send(value, lambda c: dict(core=1 - c["core"]))


def zh_swap(value):
    return send(value, lambda c: dict(zh=1 - c["zh"]))


def zl_swap(value):
    return send(value, lambda c: dict(zl=1 - c["zl"]))


def x_shift(value, k):
    return send(value, lambda c: dict(x=c["x"] + k))


def after(value, other):
    return lax.optimization_barrier((value, other))[0]


def y_shift(value, k):
    return send(value, lambda c: dict(y=c["y"] + k))


def to_slice(flip):
    def change(c):
        return dict(
            y=2 * c["zl"] + c["x"] // 2,
            zl=c["y"] // 2,
            x=(c["y"] % 2) * 2 + c["x"] % 2,
            core=c["core"] ^ flip,
        )

    return change


def to_home(flip):
    def change(c):
        moves = c["x"] % 2 != c["zh"]
        return dict(x=c["x"] ^ moves, zh=c["zh"] ^ moves, core=c["core"] ^ flip)

    return change


def rope_tables(positions):
    half_dim = HEAD_SIZE // 2
    steps_up = jnp.arange(0, half_dim, dtype=jnp.float32) * (2.0 / HEAD_SIZE)
    inverse = jnp.power(jnp.float32(rope_base), -steps_up)
    angles = positions.astype(jnp.float32)[:, None] * inverse[None, :]
    cosine, sine = jnp.cos(angles), jnp.sin(angles)
    return jnp.concatenate([cosine, cosine], 1), jnp.concatenate([-sine, sine], 1)


def rotated(vectors, cosine, sine):
    return vectors * cosine + pltpu.roll(vectors, HEAD_SIZE // 2, 1) * sine


WIDE = 640
GRANT = pltpu.CompilerParams(vmem_limit_bytes=40 * 1024 * 1024)


def total_of(refs, cols=slice(None)):
    total = refs[0][:, cols].astype(jnp.float32)
    for ref in refs[1:]:
        total += ref[:, cols].astype(jnp.float32)
    return total


def key_value_kernel(core_ref, k0, k1, k2, v0, v1, v2, scale_ref, cos_ref, sin_ref, out_ref):
    scale = scale_ref[...]
    keys = rotated(total_of((k0, k1, k2)) * scale, cos_ref[...], sin_ref[...])
    out_ref[:, :HEAD_SIZE] = keys.astype(jnp.bfloat16)
    out_ref[:, HEAD_SIZE:] = (total_of((v0, v1, v2)) * scale).astype(jnp.bfloat16)


def key_value_rows(core, sums, scale, cosine, sine):
    keys = pl.BlockSpec((HALF, HEAD_SIZE), lambda i, c: (0, 4 + 5 * c[0]))
    values = pl.BlockSpec((HALF, HEAD_SIZE), lambda i, c: (0, 9 - 5 * c[0]))
    table = pl.BlockSpec((HALF, HEAD_SIZE), lambda i, c: (0, 0))
    return pl.pallas_call(
        key_value_kernel,
        grid_spec=pltpu.PrefetchScalarGridSpec(
            num_scalar_prefetch=1,
            grid=(1,),
            in_specs=[keys] * 3
            + [values] * 3
            + [pl.BlockSpec((HALF, 1), lambda i, c: (0, 0)), table, table],
            out_specs=pl.BlockSpec((HALF, 2 * HEAD_SIZE), lambda i, c: (0, 0)),
        ),
        out_shape=jax.ShapeDtypeStruct((HALF, 2 * HEAD_SIZE), jnp.bfloat16),
    )(core.reshape(1), *sums, *sums, scale, cosine, sine)


def attention_kernel(
    s0, s1, s2, scale_ref, cos_ref, sin_ref, bias_ref, own_ref, other_ref, out_ref
):
    contract = (((1,), (1,)), ((), ()))
    for head in range(4):
        cols = slice(head * HEAD_SIZE, (head + 1) * HEAD_SIZE)
        rows = total_of((s0, s1, s2), cols) * scale_ref[...]
        queries = rotated(rows, cos_ref[...], sin_ref[...]).astype(jnp.bfloat16)

        def scores_of(ref, first):
            scores = lax.dot_general(
                queries, ref[:, :HEAD_SIZE], contract, preferred_element_type=jnp.float32
            )
            return scores * (HEAD_SIZE**-0.5) + bias_ref[:, first : first + HALF]

        own, other = scores_of(own_ref, 0), scores_of(other_ref, HALF)
        top = jnp.maximum(
            jnp.max(own, axis=-1, keepdims=True), jnp.max(other, axis=-1, keepdims=True)
        )
        own, other = jnp.exp(own - top), jnp.exp(other - top)
        total = jnp.sum(own, axis=-1, keepdims=True) + jnp.sum(other, axis=-1, keepdims=True)
        mixed = dot(own.astype(jnp.bfloat16), own_ref[:, HEAD_SIZE:]) + dot(
            other.astype(jnp.bfloat16), other_ref[:, HEAD_SIZE:]
        )
        out_ref[:, cols] = (mixed / total).astype(jnp.bfloat16)


def attention(part, sums, scale, cosine, sine, bias, own, other):
    def fixed(shape):
        return pl.BlockSpec(shape, lambda i: (0, 0))

    return pl.pallas_call(
        attention_kernel,
        grid=(1,),
        in_specs=[pl.BlockSpec((HALF, WIDE), lambda i: (0, part))] * 3
        + [
            fixed((HALF, 1)),
            fixed((HALF, HEAD_SIZE)),
            fixed((HALF, HEAD_SIZE)),
            fixed((HALF, SLOTS)),
            fixed((HALF, 2 * HEAD_SIZE)),
            fixed((HALF, 2 * HEAD_SIZE)),
        ],
        out_specs=fixed((HALF, 512)),
        out_shape=jax.ShapeDtypeStruct((HALF, 512), jnp.bfloat16),
        compiler_params=GRANT,
    )(*sums, scale, cosine, sine, bias, own, other)


def project_kernel(steps, at_ref, rows_ref, near, near_other, far, far_other, *outs):
    zh = at_ref[0]
    near_rows = rows_ref[0, :, pl.ds(pl.multiple_of(zh * 1024, 1024), 1024)]
    far_rows = rows_ref[0, :, pl.ds(pl.multiple_of((1 - zh) * 1024, 1024), 1024)]
    own = (dot(near_rows, near[...]) + dot(far_rows, far[...])).astype(jnp.bfloat16)
    other = (dot(near_rows, near_other[...]) + dot(far_rows, far_other[...])).astype(jnp.bfloat16)
    if steps == 1:
        for half, out in enumerate(outs):
            out[:, :WIDE] = own[half * 128 : half * 128 + 128]
            out[:, WIDE:] = other[half * 128 : half * 128 + 128]
        return
    for step, out in enumerate(outs):

        @pl.when(pl.program_id(0) == step)
        def _():
            out[:, :WIDE] = own
            out[:, WIDE:] = other


def project(which, zh, gathered, weights):
    steps = len(which)
    rows = 128 if steps == 1 else HALF
    outs = 2 if steps == 1 else steps
    whole = pl.BlockSpec((1024, WIDE), lambda i, at: (0, 0))
    return pl.pallas_call(
        lambda *refs: project_kernel(steps, *refs),
        grid_spec=pltpu.PrefetchScalarGridSpec(
            num_scalar_prefetch=1,
            grid=(steps,),
            in_specs=[pl.BlockSpec((1, HALF, 2048), lambda i, at: (at[1 + i], 0, 0))] + [whole] * 4,
            out_specs=[pl.BlockSpec((rows, 2 * WIDE), lambda i, at: (0, 0))] * outs,
        ),
        out_shape=[jax.ShapeDtypeStruct((rows, 2 * WIDE), jnp.bfloat16)] * outs,
        compiler_params=GRANT,
    )(jnp.stack([zh, *which]).astype(jnp.int32), gathered, *weights)


def chunk_kernel(starts, halves, at_ref, own_a, own_b, far_a, far_b, near, other, *refs):
    added, outs, rows = refs[: len(starts)], refs[len(starts) : -1], refs[-1]

    @pl.when(at_ref[1] == 1)
    def _():
        rows[:, :512] = own_a[...]
        rows[:, 512:] = own_b[...]

    @pl.when(at_ref[1] == 0)
    def _():
        rows[:, :512] = far_a[...]
        rows[:, 512:] = far_b[...]

    product = dot(rows[:, :512], near[0]) + dot(rows[:, 512:], other[0])
    parts = [product[:128], product[128:]]
    for start, ref in zip(starts, added):
        if start is None:
            parts[0] += ref[:128].astype(jnp.float32)
            parts[1] += ref[128:].astype(jnp.float32)
        else:
            parts[start] += ref[...].astype(jnp.float32)
    if halves:
        outs[0][...] = parts[0].astype(jnp.bfloat16)
        outs[1][...] = parts[1].astype(jnp.bfloat16)
    else:
        outs[0][:128] = parts[0].astype(jnp.bfloat16)
        outs[0][128:] = parts[1].astype(jnp.bfloat16)


def chunk(target, zh, attended, near, other, added=(), halves=False):
    zt, xt = target
    at = jnp.stack([zt * 2 + xt // 2, (xt % 2 == zh).astype(jnp.int32)]).astype(jnp.int32)
    rows = pl.BlockSpec((HALF, 512), lambda i, at: (0, 0))
    block = pl.BlockSpec((1, 512, 1024), lambda i, at: (at[0], 0, 0))
    size = 128 if halves else HALF
    starts = [start for _, start in added]
    out = pl.pallas_call(
        lambda *refs: chunk_kernel(starts, halves, *refs),
        grid_spec=pltpu.PrefetchScalarGridSpec(
            num_scalar_prefetch=1,
            grid=(1,),
            in_specs=[rows] * 4
            + [block] * 2
            + [pl.BlockSpec(value.shape, lambda i, at: (0, 0)) for value, _ in added],
            out_specs=[pl.BlockSpec((size, 1024), lambda i, at: (0, 0))] * (1 + halves),
            scratch_shapes=[pltpu.VMEM((HALF, 1024), jnp.bfloat16)],
        ),
        out_shape=[jax.ShapeDtypeStruct((size, 1024), jnp.bfloat16)] * (1 + halves),
        compiler_params=GRANT,
    )(at, *attended, near, other, *[value for value, _ in added])
    return out if halves else out[0]


def half_of(value, which, dim=0):
    size = value.shape[dim] // 2
    return lax.dynamic_slice_in_dim(value, which * size, size, dim)


def ordered(first, own, other, dim=0):
    return jnp.where(
        first, jnp.concatenate([own, other], dim), jnp.concatenate([other, own], dim)
    )


def dot(a, b):
    return jnp.dot(a, b, preferred_element_type=jnp.float32)


def local(tokens, norm_gain, query_weight, kv_weight, out_weight, lengths):
    core = lax.axis_index("core")
    chip = lax.axis_index(("zl", "x"))
    zl = lax.axis_index("zl")
    x = lax.axis_index("x")
    y = lax.axis_index("y")
    zh = lax.axis_index("zh")
    is_first = core == 0

    gain = lax.dynamic_slice_in_dim(norm_gain, (chip * 2 + core) * 512, 512, 0)
    wide = tokens.astype(jnp.float32)
    gained = (wide * gain[None, :]).astype(jnp.bfloat16)
    mine_out, theirs_out = half_of(gained, core), half_of(gained, 1 - core)
    mine = send(mine_out, to_slice(0))
    theirs = send(theirs_out, to_slice(1))
    block = ordered(is_first, mine, theirs, 1)

    kv_own = lax.dynamic_slice_in_dim(kv_weight, chip * 256 + core * 128, 128, 1)
    near = after(jnp.concatenate([query_weight, kv_own], axis=1), (mine_out, theirs_out))
    far_top = zh_swap(near[:512])

    beside = zl_swap(block)
    left = x_shift(block, 1)
    right = x_shift(block, -1)
    near_other = core_swap(near)
    left, right, beside, far_top, near_other = lax.optimization_barrier(
        (left, right, beside, far_top, near_other)
    )
    far_bottom = zh_swap(after(near[512:], beside))
    beside_left = x_shift(beside, 1)
    beside_right = x_shift(beside, -1)
    opposite = jnp.concatenate([x_shift(left[:128], 1), x_shift(right[128:], -1)], 0)
    beside_opposite = jnp.concatenate(
        [x_shift(beside_left[:128], 1), x_shift(beside_right[128:], -1)], 0
    )
    gathered = jnp.zeros((4, HALF, 2048), jnp.bfloat16)
    for dz, dx, part in (
        (0, 0, block),
        (0, 3, left),
        (0, 1, right),
        (1, 0, beside),
        (0, 2, opposite),
        (1, 3, beside_left),
        (1, 1, beside_right),
        (1, 2, beside_opposite),
    ):
        zs, xs = zl ^ dz, (x + dx) % 4
        gathered = lax.dynamic_update_slice(
            gathered, part[None], (zs * 2 + xs // 2, 0, (xs % 2) * 1024)
        )

    far = jnp.concatenate([far_top, far_bottom], axis=0)
    weights = (near, near_other, far, core_swap(far))

    out_near = lax.all_gather(out_weight, "y", axis=0, tiled=False)
    out_other = core_swap(out_near)

    low, high = project([(y + 2) % 4], zh, gathered, weights)
    from_below = y_shift(low, 1)
    from_above = y_shift(high, -1)
    from_below, from_above, out_other = lax.optimization_barrier(
        (from_below, from_above, out_other)
    )
    upper, lower, kept = project([(y + 1) % 4, (y + 3) % 4, y], zh, gathered, weights)
    upper = lax.dynamic_update_slice(upper, upper[:128] + from_below, (0, 0))
    lower = lax.dynamic_update_slice(lower, lower[128:] + from_above, (128, 0))
    sums = (kept, y_shift(upper, 1), y_shift(lower, -1))

    slice_gain = lax.dynamic_slice_in_dim(norm_gain, y * 2048, 2048, 0)
    plain = gathered.astype(jnp.float32) * (1.0 / slice_gain)
    squares = jnp.sum(plain * plain, axis=-1)
    total = lax.dynamic_index_in_dim(squares, y, 0, keepdims=False)
    for k in (1, 2, 3):
        total += y_shift(lax.dynamic_index_in_dim(squares, (y + k) % 4, 0, keepdims=False), k)
    scale = lax.rsqrt(total / 8192.0 + norm_eps)[:, None]

    own_slots = core * HALF + jnp.arange(HALF, dtype=jnp.int32)
    slot_k = jnp.concatenate([own_slots, (1 - core) * HALF + jnp.arange(HALF, dtype=jnp.int32)])
    allowed = (slot_k[None, :] <= own_slots[:, None]) & (slot_k[None, :] < lengths[0])
    bias = jnp.where(allowed, 0.0, -jnp.inf).astype(jnp.float32)
    cosine, sine = rope_tables(own_slots)

    kv_rows = key_value_rows(core, sums, scale, cosine, sine)
    kv_other = core_swap(kv_rows)
    own_a = attention(0, sums, scale, cosine, sine, bias, kv_rows, kv_other)
    far_a = zh_swap(own_a)
    own_b = attention(1, sums, scale, cosine, sine, bias, kv_rows, kv_other)
    far_b = zh_swap(own_b)
    attended = (own_a, own_b, far_a, far_b)

    def product(dz, dx, added=(), halves=False):
        return chunk((zl ^ dz, (x + dx) % 4), zh, attended, out_near, out_other, added, halves)

    low, high = product(1, 2, halves=True)
    beside_low, beside_high = x_shift(low, 1), x_shift(high, -1)
    low, high = product(0, 2, halves=True)
    beside_low, beside_high, low, high = lax.optimization_barrier(
        (beside_low, beside_high, low, high)
    )
    here_low, here_high = x_shift(low, 1), x_shift(high, -1)
    beside_a = x_shift(product(1, 1, [(beside_low, 0)]), 1)
    beside_b = x_shift(product(1, 3, [(beside_high, 1)]), -1)
    here_a = x_shift(product(0, 1, [(here_low, 0)]), 1)
    here_b = x_shift(product(0, 3, [(here_high, 1)]), -1)
    across = zl_swap(product(1, 0, [(beside_a, None), (beside_b, None)]))
    mixed = product(0, 0, [(here_a, None), (here_b, None), (across, None)])
    keep = send(half_of(mixed, core, 1), to_home(0))
    got = send(half_of(mixed, 1 - core, 1), to_home(1))
    return (wide + ordered(is_first, keep, got, 0).astype(jnp.float32)).astype(jnp.bfloat16)


def solution(mesh):
    split = Mesh(mesh.devices.reshape(SIZES), AXES)
    gx, gy = ("zl", "x", "core"), ("y", "zh")
    placed = (P(gy, gx), P(), P(gy, gx), P(gy, None), P(gx, gy), P(gy))
    return jax.shard_map(
        local, mesh=split, in_specs=placed, out_specs=P(gy, gx), check_vma=False
    )
```

time: 274 us -> 294 us (1.073)
  matrix products: 36.8 us -> 0 us
  Pallas kernels: 9.63 us -> 39.3 us
  waiting for transfers between devices: 113 us -> 132 us
  starting transfers between devices: 57.4 us -> 72 us
  other arithmetic: 17.8 us -> 9.96 us
    reduce_scatter x2 -> x0, waiting for transfers between devices: 70.7 us -> none  [the longest x1 51.3 us: local(): lax.psum_scatter(partial.reshape(8, HALF, 1024), ('zl', 'x'), scatter_dim...]
    all_gather x1, waiting for transfers between devices: 0.02 us -> 49.2 us  [local(): out_near = lax.all_gather(out_weight, 'y', axis=0, tiled=False)]
    ppermute x22 -> x37, waiting for transfers between devices: 41.7 us -> 82.1 us  [send(): return lax.ppermute(value, AXES, pairs(change))]
    dot_general x5 -> x0, matrix products: 36.8 us -> none  [the longest x1 27.3 us: dot(): return jnp.dot(a, b, preferred_element_type=jnp.float32)]
    pallas_call x2 -> x13, Pallas kernels: 9.63 us -> 39.3 us  [the longest x8 24.4 us: chunk(): pl.pallas_call(lambda *refs: chunk_kernel(starts, halves, *refs), grid_sp...]
    unnamed x10 -> x41, local copies, waits for them, and re-layouts: 0.67 us -> 15.9 us
    ppermute x22 -> x37, starting transfers between devices: 57.3 us -> 72 us  [send(): return lax.ppermute(value, AXES, pairs(change))]
    dynamic_update_slice x5, local copies, waits for them, and re-layouts: 7.42 us -> 2.33 us  [local(): lax.dynamic_update_slice(gathered, part[None], (zs * 2 + xs // 2, 0, xs %...]
  transfers between devices with their start and end apart: 25 -> 38, of which waited for: 13 -> 22; matrix products, arithmetic and copies ran while one was open for 25% -> 6% of each run, Pallas kernels for 4% -> 9%
where the time goes in v5:
time: 294 us; the launch traced here: 292 us
  waiting for transfers between devices  132 us (45%)
  starting transfers between devices  72 us (24%)
  Pallas kernels  39.3 us (13%)
  local copies, waits for them, and re-layouts  24.4 us (8%)
  between operations  14.5 us (5%)
  other arithmetic  9.96 us (3%)
    ppermute x37, waiting for transfers between devices, send(): return lax.ppermute(value, AXES, pairs(change))  82.1 us
    ppermute x37, starting transfers between devices, send(): return lax.ppermute(value, AXES, pairs(change))  72 us
    all_gather x1, waiting for transfers between devices, local(): out_near = lax.all_gather(out_weight, 'y', axis=0, tiled=False)  49.2 us
    pallas_call x8, Pallas kernels, chunk(): pl.pallas_call(lambda *refs: chunk_kernel(starts, halves, *refs), grid_sp...  24.4 us
    unnamed x41, local copies, waits for them, and re-layouts  15.9 us
    pallas_call x2, Pallas kernels, project(): pl.pallas_call(lambda *refs: project_kernel(steps, *refs), grid_spec=pltp...  9.42 us
  transfers between devices with their start and end apart: 38, of which 22 were waited for; matrix products, arithmetic and copies ran while one was open for 6% of the time, Pallas kernels for 9%

profile of v5, /device:TPU:3, one launch (start us, length us, event | category | flops | bytes accessed | tf_op | source)
XLA Modules:
  0.0 292.2 jit_solution(8150891543237297516)
XLA Ops:
  10.5 49.2 %all-gather.3.cloned.1.call-done = bf16[2048,1024]{1,0:T(8,128)(2,1)} async-done(((bf16[512,1024]{1,0:T(8,128)(2,1)}), bf16[2048,1024]{1,0:T(8,128)(2,1)}) %all-gather.3.cloned.1.call-update) | async-done | bytes 4194320 | tf_op jit(solution)/shard_map/all_gather | solution.py:345
  69.1 15.5 %collective-permute-start.2 = (bf16[256,1024]{1,0:T(8,128)(2,1)}, bf16[256,1024]{1,0:T(8,128)(2,1)}, u32[]{:S(2)}, u32[]{:S(2)}) collective-permute-start(bf16[256,1024]{1,0:T(8,128)(2,1)} %maximum_select_fusion.1), channel_id=1, source_target_pairs={{0,16},{1,17},{2,18},{3,19},{4,20},{5,21},{6,22},{7,23},{8,24},{9,... | collective-permute-start | bytes 1572872 | tf_op jit(solution)/shard_map/ppermute | solution.py:41
  84.5 6.6 %collective-permute-done.5 = bf16[512,640]{1,0:T(8,128)(2,1)} collective-permute-done((bf16[512,640]{1,0:T(8,128)(2,1)}, bf16[512,640]{1,0:T(8,128)(2,1)}, u32[]{:S(2)}, u32[]{:S(2)}) %collective-permute-start.5) | collective-permute-done | bytes 655392 | tf_op jit(solution)/shard_map/ppermute | solution.py:41
  92.0 4.0 %collective-permute-done.2 = bf16[256,1024]{1,0:T(8,128)(2,1)} collective-permute-done((bf16[256,1024]{1,0:T(8,128)(2,1)}, bf16[256,1024]{1,0:T(8,128)(2,1)}, u32[]{:S(2)}, u32[]{:S(2)}) %collective-permute-start.2) | collective-permute-done | bytes 524320 | tf_op jit(solution)/shard_map/ppermute | solution.py:41
  97.9 5.6 %collective-permute-done.4 = bf16[256,1024]{1,0:T(8,128)(2,1)} collective-permute-done((bf16[256,1024]{1,0:T(8,128)(2,1)}, bf16[256,1024]{1,0:T(8,128)(2,1)}, u32[]{:S(2)}, u32[]{:S(2)}) %collective-permute-start.4) | collective-permute-done | bytes 524320 | tf_op jit(solution)/shard_map/ppermute | solution.py:41
  113.1 6.1 %collective-permute-done.13 = bf16[512,640]{1,0:T(8,128)(2,1)S(1)} collective-permute-done((bf16[512,640]{1,0:T(8,128)(2,1)}, bf16[512,640]{1,0:T(8,128)(2,1)S(1)}, u32[]{:S(2)}, u32[]{:S(2)}) %collective-permute-start.13) | collective-permute-done | bytes 655392 | tf_op jit(solution)/shard_map/ppermute | solution.py:41
  119.3 3.3 %collective-permute-start.14 = (bf16[1024,640]{1,0:T(8,128)(2,1)S(1)}, bf16[1024,640]{1,0:T(8,128)(2,1)S(1)}, u32[]{:S(2)}, u32[]{:S(2)}) collective-permute-start(bf16[1024,640]{1,0:T(8,128)(2,1)S(1)} %constant_dynamic-update-slice_fusion.refs_4_), channel_id=1, source_target_pairs={{0,8},{1,9},{2,10},{3,11},{4,12},{5,13},{6,14},{7,15},{8,0},{9,1},... | collective-permute-start | bytes 3932168 | tf_op jit(solution)/shard_map/ppermute | solution.py:41
  127.6 3.2 %collective-permute-done.7 = bf16[128,1024]{1,0:T(8,128)(2,1)S(1)} collective-permute-done((bf16[128,1024]{1,0:T(8,128)(2,1)S(1)}, bf16[128,1024]{1,0:T(8,128)(2,1)S(1)}, u32[]{:S(2)}, u32[]{:S(2)}) %collective-permute-start.7) | collective-permute-done | bytes 262176 | tf_op jit(solution)/shard_map/ppermute | solution.py:41
  132.7 3.5 %collective-permute-done.12 = bf16[128,1024]{1,0:T(8,128)(2,1)S(1)} collective-permute-done((bf16[128,1024]{1,0:T(8,128)(2,1)S(1)}, bf16[128,1024]{1,0:T(8,128)(2,1)S(1)}, u32[]{:S(2)}, u32[]{:S(2)}) %collective-permute-start.12) | collective-permute-done | bytes 262176 | tf_op jit(solution)/shard_map/ppermute | solution.py:41
  144.4 7.1 %shard_map.64 = (bf16[256,1280]{1,0:T(8,128)(2,1)}, bf16[256,1280]{1,0:T(8,128)(2,1)S(1)}, bf16[256,1280]{1,0:T(8,128)(2,1)S(1)}) custom-call(s32[4]{0:T(128)S(1)} %pad_add_fusion.2.refs_0_, bf16[4,256,2048]{2,1,0:T(8,128)(2,1)S(1)} %fusion.4.refs_1_, bf16[1024,640]{1,0:T(8,128)(2,1)S(1)} %pad_maximum_fusion.refs_2_, ...), custom_call_target="tpu_custom_call" | custom-call | tf_op jit(solution)/shard_map/pallas_call | solution.py:210
  159.1 4.8 %collective-permute-done.22 = f32[256]{0:T(256)S(1)} collective-permute-done((f32[256]{0:T(256)S(1)}, f32[256]{0:T(256)S(1)}, u32[]{:S(2)}, u32[]{:S(2)}) %collective-permute-start.22) | collective-permute-done | bytes 1056 | tf_op jit(solution)/shard_map/ppermute | solution.py:41
  168.3 9.2 %collective-permute-start.23 = (bf16[256,256]{1,0:T(8,128)(2,1)}, bf16[256,256]{1,0:T(8,128)(2,1)S(1)}, u32[]{:S(2)}, u32[]{:S(2)}) collective-permute-start(bf16[256,256]{1,0:T(8,128)(2,1)} %shard_map.66.own_ref), channel_id=1, source_target_pairs={{0,8},{1,9},{2,10},{3,11},{4,12},{5,13},{6,14},{7,15},{8,0},{9,1},... | collective-permute-start | bytes 393224 | tf_op jit(solution)/shard_map/ppermute | solution.py:41
  188.5 4.2 %collective-permute-done.24.refs_3_ = bf16[256,512]{1,0:T(8,128)(2,1)S(1)} collective-permute-done((bf16[256,512]{1,0:T(8,128)(2,1)S(1)}, bf16[256,512]{1,0:T(8,128)(2,1)S(1)}, u32[]{:S(2)}, u32[]{:S(2)}) %collective-permute-start.24) | collective-permute-done | bytes 262176 | tf_op jit(solution)/shard_map/ppermute | solution.py:41
  192.7 5.6 %collective-permute-done.25.refs_4_ = bf16[256,512]{1,0:T(8,128)(2,1)S(1)} collective-permute-done((bf16[256,512]{1,0:T(8,128)(2,1)S(1)}, bf16[256,512]{1,0:T(8,128)(2,1)S(1)}, u32[]{:S(2)}, u32[]{:S(2)}) %collective-permute-start.25) | collective-permute-done | bytes 262176 | tf_op jit(solution)/shard_map/ppermute | solution.py:41
  208.4 3.2 %shard_map.70 = (bf16[128,1024]{1,0:T(8,128)(2,1)S(1)}, bf16[128,1024]{1,0:T(8,128)(2,1)}) custom-call(s32[2]{0:T(128)S(1)} %get-tuple-element.65.refs_0_, bf16[256,512]{1,0:T(8,128)(2,1)S(1)} %shard_map.67.refs_1_, bf16[256,512]{1,0:T(8,128)(2,1)S(1)} %shard_map.68.refs_2_, bf16[256,512]{1,0:T(8,128)(2,1)S(1)} %collective-permute-done.24.refs_3_, ...), custom_call_target="tpu_custom_call" | custom-call | tf_op jit(solution)/shard_map/pallas_call | solution.py:259
  211.7 3.3 %shard_map.73 = bf16[256,1024]{1,0:T(8,128)(2,1)} custom-call(s32[2]{0:T(128)S(1)} %pad_add_fusion.9.refs_0_, bf16[256,512]{1,0:T(8,128)(2,1)S(1)} %shard_map.67.refs_1_, bf16[256,512]{1,0:T(8,128)(2,1)S(1)} %shard_map.68.refs_2_, bf16[256,512]{1,0:T(8,128)(2,1)S(1)} %collective-permute-done.24.refs_3_, ...), custom_call_target="tpu_custom_call" | custom-call | tf_op jit(solution)/shard_map/pallas_call | solution.py:259
  216.5 3.3 %shard_map.74 = bf16[256,1024]{1,0:T(8,128)(2,1)} custom-call(s32[2]{0:T(128)S(1)} %pad_add_fusion.10.refs_0_, bf16[256,512]{1,0:T(8,128)(2,1)S(1)} %shard_map.67.refs_1_, bf16[256,512]{1,0:T(8,128)(2,1)S(1)} %shard_map.68.refs_2_, bf16[256,512]{1,0:T(8,128)(2,1)S(1)} %collective-permute-done.24.refs_3_, ...), custom_call_target="tpu_custom_call" | custom-call | tf_op jit(solution)/shard_map/pallas_call | solution.py:259
  223.8 10.2 %collective-permute-done.28.refs_7_ = bf16[128,1024]{1,0:T(8,128)(2,1)S(1)} collective-permute-done((bf16[128,1024]{1,0:T(8,128)(2,1)S(1)}, bf16[128,1024]{1,0:T(8,128)(2,1)S(1)}, u32[]{:S(2)}, u32[]{:S(2)}) %collective-permute-start.28) | collective-permute-done | bytes 262176 | tf_op jit(solution)/shard_map/ppermute | solution.py:41
  236.2 3.3 %shard_map.71 = bf16[256,1024]{1,0:T(8,128)(2,1)} custom-call(s32[2]{0:T(128)S(1)} %pad_add_fusion.4.refs_0_, bf16[256,512]{1,0:T(8,128)(2,1)S(1)} %shard_map.67.refs_1_, bf16[256,512]{1,0:T(8,128)(2,1)S(1)} %shard_map.68.refs_2_, bf16[256,512]{1,0:T(8,128)(2,1)S(1)} %collective-permute-done.24.refs_3_, ...), custom_call_target="tpu_custom_call" | custom-call | tf_op jit(solution)/shard_map/pallas_call | solution.py:259
  239.5 3.3 %shard_map.72 = bf16[256,1024]{1,0:T(8,128)(2,1)} custom-call(s32[2]{0:T(128)S(1)} %pad_add_fusion.7.refs_0_, bf16[256,512]{1,0:T(8,128)(2,1)S(1)} %shard_map.67.refs_1_, bf16[256,512]{1,0:T(8,128)(2,1)S(1)} %shard_map.68.refs_2_, bf16[256,512]{1,0:T(8,128)(2,1)S(1)} %collective-permute-done.24.refs_3_, ...), custom_call_target="tpu_custom_call" | custom-call | tf_op jit(solution)/shard_map/pallas_call | solution.py:259
  253.9 6.2 %collective-permute-done.34.refs_9_ = bf16[256,1024]{1,0:T(8,128)(2,1)S(1)} collective-permute-done((bf16[256,1024]{1,0:T(8,128)(2,1)S(1)}, bf16[256,1024]{1,0:T(8,128)(2,1)S(1)}, u32[]{:S(2)}, u32[]{:S(2)}) %collective-permute-start.34) | collective-permute-done | bytes 524320 | tf_op jit(solution)/shard_map/ppermute | solution.py:41
  265.2 6.6 %collective-permute-start.36 = (bf16[256,512]{1,0:T(8,128)(2,1)S(1)}, bf16[256,512]{1,0:T(8,128)(2,1)S(1)}, u32[]{:S(2)}, u32[]{:S(2)}) collective-permute-start(bf16[256,512]{1,0:T(8,128)(2,1)S(1)} %get-tuple-element.54), channel_id=1, source_target_pairs={{0,8},{1,24},{2,10},{3,26},{4,12},{5,28},{6,14},{7,30},{8,0},{9,16... | collective-permute-start | bytes 786440 | tf_op jit(solution)/shard_map/ppermute | solution.py:41
  274.8 3.4 %collective-permute-done.36 = bf16[256,512]{1,0:T(8,128)(2,1)S(1)} collective-permute-done((bf16[256,512]{1,0:T(8,128)(2,1)S(1)}, bf16[256,512]{1,0:T(8,128)(2,1)S(1)}, u32[]{:S(2)}, u32[]{:S(2)}) %collective-permute-start.36) | collective-permute-done | bytes 262176 | tf_op jit(solution)/shard_map/ppermute | solution.py:41
  278.2 6.1 %collective-permute-done.35 = bf16[256,512]{1,0:T(8,128)(2,1)S(1)} collective-permute-done((bf16[256,512]{1,0:T(8,128)(2,1)S(1)}, bf16[256,512]{1,0:T(8,128)(2,1)S(1)}, u32[]{:S(2)}, u32[]{:S(2)}) %collective-permute-start.35) | collective-permute-done | bytes 262176 | tf_op jit(solution)/shard_map/ppermute | solution.py:41
  (155 shorter events, 100.8 us)
Async XLA Ops:
  6.5 53.2 %all-gather.3.cloned.1.call-start = ((), (), s32[]{:S(2)}) async-start(), calls=%async_computation | async-start | bytes 5242880 | tf_op jit(solution)/shard_map/all_gather | solution.py:345
  59.7 91.7 %collective-permute-start.17 = (bf16[4,512,1024]{2,1,0:T(8,128)(2,1)}, bf16[4,512,1024]{2,1,0:T(8,128)(2,1)}, u32[]{:S(2)}, u32[]{:S(2)}) collective-permute-start(bf16[4,512,1024]{2,1,0:T(8,128)(2,1)} %bitcast.46), channel_id=1, source_target_pairs={{0,8},{1,9},{2,10},{3,11},{4,12},{5,13},{6,14},{7,15},{8,0},{9,1},... | collective-permute-start | bytes 12582920 | tf_op jit(solution)/shard_map/ppermute | solution.py:41
  61.1 42.4 %collective-permute-start.6 = (bf16[1024,640]{1,0:T(8,128)(2,1)S(1)}, bf16[1024,640]{1,0:T(8,128)(2,1)S(1)}, u32[]{:S(2)}, u32[]{:S(2)}) collective-permute-start(bf16[1024,640]{1,0:T(8,128)(2,1)S(1)} %pad_maximum_fusion.refs_2_), channel_id=1, source_target_pairs={{0,8},{1,9},{2,10},{3,11},{4,12},{5,13},{6,14},{7,15},{8,0},{9,1},... | collective-permute-start | bytes 3932168 | tf_op jit(solution)/shard_map/ppermute | solution.py:41
  62.3 28.8 %collective-permute-start.5 = (bf16[512,640]{1,0:T(8,128)(2,1)}, bf16[512,640]{1,0:T(8,128)(2,1)}, u32[]{:S(2)}, u32[]{:S(2)}) collective-permute-start(bf16[512,640]{1,0:T(8,128)(2,1)} %get-tuple-element.52), channel_id=1, source_target_pairs={{0,1},{1,0},{2,3},{3,2},{4,5},{5,4},{6,7},{7,6},{8,9},{9,8},{10,11... | collective-permute-start | bytes 1966088 | tf_op jit(solution)/shard_map/ppermute | solution.py:41
  69.1 26.9 %collective-permute-start.2 = (bf16[256,1024]{1,0:T(8,128)(2,1)}, bf16[256,1024]{1,0:T(8,128)(2,1)}, u32[]{:S(2)}, u32[]{:S(2)}) collective-permute-start(bf16[256,1024]{1,0:T(8,128)(2,1)} %maximum_select_fusion.1), channel_id=1, source_target_pairs={{0,16},{1,17},{2,18},{3,19},{4,20},{5,21},{6,22},{7,23},{8,24},{9,... | collective-permute-start | bytes 1572872 | tf_op jit(solution)/shard_map/ppermute | solution.py:41
  84.5 13.3 %collective-permute-start.3 = (bf16[256,1024]{1,0:T(8,128)(2,1)}, bf16[256,1024]{1,0:T(8,128)(2,1)S(1)}, u32[]{:S(2)}, u32[]{:S(2)}) collective-permute-start(bf16[256,1024]{1,0:T(8,128)(2,1)} %maximum_select_fusion.1), channel_id=1, source_target_pairs={{0,48},{1,49},{2,50},{3,51},{4,52},{5,53},{6,54},{7,55},{8,56},{9,... | collective-permute-start | bytes 1572872 | tf_op jit(solution)/shard_map/ppermute | solution.py:41
  91.1 12.4 %collective-permute-start.4 = (bf16[256,1024]{1,0:T(8,128)(2,1)}, bf16[256,1024]{1,0:T(8,128)(2,1)}, u32[]{:S(2)}, u32[]{:S(2)}) collective-permute-start(bf16[256,1024]{1,0:T(8,128)(2,1)} %maximum_select_fusion.1), channel_id=1, source_target_pairs={{0,64},{1,65},{2,66},{3,67},{4,68},{5,69},{6,70},{7,71},{8,72},{9,... | collective-permute-start | bytes 1572872 | tf_op jit(solution)/shard_map/ppermute | solution.py:41
  103.5 15.7 %collective-permute-start.13 = (bf16[512,640]{1,0:T(8,128)(2,1)}, bf16[512,640]{1,0:T(8,128)(2,1)S(1)}, u32[]{:S(2)}, u32[]{:S(2)}) collective-permute-start(bf16[512,640]{1,0:T(8,128)(2,1)} %get-tuple-element.34), channel_id=1, source_target_pairs={{0,1},{1,0},{2,3},{3,2},{4,5},{5,4},{6,7},{7,6},{8,9},{9,8},{10,11... | collective-permute-start | bytes 1966088 | tf_op jit(solution)/shard_map/ppermute | solution.py:41
  107.9 24.6 %collective-permute-start.9 = (bf16[256,1024]{1,0:T(8,128)(2,1)}, bf16[256,1024]{1,0:T(8,128)(2,1)S(1)}, u32[]{:S(2)}, u32[]{:S(2)}) collective-permute-start(bf16[256,1024]{1,0:T(8,128)(2,1)} %collective-permute-done.4), channel_id=1, source_target_pairs={{0,16},{1,17},{2,18},{3,19},{4,20},{5,21},{6,22},{7,23},{8,24},{9,... | collective-permute-start | bytes 1572872 | tf_op jit(solution)/shard_map/ppermute | solution.py:41
  109.1 21.7 %collective-permute-start.10 = (bf16[256,1024]{1,0:T(8,128)(2,1)}, bf16[256,1024]{1,0:T(8,128)(2,1)S(1)}, u32[]{:S(2)}, u32[]{:S(2)}) collective-permute-start(bf16[256,1024]{1,0:T(8,128)(2,1)} %collective-permute-done.4), channel_id=1, source_target_pairs={{0,48},{1,49},{2,50},{3,51},{4,52},{5,53},{6,54},{7,55},{8,56},{9,... | collective-permute-start | bytes 1572872 | tf_op jit(solution)/shard_map/ppermute | solution.py:41
  109.4 16.1 %collective-permute-start.8 = (bf16[128,1024]{1,0:T(8,128)(2,1)S(1)}, bf16[128,1024]{1,0:T(8,128)(2,1)S(1)}, u32[]{:S(2)}, u32[]{:S(2)}) collective-permute-start(bf16[128,1024]{1,0:T(8,128)(2,1)S(1)} %slice.26), channel_id=1, source_target_pairs={{0,48},{1,49},{2,50},{3,51},{4,52},{5,53},{6,54},{7,55},{8,56},{9,... | collective-permute-start | bytes 786440 | tf_op jit(solution)/shard_map/ppermute | solution.py:41
  119.3 18.6 %collective-permute-start.14 = (bf16[1024,640]{1,0:T(8,128)(2,1)S(1)}, bf16[1024,640]{1,0:T(8,128)(2,1)S(1)}, u32[]{:S(2)}, u32[]{:S(2)}) collective-permute-start(bf16[1024,640]{1,0:T(8,128)(2,1)S(1)} %constant_dynamic-update-slice_fusion.refs_4_), channel_id=1, source_target_pairs={{0,8},{1,9},{2,10},{3,11},{4,12},{5,13},{6,14},{7,15},{8,0},{9,1},... | collective-permute-start | bytes 3932168 | tf_op jit(solution)/shard_map/ppermute | solution.py:41
  140.2 11.2 %collective-permute-start.15 = (bf16[128,1280]{1,0:T(8,128)(2,1)S(1)}, bf16[128,1280]{1,0:T(8,128)(2,1)S(1)}, u32[]{:S(2)}, u32[]{:S(2)}) collective-permute-start(bf16[128,1280]{1,0:T(8,128)(2,1)S(1)} %get-tuple-element.37), channel_id=1, source_target_pairs={{0,2},{1,3},{2,4},{3,5},{4,6},{5,7},{6,0},{7,1},{8,10},{9,11},{10,... | collective-permute-start | bytes 983048 | tf_op jit(solution)/shard_map/ppermute | solution.py:41
  153.5 11.7 %collective-permute-start.18 = (bf16[256,1280]{1,0:T(8,128)(2,1)}, bf16[256,1280]{1,0:T(8,128)(2,1)S(1)}, u32[]{:S(2)}, u32[]{:S(2)}) collective-permute-start(bf16[256,1280]{1,0:T(8,128)(2,1)} %add_dynamic-update-slice_fusion.1), channel_id=1, source_target_pairs={{0,2},{1,3},{2,4},{3,5},{4,6},{5,7},{6,0},{7,1},{8,10},{9,11},{10,... | collective-permute-start | bytes 1966088 | tf_op jit(solution)/shard_map/ppermute | solution.py:41
  153.6 11.6 %collective-permute-start.19 = (bf16[256,1280]{1,0:T(8,128)(2,1)S(1)}, bf16[256,1280]{1,0:T(8,128)(2,1)S(1)}, u32[]{:S(2)}, u32[]{:S(2)}) collective-permute-start(bf16[256,1280]{1,0:T(8,128)(2,1)S(1)} %add_dynamic-update-slice_fusion), channel_id=1, source_target_pairs={{0,6},{1,7},{2,0},{3,1},{4,2},{5,3},{6,4},{7,5},{8,14},{9,15},{10,... | collective-permute-start | bytes 1966088 | tf_op jit(solution)/shard_map/ppermute | solution.py:41
  185.4 12.9 %collective-permute-start.25 = (bf16[256,512]{1,0:T(8,128)(2,1)S(1)}, bf16[256,512]{1,0:T(8,128)(2,1)S(1)}, u32[]{:S(2)}, u32[]{:S(2)}) collective-permute-start(bf16[256,512]{1,0:T(8,128)(2,1)S(1)} %shard_map.68.refs_2_), channel_id=1, source_target_pairs={{0,1},{1,0},{2,3},{3,2},{4,5},{5,4},{6,7},{7,6},{8,9},{9,8},{10,11... | collective-permute-start | bytes 786440 | tf_op jit(solution)/shard_map/ppermute | solution.py:41
  215.0 30.1 %collective-permute-start.32 = (bf16[256,1024]{1,0:T(8,128)(2,1)}, bf16[256,1024]{1,0:T(8,128)(2,1)S(1)}, u32[]{:S(2)}, u32[]{:S(2)}) collective-permute-start(bf16[256,1024]{1,0:T(8,128)(2,1)} %shard_map.73), channel_id=1, source_target_pairs={{0,16},{1,17},{2,18},{3,19},{4,20},{5,21},{6,22},{7,23},{8,24},{9,... | collective-permute-start | bytes 1572872 | tf_op jit(solution)/shard_map/ppermute | solution.py:41
  219.8 26.0 %collective-permute-start.33 = (bf16[256,1024]{1,0:T(8,128)(2,1)}, bf16[256,1024]{1,0:T(8,128)(2,1)}, u32[]{:S(2)}, u32[]{:S(2)}) collective-permute-start(bf16[256,1024]{1,0:T(8,128)(2,1)} %shard_map.74), channel_id=1, source_target_pairs={{0,48},{1,49},{2,50},{3,51},{4,52},{5,53},{6,54},{7,55},{8,56},{9,... | collective-permute-start | bytes 1572872 | tf_op jit(solution)/shard_map/ppermute | solution.py:41
  220.9 13.1 %collective-permute-start.28 = (bf16[128,1024]{1,0:T(8,128)(2,1)S(1)}, bf16[128,1024]{1,0:T(8,128)(2,1)S(1)}, u32[]{:S(2)}, u32[]{:S(2)}) collective-permute-start(bf16[128,1024]{1,0:T(8,128)(2,1)S(1)} %get-tuple-element.47), channel_id=1, source_target_pairs={{0,16},{1,17},{2,18},{3,19},{4,20},{5,21},{6,22},{7,23},{8,24},{9,... | collective-permute-start | bytes 786440 | tf_op jit(solution)/shard_map/ppermute | solution.py:41
  222.2 17.3 %collective-permute-start.30 = (bf16[128,1024]{1,0:T(8,128)(2,1)}, bf16[128,1024]{1,0:T(8,128)(2,1)S(1)}, u32[]{:S(2)}, u32[]{:S(2)}) collective-permute-start(bf16[128,1024]{1,0:T(8,128)(2,1)} %get-tuple-element.48), channel_id=1, source_target_pairs={{0,48},{1,49},{2,50},{3,51},{4,52},{5,53},{6,54},{7,55},{8,56},{9,... | collective-permute-start | bytes 786440 | tf_op jit(solution)/shard_map/ppermute | solution.py:41
  239.5 12.2 %collective-permute-start.29 = (bf16[256,1024]{1,0:T(8,128)(2,1)}, bf16[256,1024]{1,0:T(8,128)(2,1)S(1)}, u32[]{:S(2)}, u32[]{:S(2)}) collective-permute-start(bf16[256,1024]{1,0:T(8,128)(2,1)} %shard_map.71), channel_id=1, source_target_pairs={{0,16},{1,17},{2,18},{3,19},{4,20},{5,21},{6,22},{7,23},{8,24},{9,... | collective-permute-start | bytes 1572872 | tf_op jit(solution)/shard_map/ppermute | solution.py:41
  242.8 11.1 %collective-permute-start.31 = (bf16[256,1024]{1,0:T(8,128)(2,1)}, bf16[256,1024]{1,0:T(8,128)(2,1)}, u32[]{:S(2)}, u32[]{:S(2)}) collective-permute-start(bf16[256,1024]{1,0:T(8,128)(2,1)} %shard_map.72), channel_id=1, source_target_pairs={{0,48},{1,49},{2,50},{3,51},{4,52},{5,53},{6,54},{7,55},{8,56},{9,... | collective-permute-start | bytes 1572872 | tf_op jit(solution)/shard_map/ppermute | solution.py:41
  265.2 13.0 %collective-permute-start.36 = (bf16[256,512]{1,0:T(8,128)(2,1)S(1)}, bf16[256,512]{1,0:T(8,128)(2,1)S(1)}, u32[]{:S(2)}, u32[]{:S(2)}) collective-permute-start(bf16[256,512]{1,0:T(8,128)(2,1)S(1)} %get-tuple-element.54), channel_id=1, source_target_pairs={{0,8},{1,24},{2,10},{3,26},{4,12},{5,28},{6,14},{7,30},{8,0},{9,16... | collective-permute-start | bytes 786440 | tf_op jit(solution)/shard_map/ppermute | solution.py:41
  271.8 12.5 %collective-permute-start.35 = (bf16[256,512]{1,0:T(8,128)(2,1)S(1)}, bf16[256,512]{1,0:T(8,128)(2,1)S(1)}, u32[]{:S(2)}, u32[]{:S(2)}) collective-permute-start(bf16[256,512]{1,0:T(8,128)(2,1)S(1)} %get-tuple-element.53), channel_id=1, source_target_pairs={{0,0},{1,16},{2,2},{3,18},{4,4},{5,20},{6,6},{7,22},{8,8},{9,24},{... | collective-permute-start | bytes 786440 | tf_op jit(solution)/shard_map/ppermute | solution.py:41
  (34 other events, 246.8 us)
Sparse Core Ops, SparseCore 0:
  9.0 50.6 all-gather.2

commit v6 on v5

--- a/solution.py
+++ b/solution.py
@@ -99,7 +99,7 @@
 
 
 WIDE = 640
-GRANT = pltpu.CompilerParams(vmem_limit_bytes=40 * 1024 * 1024)
+GRANT = pltpu.CompilerParams(vmem_limit_bytes=56 * 1024 * 1024)
 
 
 def total_of(refs, cols=slice(None)):
@@ -220,57 +220,58 @@
     )(jnp.stack([zh, *which]).astype(jnp.int32), gathered, *weights)
 
 
-def chunk_kernel(starts, halves, at_ref, own_a, own_b, far_a, far_b, near, other, *refs):
-    added, outs, rows = refs[: len(starts)], refs[len(starts) : -1], refs[-1]
-
-    @pl.when(at_ref[1] == 1)
+def products_kernel(split, steps, at_ref, own_a, own_b, far_a, far_b, near, other, *refs):
+    outs, rows = refs[:-1], refs[-1]
+    step = pl.program_id(0)
+
+    @pl.when(at_ref[steps + step] == 1)
     def _():
         rows[:, :512] = own_a[...]
         rows[:, 512:] = own_b[...]
 
-    @pl.when(at_ref[1] == 0)
+    @pl.when(at_ref[steps + step] == 0)
     def _():
         rows[:, :512] = far_a[...]
         rows[:, 512:] = far_b[...]
 
     product = dot(rows[:, :512], near[0]) + dot(rows[:, 512:], other[0])
-    parts = [product[:128], product[128:]]
-    for start, ref in zip(starts, added):
-        if start is None:
-            parts[0] += ref[:128].astype(jnp.float32)
-            parts[1] += ref[128:].astype(jnp.float32)
-        else:
-            parts[start] += ref[...].astype(jnp.float32)
-    if halves:
-        outs[0][...] = parts[0].astype(jnp.bfloat16)
-        outs[1][...] = parts[1].astype(jnp.bfloat16)
-    else:
-        outs[0][:128] = parts[0].astype(jnp.bfloat16)
-        outs[0][128:] = parts[1].astype(jnp.bfloat16)
-
-
-def chunk(target, zh, attended, near, other, added=(), halves=False):
-    zt, xt = target
-    at = jnp.stack([zt * 2 + xt // 2, (xt % 2 == zh).astype(jnp.int32)]).astype(jnp.int32)
+    product = product.astype(jnp.bfloat16)
+    for i in range(steps):
+
+        @pl.when(step == i)
+        def _():
+            if split:
+                outs[0][i * 128 : i * 128 + 128] = product[:128]
+                outs[1][i * 128 : i * 128 + 128] = product[128:]
+            else:
+                outs[i][...] = product
+
+
+def products(targets, zh, attended, near, other, split=False):
+    steps = len(targets)
+    blocks = [zt * 2 + xt // 2 for zt, xt in targets]
+    owns = [xt % 2 == zh for _, xt in targets]
+    at = jnp.stack([v.astype(jnp.int32) for v in blocks + owns])
     rows = pl.BlockSpec((HALF, 512), lambda i, at: (0, 0))
-    block = pl.BlockSpec((1, 512, 1024), lambda i, at: (at[0], 0, 0))
-    size = 128 if halves else HALF
-    starts = [start for _, start in added]
-    out = pl.pallas_call(
-        lambda *refs: chunk_kernel(starts, halves, *refs),
+    block = pl.BlockSpec((1, 512, 1024), lambda i, at: (at[i], 0, 0))
+    count = 2 if split else steps
+    return pl.pallas_call(
+        lambda *refs: products_kernel(split, steps, *refs),
         grid_spec=pltpu.PrefetchScalarGridSpec(
             num_scalar_prefetch=1,
-            grid=(1,),
-            in_specs=[rows] * 4
-            + [block] * 2
-            + [pl.BlockSpec(value.shape, lambda i, at: (0, 0)) for value, _ in added],
-            out_specs=[pl.BlockSpec((size, 1024), lambda i, at: (0, 0))] * (1 + halves),
+            grid=(steps,),
+            in_specs=[rows] * 4 + [block] * 2,
+            out_specs=[pl.BlockSpec((HALF, 1024), lambda i, at: (0, 0))] * count,
             scratch_shapes=[pltpu.VMEM((HALF, 1024), jnp.bfloat16)],
         ),
-        out_shape=[jax.ShapeDtypeStruct((size, 1024), jnp.bfloat16)] * (1 + halves),
+        out_shape=[jax.ShapeDtypeStruct((HALF, 1024), jnp.bfloat16)] * count,
         compiler_params=GRANT,
-    )(at, *attended, near, other, *[value for value, _ in added])
-    return out if halves else out[0]
+    )(at, *attended, near, other)
+
+
+def add_rows(value, arrived, start):
+    rows = arrived.shape[0]
+    return lax.dynamic_update_slice(value, value[start : start + rows] + arrived, (start, 0))
 
 
 def half_of(value, which, dim=0):
@@ -308,14 +309,13 @@
     kv_own = lax.dynamic_slice_in_dim(kv_weight, chip * 256 + core * 128, 128, 1)
     near = after(jnp.concatenate([query_weight, kv_own], axis=1), (mine_out, theirs_out))
     far_top = zh_swap(near[:512])
+    near_other = core_swap(near)
+    block, far_top, near_other = lax.optimization_barrier((block, far_top, near_other))
 
     beside = zl_swap(block)
     left = x_shift(block, 1)
     right = x_shift(block, -1)
-    near_other = core_swap(near)
-    left, right, beside, far_top, near_other = lax.optimization_barrier(
-        (left, right, beside, far_top, near_other)
-    )
+    left, right, beside = lax.optimization_barrier((left, right, beside))
     far_bottom = zh_swap(after(near[512:], beside))
     beside_left = x_shift(beside, 1)
     beside_right = x_shift(beside, -1)
@@ -343,17 +343,17 @@
     weights = (near, near_other, far, core_swap(far))
 
     out_near = lax.all_gather(out_weight, "y", axis=0, tiled=False)
-    out_other = core_swap(out_near)
 
     low, high = project([(y + 2) % 4], zh, gathered, weights)
     from_below = y_shift(low, 1)
     from_above = y_shift(high, -1)
-    from_below, from_above, out_other = lax.optimization_barrier(
-        (from_below, from_above, out_other)
+    upper, lower, kept = project([(y + 1) % 4, (y + 3) % 4, y], zh, gathered, weights)
+    from_below, from_above, upper, lower, kept = lax.optimization_barrier(
+        (from_below, from_above, upper, lower, kept)
     )
-    upper, lower, kept = project([(y + 1) % 4, (y + 3) % 4, y], zh, gathered, weights)
-    upper = lax.dynamic_update_slice(upper, upper[:128] + from_below, (0, 0))
-    lower = lax.dynamic_update_slice(lower, lower[128:] + from_above, (128, 0))
+    out_other = core_swap(after(out_near, (from_below, from_above)))
+    upper = add_rows(upper, from_below, 0)
+    lower = add_rows(lower, from_above, 128)
     sums = (kept, y_shift(upper, 1), y_shift(lower, -1))
 
     slice_gain = lax.dynamic_slice_in_dim(norm_gain, y * 2048, 2048, 0)
@@ -378,22 +378,25 @@
     far_b = zh_swap(own_b)
     attended = (own_a, own_b, far_a, far_b)
 
-    def product(dz, dx, added=(), halves=False):
-        return chunk((zl ^ dz, (x + dx) % 4), zh, attended, out_near, out_other, added, halves)
-
-    low, high = product(1, 2, halves=True)
-    beside_low, beside_high = x_shift(low, 1), x_shift(high, -1)
-    low, high = product(0, 2, halves=True)
-    beside_low, beside_high, low, high = lax.optimization_barrier(
-        (beside_low, beside_high, low, high)
+    def made(moves, split=False):
+        targets = [(zl ^ dz, (x + dx) % 4) for dz, dx in moves]
+        return products(targets, zh, attended, out_near, out_other, split)
+
+    low, high = made([(1, 2), (0, 2)], True)
+    from_left, from_right = x_shift(low, 1), x_shift(high, -1)
+    beside_a, beside_b, here_a, here_b, beside, mixed = made(
+        [(1, 1), (1, 3), (0, 1), (0, 3), (1, 0), (0, 0)]
     )
-    here_low, here_high = x_shift(low, 1), x_shift(high, -1)
-    beside_a = x_shift(product(1, 1, [(beside_low, 0)]), 1)
-    beside_b = x_shift(product(1, 3, [(beside_high, 1)]), -1)
-    here_a = x_shift(product(0, 1, [(here_low, 0)]), 1)
-    here_b = x_shift(product(0, 3, [(here_high, 1)]), -1)
-    across = zl_swap(product(1, 0, [(beside_a, None), (beside_b, None)]))
-    mixed = product(0, 0, [(here_a, None), (here_b, None), (across, None)])
+    beside_a = x_shift(add_rows(beside_a, from_left[:128], 0), 1)
+    beside_b = x_shift(add_rows(beside_b, from_right[:128], 128), -1)
+    here_a = x_shift(add_rows(here_a, from_left[128:], 0), 1)
+    here_b = x_shift(add_rows(here_b, from_right[128:], 128), -1)
+
+    def sum_of(*values):
+        return sum(v.astype(jnp.float32) for v in values).astype(jnp.bfloat16)
+
+    across = zl_swap(sum_of(beside, beside_a, beside_b))
+    mixed = sum_of(mixed, here_a, here_b, across)
     keep = send(half_of(mixed, core, 1), to_home(0))
     got = send(half_of(mixed, 1 - core, 1), to_home(1))
     return (wide + ordered(is_first, keep, got, 0).astype(jnp.float32)).astype(jnp.bfloat16)

time: 294 us -> 248 us (0.84)
  waiting for transfers between devices: 132 us -> 101 us
  starting transfers between devices: 72 us -> 53.7 us
  other arithmetic: 9.96 us -> 21.2 us
  local copies, waits for them, and re-layouts: 24.4 us -> 14.2 us
  Pallas kernels: 39.3 us -> 42.6 us
    all_gather x1, waiting for transfers between devices: 49.2 us -> 0.02 us  [local(): out_near = lax.all_gather(out_weight, 'y', axis=0, tiled=False)]
    ppermute x37 -> x35, starting transfers between devices: 72 us -> 53.7 us  [send(): return lax.ppermute(value, AXES, pairs(change))]
    ppermute x37 -> x35, waiting for transfers between devices: 82.1 us -> 100 us  [send(): return lax.ppermute(value, AXES, pairs(change))]
    pallas_call x8 -> x2, Pallas kernels: 24.4 us -> 16.1 us  [products(): pl.pallas_call(lambda *refs: products_kernel(split, steps, *refs), grid_s...]
    unnamed x41 -> x39, local copies, waits for them, and re-layouts: 15.9 us -> 7.67 us
    pallas_call x2, Pallas kernels: 9.42 us -> 16.5 us  [project(): pl.pallas_call(lambda *refs: project_kernel(steps, *refs), grid_spec=pltp...]
    dynamic_update_slice x2 -> x4, other arithmetic: 2.15 us -> 7.68 us  [add_rows(): lax.dynamic_update_slice(value, value[start:start + rows] + arrived, (sta...]
    pallas_call x2, Pallas kernels: 3.47 us -> 8.02 us  [attention(): pl.pallas_call(attention_kernel, grid=(1,), in_specs=[pl.BlockSpec((HALF,...]
  transfers between devices with their start and end apart: 38 -> 36, of which waited for: 22 -> 18; matrix products, arithmetic and copies ran while one was open for 6% -> 11% of each run, Pallas kernels for 9% -> 15%
where the time goes in v6:
time: 248 us; the launch traced here: 247 us
  waiting for transfers between devices  101 us (41%)
  starting transfers between devices  53.7 us (22%)
  Pallas kernels  42.6 us (17%)
  other arithmetic  21.2 us (9%)
  between operations  14.4 us (6%)
  local copies, waits for them, and re-layouts  14.2 us (6%)
    ppermute x35, waiting for transfers between devices, send(): return lax.ppermute(value, AXES, pairs(change))  100 us
    ppermute x35, starting transfers between devices, send(): return lax.ppermute(value, AXES, pairs(change))  53.7 us
    pallas_call x2, Pallas kernels, project(): pl.pallas_call(lambda *refs: project_kernel(steps, *refs), grid_spec=pltp...  16.5 us
    pallas_call x2, Pallas kernels, products(): pl.pallas_call(lambda *refs: products_kernel(split, steps, *refs), grid_s...  16.1 us
    pallas_call x2, Pallas kernels, attention(): pl.pallas_call(attention_kernel, grid=(1,), in_specs=[pl.BlockSpec((HALF,...  8.02 us
    dynamic_update_slice x4, other arithmetic, add_rows(): lax.dynamic_update_slice(value, value[start:start + rows] + arrived, (sta...  7.68 us
    unnamed x39, local copies, waits for them, and re-layouts  7.67 us
  transfers between devices with their start and end apart: 36, of which 18 were waited for; matrix products, arithmetic and copies ran while one was open for 11% of the time, Pallas kernels for 15%

profile of v6, /device:TPU:3, one launch (start us, length us, event | category | flops | bytes accessed | tf_op | source)
XLA Modules:
  0.0 247.2 jit_solution(18305996671483757031)
XLA Ops:
  12.3 3.6 %collective-permute-start.2 = (bf16[512,640]{1,0:T(8,128)(2,1)}, bf16[512,640]{1,0:T(8,128)(2,1)}, u32[]{:S(2)}, u32[]{:S(2)}) collective-permute-start(bf16[512,640]{1,0:T(8,128)(2,1)} %get-tuple-element.60), channel_id=1, source_target_pairs={{0,1},{1,0},{2,3},{3,2},{4,5},{5,4},{6,7},{7,6},{8,9},{9,8},{10,11... | collective-permute-start | bytes 1966088 | tf_op jit(solution)/shard_map/ppermute | solution.py:41
  18.9 23.5 %collective-permute-done.2 = bf16[512,640]{1,0:T(8,128)(2,1)} collective-permute-done((bf16[512,640]{1,0:T(8,128)(2,1)}, bf16[512,640]{1,0:T(8,128)(2,1)}, u32[]{:S(2)}, u32[]{:S(2)}) %collective-permute-start.2) | collective-permute-done | bytes 655392 | tf_op jit(solution)/shard_map/ppermute | solution.py:41
  43.9 11.4 %collective-permute-done.4 = bf16[256,1024]{1,0:T(8,128)(2,1)S(1)} collective-permute-done((bf16[256,1024]{1,0:T(8,128)(2,1)S(1)}, bf16[256,1024]{1,0:T(8,128)(2,1)S(1)}, u32[]{:S(2)}, u32[]{:S(2)}) %collective-permute-start.4) | collective-permute-done | bytes 524320 | tf_op jit(solution)/shard_map/ppermute | solution.py:41
  66.3 7.0 %collective-permute-done.13 = bf16[512,640]{1,0:T(8,128)(2,1)} collective-permute-done((bf16[512,640]{1,0:T(8,128)(2,1)}, bf16[512,640]{1,0:T(8,128)(2,1)}, u32[]{:S(2)}, u32[]{:S(2)}) %collective-permute-start.13) | collective-permute-done | bytes 655392 | tf_op jit(solution)/shard_map/ppermute | solution.py:41
  81.4 3.8 %collective-permute-done.12 = bf16[128,1024]{1,0:T(8,128)(2,1)S(1)} collective-permute-done((bf16[128,1024]{1,0:T(8,128)(2,1)S(1)}, bf16[128,1024]{1,0:T(8,128)(2,1)S(1)}, u32[]{:S(2)}, u32[]{:S(2)}) %collective-permute-start.12) | collective-permute-done | bytes 262176 | tf_op jit(solution)/shard_map/ppermute | solution.py:41
  90.9 6.1 %shard_map.64 = (bf16[128,1280]{1,0:T(8,128)(2,1)}, bf16[128,1280]{1,0:T(8,128)(2,1)}) custom-call(s32[2]{0:T(128)} %pad_add_fusion.1.refs_0_, bf16[4,256,2048]{2,1,0:T(8,128)(2,1)} %copy-done, bf16[1024,640]{1,0:T(8,128)(2,1)} %copy-done.1, bf16[1024,640]{1,0:T(8,128)(2,1)} %copy-done.5, bf16[1024,640]{1,0:T(8,128)(2,1)} %copy-done.4, ...), custom_call_target="tpu_custom_call" | custom-call | tf_op jit(solution)/shard_map/pallas_call | solution.py:210
  100.8 10.4 %shard_map.65 = (bf16[256,1280]{1,0:T(8,128)(2,1)}, bf16[256,1280]{1,0:T(8,128)(2,1)}, bf16[256,1280]{1,0:T(8,128)(2,1)}) custom-call(s32[4]{0:T(128)} %pad_add_fusion.2.refs_0_, bf16[4,256,2048]{2,1,0:T(8,128)(2,1)} %copy-done, bf16[1024,640]{1,0:T(8,128)(2,1)} %copy-done.1, bf16[1024,640]{1,0:T(8,128)(2,1)} %copy-done.5, bf16[1024,640]{1,0:T(8,128)(2,1)} %copy-done.4, ...), custom_call_target="tpu_custom_call" | custom-call | tf_op jit(solution)/shard_map/pallas_call | solution.py:210
  111.2 4.8 %collective-permute-start.25 = (bf16[4,512,1024]{2,1,0:T(8,128)(2,1)}, bf16[4,512,1024]{2,1,0:T(8,128)(2,1)}, u32[]{:S(2)}, u32[]{:S(2)}) collective-permute-start(bf16[4,512,1024]{2,1,0:T(8,128)(2,1)} %bitcast.46), channel_id=1, source_target_pairs={{0,8},{1,9},{2,10},{3,11},{4,12},{5,13},{6,14},{7,15},{8,0},{9,1},... | collective-permute-start | bytes 12582920 | tf_op jit(solution)/shard_map/ppermute | solution.py:41
  124.4 3.3 %multiply_reduce_fusion = f32[4,256]{1,0:T(4,128)S(1)} fusion(bf16[4,256,2048]{2,1,0:T(8,128)(2,1)} %copy-done, f32[2048]{0:T(1024)S(1)} %dynamic-slice_divide_fusion), kind=kLoop, calls=%fused_computation | loop fusion | flops 8387584 | bytes 4206592 | tf_op jit(solution)/shard_map/reduce_sum | solution.py:361
  129.2 9.1 %collective-permute-done.21 = f32[256]{0:T(256)S(1)} collective-permute-done((f32[256]{0:T(256)S(1)}, f32[256]{0:T(256)S(1)}, u32[]{:S(2)}, u32[]{:S(2)}) %collective-permute-start.21) | collective-permute-done | bytes 1056 | tf_op jit(solution)/shard_map/ppermute | solution.py:41
  139.5 3.3 %collective-permute-done.19 = f32[256]{0:T(256)S(1)} collective-permute-done((f32[256]{0:T(256)S(1)}, f32[256]{0:T(256)S(1)}, u32[]{:S(2)}, u32[]{:S(2)}) %collective-permute-start.19) | collective-permute-done | bytes 1056 | tf_op jit(solution)/shard_map/ppermute | solution.py:41
  150.6 4.0 %shard_map.67.refs_1_ = bf16[256,512]{1,0:T(8,128)(2,1)} custom-call(bf16[256,1280]{1,0:T(8,128)(2,1)} %get-tuple-element.45.k0.v0.s0, bf16[256,1280]{1,0:T(8,128)(2,1)} %copy-done.2, bf16[256,1280]{1,0:T(8,128)(2,1)} %copy-done.3, f32[256,1]{1,0:T(8,128)} %copy.8.scale_ref, f32[256,128]{1,0:T(8,128)} %get-tuple-element.76.cos_ref, ...), custom_call_target="tpu_custom_call" | custom-call | tf_op jit(solution)/shard_map/pallas_call | solution.py:168
  155.1 4.0 %shard_map.68.refs_2_ = bf16[256,512]{1,0:T(8,128)(2,1)} custom-call(bf16[256,1280]{1,0:T(8,128)(2,1)} %get-tuple-element.45.k0.v0.s0, bf16[256,1280]{1,0:T(8,128)(2,1)} %copy-done.2, bf16[256,1280]{1,0:T(8,128)(2,1)} %copy-done.3, f32[256,1]{1,0:T(8,128)} %copy.8.scale_ref, f32[256,128]{1,0:T(8,128)} %get-tuple-element.76.cos_ref, ...), custom_call_target="tpu_custom_call" | custom-call | tf_op jit(solution)/shard_map/pallas_call | solution.py:168
  163.9 5.6 %collective-permute-done.24.refs_4_ = bf16[256,512]{1,0:T(8,128)(2,1)S(1)} collective-permute-done((bf16[256,512]{1,0:T(8,128)(2,1)}, bf16[256,512]{1,0:T(8,128)(2,1)S(1)}, u32[]{:S(2)}, u32[]{:S(2)}) %collective-permute-start.24) | collective-permute-done | bytes 262176 | tf_op jit(solution)/shard_map/ppermute | solution.py:41
  170.2 5.1 %shard_map.70 = (bf16[256,1024]{1,0:T(8,128)(2,1)}, bf16[256,1024]{1,0:T(8,128)(2,1)}) custom-call(s32[4]{0:T(128)} %pad_add_fusion.3.refs_0_, bf16[256,512]{1,0:T(8,128)(2,1)} %shard_map.67.refs_1_, bf16[256,512]{1,0:T(8,128)(2,1)} %shard_map.68.refs_2_, bf16[256,512]{1,0:T(8,128)(2,1)} %copy-done.12, bf16[256,512]{1,0:T(8,128)(2,1)} %copy-done.13, ...), custom_call_target="tpu_custom_call" | custom-call | tf_op jit(solution)/shard_map/pallas_call | solution.py:258
  175.3 2.9 %collective-permute-start.28 = (bf16[256,1024]{1,0:T(8,128)(2,1)}, bf16[256,1024]{1,0:T(8,128)(2,1)S(1)}, u32[]{:S(2)}, u32[]{:S(2)}) collective-permute-start(bf16[256,1024]{1,0:T(8,128)(2,1)} %get-tuple-element.55), channel_id=1, source_target_pairs={{0,48},{1,49},{2,50},{3,51},{4,52},{5,53},{6,54},{7,55},{8,56},{9,... | collective-permute-start | bytes 1572872 | tf_op jit(solution)/shard_map/ppermute | solution.py:41
  178.9 10.9 %shard_map.69 = (bf16[256,1024]{1,0:T(8,128)(2,1)}, bf16[256,1024]{1,0:T(8,128)(2,1)}, bf16[256,1024]{1,0:T(8,128)(2,1)}, bf16[256,1024]{1,0:T(8,128)(2,1)}, bf1...) custom-call(s32[12]{0:T(128)} %stack.92.refs_0_, bf16[256,512]{1,0:T(8,128)(2,1)} %shard_map.67.refs_1_, ...), custom_call_target="tpu_custom_call" | custom-call | tf_op jit(solution)/shard_map/pallas_call | solution.py:258
  197.0 7.2 %collective-permute-done.31 = bf16[256,1024]{1,0:T(8,128)(2,1)S(1)} collective-permute-done((bf16[256,1024]{1,0:T(8,128)(2,1)}, bf16[256,1024]{1,0:T(8,128)(2,1)S(1)}, u32[]{:S(2)}, u32[]{:S(2)}) %collective-permute-start.31) | collective-permute-done | bytes 524320 | tf_op jit(solution)/shard_map/ppermute | solution.py:41
  204.2 2.9 %collective-permute-done.30 = bf16[256,1024]{1,0:T(8,128)(2,1)S(1)} collective-permute-done((bf16[256,1024]{1,0:T(8,128)(2,1)}, bf16[256,1024]{1,0:T(8,128)(2,1)S(1)}, u32[]{:S(2)}, u32[]{:S(2)}) %collective-permute-start.30) | collective-permute-done | bytes 524320 | tf_op jit(solution)/shard_map/ppermute | solution.py:41
  209.0 6.4 %collective-permute-done.29 = bf16[256,1024]{1,0:T(8,128)(2,1)S(1)} collective-permute-done((bf16[256,1024]{1,0:T(8,128)(2,1)}, bf16[256,1024]{1,0:T(8,128)(2,1)S(1)}, u32[]{:S(2)}, u32[]{:S(2)}) %collective-permute-start.29) | collective-permute-done | bytes 524320 | tf_op jit(solution)/shard_map/ppermute | solution.py:41
  215.4 2.9 %collective-permute-done.27 = bf16[256,1024]{1,0:T(8,128)(2,1)S(1)} collective-permute-done((bf16[256,1024]{1,0:T(8,128)(2,1)}, bf16[256,1024]{1,0:T(8,128)(2,1)S(1)}, u32[]{:S(2)}, u32[]{:S(2)}) %collective-permute-start.27) | collective-permute-done | bytes 524320 | tf_op jit(solution)/shard_map/ppermute | solution.py:41
  218.8 8.0 %collective-permute-start.34 = (bf16[256,512]{1,0:T(8,128)(2,1)S(1)}, bf16[256,512]{1,0:T(8,128)(2,1)S(1)}, u32[]{:S(2)}, u32[]{:S(2)}) collective-permute-start(bf16[256,512]{1,0:T(8,128)(2,1)S(1)} %get-tuple-element.62), channel_id=1, source_target_pairs={{0,8},{1,24},{2,10},{3,26},{4,12},{5,28},{6,14},{7,30},{8,0},{9,16... | collective-permute-start | bytes 786440 | tf_op jit(solution)/shard_map/ppermute | solution.py:41
  229.4 4.3 %collective-permute-done.34 = bf16[256,512]{1,0:T(8,128)(2,1)S(1)} collective-permute-done((bf16[256,512]{1,0:T(8,128)(2,1)S(1)}, bf16[256,512]{1,0:T(8,128)(2,1)S(1)}, u32[]{:S(2)}, u32[]{:S(2)}) %collective-permute-start.34) | collective-permute-done | bytes 262176 | tf_op jit(solution)/shard_map/ppermute | solution.py:41
  233.6 5.7 %collective-permute-done.33 = bf16[256,512]{1,0:T(8,128)(2,1)S(1)} collective-permute-done((bf16[256,512]{1,0:T(8,128)(2,1)S(1)}, bf16[256,512]{1,0:T(8,128)(2,1)S(1)}, u32[]{:S(2)}, u32[]{:S(2)}) %collective-permute-start.33) | collective-permute-done | bytes 262176 | tf_op jit(solution)/shard_map/ppermute | solution.py:41
  (142 shorter events, 76.3 us)
Async XLA Ops:
  6.5 104.7 %all-gather.3.cloned.1.call-start = ((), (), s32[]{:S(2)}) async-start(), calls=%async_computation | async-start | bytes 5242880 | tf_op jit(solution)/shard_map/all_gather | solution.py:345
  10.3 32.1 %collective-permute-start.3 = (bf16[1024,640]{1,0:T(8,128)(2,1)S(1)}, bf16[1024,640]{1,0:T(8,128)(2,1)S(1)}, u32[]{:S(2)}, u32[]{:S(2)}) collective-permute-start(bf16[1024,640]{1,0:T(8,128)(2,1)S(1)} %pad_maximum_fusion.refs_2_), channel_id=1, source_target_pairs={{0,8},{1,9},{2,10},{3,11},{4,12},{5,13},{6,14},{7,15},{8,0},{9,1},... | collective-permute-start | bytes 3932168 | tf_op jit(solution)/shard_map/ppermute | solution.py:41
  12.3 30.1 %collective-permute-start.2 = (bf16[512,640]{1,0:T(8,128)(2,1)}, bf16[512,640]{1,0:T(8,128)(2,1)}, u32[]{:S(2)}, u32[]{:S(2)}) collective-permute-start(bf16[512,640]{1,0:T(8,128)(2,1)} %get-tuple-element.60), channel_id=1, source_target_pairs={{0,1},{1,0},{2,3},{3,2},{4,5},{5,4},{6,7},{7,6},{8,9},{9,8},{10,11... | collective-permute-start | bytes 1966088 | tf_op jit(solution)/shard_map/ppermute | solution.py:41
  42.4 12.8 %collective-permute-start.4 = (bf16[256,1024]{1,0:T(8,128)(2,1)S(1)}, bf16[256,1024]{1,0:T(8,128)(2,1)S(1)}, u32[]{:S(2)}, u32[]{:S(2)}) collective-permute-start(bf16[256,1024]{1,0:T(8,128)(2,1)S(1)} %maximum_select_fusion), channel_id=1, source_target_pairs={{0,16},{1,17},{2,18},{3,19},{4,20},{5,21},{6,22},{7,23},{8,24},{9,... | collective-permute-start | bytes 1572872 | tf_op jit(solution)/shard_map/ppermute | solution.py:41
  43.6 12.5 %collective-permute-start.5 = (bf16[256,1024]{1,0:T(8,128)(2,1)S(1)}, bf16[256,1024]{1,0:T(8,128)(2,1)S(1)}, u32[]{:S(2)}, u32[]{:S(2)}) collective-permute-start(bf16[256,1024]{1,0:T(8,128)(2,1)S(1)} %maximum_select_fusion), channel_id=1, source_target_pairs={{0,48},{1,49},{2,50},{3,51},{4,52},{5,53},{6,54},{7,55},{8,56},{9,... | collective-permute-start | bytes 1572872 | tf_op jit(solution)/shard_map/ppermute | solution.py:41
  43.9 12.3 %collective-permute-start.6 = (bf16[256,1024]{1,0:T(8,128)(2,1)S(1)}, bf16[256,1024]{1,0:T(8,128)(2,1)S(1)}, u32[]{:S(2)}, u32[]{:S(2)}) collective-permute-start(bf16[256,1024]{1,0:T(8,128)(2,1)S(1)} %maximum_select_fusion), channel_id=1, source_target_pairs={{0,64},{1,65},{2,66},{3,67},{4,68},{5,69},{6,70},{7,71},{8,72},{9,... | collective-permute-start | bytes 1572872 | tf_op jit(solution)/shard_map/ppermute | solution.py:41
  57.1 16.1 %collective-permute-start.13 = (bf16[512,640]{1,0:T(8,128)(2,1)}, bf16[512,640]{1,0:T(8,128)(2,1)}, u32[]{:S(2)}, u32[]{:S(2)}) collective-permute-start(bf16[512,640]{1,0:T(8,128)(2,1)} %get-tuple-element.39), channel_id=1, source_target_pairs={{0,1},{1,0},{2,3},{3,2},{4,5},{5,4},{6,7},{7,6},{8,9},{9,8},{10,11... | collective-permute-start | bytes 1966088 | tf_op jit(solution)/shard_map/ppermute | solution.py:41
  62.1 19.1 %collective-permute-start.9 = (bf16[256,1024]{1,0:T(8,128)(2,1)S(1)}, bf16[256,1024]{1,0:T(8,128)(2,1)S(1)}, u32[]{:S(2)}, u32[]{:S(2)}) collective-permute-start(bf16[256,1024]{1,0:T(8,128)(2,1)S(1)} %copy-done.17), channel_id=1, source_target_pairs={{0,16},{1,17},{2,18},{3,19},{4,20},{5,21},{6,22},{7,23},{8,24},{9,... | collective-permute-start | bytes 1572872 | tf_op jit(solution)/shard_map/ppermute | solution.py:41
  63.1 16.2 %collective-permute-start.10 = (bf16[256,1024]{1,0:T(8,128)(2,1)S(1)}, bf16[256,1024]{1,0:T(8,128)(2,1)S(1)}, u32[]{:S(2)}, u32[]{:S(2)}) collective-permute-start(bf16[256,1024]{1,0:T(8,128)(2,1)S(1)} %copy-done.17), channel_id=1, source_target_pairs={{0,48},{1,49},{2,50},{3,51},{4,52},{5,53},{6,54},{7,55},{8,56},{9,... | collective-permute-start | bytes 1572872 | tf_op jit(solution)/shard_map/ppermute | solution.py:41
  63.6 15.7 %collective-permute-start.8 = (bf16[128,1024]{1,0:T(8,128)(2,1)S(1)}, bf16[128,1024]{1,0:T(8,128)(2,1)S(1)}, u32[]{:S(2)}, u32[]{:S(2)}) collective-permute-start(bf16[128,1024]{1,0:T(8,128)(2,1)S(1)} %slice.50), channel_id=1, source_target_pairs={{0,48},{1,49},{2,50},{3,51},{4,52},{5,53},{6,54},{7,55},{8,56},{9,... | collective-permute-start | bytes 786440 | tf_op jit(solution)/shard_map/ppermute | solution.py:41
  66.2 13.1 %collective-permute-start.7 = (bf16[128,1024]{1,0:T(8,128)(2,1)S(1)}, bf16[128,1024]{1,0:T(8,128)(2,1)S(1)}, u32[]{:S(2)}, u32[]{:S(2)}) collective-permute-start(bf16[128,1024]{1,0:T(8,128)(2,1)S(1)} %slice.49), channel_id=1, source_target_pairs={{0,16},{1,17},{2,18},{3,19},{4,20},{5,21},{6,22},{7,23},{8,24},{9,... | collective-permute-start | bytes 786440 | tf_op jit(solution)/shard_map/ppermute | solution.py:41
  74.5 13.3 %collective-permute-start.14 = (bf16[1024,640]{1,0:T(8,128)(2,1)S(1)}, bf16[1024,640]{1,0:T(8,128)(2,1)S(1)}, u32[]{:S(2)}, u32[]{:S(2)}) collective-permute-start(bf16[1024,640]{1,0:T(8,128)(2,1)S(1)} %constant_dynamic-update-slice_fusion.refs_4_), channel_id=1, source_target_pairs={{0,8},{1,9},{2,10},{3,11},{4,12},{5,13},{6,14},{7,15},{8,0},{9,1},... | collective-permute-start | bytes 3932168 | tf_op jit(solution)/shard_map/ppermute | solution.py:41
  97.0 14.2 %collective-permute-start.15 = (bf16[128,1280]{1,0:T(8,128)(2,1)}, bf16[128,1280]{1,0:T(8,128)(2,1)S(1)}, u32[]{:S(2)}, u32[]{:S(2)}) collective-permute-start(bf16[128,1280]{1,0:T(8,128)(2,1)} %get-tuple-element.40), channel_id=1, source_target_pairs={{0,2},{1,3},{2,4},{3,5},{4,6},{5,7},{6,0},{7,1},{8,10},{9,11},{10,... | collective-permute-start | bytes 983048 | tf_op jit(solution)/shard_map/ppermute | solution.py:41
  98.3 12.9 %collective-permute-start.16 = (bf16[128,1280]{1,0:T(8,128)(2,1)}, bf16[128,1280]{1,0:T(8,128)(2,1)S(1)}, u32[]{:S(2)}, u32[]{:S(2)}) collective-permute-start(bf16[128,1280]{1,0:T(8,128)(2,1)} %get-tuple-element.41), channel_id=1, source_target_pairs={{0,6},{1,7},{2,0},{3,1},{4,2},{5,3},{6,4},{7,5},{8,14},{9,15},{10,... | collective-permute-start | bytes 983048 | tf_op jit(solution)/shard_map/ppermute | solution.py:41
  111.2 58.3 %collective-permute-start.25 = (bf16[4,512,1024]{2,1,0:T(8,128)(2,1)}, bf16[4,512,1024]{2,1,0:T(8,128)(2,1)}, u32[]{:S(2)}, u32[]{:S(2)}) collective-permute-start(bf16[4,512,1024]{2,1,0:T(8,128)(2,1)} %bitcast.46), channel_id=1, source_target_pairs={{0,8},{1,9},{2,10},{3,11},{4,12},{5,13},{6,14},{7,15},{8,0},{9,1},... | collective-permute-start | bytes 12582920 | tf_op jit(solution)/shard_map/ppermute | solution.py:41
  119.9 23.7 %collective-permute-start.17 = (bf16[256,1280]{1,0:T(8,128)(2,1)}, bf16[256,1280]{1,0:T(8,128)(2,1)S(1)}, u32[]{:S(2)}, u32[]{:S(2)}) collective-permute-start(bf16[256,1280]{1,0:T(8,128)(2,1)} %add_dynamic-update-slice_fusion.1), channel_id=1, source_target_pairs={{0,2},{1,3},{2,4},{3,5},{4,6},{5,7},{6,0},{7,1},{8,10},{9,11},{10,... | collective-permute-start | bytes 1966088 | tf_op jit(solution)/shard_map/ppermute | solution.py:41
  121.8 21.8 %collective-permute-start.18 = (bf16[256,1280]{1,0:T(8,128)(2,1)}, bf16[256,1280]{1,0:T(8,128)(2,1)S(1)}, u32[]{:S(2)}, u32[]{:S(2)}) collective-permute-start(bf16[256,1280]{1,0:T(8,128)(2,1)} %add_dynamic-update-slice_fusion), channel_id=1, source_target_pairs={{0,6},{1,7},{2,0},{3,1},{4,2},{5,3},{6,4},{7,5},{8,14},{9,15},{10,... | collective-permute-start | bytes 1966088 | tf_op jit(solution)/shard_map/ppermute | solution.py:41
  175.3 14.6 %collective-permute-start.28 = (bf16[256,1024]{1,0:T(8,128)(2,1)}, bf16[256,1024]{1,0:T(8,128)(2,1)S(1)}, u32[]{:S(2)}, u32[]{:S(2)}) collective-permute-start(bf16[256,1024]{1,0:T(8,128)(2,1)} %get-tuple-element.55), channel_id=1, source_target_pairs={{0,48},{1,49},{2,50},{3,51},{4,52},{5,53},{6,54},{7,55},{8,56},{9,... | collective-permute-start | bytes 1572872 | tf_op jit(solution)/shard_map/ppermute | solution.py:41
  178.3 15.2 %collective-permute-start.26 = (bf16[256,1024]{1,0:T(8,128)(2,1)}, bf16[256,1024]{1,0:T(8,128)(2,1)S(1)}, u32[]{:S(2)}, u32[]{:S(2)}) collective-permute-start(bf16[256,1024]{1,0:T(8,128)(2,1)} %get-tuple-element.53), channel_id=1, source_target_pairs={{0,16},{1,17},{2,18},{3,19},{4,20},{5,21},{6,22},{7,23},{8,24},{9,... | collective-permute-start | bytes 1572872 | tf_op jit(solution)/shard_map/ppermute | solution.py:41
  192.0 12.2 %collective-permute-start.31 = (bf16[256,1024]{1,0:T(8,128)(2,1)}, bf16[256,1024]{1,0:T(8,128)(2,1)S(1)}, u32[]{:S(2)}, u32[]{:S(2)}) collective-permute-start(bf16[256,1024]{1,0:T(8,128)(2,1)} %get-tuple-element.66), channel_id=1, source_target_pairs={{0,48},{1,49},{2,50},{3,51},{4,52},{5,53},{6,54},{7,55},{8,56},{9,... | collective-permute-start | bytes 1572872 | tf_op jit(solution)/shard_map/ppermute | solution.py:41
  195.5 19.9 %collective-permute-start.29 = (bf16[256,1024]{1,0:T(8,128)(2,1)}, bf16[256,1024]{1,0:T(8,128)(2,1)S(1)}, u32[]{:S(2)}, u32[]{:S(2)}) collective-permute-start(bf16[256,1024]{1,0:T(8,128)(2,1)} %get-tuple-element.65), channel_id=1, source_target_pairs={{0,48},{1,49},{2,50},{3,51},{4,52},{5,53},{6,54},{7,55},{8,56},{9,... | collective-permute-start | bytes 1572872 | tf_op jit(solution)/shard_map/ppermute | solution.py:41
  197.0 21.4 %collective-permute-start.27 = (bf16[256,1024]{1,0:T(8,128)(2,1)}, bf16[256,1024]{1,0:T(8,128)(2,1)S(1)}, u32[]{:S(2)}, u32[]{:S(2)}) collective-permute-start(bf16[256,1024]{1,0:T(8,128)(2,1)} %get-tuple-element.63), channel_id=1, source_target_pairs={{0,16},{1,17},{2,18},{3,19},{4,20},{5,21},{6,22},{7,23},{8,24},{9,... | collective-permute-start | bytes 1572872 | tf_op jit(solution)/shard_map/ppermute | solution.py:41
  218.8 14.9 %collective-permute-start.34 = (bf16[256,512]{1,0:T(8,128)(2,1)S(1)}, bf16[256,512]{1,0:T(8,128)(2,1)S(1)}, u32[]{:S(2)}, u32[]{:S(2)}) collective-permute-start(bf16[256,512]{1,0:T(8,128)(2,1)S(1)} %get-tuple-element.62), channel_id=1, source_target_pairs={{0,8},{1,24},{2,10},{3,26},{4,12},{5,28},{6,14},{7,30},{8,0},{9,16... | collective-permute-start | bytes 786440 | tf_op jit(solution)/shard_map/ppermute | solution.py:41
  226.8 12.5 %collective-permute-start.33 = (bf16[256,512]{1,0:T(8,128)(2,1)S(1)}, bf16[256,512]{1,0:T(8,128)(2,1)S(1)}, u32[]{:S(2)}, u32[]{:S(2)}) collective-permute-start(bf16[256,512]{1,0:T(8,128)(2,1)S(1)} %get-tuple-element.61), channel_id=1, source_target_pairs={{0,0},{1,16},{2,2},{3,18},{4,4},{5,20},{6,6},{7,22},{8,8},{9,24},{... | collective-permute-start | bytes 786440 | tf_op jit(solution)/shard_map/ppermute | solution.py:41
  (31 other events, 276.8 us)
Sparse Core Ops, SparseCore 0:
  9.0 57.1 all-gather.2

commit v7 on v6

--- a/solution.py
+++ b/solution.py
@@ -99,7 +99,7 @@
 
 
 WIDE = 640
-GRANT = pltpu.CompilerParams(vmem_limit_bytes=56 * 1024 * 1024)
+GRANT = pltpu.CompilerParams(vmem_limit_bytes=24 * 1024 * 1024)
 
 
 def total_of(refs, cols=slice(None)):
@@ -220,31 +220,29 @@
     )(jnp.stack([zh, *which]).astype(jnp.int32), gathered, *weights)
 
 
-def products_kernel(split, steps, at_ref, own_a, own_b, far_a, far_b, near, other, *refs):
-    outs, rows = refs[:-1], refs[-1]
+def products_kernel(split, steps, at_ref, own_a, own_b, far_a, far_b, near, other, *outs):
     step = pl.program_id(0)
+
+    def put(left, right):
+        product = dot(left[...], near[0]) + dot(right[...], other[0])
+        product = product.astype(jnp.bfloat16)
+        for i in range(steps):
+
+            @pl.when(step == i)
+            def _():
+                if split:
+                    outs[0][i * 128 : i * 128 + 128] = product[:128]
+                    outs[1][i * 128 : i * 128 + 128] = product[128:]
+                else:
+                    outs[i][...] = product
 
     @pl.when(at_ref[steps + step] == 1)
     def _():
-        rows[:, :512] = own_a[...]
-        rows[:, 512:] = own_b[...]
+        put(own_a, own_b)
 
     @pl.when(at_ref[steps + step] == 0)
     def _():
-        rows[:, :512] = far_a[...]
-        rows[:, 512:] = far_b[...]
-
-    product = dot(rows[:, :512], near[0]) + dot(rows[:, 512:], other[0])
-    product = product.astype(jnp.bfloat16)
-    for i in range(steps):
-
-        @pl.when(step == i)
-        def _():
-            if split:
-                outs[0][i * 128 : i * 128 + 128] = product[:128]
-                outs[1][i * 128 : i * 128 + 128] = product[128:]
-            else:
-                outs[i][...] = product
+        put(far_a, far_b)
 
 
 def products(targets, zh, attended, near, other, split=False):
@@ -262,7 +260,6 @@
             grid=(steps,),
             in_specs=[rows] * 4 + [block] * 2,
             out_specs=[pl.BlockSpec((HALF, 1024), lambda i, at: (0, 0))] * count,
-            scratch_shapes=[pltpu.VMEM((HALF, 1024), jnp.bfloat16)],
         ),
         out_shape=[jax.ShapeDtypeStruct((HALF, 1024), jnp.bfloat16)] * count,
         compiler_params=GRANT,
@@ -307,16 +304,15 @@
     block = ordered(is_first, mine, theirs, 1)
 
     kv_own = lax.dynamic_slice_in_dim(kv_weight, chip * 256 + core * 128, 128, 1)
-    near = after(jnp.concatenate([query_weight, kv_own], axis=1), (mine_out, theirs_out))
-    far_top = zh_swap(near[:512])
+    near = jnp.concatenate([query_weight, kv_own], axis=1)
+    block, near = lax.optimization_barrier((block, near))
     near_other = core_swap(near)
-    block, far_top, near_other = lax.optimization_barrier((block, far_top, near_other))
 
     beside = zl_swap(block)
     left = x_shift(block, 1)
     right = x_shift(block, -1)
-    left, right, beside = lax.optimization_barrier((left, right, beside))
-    far_bottom = zh_swap(after(near[512:], beside))
+    left, right, near_other = lax.optimization_barrier((left, right, near_other))
+    far = zh_swap(near)
     beside_left = x_shift(beside, 1)
     beside_right = x_shift(beside, -1)
     opposite = jnp.concatenate([x_shift(left[:128], 1), x_shift(right[128:], -1)], 0)
@@ -339,10 +335,10 @@
             gathered, part[None], (zs * 2 + xs // 2, 0, (xs % 2) * 1024)
         )
 
-    far = jnp.concatenate([far_top, far_bottom], axis=0)
+    far = after(far, (opposite, beside_left, beside_right))
     weights = (near, near_other, far, core_swap(far))
 
-    out_near = lax.all_gather(out_weight, "y", axis=0, tiled=False)
+    out_near = lax.all_gather(after(out_weight, block), "y", axis=0, tiled=False)
 
     low, high = project([(y + 2) % 4], zh, gathered, weights)
     from_below = y_shift(low, 1)

time: 248 us -> 234 us (0.944)
  waiting for transfers between devices: 101 us -> 78.9 us
  local copies, waits for them, and re-layouts: 14.2 us -> 27.1 us
  Pallas kernels: 42.6 us -> 31.1 us
  starting transfers between devices: 53.7 us -> 62.3 us
  other arithmetic: 21.2 us -> 18.5 us
    ppermute x35 -> x34, waiting for transfers between devices: 100 us -> 78.8 us  [send(): return lax.ppermute(value, AXES, pairs(change))]
    ppermute x35 -> x34, starting transfers between devices: 53.7 us -> 62.3 us  [send(): return lax.ppermute(value, AXES, pairs(change))]
    unnamed x39 -> x45, local copies, waits for them, and re-layouts: 7.67 us -> 15.4 us
    pallas_call x2, Pallas kernels: 8.02 us -> 3.47 us  [attention(): pl.pallas_call(attention_kernel, grid=(1,), in_specs=[pl.BlockSpec((HALF,...]
    dynamic_update_slice x6 -> x7, local copies, waits for them, and re-layouts: 0.32 us -> 4.5 us  [local(): lax.dynamic_update_slice(gathered, part[None], (zs * 2 + xs // 2, 0, xs %...]
    pallas_call x2, Pallas kernels: 16.5 us -> 12.9 us  [project(): pl.pallas_call(lambda *refs: project_kernel(steps, *refs), grid_spec=pltp...]
    pallas_call x2, Pallas kernels: 16.1 us -> 12.6 us  [products(): pl.pallas_call(lambda *refs: products_kernel(split, steps, *refs), grid_s...]
  transfers between devices with their start and end apart: 36 -> 35, of which waited for: 18 -> 17; matrix products, arithmetic and copies ran while one was open for 11% -> 11% of each run, Pallas kernels for 15% -> 12%
where the time goes in v7:
time: 234 us; the launch traced here: 232 us
  waiting for transfers between devices  78.9 us (34%)
  starting transfers between devices  62.3 us (27%)
  Pallas kernels  31.1 us (13%)
  local copies, waits for them, and re-layouts  27.1 us (12%)
  other arithmetic  18.5 us (8%)
  between operations  14.5 us (6%)
    ppermute x34, waiting for transfers between devices, send(): return lax.ppermute(value, AXES, pairs(change))  78.8 us
    ppermute x34, starting transfers between devices, send(): return lax.ppermute(value, AXES, pairs(change))  62.3 us
    unnamed x45, local copies, waits for them, and re-layouts  15.4 us
    pallas_call x2, Pallas kernels, project(): pl.pallas_call(lambda *refs: project_kernel(steps, *refs), grid_spec=pltp...  12.9 us
    pallas_call x2, Pallas kernels, products(): pl.pallas_call(lambda *refs: products_kernel(split, steps, *refs), grid_s...  12.6 us
    dynamic_update_slice x4, other arithmetic, add_rows(): lax.dynamic_update_slice(value, value[start:start + rows] + arrived, (sta...  6.28 us
  transfers between devices with their start and end apart: 35, of which 17 were waited for; matrix products, arithmetic and copies ran while one was open for 11% of the time, Pallas kernels for 12%

profile of v7, /device:TPU:3, one launch (start us, length us, event | category | flops | bytes accessed | tf_op | source)
XLA Modules:
  0.0 232.3 jit_solution(1366380761055140769)
XLA Ops:
  12.5 15.2 %collective-permute-start.5 = (bf16[256,1024]{1,0:T(8,128)(2,1)S(1)}, bf16[256,1024]{1,0:T(8,128)(2,1)}, u32[]{:S(2)}, u32[]{:S(2)}) collective-permute-start(bf16[256,1024]{1,0:T(8,128)(2,1)S(1)} %maximum_select_fusion), channel_id=1, source_target_pairs={{0,64},{1,65},{2,66},{3,67},{4,68},{5,69},{6,70},{7,71},{8,72},{9,... | collective-permute-start | bytes 1572872 | tf_op jit(solution)/shard_map/ppermute | solution.py:41
  27.8 3.3 %collective-permute-start.2 = (bf16[256,1024]{1,0:T(8,128)(2,1)S(1)}, bf16[256,1024]{1,0:T(8,128)(2,1)S(1)}, u32[]{:S(2)}, u32[]{:S(2)}) collective-permute-start(bf16[256,1024]{1,0:T(8,128)(2,1)S(1)} %maximum_select_fusion), channel_id=1, source_target_pairs={{0,16},{1,17},{2,18},{3,19},{4,20},{5,21},{6,22},{7,23},{8,24},{9,... | collective-permute-start | bytes 1572872 | tf_op jit(solution)/shard_map/ppermute | solution.py:41
  31.1 3.3 %collective-permute-start.12 = (bf16[1024,640]{1,0:T(8,128)(2,1)S(1)}, bf16[1024,640]{1,0:T(8,128)(2,1)}, u32[]{:S(2)}, u32[]{:S(2)}) collective-permute-start(bf16[1024,640]{1,0:T(8,128)(2,1)S(1)} %pad_maximum_fusion.refs_2_), channel_id=1, source_target_pairs={{0,1},{1,0},{2,3},{3,2},{4,5},{5,4},{6,7},{7,6},{8,9},{9,8},{10,11... | collective-permute-start | bytes 3932168 | tf_op jit(solution)/shard_map/ppermute | solution.py:41
  34.4 5.7 %collective-permute-done.5 = bf16[256,1024]{1,0:T(8,128)(2,1)} collective-permute-done((bf16[256,1024]{1,0:T(8,128)(2,1)S(1)}, bf16[256,1024]{1,0:T(8,128)(2,1)}, u32[]{:S(2)}, u32[]{:S(2)}) %collective-permute-start.5) | collective-permute-done | bytes 524320 | tf_op jit(solution)/shard_map/ppermute | solution.py:41
  49.6 8.7 %collective-permute-done.9 = bf16[256,1024]{1,0:T(8,128)(2,1)} collective-permute-done((bf16[256,1024]{1,0:T(8,128)(2,1)}, bf16[256,1024]{1,0:T(8,128)(2,1)}, u32[]{:S(2)}, u32[]{:S(2)}) %collective-permute-start.9) | collective-permute-done | bytes 524320 | tf_op jit(solution)/shard_map/ppermute | solution.py:41
  64.5 6.8 %collective-permute-done.7 = bf16[128,1024]{1,0:T(8,128)(2,1)S(1)} collective-permute-done((bf16[128,1024]{1,0:T(8,128)(2,1)S(1)}, bf16[128,1024]{1,0:T(8,128)(2,1)S(1)}, u32[]{:S(2)}, u32[]{:S(2)}) %collective-permute-start.7) | collective-permute-done | bytes 262176 | tf_op jit(solution)/shard_map/ppermute | solution.py:41
  78.3 5.4 %shard_map.64 = (bf16[128,1280]{1,0:T(8,128)(2,1)}, bf16[128,1280]{1,0:T(8,128)(2,1)}) custom-call(s32[2]{0:T(128)S(1)} %pad_add_fusion.1.refs_0_, bf16[4,256,2048]{2,1,0:T(8,128)(2,1)S(1)} %fusion.2.refs_1_, bf16[1024,640]{1,0:T(8,128)(2,1)S(1)} %pad_maximum_fusion.refs_2_, bf16[1024,640]{1,0:T(8,128)(2,1)S(1)} %collective-permute-done.4.refs_3_, ...), custom_call_target="tpu_custom_call" | custom-call | tf_op jit(solution)/shard_map/pallas_call | solution.py:210
  90.0 7.5 %shard_map.65 = (bf16[256,1280]{1,0:T(8,128)(2,1)S(1)}, bf16[256,1280]{1,0:T(8,128)(2,1)S(1)}, bf16[256,1280]{1,0:T(8,128)(2,1)S(1)}) custom-call(s32[4]{0:T(128)S(1)} %pad_add_fusion.2.refs_0_, bf16[4,256,2048]{2,1,0:T(8,128)(2,1)S(1)} %copy-done.1, bf16[1024,640]{1,0:T(8,128)(2,1)S(1)} %pad_maximum_fusion.refs_2_, ...), custom_call_target="tpu_custom_call" | custom-call | tf_op jit(solution)/shard_map/pallas_call | solution.py:210
  105.0 2.9 %collective-permute-start.17 = (bf16[256,1280]{1,0:T(8,128)(2,1)S(1)}, bf16[256,1280]{1,0:T(8,128)(2,1)S(1)}, u32[]{:S(2)}, u32[]{:S(2)}) collective-permute-start(bf16[256,1280]{1,0:T(8,128)(2,1)S(1)} %add_dynamic-update-slice_fusion), channel_id=1, source_target_pairs={{0,6},{1,7},{2,0},{3,1},{4,2},{5,3},{6,4},{7,5},{8,14},{9,15},{10,... | collective-permute-start | bytes 1966088 | tf_op jit(solution)/shard_map/ppermute | solution.py:41
  107.9 3.3 %multiply_reduce_fusion = f32[4,256]{1,0:T(4,128)S(1)} fusion(bf16[4,256,2048]{2,1,0:T(8,128)(2,1)} %copy-done, f32[2048]{0:T(1024)S(1)} %dynamic-slice_divide_fusion), kind=kLoop, calls=%fused_computation | loop fusion | flops 8387584 | bytes 4206592 | tf_op jit(solution)/shard_map/reduce_sum | solution.py:357
  112.7 8.9 %collective-permute-done.20 = f32[256]{0:T(256)S(1)} collective-permute-done((f32[256]{0:T(256)S(1)}, f32[256]{0:T(256)S(1)}, u32[]{:S(2)}, u32[]{:S(2)}) %collective-permute-start.20) | collective-permute-done | bytes 1056 | tf_op jit(solution)/shard_map/ppermute | solution.py:41
  121.7 4.5 %collective-permute-done.18 = f32[256]{0:T(256)S(1)} collective-permute-done((f32[256]{0:T(256)S(1)}, f32[256]{0:T(256)S(1)}, u32[]{:S(2)}, u32[]{:S(2)}) %collective-permute-start.18) | collective-permute-done | bytes 1056 | tf_op jit(solution)/shard_map/ppermute | solution.py:41
  144.0 3.3 %collective-permute-done.22.refs_3_ = bf16[256,512]{1,0:T(8,128)(2,1)S(1)} collective-permute-done((bf16[256,512]{1,0:T(8,128)(2,1)S(1)}, bf16[256,512]{1,0:T(8,128)(2,1)S(1)}, u32[]{:S(2)}, u32[]{:S(2)}) %collective-permute-start.22) | collective-permute-done | bytes 262176 | tf_op jit(solution)/shard_map/ppermute | solution.py:41
  147.3 5.6 %collective-permute-done.23.refs_4_ = bf16[256,512]{1,0:T(8,128)(2,1)S(1)} collective-permute-done((bf16[256,512]{1,0:T(8,128)(2,1)S(1)}, bf16[256,512]{1,0:T(8,128)(2,1)S(1)}, u32[]{:S(2)}, u32[]{:S(2)}) %collective-permute-start.23) | collective-permute-done | bytes 262176 | tf_op jit(solution)/shard_map/ppermute | solution.py:41
  155.1 4.3 %shard_map.70 = (bf16[256,1024]{1,0:T(8,128)(2,1)}, bf16[256,1024]{1,0:T(8,128)(2,1)}) custom-call(s32[4]{0:T(128)S(1)} %pad_add_fusion.3.refs_0_, bf16[256,512]{1,0:T(8,128)(2,1)S(1)} %shard_map.67.refs_1_, bf16[256,512]{1,0:T(8,128)(2,1)S(1)} %shard_map.68.refs_2_, bf16[256,512]{1,0:T(8,128)(2,1)S(1)} %collective-permute-done.22.refs_3_, ...), custom_call_target="tpu_custom_call" | custom-call | tf_op jit(solution)/shard_map/pallas_call | solution.py:256
  163.4 8.4 %shard_map.69 = (bf16[256,1024]{1,0:T(8,128)(2,1)S(1)}, bf16[256,1024]{1,0:T(8,128)(2,1)S(1)}, bf16[256,1024]{1,0:T(8,128)(2,1)S(1)}, bf16[256,1024]{1,0:T(8,128...) custom-call(s32[12]{0:T(128)S(1)} %stack.92.refs_0_, bf16[256,512]{1,0:T(8,128)(2,1)S(1)} %shard_map.67.refs_1_, ...), custom_call_target="tpu_custom_call" | custom-call | tf_op jit(solution)/shard_map/pallas_call | solution.py:256
  177.8 3.1 %collective-permute-start.28 = (bf16[256,1024]{1,0:T(8,128)(2,1)}, bf16[256,1024]{1,0:T(8,128)(2,1)S(1)}, u32[]{:S(2)}, u32[]{:S(2)}) collective-permute-start(bf16[256,1024]{1,0:T(8,128)(2,1)} %get-tuple-element.61), channel_id=1, source_target_pairs={{0,48},{1,49},{2,50},{3,51},{4,52},{5,53},{6,54},{7,55},{8,56},{9,... | collective-permute-start | bytes 1572872 | tf_op jit(solution)/shard_map/ppermute | solution.py:41
  180.8 6.0 %collective-permute-done.30 = bf16[256,1024]{1,0:T(8,128)(2,1)S(1)} collective-permute-done((bf16[256,1024]{1,0:T(8,128)(2,1)S(1)}, bf16[256,1024]{1,0:T(8,128)(2,1)S(1)}, u32[]{:S(2)}, u32[]{:S(2)}) %collective-permute-start.30) | collective-permute-done | bytes 524320 | tf_op jit(solution)/shard_map/ppermute | solution.py:41
  186.9 3.7 %collective-permute-done.29 = bf16[256,1024]{1,0:T(8,128)(2,1)S(1)} collective-permute-done((bf16[256,1024]{1,0:T(8,128)(2,1)S(1)}, bf16[256,1024]{1,0:T(8,128)(2,1)S(1)}, u32[]{:S(2)}, u32[]{:S(2)}) %collective-permute-start.29) | collective-permute-done | bytes 524320 | tf_op jit(solution)/shard_map/ppermute | solution.py:41
  191.7 6.6 %collective-permute-done.28 = bf16[256,1024]{1,0:T(8,128)(2,1)S(1)} collective-permute-done((bf16[256,1024]{1,0:T(8,128)(2,1)}, bf16[256,1024]{1,0:T(8,128)(2,1)S(1)}, u32[]{:S(2)}, u32[]{:S(2)}) %collective-permute-start.28) | collective-permute-done | bytes 524320 | tf_op jit(solution)/shard_map/ppermute | solution.py:41
  198.2 3.7 %collective-permute-done.26 = bf16[256,1024]{1,0:T(8,128)(2,1)} collective-permute-done((bf16[256,1024]{1,0:T(8,128)(2,1)S(1)}, bf16[256,1024]{1,0:T(8,128)(2,1)}, u32[]{:S(2)}, u32[]{:S(2)}) %collective-permute-start.26) | collective-permute-done | bytes 524320 | tf_op jit(solution)/shard_map/ppermute | solution.py:41
  203.6 8.8 %collective-permute-start.33 = (bf16[256,512]{1,0:T(8,128)(2,1)S(1)}, bf16[256,512]{1,0:T(8,128)(2,1)S(1)}, u32[]{:S(2)}, u32[]{:S(2)}) collective-permute-start(bf16[256,512]{1,0:T(8,128)(2,1)S(1)} %get-tuple-element.58), channel_id=1, source_target_pairs={{0,8},{1,24},{2,10},{3,26},{4,12},{5,28},{6,14},{7,30},{8,0},{9,16... | collective-permute-start | bytes 786440 | tf_op jit(solution)/shard_map/ppermute | solution.py:41
  214.2 4.5 %collective-permute-done.33 = bf16[256,512]{1,0:T(8,128)(2,1)S(1)} collective-permute-done((bf16[256,512]{1,0:T(8,128)(2,1)S(1)}, bf16[256,512]{1,0:T(8,128)(2,1)S(1)}, u32[]{:S(2)}, u32[]{:S(2)}) %collective-permute-start.33) | collective-permute-done | bytes 262176 | tf_op jit(solution)/shard_map/ppermute | solution.py:41
  218.7 5.6 %collective-permute-done.32 = bf16[256,512]{1,0:T(8,128)(2,1)S(1)} collective-permute-done((bf16[256,512]{1,0:T(8,128)(2,1)S(1)}, bf16[256,512]{1,0:T(8,128)(2,1)S(1)}, u32[]{:S(2)}, u32[]{:S(2)}) %collective-permute-start.32) | collective-permute-done | bytes 262176 | tf_op jit(solution)/shard_map/ppermute | solution.py:41
  (145 shorter events, 78.7 us)
Async XLA Ops:
  6.5 92.7 %all-gather.3.cloned.1.call-start = ((), (), s32[]{:S(2)}) async-start(), calls=%async_computation | async-start | bytes 5242880 | tf_op jit(solution)/shard_map/all_gather | solution.py:341
  12.4 34.6 %collective-permute-start.4 = (bf16[1024,640]{1,0:T(8,128)(2,1)S(1)}, bf16[1024,640]{1,0:T(8,128)(2,1)S(1)}, u32[]{:S(2)}, u32[]{:S(2)}) collective-permute-start(bf16[1024,640]{1,0:T(8,128)(2,1)S(1)} %pad_maximum_fusion.refs_2_), channel_id=1, source_target_pairs={{0,8},{1,9},{2,10},{3,11},{4,12},{5,13},{6,14},{7,15},{8,0},{9,1},... | collective-permute-start | bytes 3932168 | tf_op jit(solution)/shard_map/ppermute | solution.py:41
  12.5 27.5 %collective-permute-start.5 = (bf16[256,1024]{1,0:T(8,128)(2,1)S(1)}, bf16[256,1024]{1,0:T(8,128)(2,1)}, u32[]{:S(2)}, u32[]{:S(2)}) collective-permute-start(bf16[256,1024]{1,0:T(8,128)(2,1)S(1)} %maximum_select_fusion), channel_id=1, source_target_pairs={{0,64},{1,65},{2,66},{3,67},{4,68},{5,69},{6,70},{7,71},{8,72},{9,... | collective-permute-start | bytes 1572872 | tf_op jit(solution)/shard_map/ppermute | solution.py:41
  27.8 14.3 %collective-permute-start.2 = (bf16[256,1024]{1,0:T(8,128)(2,1)S(1)}, bf16[256,1024]{1,0:T(8,128)(2,1)S(1)}, u32[]{:S(2)}, u32[]{:S(2)}) collective-permute-start(bf16[256,1024]{1,0:T(8,128)(2,1)S(1)} %maximum_select_fusion), channel_id=1, source_target_pairs={{0,16},{1,17},{2,18},{3,19},{4,20},{5,21},{6,22},{7,23},{8,24},{9,... | collective-permute-start | bytes 1572872 | tf_op jit(solution)/shard_map/ppermute | solution.py:41
  31.1 40.2 %collective-permute-start.12 = (bf16[1024,640]{1,0:T(8,128)(2,1)S(1)}, bf16[1024,640]{1,0:T(8,128)(2,1)}, u32[]{:S(2)}, u32[]{:S(2)}) collective-permute-start(bf16[1024,640]{1,0:T(8,128)(2,1)S(1)} %pad_maximum_fusion.refs_2_), channel_id=1, source_target_pairs={{0,1},{1,0},{2,3},{3,2},{4,5},{5,4},{6,7},{7,6},{8,9},{9,8},{10,11... | collective-permute-start | bytes 3932168 | tf_op jit(solution)/shard_map/ppermute | solution.py:41
  34.4 12.6 %collective-permute-start.3 = (bf16[256,1024]{1,0:T(8,128)(2,1)S(1)}, bf16[256,1024]{1,0:T(8,128)(2,1)}, u32[]{:S(2)}, u32[]{:S(2)}) collective-permute-start(bf16[256,1024]{1,0:T(8,128)(2,1)S(1)} %maximum_select_fusion), channel_id=1, source_target_pairs={{0,48},{1,49},{2,50},{3,51},{4,52},{5,53},{6,54},{7,55},{8,56},{9,... | collective-permute-start | bytes 1572872 | tf_op jit(solution)/shard_map/ppermute | solution.py:41
  40.0 18.2 %collective-permute-start.9 = (bf16[256,1024]{1,0:T(8,128)(2,1)}, bf16[256,1024]{1,0:T(8,128)(2,1)}, u32[]{:S(2)}, u32[]{:S(2)}) collective-permute-start(bf16[256,1024]{1,0:T(8,128)(2,1)} %collective-permute-done.5), channel_id=1, source_target_pairs={{0,48},{1,49},{2,50},{3,51},{4,52},{5,53},{6,54},{7,55},{8,56},{9,... | collective-permute-start | bytes 1572872 | tf_op jit(solution)/shard_map/ppermute | solution.py:41
  42.8 16.8 %collective-permute-start.8 = (bf16[256,1024]{1,0:T(8,128)(2,1)}, bf16[256,1024]{1,0:T(8,128)(2,1)}, u32[]{:S(2)}, u32[]{:S(2)}) collective-permute-start(bf16[256,1024]{1,0:T(8,128)(2,1)} %collective-permute-done.5), channel_id=1, source_target_pairs={{0,16},{1,17},{2,18},{3,19},{4,20},{5,21},{6,22},{7,23},{8,24},{9,... | collective-permute-start | bytes 1572872 | tf_op jit(solution)/shard_map/ppermute | solution.py:41
  48.0 16.5 %collective-permute-start.6 = (bf16[128,1024]{1,0:T(8,128)(2,1)S(1)}, bf16[128,1024]{1,0:T(8,128)(2,1)S(1)}, u32[]{:S(2)}, u32[]{:S(2)}) collective-permute-start(bf16[128,1024]{1,0:T(8,128)(2,1)S(1)} %slice.42), channel_id=1, source_target_pairs={{0,16},{1,17},{2,18},{3,19},{4,20},{5,21},{6,22},{7,23},{8,24},{9,... | collective-permute-start | bytes 786440 | tf_op jit(solution)/shard_map/ppermute | solution.py:41
  59.2 19.0 %collective-permute-start.11 = (bf16[128,1024]{1,0:T(8,128)(2,1)S(1)}, bf16[128,1024]{1,0:T(8,128)(2,1)S(1)}, u32[]{:S(2)}, u32[]{:S(2)}) collective-permute-start(bf16[128,1024]{1,0:T(8,128)(2,1)S(1)} %slice.57), channel_id=1, source_target_pairs={{0,48},{1,49},{2,50},{3,51},{4,52},{5,53},{6,54},{7,55},{8,56},{9,... | collective-permute-start | bytes 786440 | tf_op jit(solution)/shard_map/ppermute | solution.py:41
  60.6 17.6 %collective-permute-start.10 = (bf16[128,1024]{1,0:T(8,128)(2,1)S(1)}, bf16[128,1024]{1,0:T(8,128)(2,1)S(1)}, u32[]{:S(2)}, u32[]{:S(2)}) collective-permute-start(bf16[128,1024]{1,0:T(8,128)(2,1)S(1)} %slice.56), channel_id=1, source_target_pairs={{0,16},{1,17},{2,18},{3,19},{4,20},{5,21},{6,22},{7,23},{8,24},{9,... | collective-permute-start | bytes 786440 | tf_op jit(solution)/shard_map/ppermute | solution.py:41
  83.7 15.5 %collective-permute-start.14 = (bf16[128,1280]{1,0:T(8,128)(2,1)}, bf16[128,1280]{1,0:T(8,128)(2,1)}, u32[]{:S(2)}, u32[]{:S(2)}) collective-permute-start(bf16[128,1280]{1,0:T(8,128)(2,1)} %get-tuple-element.37), channel_id=1, source_target_pairs={{0,2},{1,3},{2,4},{3,5},{4,6},{5,7},{6,0},{7,1},{8,10},{9,11},{10,... | collective-permute-start | bytes 983048 | tf_op jit(solution)/shard_map/ppermute | solution.py:41
  84.3 14.9 %collective-permute-start.15 = (bf16[128,1280]{1,0:T(8,128)(2,1)}, bf16[128,1280]{1,0:T(8,128)(2,1)}, u32[]{:S(2)}, u32[]{:S(2)}) collective-permute-start(bf16[128,1280]{1,0:T(8,128)(2,1)} %get-tuple-element.38), channel_id=1, source_target_pairs={{0,6},{1,7},{2,0},{3,1},{4,2},{5,3},{6,4},{7,5},{8,14},{9,15},{10,... | collective-permute-start | bytes 983048 | tf_op jit(solution)/shard_map/ppermute | solution.py:41
  99.2 53.7 %collective-permute-start.24 = (bf16[4,512,1024]{2,1,0:T(8,128)(2,1)}, bf16[4,512,1024]{2,1,0:T(8,128)(2,1)}, u32[]{:S(2)}, u32[]{:S(2)}) collective-permute-start(bf16[4,512,1024]{2,1,0:T(8,128)(2,1)} %bitcast.44), channel_id=1, source_target_pairs={{0,8},{1,9},{2,10},{3,11},{4,12},{5,13},{6,14},{7,15},{8,0},{9,1},... | collective-permute-start | bytes 12582920 | tf_op jit(solution)/shard_map/ppermute | solution.py:41
  103.9 23.1 %collective-permute-start.16 = (bf16[256,1280]{1,0:T(8,128)(2,1)}, bf16[256,1280]{1,0:T(8,128)(2,1)S(1)}, u32[]{:S(2)}, u32[]{:S(2)}) collective-permute-start(bf16[256,1280]{1,0:T(8,128)(2,1)} %add_dynamic-update-slice_fusion.1), channel_id=1, source_target_pairs={{0,2},{1,3},{2,4},{3,5},{4,6},{5,7},{6,0},{7,1},{8,10},{9,11},{10,... | collective-permute-start | bytes 1966088 | tf_op jit(solution)/shard_map/ppermute | solution.py:41
  105.0 21.9 %collective-permute-start.17 = (bf16[256,1280]{1,0:T(8,128)(2,1)S(1)}, bf16[256,1280]{1,0:T(8,128)(2,1)S(1)}, u32[]{:S(2)}, u32[]{:S(2)}) collective-permute-start(bf16[256,1280]{1,0:T(8,128)(2,1)S(1)} %add_dynamic-update-slice_fusion), channel_id=1, source_target_pairs={{0,6},{1,7},{2,0},{3,1},{4,2},{5,3},{6,4},{7,5},{8,14},{9,15},{10,... | collective-permute-start | bytes 1966088 | tf_op jit(solution)/shard_map/ppermute | solution.py:41
  159.4 13.0 %collective-permute-start.27 = (bf16[256,1024]{1,0:T(8,128)(2,1)}, bf16[256,1024]{1,0:T(8,128)(2,1)}, u32[]{:S(2)}, u32[]{:S(2)}) collective-permute-start(bf16[256,1024]{1,0:T(8,128)(2,1)} %get-tuple-element.53), channel_id=1, source_target_pairs={{0,48},{1,49},{2,50},{3,51},{4,52},{5,53},{6,54},{7,55},{8,56},{9,... | collective-permute-start | bytes 1572872 | tf_op jit(solution)/shard_map/ppermute | solution.py:41
  160.2 16.1 %collective-permute-start.25 = (bf16[256,1024]{1,0:T(8,128)(2,1)}, bf16[256,1024]{1,0:T(8,128)(2,1)}, u32[]{:S(2)}, u32[]{:S(2)}) collective-permute-start(bf16[256,1024]{1,0:T(8,128)(2,1)} %get-tuple-element.51), channel_id=1, source_target_pairs={{0,16},{1,17},{2,18},{3,19},{4,20},{5,21},{6,22},{7,23},{8,24},{9,... | collective-permute-start | bytes 1572872 | tf_op jit(solution)/shard_map/ppermute | solution.py:41
  174.5 12.4 %collective-permute-start.30 = (bf16[256,1024]{1,0:T(8,128)(2,1)S(1)}, bf16[256,1024]{1,0:T(8,128)(2,1)S(1)}, u32[]{:S(2)}, u32[]{:S(2)}) collective-permute-start(bf16[256,1024]{1,0:T(8,128)(2,1)S(1)} %get-tuple-element.62), channel_id=1, source_target_pairs={{0,48},{1,49},{2,50},{3,51},{4,52},{5,53},{6,54},{7,55},{8,56},{9,... | collective-permute-start | bytes 1572872 | tf_op jit(solution)/shard_map/ppermute | solution.py:41
  177.6 13.0 %collective-permute-start.29 = (bf16[256,1024]{1,0:T(8,128)(2,1)S(1)}, bf16[256,1024]{1,0:T(8,128)(2,1)S(1)}, u32[]{:S(2)}, u32[]{:S(2)}) collective-permute-start(bf16[256,1024]{1,0:T(8,128)(2,1)S(1)} %get-tuple-element.60), channel_id=1, source_target_pairs={{0,16},{1,17},{2,18},{3,19},{4,20},{5,21},{6,22},{7,23},{8,24},{9,... | collective-permute-start | bytes 1572872 | tf_op jit(solution)/shard_map/ppermute | solution.py:41
  177.8 20.4 %collective-permute-start.28 = (bf16[256,1024]{1,0:T(8,128)(2,1)}, bf16[256,1024]{1,0:T(8,128)(2,1)S(1)}, u32[]{:S(2)}, u32[]{:S(2)}) collective-permute-start(bf16[256,1024]{1,0:T(8,128)(2,1)} %get-tuple-element.61), channel_id=1, source_target_pairs={{0,48},{1,49},{2,50},{3,51},{4,52},{5,53},{6,54},{7,55},{8,56},{9,... | collective-permute-start | bytes 1572872 | tf_op jit(solution)/shard_map/ppermute | solution.py:41
  180.8 21.1 %collective-permute-start.26 = (bf16[256,1024]{1,0:T(8,128)(2,1)S(1)}, bf16[256,1024]{1,0:T(8,128)(2,1)}, u32[]{:S(2)}, u32[]{:S(2)}) collective-permute-start(bf16[256,1024]{1,0:T(8,128)(2,1)S(1)} %get-tuple-element.59), channel_id=1, source_target_pairs={{0,16},{1,17},{2,18},{3,19},{4,20},{5,21},{6,22},{7,23},{8,24},{9,... | collective-permute-start | bytes 1572872 | tf_op jit(solution)/shard_map/ppermute | solution.py:41
  203.6 15.2 %collective-permute-start.33 = (bf16[256,512]{1,0:T(8,128)(2,1)S(1)}, bf16[256,512]{1,0:T(8,128)(2,1)S(1)}, u32[]{:S(2)}, u32[]{:S(2)}) collective-permute-start(bf16[256,512]{1,0:T(8,128)(2,1)S(1)} %get-tuple-element.58), channel_id=1, source_target_pairs={{0,8},{1,24},{2,10},{3,26},{4,12},{5,28},{6,14},{7,30},{8,0},{9,16... | collective-permute-start | bytes 786440 | tf_op jit(solution)/shard_map/ppermute | solution.py:41
  212.3 12.0 %collective-permute-start.32 = (bf16[256,512]{1,0:T(8,128)(2,1)S(1)}, bf16[256,512]{1,0:T(8,128)(2,1)S(1)}, u32[]{:S(2)}, u32[]{:S(2)}) collective-permute-start(bf16[256,512]{1,0:T(8,128)(2,1)S(1)} %get-tuple-element.57), channel_id=1, source_target_pairs={{0,0},{1,16},{2,2},{3,18},{4,4},{5,20},{6,6},{7,22},{8,8},{9,24},{... | collective-permute-start | bytes 786440 | tf_op jit(solution)/shard_map/ppermute | solution.py:41
  (33 other events, 274.5 us)
Sparse Core Ops, SparseCore 0:
  12.5 64.2 all-gather.2

commit v8 on v7

--- a/solution.py
+++ b/solution.py
@@ -183,41 +183,51 @@
     )(*sums, scale, cosine, sine, bias, own, other)
 
 
-def project_kernel(steps, at_ref, rows_ref, near, near_other, far, far_other, *outs):
-    zh = at_ref[0]
+def project_kernel(at_ref, rows_ref, near, near_other, near_kv, far, far_other, *outs):
+    zh, core = at_ref[0], at_ref[1]
+    step = pl.program_id(0)
     near_rows = rows_ref[0, :, pl.ds(pl.multiple_of(zh * 1024, 1024), 1024)]
     far_rows = rows_ref[0, :, pl.ds(pl.multiple_of((1 - zh) * 1024, 1024), 1024)]
-    own = (dot(near_rows, near[...]) + dot(far_rows, far[...])).astype(jnp.bfloat16)
-    other = (dot(near_rows, near_other[...]) + dot(far_rows, far_other[...])).astype(jnp.bfloat16)
-    if steps == 1:
-        for half, out in enumerate(outs):
-            out[:, :WIDE] = own[half * 128 : half * 128 + 128]
-            out[:, WIDE:] = other[half * 128 : half * 128 + 128]
-        return
-    for step, out in enumerate(outs):
-
-        @pl.when(pl.program_id(0) == step)
-        def _():
-            out[:, :WIDE] = own
-            out[:, WIDE:] = other
-
-
-def project(which, zh, gathered, weights):
+
+    def put(start, near_part, far_part):
+        cols = slice(start, start + near_part.shape[1])
+        value = (dot(near_rows, near_part) + dot(far_rows, far_part)).astype(jnp.bfloat16)
+        if outs[0].shape[0] == 128:
+            outs[0][:, cols] = value[:128]
+            outs[1][:, cols] = value[128:]
+        elif len(outs) == 1:
+            outs[0][:, cols] = value
+        else:
+            for i, out in enumerate(outs):
+
+                @pl.when(step == i)
+                def _():
+                    out[:, cols] = value
+
+    def kv_cols(which):
+        return near_kv[:, pl.ds(pl.multiple_of(which * HEAD_SIZE, HEAD_SIZE), HEAD_SIZE)]
+
+    put(0, near[...], far[:, :512])
+    put(512, kv_cols(core), far[:, 512:])
+    put(WIDE, near_other[...], far_other[:, :512])
+    put(WIDE + 512, kv_cols(1 - core), far_other[:, 512:])
+
+
+def project(which, zh, core, gathered, weights, halves=False):
     steps = len(which)
-    rows = 128 if steps == 1 else HALF
-    outs = 2 if steps == 1 else steps
-    whole = pl.BlockSpec((1024, WIDE), lambda i, at: (0, 0))
+    rows, outs = (128, 2) if halves else (HALF, steps)
     return pl.pallas_call(
-        lambda *refs: project_kernel(steps, *refs),
+        project_kernel,
         grid_spec=pltpu.PrefetchScalarGridSpec(
             num_scalar_prefetch=1,
             grid=(steps,),
-            in_specs=[pl.BlockSpec((1, HALF, 2048), lambda i, at: (at[1 + i], 0, 0))] + [whole] * 4,
+            in_specs=[pl.BlockSpec((1, HALF, 2048), lambda i, at: (at[2 + i], 0, 0))]
+            + [pl.BlockSpec(w.shape, lambda i, at: (0, 0)) for w in weights],
             out_specs=[pl.BlockSpec((rows, 2 * WIDE), lambda i, at: (0, 0))] * outs,
         ),
         out_shape=[jax.ShapeDtypeStruct((rows, 2 * WIDE), jnp.bfloat16)] * outs,
         compiler_params=GRANT,
-    )(jnp.stack([zh, *which]).astype(jnp.int32), gathered, *weights)
+    )(jnp.stack([zh, core, *which]).astype(jnp.int32), gathered, *weights)
 
 
 def products_kernel(split, steps, at_ref, own_a, own_b, far_a, far_b, near, other, *outs):
@@ -295,30 +305,42 @@
     zh = lax.axis_index("zh")
     is_first = core == 0
 
+    near_other = core_swap(query_weight)
+
     gain = lax.dynamic_slice_in_dim(norm_gain, (chip * 2 + core) * 512, 512, 0)
     wide = tokens.astype(jnp.float32)
     gained = (wide * gain[None, :]).astype(jnp.bfloat16)
-    mine_out, theirs_out = half_of(gained, core), half_of(gained, 1 - core)
-    mine = send(mine_out, to_slice(0))
-    theirs = send(theirs_out, to_slice(1))
+    mine = send(half_of(gained, core), to_slice(0))
+    theirs = send(half_of(gained, 1 - core), to_slice(1))
     block = ordered(is_first, mine, theirs, 1)
 
+    kv_near = lax.dynamic_slice_in_dim(kv_weight, chip * 256, 256, 1)
     kv_own = lax.dynamic_slice_in_dim(kv_weight, chip * 256 + core * 128, 128, 1)
     near = jnp.concatenate([query_weight, kv_own], axis=1)
-    block, near = lax.optimization_barrier((block, near))
-    near_other = core_swap(near)
+    slice_gain = 1.0 / lax.dynamic_slice_in_dim(norm_gain, y * 2048, 2048, 0)
+    own_slots = core * HALF + jnp.arange(HALF, dtype=jnp.int32)
+    slot_k = jnp.concatenate([own_slots, (1 - core) * HALF + jnp.arange(HALF, dtype=jnp.int32)])
+    allowed = (slot_k[None, :] <= own_slots[:, None]) & (slot_k[None, :] < lengths[0])
+    bias = jnp.where(allowed, 0.0, -jnp.inf).astype(jnp.float32)
+    cosine, sine = rope_tables(own_slots)
+    block, near_other, kv_near, near = lax.optimization_barrier((block, near_other, kv_near, near))
+    block, slice_gain, bias, cosine, sine = lax.optimization_barrier(
+        (block, slice_gain, bias, cosine, sine)
+    )
 
     beside = zl_swap(block)
     left = x_shift(block, 1)
     right = x_shift(block, -1)
-    left, right, near_other = lax.optimization_barrier((left, right, near_other))
     far = zh_swap(near)
+    left, right = lax.optimization_barrier((left, right))
     beside_left = x_shift(beside, 1)
     beside_right = x_shift(beside, -1)
     opposite = jnp.concatenate([x_shift(left[:128], 1), x_shift(right[128:], -1)], 0)
     beside_opposite = jnp.concatenate(
         [x_shift(beside_left[:128], 1), x_shift(beside_right[128:], -1)], 0
     )
+    far = after(far, (opposite, beside_left, beside_right))
+    weights = (query_weight, near_other, kv_near, far, core_swap(far))
     gathered = jnp.zeros((4, HALF, 2048), jnp.bfloat16)
     for dz, dx, part in (
         (0, 0, block),
@@ -335,39 +357,31 @@
             gathered, part[None], (zs * 2 + xs // 2, 0, (xs % 2) * 1024)
         )
 
-    far = after(far, (opposite, beside_left, beside_right))
-    weights = (near, near_other, far, core_swap(far))
-
     out_near = lax.all_gather(after(out_weight, block), "y", axis=0, tiled=False)
 
-    low, high = project([(y + 2) % 4], zh, gathered, weights)
+    low, high = project([(y + 2) % 4], zh, core, gathered, weights, True)
     from_below = y_shift(low, 1)
     from_above = y_shift(high, -1)
-    upper, lower, kept = project([(y + 1) % 4, (y + 3) % 4, y], zh, gathered, weights)
-    from_below, from_above, upper, lower, kept = lax.optimization_barrier(
-        (from_below, from_above, upper, lower, kept)
-    )
-    out_other = core_swap(after(out_near, (from_below, from_above)))
+    upper, lower = project([(y + 1) % 4, (y + 3) % 4], zh, core, gathered, weights)
+    from_below, from_above, upper, lower = lax.optimization_barrier(
+        (from_below, from_above, upper, lower)
+    )
     upper = add_rows(upper, from_below, 0)
     lower = add_rows(lower, from_above, 128)
+    gathered, upper, lower = lax.optimization_barrier((gathered, upper, lower))
+    (kept,) = project([y], zh, core, gathered, weights)
     sums = (kept, y_shift(upper, 1), y_shift(lower, -1))
 
-    slice_gain = lax.dynamic_slice_in_dim(norm_gain, y * 2048, 2048, 0)
-    plain = gathered.astype(jnp.float32) * (1.0 / slice_gain)
+    plain = gathered.astype(jnp.float32) * slice_gain
     squares = jnp.sum(plain * plain, axis=-1)
     total = lax.dynamic_index_in_dim(squares, y, 0, keepdims=False)
     for k in (1, 2, 3):
         total += y_shift(lax.dynamic_index_in_dim(squares, (y + k) % 4, 0, keepdims=False), k)
     scale = lax.rsqrt(total / 8192.0 + norm_eps)[:, None]
 
-    own_slots = core * HALF + jnp.arange(HALF, dtype=jnp.int32)
-    slot_k = jnp.concatenate([own_slots, (1 - core) * HALF + jnp.arange(HALF, dtype=jnp.int32)])
-    allowed = (slot_k[None, :] <= own_slots[:, None]) & (slot_k[None, :] < lengths[0])
-    bias = jnp.where(allowed, 0.0, -jnp.inf).astype(jnp.float32)
-    cosine, sine = rope_tables(own_slots)
-
     kv_rows = key_value_rows(core, sums, scale, cosine, sine)
     kv_other = core_swap(kv_rows)
+    out_other = core_swap(after(out_near, kv_other))
     own_a = attention(0, sums, scale, cosine, sine, bias, kv_rows, kv_other)
     far_a = zh_swap(own_a)
     own_b = attention(1, sums, scale, cosine, sine, bias, kv_rows, kv_other)

time: 234 us -> 251 us (1.073)
  waiting for transfers between devices: 78.9 us -> 103 us
  starting transfers between devices: 62.3 us -> 55.6 us
    ppermute x34, waiting for transfers between devices: 78.8 us -> 103 us  [send(): return lax.ppermute(value, AXES, pairs(change))]
    ppermute x34, starting transfers between devices: 62.3 us -> 55.6 us  [send(): return lax.ppermute(value, AXES, pairs(change))]
    pallas_call x2 -> x3, Pallas kernels: 12.9 us -> 11.8 us  [project(): pl.pallas_call(project_kernel, grid_spec=pltpu.PrefetchScalarGridSpec(num...]
    unnamed x45 -> x57, local copies, waits for them, and re-layouts: 15.4 us -> 15.4 us
  transfers between devices with their start and end apart: 35 -> 35, of which waited for: 17 -> 17; matrix products, arithmetic and copies ran while one was open for 11% -> 10% of each run, Pallas kernels for 12% -> 11%
where the time goes in v8:
time: 251 us; the launch traced here: 250 us
  waiting for transfers between devices  103 us (41%)
  starting transfers between devices  55.6 us (22%)
  Pallas kernels  31.3 us (12%)
  local copies, waits for them, and re-layouts  26 us (10%)
  other arithmetic  19.5 us (8%)
  between operations  14.5 us (6%)
    ppermute x34, waiting for transfers between devices, send(): return lax.ppermute(value, AXES, pairs(change))  103 us
    ppermute x34, starting transfers between devices, send(): return lax.ppermute(value, AXES, pairs(change))  55.6 us
    unnamed x57, local copies, waits for them, and re-layouts  15.4 us
    pallas_call x2, Pallas kernels, products(): pl.pallas_call(lambda *refs: products_kernel(split, steps, *refs), grid_s...  12 us
    pallas_call x3, Pallas kernels, project(): pl.pallas_call(project_kernel, grid_spec=pltpu.PrefetchScalarGridSpec(num...  11.8 us
    dynamic_update_slice x4, other arithmetic, add_rows(): lax.dynamic_update_slice(value, value[start:start + rows] + arrived, (sta...  6.42 us
    pallas_call x2, Pallas kernels, attention(): pl.pallas_call(attention_kernel, grid=(1,), in_specs=[pl.BlockSpec((HALF,...  5.46 us
  transfers between devices with their start and end apart: 35, of which 17 were waited for; matrix products, arithmetic and copies ran while one was open for 10% of the time, Pallas kernels for 11%

profile of v8, /device:TPU:3, one launch (start us, length us, event | category | flops | bytes accessed | tf_op | source)
XLA Modules:
  0.0 249.7 jit_solution(17734617182803617124)
XLA Ops:
  20.8 3.7 %collective-permute-start.12 = (bf16[1024,640]{1,0:T(8,128)(2,1)}, bf16[1024,640]{1,0:T(8,128)(2,1)S(1)}, u32[]{:S(2)}, u32[]{:S(2)}) collective-permute-start(bf16[1024,640]{1,0:T(8,128)(2,1)} %pad_maximum_fusion), channel_id=1, source_target_pairs={{0,1},{1,0},{2,3},{3,2},{4,5},{5,4},{6,7},{7,6},{8,9},{9,8},{10,11... | collective-permute-start | bytes 3932168 | tf_op jit(solution)/shard_map/ppermute | solution.py:41
  24.5 8.2 %collective-permute-start.3 = (bf16[256,1024]{1,0:T(8,128)(2,1)}, bf16[256,1024]{1,0:T(8,128)(2,1)}, u32[]{:S(2)}, u32[]{:S(2)}) collective-permute-start(bf16[256,1024]{1,0:T(8,128)(2,1)} %maximum_select_fusion), channel_id=1, source_target_pairs={{0,16},{1,17},{2,18},{3,19},{4,20},{5,21},{6,22},{7,23},{8,24},{9,... | collective-permute-start | bytes 1572872 | tf_op jit(solution)/shard_map/ppermute | solution.py:41
  32.7 2.8 %collective-permute-start.5 = (bf16[256,1024]{1,0:T(8,128)(2,1)}, bf16[256,1024]{1,0:T(8,128)(2,1)}, u32[]{:S(2)}, u32[]{:S(2)}) collective-permute-start(bf16[256,1024]{1,0:T(8,128)(2,1)} %maximum_select_fusion), channel_id=1, source_target_pairs={{0,64},{1,65},{2,66},{3,67},{4,68},{5,69},{6,70},{7,71},{8,72},{9,... | collective-permute-start | bytes 1572872 | tf_op jit(solution)/shard_map/ppermute | solution.py:41
  35.6 8.0 %collective-permute-done.3 = bf16[256,1024]{1,0:T(8,128)(2,1)} collective-permute-done((bf16[256,1024]{1,0:T(8,128)(2,1)}, bf16[256,1024]{1,0:T(8,128)(2,1)}, u32[]{:S(2)}, u32[]{:S(2)}) %collective-permute-start.3) | collective-permute-done | bytes 524320 | tf_op jit(solution)/shard_map/ppermute | solution.py:41
  47.4 24.7 %collective-permute-done.5 = bf16[256,1024]{1,0:T(8,128)(2,1)} collective-permute-done((bf16[256,1024]{1,0:T(8,128)(2,1)}, bf16[256,1024]{1,0:T(8,128)(2,1)}, u32[]{:S(2)}, u32[]{:S(2)}) %collective-permute-start.5) | collective-permute-done | bytes 524320 | tf_op jit(solution)/shard_map/ppermute | solution.py:41
  72.2 3.4 %collective-permute-start.8 = (bf16[256,1024]{1,0:T(8,128)(2,1)}, bf16[256,1024]{1,0:T(8,128)(2,1)S(1)}, u32[]{:S(2)}, u32[]{:S(2)}) collective-permute-start(bf16[256,1024]{1,0:T(8,128)(2,1)} %collective-permute-done.5), channel_id=1, source_target_pairs={{0,16},{1,17},{2,18},{3,19},{4,20},{5,21},{6,22},{7,23},{8,24},{9,... | collective-permute-start | bytes 1572872 | tf_op jit(solution)/shard_map/ppermute | solution.py:41
  79.9 13.4 %collective-permute-done.7 = bf16[128,1024]{1,0:T(8,128)(2,1)S(1)} collective-permute-done((bf16[128,1024]{1,0:T(8,128)(2,1)S(1)}, bf16[128,1024]{1,0:T(8,128)(2,1)S(1)}, u32[]{:S(2)}, u32[]{:S(2)}) %collective-permute-start.7) | collective-permute-done | bytes 262176 | tf_op jit(solution)/shard_map/ppermute | solution.py:41
  99.9 6.2 %collective-permute-done.11 = bf16[128,1024]{1,0:T(8,128)(2,1)S(1)} collective-permute-done((bf16[128,1024]{1,0:T(8,128)(2,1)S(1)}, bf16[128,1024]{1,0:T(8,128)(2,1)S(1)}, u32[]{:S(2)}, u32[]{:S(2)}) %collective-permute-start.11) | collective-permute-done | bytes 262176 | tf_op jit(solution)/shard_map/ppermute | solution.py:41
  107.6 3.2 %shard_map.64 = (bf16[128,1280]{1,0:T(8,128)(2,1)}, bf16[128,1280]{1,0:T(8,128)(2,1)}) custom-call(s32[3]{0:T(128)S(1)} %pad_add_fusion.3.at_ref, bf16[4,256,2048]{2,1,0:T(8,128)(2,1)S(1)} %fusion.2.rows_ref, bf16[1024,512]{1,0:T(8,128)(2,1)S(1)} %copy-done.3, bf16[1024,512]{1,0:T(8,128)(2,1)S(1)} %collective-permute-done.2.near_other, ...), custom_call_target="tpu_custom_call" | custom-call | tf_op jit(solution)/shard_map/pallas_call | solution.py:219
  110.8 2.7 %collective-permute-start.15 = (bf16[128,1280]{1,0:T(8,128)(2,1)}, bf16[128,1280]{1,0:T(8,128)(2,1)}, u32[]{:S(2)}, u32[]{:S(2)}) collective-permute-start(bf16[128,1280]{1,0:T(8,128)(2,1)} %get-tuple-element.47), channel_id=1, source_target_pairs={{0,6},{1,7},{2,0},{3,1},{4,2},{5,3},{6,4},{7,5},{8,14},{9,15},{10,... | collective-permute-start | bytes 983048 | tf_op jit(solution)/shard_map/ppermute | solution.py:41
  118.1 6.3 %shard_map.65 = (bf16[256,1280]{1,0:T(8,128)(2,1)}, bf16[256,1280]{1,0:T(8,128)(2,1)}) custom-call(s32[4]{0:T(128)S(1)} %pad_add_fusion.4.at_ref, bf16[4,256,2048]{2,1,0:T(8,128)(2,1)S(1)} %copy-done.1, bf16[1024,512]{1,0:T(8,128)(2,1)S(1)} %copy-done.3, bf16[1024,512]{1,0:T(8,128)(2,1)S(1)} %collective-permute-done.2.near_other, ...), custom_call_target="tpu_custom_call" | custom-call | tf_op jit(solution)/shard_map/pallas_call | solution.py:219
  128.3 2.7 %collective-permute-start.17 = (bf16[256,1280]{1,0:T(8,128)(2,1)}, bf16[256,1280]{1,0:T(8,128)(2,1)}, u32[]{:S(2)}, u32[]{:S(2)}) collective-permute-start(bf16[256,1280]{1,0:T(8,128)(2,1)} %add_dynamic-update-slice_fusion), channel_id=1, source_target_pairs={{0,6},{1,7},{2,0},{3,1},{4,2},{5,3},{6,4},{7,5},{8,14},{9,15},{10,... | collective-permute-start | bytes 1966088 | tf_op jit(solution)/shard_map/ppermute | solution.py:41
  137.0 6.6 %collective-permute-done.20 = f32[256]{0:T(256)S(1)} collective-permute-done((f32[256]{0:T(256)S(1)}, f32[256]{0:T(256)S(1)}, u32[]{:S(2)}, u32[]{:S(2)}) %collective-permute-start.20) | collective-permute-done | bytes 1056 | tf_op jit(solution)/shard_map/ppermute | solution.py:41
  154.3 2.7 %shard_map.68.refs_1_ = bf16[256,512]{1,0:T(8,128)(2,1)S(1)} custom-call(bf16[256,1280]{1,0:T(8,128)(2,1)S(1)} %copy-done.7, bf16[256,1280]{1,0:T(8,128)(2,1)S(1)} %copy-done.12, bf16[256,1280]{1,0:T(8,128)(2,1)} %collective-permute-done.17.k2.v2.s2, f32[256,1]{1,0:T(8,128)S(1)} %copy-done.20, f32[256,128]{1,0:T(8,128)S(1)} %copy-done.18, ...), custom_call_target="tpu_custom_call" | custom-call | tf_op jit(solution)/shard_map/pallas_call | solution.py:168
  158.9 2.7 %shard_map.69.refs_2_ = bf16[256,512]{1,0:T(8,128)(2,1)S(1)} custom-call(bf16[256,1280]{1,0:T(8,128)(2,1)S(1)} %copy-done.7, bf16[256,1280]{1,0:T(8,128)(2,1)S(1)} %copy-done.12, bf16[256,1280]{1,0:T(8,128)(2,1)} %collective-permute-done.17.k2.v2.s2, f32[256,1]{1,0:T(8,128)S(1)} %copy-done.20, f32[256,128]{1,0:T(8,128)S(1)} %copy-done.18, ...), custom_call_target="tpu_custom_call" | custom-call | tf_op jit(solution)/shard_map/pallas_call | solution.py:168
  163.8 2.6 %collective-permute-done.22.refs_3_ = bf16[256,512]{1,0:T(8,128)(2,1)} collective-permute-done((bf16[256,512]{1,0:T(8,128)(2,1)S(1)}, bf16[256,512]{1,0:T(8,128)(2,1)}, u32[]{:S(2)}, u32[]{:S(2)}) %collective-permute-start.22) | collective-permute-done | bytes 262176 | tf_op jit(solution)/shard_map/ppermute | solution.py:41
  166.4 5.5 %collective-permute-done.23.refs_4_ = bf16[256,512]{1,0:T(8,128)(2,1)S(1)} collective-permute-done((bf16[256,512]{1,0:T(8,128)(2,1)S(1)}, bf16[256,512]{1,0:T(8,128)(2,1)S(1)}, u32[]{:S(2)}, u32[]{:S(2)}) %collective-permute-start.23) | collective-permute-done | bytes 262176 | tf_op jit(solution)/shard_map/ppermute | solution.py:41
  174.2 4.4 %shard_map.71 = (bf16[256,1024]{1,0:T(8,128)(2,1)}, bf16[256,1024]{1,0:T(8,128)(2,1)}) custom-call(s32[4]{0:T(128)S(1)} %pad_add_fusion.5.refs_0_, bf16[256,512]{1,0:T(8,128)(2,1)S(1)} %shard_map.68.refs_1_, bf16[256,512]{1,0:T(8,128)(2,1)S(1)} %shard_map.69.refs_2_, bf16[256,512]{1,0:T(8,128)(2,1)} %collective-permute-done.22.refs_3_, ...), custom_call_target="tpu_custom_call" | custom-call | tf_op jit(solution)/shard_map/pallas_call | solution.py:266
  184.2 7.6 %shard_map.70 = (bf16[256,1024]{1,0:T(8,128)(2,1)S(1)}, bf16[256,1024]{1,0:T(8,128)(2,1)S(1)}, bf16[256,1024]{1,0:T(8,128)(2,1)S(1)}, bf16[256,1024]{1,0:T(8,128...) custom-call(s32[12]{0:T(128)S(1)} %stack.101.refs_0_, bf16[256,512]{1,0:T(8,128)(2,1)S(1)} %shard_map.68.refs_1_, ...), custom_call_target="tpu_custom_call" | custom-call | tf_op jit(solution)/shard_map/pallas_call | solution.py:266
  198.5 7.9 %collective-permute-done.30 = bf16[256,1024]{1,0:T(8,128)(2,1)S(1)} collective-permute-done((bf16[256,1024]{1,0:T(8,128)(2,1)S(1)}, bf16[256,1024]{1,0:T(8,128)(2,1)S(1)}, u32[]{:S(2)}, u32[]{:S(2)}) %collective-permute-start.30) | collective-permute-done | bytes 524320 | tf_op jit(solution)/shard_map/ppermute | solution.py:41
  209.8 7.9 %collective-permute-done.28 = bf16[256,1024]{1,0:T(8,128)(2,1)} collective-permute-done((bf16[256,1024]{1,0:T(8,128)(2,1)S(1)}, bf16[256,1024]{1,0:T(8,128)(2,1)}, u32[]{:S(2)}, u32[]{:S(2)}) %collective-permute-start.28) | collective-permute-done | bytes 524320 | tf_op jit(solution)/shard_map/ppermute | solution.py:41
  221.5 6.7 %collective-permute-start.33 = (bf16[256,512]{1,0:T(8,128)(2,1)S(1)}, bf16[256,512]{1,0:T(8,128)(2,1)S(1)}, u32[]{:S(2)}, u32[]{:S(2)}) collective-permute-start(bf16[256,512]{1,0:T(8,128)(2,1)S(1)} %get-tuple-element.72), channel_id=1, source_target_pairs={{0,8},{1,24},{2,10},{3,26},{4,12},{5,28},{6,14},{7,30},{8,0},{9,16... | collective-permute-start | bytes 786440 | tf_op jit(solution)/shard_map/ppermute | solution.py:41
  230.6 4.5 %collective-permute-done.33 = bf16[256,512]{1,0:T(8,128)(2,1)S(1)} collective-permute-done((bf16[256,512]{1,0:T(8,128)(2,1)S(1)}, bf16[256,512]{1,0:T(8,128)(2,1)S(1)}, u32[]{:S(2)}, u32[]{:S(2)}) %collective-permute-start.33) | collective-permute-done | bytes 262176 | tf_op jit(solution)/shard_map/ppermute | solution.py:41
  235.2 5.6 %collective-permute-done.32 = bf16[256,512]{1,0:T(8,128)(2,1)S(1)} collective-permute-done((bf16[256,512]{1,0:T(8,128)(2,1)S(1)}, bf16[256,512]{1,0:T(8,128)(2,1)S(1)}, u32[]{:S(2)}, u32[]{:S(2)}) %collective-permute-start.32) | collective-permute-done | bytes 262176 | tf_op jit(solution)/shard_map/ppermute | solution.py:41
  (160 shorter events, 85.2 us)
Async XLA Ops:
  6.5 145.4 %all-gather.3.cloned.1.call-start = ((), (), s32[]{:S(2)}) async-start(), calls=%async_computation | async-start | bytes 5242880 | tf_op jit(solution)/shard_map/all_gather | solution.py:360
  20.8 72.6 %collective-permute-start.12 = (bf16[1024,640]{1,0:T(8,128)(2,1)}, bf16[1024,640]{1,0:T(8,128)(2,1)S(1)}, u32[]{:S(2)}, u32[]{:S(2)}) collective-permute-start(bf16[1024,640]{1,0:T(8,128)(2,1)} %pad_maximum_fusion), channel_id=1, source_target_pairs={{0,1},{1,0},{2,3},{3,2},{4,5},{5,4},{6,7},{7,6},{8,9},{9,8},{10,11... | collective-permute-start | bytes 3932168 | tf_op jit(solution)/shard_map/ppermute | solution.py:41
  24.5 19.1 %collective-permute-start.3 = (bf16[256,1024]{1,0:T(8,128)(2,1)}, bf16[256,1024]{1,0:T(8,128)(2,1)}, u32[]{:S(2)}, u32[]{:S(2)}) collective-permute-start(bf16[256,1024]{1,0:T(8,128)(2,1)} %maximum_select_fusion), channel_id=1, source_target_pairs={{0,16},{1,17},{2,18},{3,19},{4,20},{5,21},{6,22},{7,23},{8,24},{9,... | collective-permute-start | bytes 1572872 | tf_op jit(solution)/shard_map/ppermute | solution.py:41
  32.7 12.8 %collective-permute-start.4 = (bf16[256,1024]{1,0:T(8,128)(2,1)}, bf16[256,1024]{1,0:T(8,128)(2,1)}, u32[]{:S(2)}, u32[]{:S(2)}) collective-permute-start(bf16[256,1024]{1,0:T(8,128)(2,1)} %maximum_select_fusion), channel_id=1, source_target_pairs={{0,48},{1,49},{2,50},{3,51},{4,52},{5,53},{6,54},{7,55},{8,56},{9,... | collective-permute-start | bytes 1572872 | tf_op jit(solution)/shard_map/ppermute | solution.py:41
  32.7 39.4 %collective-permute-start.5 = (bf16[256,1024]{1,0:T(8,128)(2,1)}, bf16[256,1024]{1,0:T(8,128)(2,1)}, u32[]{:S(2)}, u32[]{:S(2)}) collective-permute-start(bf16[256,1024]{1,0:T(8,128)(2,1)} %maximum_select_fusion), channel_id=1, source_target_pairs={{0,64},{1,65},{2,66},{3,67},{4,68},{5,69},{6,70},{7,71},{8,72},{9,... | collective-permute-start | bytes 1572872 | tf_op jit(solution)/shard_map/ppermute | solution.py:41
  46.5 33.4 %collective-permute-start.6 = (bf16[128,1024]{1,0:T(8,128)(2,1)S(1)}, bf16[128,1024]{1,0:T(8,128)(2,1)S(1)}, u32[]{:S(2)}, u32[]{:S(2)}) collective-permute-start(bf16[128,1024]{1,0:T(8,128)(2,1)S(1)} %slice.42), channel_id=1, source_target_pairs={{0,16},{1,17},{2,18},{3,19},{4,20},{5,21},{6,22},{7,23},{8,24},{9,... | collective-permute-start | bytes 786440 | tf_op jit(solution)/shard_map/ppermute | solution.py:41
  72.2 21.2 %collective-permute-start.8 = (bf16[256,1024]{1,0:T(8,128)(2,1)}, bf16[256,1024]{1,0:T(8,128)(2,1)S(1)}, u32[]{:S(2)}, u32[]{:S(2)}) collective-permute-start(bf16[256,1024]{1,0:T(8,128)(2,1)} %collective-permute-done.5), channel_id=1, source_target_pairs={{0,16},{1,17},{2,18},{3,19},{4,20},{5,21},{6,22},{7,23},{8,24},{9,... | collective-permute-start | bytes 1572872 | tf_op jit(solution)/shard_map/ppermute | solution.py:41
  75.6 17.8 %collective-permute-start.9 = (bf16[256,1024]{1,0:T(8,128)(2,1)}, bf16[256,1024]{1,0:T(8,128)(2,1)S(1)}, u32[]{:S(2)}, u32[]{:S(2)}) collective-permute-start(bf16[256,1024]{1,0:T(8,128)(2,1)} %collective-permute-done.5), channel_id=1, source_target_pairs={{0,48},{1,49},{2,50},{3,51},{4,52},{5,53},{6,54},{7,55},{8,56},{9,... | collective-permute-start | bytes 1572872 | tf_op jit(solution)/shard_map/ppermute | solution.py:41
  77.2 16.2 %collective-permute-start.7 = (bf16[128,1024]{1,0:T(8,128)(2,1)S(1)}, bf16[128,1024]{1,0:T(8,128)(2,1)S(1)}, u32[]{:S(2)}, u32[]{:S(2)}) collective-permute-start(bf16[128,1024]{1,0:T(8,128)(2,1)S(1)} %slice.43), channel_id=1, source_target_pairs={{0,48},{1,49},{2,50},{3,51},{4,52},{5,53},{6,54},{7,55},{8,56},{9,... | collective-permute-start | bytes 786440 | tf_op jit(solution)/shard_map/ppermute | solution.py:41
  93.4 14.2 %collective-permute-start.13 = (bf16[1024,640]{1,0:T(8,128)(2,1)S(1)}, bf16[1024,640]{1,0:T(8,128)(2,1)S(1)}, u32[]{:S(2)}, u32[]{:S(2)}) collective-permute-start(bf16[1024,640]{1,0:T(8,128)(2,1)S(1)} %collective-permute-done.12.far), channel_id=1, source_target_pairs={{0,8},{1,9},{2,10},{3,11},{4,12},{5,13},{6,14},{7,15},{8,0},{9,1},... | collective-permute-start | bytes 3932168 | tf_op jit(solution)/shard_map/ppermute | solution.py:41
  110.8 13.6 %collective-permute-start.14 = (bf16[128,1280]{1,0:T(8,128)(2,1)}, bf16[128,1280]{1,0:T(8,128)(2,1)}, u32[]{:S(2)}, u32[]{:S(2)}) collective-permute-start(bf16[128,1280]{1,0:T(8,128)(2,1)} %get-tuple-element.46), channel_id=1, source_target_pairs={{0,2},{1,3},{2,4},{3,5},{4,6},{5,7},{6,0},{7,1},{8,10},{9,11},{10,... | collective-permute-start | bytes 983048 | tf_op jit(solution)/shard_map/ppermute | solution.py:41
  110.8 13.6 %collective-permute-start.15 = (bf16[128,1280]{1,0:T(8,128)(2,1)}, bf16[128,1280]{1,0:T(8,128)(2,1)}, u32[]{:S(2)}, u32[]{:S(2)}) collective-permute-start(bf16[128,1280]{1,0:T(8,128)(2,1)} %get-tuple-element.47), channel_id=1, source_target_pairs={{0,6},{1,7},{2,0},{3,1},{4,2},{5,3},{6,4},{7,5},{8,14},{9,15},{10,... | collective-permute-start | bytes 983048 | tf_op jit(solution)/shard_map/ppermute | solution.py:41
  128.3 17.1 %collective-permute-start.16 = (bf16[256,1280]{1,0:T(8,128)(2,1)}, bf16[256,1280]{1,0:T(8,128)(2,1)S(1)}, u32[]{:S(2)}, u32[]{:S(2)}) collective-permute-start(bf16[256,1280]{1,0:T(8,128)(2,1)} %add_dynamic-update-slice_fusion.1), channel_id=1, source_target_pairs={{0,2},{1,3},{2,4},{3,5},{4,6},{5,7},{6,0},{7,1},{8,10},{9,11},{10,... | collective-permute-start | bytes 1966088 | tf_op jit(solution)/shard_map/ppermute | solution.py:41
  128.3 17.1 %collective-permute-start.17 = (bf16[256,1280]{1,0:T(8,128)(2,1)}, bf16[256,1280]{1,0:T(8,128)(2,1)}, u32[]{:S(2)}, u32[]{:S(2)}) collective-permute-start(bf16[256,1280]{1,0:T(8,128)(2,1)} %add_dynamic-update-slice_fusion), channel_id=1, source_target_pairs={{0,6},{1,7},{2,0},{3,1},{4,2},{5,3},{6,4},{7,5},{8,14},{9,15},{10,... | collective-permute-start | bytes 1966088 | tf_op jit(solution)/shard_map/ppermute | solution.py:41
  132.8 11.8 %collective-permute-start.18 = (f32[256]{0:T(256)S(1)}, f32[256]{0:T(256)S(1)}, u32[]{:S(2)}, u32[]{:S(2)}) collective-permute-start(f32[256]{0:T(256)S(1)} %bitcast.49), channel_id=1, source_target_pairs={{0,2},{1,3},{2,4},{3,5},{4,6},{5,7},{6,0},{7,1},{8,10},{9,11},{10,... | collective-permute-start | bytes 3080 | tf_op jit(solution)/shard_map/ppermute | solution.py:41
  151.9 20.1 %collective-permute-start.24 = (bf16[4,512,1024]{2,1,0:T(8,128)(2,1)}, bf16[4,512,1024]{2,1,0:T(8,128)(2,1)}, u32[]{:S(2)}, u32[]{:S(2)}) collective-permute-start(bf16[4,512,1024]{2,1,0:T(8,128)(2,1)} %bitcast.44), channel_id=1, source_target_pairs={{0,8},{1,9},{2,10},{3,11},{4,12},{5,13},{6,14},{7,15},{8,0},{9,1},... | collective-permute-start | bytes 12582920 | tf_op jit(solution)/shard_map/ppermute | solution.py:41
  178.6 14.0 %collective-permute-start.27 = (bf16[256,1024]{1,0:T(8,128)(2,1)}, bf16[256,1024]{1,0:T(8,128)(2,1)}, u32[]{:S(2)}, u32[]{:S(2)}) collective-permute-start(bf16[256,1024]{1,0:T(8,128)(2,1)} %get-tuple-element.67), channel_id=1, source_target_pairs={{0,48},{1,49},{2,50},{3,51},{4,52},{5,53},{6,54},{7,55},{8,56},{9,... | collective-permute-start | bytes 1572872 | tf_op jit(solution)/shard_map/ppermute | solution.py:41
  181.0 14.7 %collective-permute-start.25 = (bf16[256,1024]{1,0:T(8,128)(2,1)}, bf16[256,1024]{1,0:T(8,128)(2,1)}, u32[]{:S(2)}, u32[]{:S(2)}) collective-permute-start(bf16[256,1024]{1,0:T(8,128)(2,1)} %get-tuple-element.65), channel_id=1, source_target_pairs={{0,16},{1,17},{2,18},{3,19},{4,20},{5,21},{6,22},{7,23},{8,24},{9,... | collective-permute-start | bytes 1572872 | tf_op jit(solution)/shard_map/ppermute | solution.py:41
  193.9 12.5 %collective-permute-start.30 = (bf16[256,1024]{1,0:T(8,128)(2,1)S(1)}, bf16[256,1024]{1,0:T(8,128)(2,1)S(1)}, u32[]{:S(2)}, u32[]{:S(2)}) collective-permute-start(bf16[256,1024]{1,0:T(8,128)(2,1)S(1)} %get-tuple-element.76), channel_id=1, source_target_pairs={{0,48},{1,49},{2,50},{3,51},{4,52},{5,53},{6,54},{7,55},{8,56},{9,... | collective-permute-start | bytes 1572872 | tf_op jit(solution)/shard_map/ppermute | solution.py:41
  196.9 11.7 %collective-permute-start.29 = (bf16[256,1024]{1,0:T(8,128)(2,1)S(1)}, bf16[256,1024]{1,0:T(8,128)(2,1)S(1)}, u32[]{:S(2)}, u32[]{:S(2)}) collective-permute-start(bf16[256,1024]{1,0:T(8,128)(2,1)S(1)} %get-tuple-element.74), channel_id=1, source_target_pairs={{0,16},{1,17},{2,18},{3,19},{4,20},{5,21},{6,22},{7,23},{8,24},{9,... | collective-permute-start | bytes 1572872 | tf_op jit(solution)/shard_map/ppermute | solution.py:41
  197.0 20.7 %collective-permute-start.28 = (bf16[256,1024]{1,0:T(8,128)(2,1)S(1)}, bf16[256,1024]{1,0:T(8,128)(2,1)}, u32[]{:S(2)}, u32[]{:S(2)}) collective-permute-start(bf16[256,1024]{1,0:T(8,128)(2,1)S(1)} %get-tuple-element.75), channel_id=1, source_target_pairs={{0,48},{1,49},{2,50},{3,51},{4,52},{5,53},{6,54},{7,55},{8,56},{9,... | collective-permute-start | bytes 1572872 | tf_op jit(solution)/shard_map/ppermute | solution.py:41
  198.5 21.4 %collective-permute-start.26 = (bf16[256,1024]{1,0:T(8,128)(2,1)S(1)}, bf16[256,1024]{1,0:T(8,128)(2,1)}, u32[]{:S(2)}, u32[]{:S(2)}) collective-permute-start(bf16[256,1024]{1,0:T(8,128)(2,1)S(1)} %get-tuple-element.73), channel_id=1, source_target_pairs={{0,16},{1,17},{2,18},{3,19},{4,20},{5,21},{6,22},{7,23},{8,24},{9,... | collective-permute-start | bytes 1572872 | tf_op jit(solution)/shard_map/ppermute | solution.py:41
  221.5 13.6 %collective-permute-start.33 = (bf16[256,512]{1,0:T(8,128)(2,1)S(1)}, bf16[256,512]{1,0:T(8,128)(2,1)S(1)}, u32[]{:S(2)}, u32[]{:S(2)}) collective-permute-start(bf16[256,512]{1,0:T(8,128)(2,1)S(1)} %get-tuple-element.72), channel_id=1, source_target_pairs={{0,8},{1,24},{2,10},{3,26},{4,12},{5,28},{6,14},{7,30},{8,0},{9,16... | collective-permute-start | bytes 786440 | tf_op jit(solution)/shard_map/ppermute | solution.py:41
  228.2 12.6 %collective-permute-start.32 = (bf16[256,512]{1,0:T(8,128)(2,1)S(1)}, bf16[256,512]{1,0:T(8,128)(2,1)S(1)}, u32[]{:S(2)}, u32[]{:S(2)}) collective-permute-start(bf16[256,512]{1,0:T(8,128)(2,1)S(1)} %get-tuple-element.71), channel_id=1, source_target_pairs={{0,0},{1,16},{2,2},{3,18},{4,4},{5,20},{6,6},{7,22},{8,8},{9,24},{... | collective-permute-start | bytes 786440 | tf_op jit(solution)/shard_map/ppermute | solution.py:41
  (39 other events, 423.3 us)
Sparse Core Ops, SparseCore 0:
  20.9 58.1 all-gather.2

commit v9 on v8

--- a/solution.py
+++ b/solution.py
@@ -230,7 +230,34 @@
     )(jnp.stack([zh, core, *which]).astype(jnp.int32), gathered, *weights)
 
 
-def products_kernel(split, steps, at_ref, own_a, own_b, far_a, far_b, near, other, *outs):
+def halves_kernel(at_ref, own_a, own_b, far_a, far_b, near, other, low, high, held, sems):
+    copies = []
+    for i in range(2):
+        for j, source in enumerate((near, other)):
+            copy = pltpu.make_async_copy(source.at[at_ref[i]], held.at[i, j], sems.at[i, j])
+            copy.start()
+            copies.append(copy)
+
+    def put(i, left, right):
+        product = dot(left[...], held[i, 0]) + dot(right[...], held[i, 1])
+        product = product.astype(jnp.bfloat16)
+        low[i * 128 : i * 128 + 128] = product[:128]
+        high[i * 128 : i * 128 + 128] = product[128:]
+
+    for i in range(2):
+        copies[2 * i].wait()
+        copies[2 * i + 1].wait()
+
+        @pl.when(at_ref[2 + i] == 1)
+        def _():
+            put(i, own_a, own_b)
+
+        @pl.when(at_ref[2 + i] == 0)
+        def _():
+            put(i, far_a, far_b)
+
+
+def products_kernel(steps, at_ref, own_a, own_b, far_a, far_b, near, other, *outs):
     step = pl.program_id(0)
 
     def put(left, right):
@@ -240,11 +267,7 @@
 
             @pl.when(step == i)
             def _():
-                if split:
-                    outs[0][i * 128 : i * 128 + 128] = product[:128]
-                    outs[1][i * 128 : i * 128 + 128] = product[128:]
-                else:
-                    outs[i][...] = product
+                outs[i][...] = product
 
     @pl.when(at_ref[steps + step] == 1)
     def _():
@@ -262,14 +285,22 @@
     at = jnp.stack([v.astype(jnp.int32) for v in blocks + owns])
     rows = pl.BlockSpec((HALF, 512), lambda i, at: (0, 0))
     block = pl.BlockSpec((1, 512, 1024), lambda i, at: (at[i], 0, 0))
+    scratch = []
+    if split:
+        block = pl.BlockSpec(memory_space=pltpu.HBM)
+        scratch = [
+            pltpu.VMEM((2, 2, 512, 1024), jnp.bfloat16),
+            pltpu.SemaphoreType.DMA((2, 2)),
+        ]
     count = 2 if split else steps
     return pl.pallas_call(
-        lambda *refs: products_kernel(split, steps, *refs),
+        halves_kernel if split else lambda *refs: products_kernel(steps, *refs),
         grid_spec=pltpu.PrefetchScalarGridSpec(
             num_scalar_prefetch=1,
-            grid=(steps,),
+            grid=(1 if split else steps,),
             in_specs=[rows] * 4 + [block] * 2,
             out_specs=[pl.BlockSpec((HALF, 1024), lambda i, at: (0, 0))] * count,
+            scratch_shapes=scratch,
         ),
         out_shape=[jax.ShapeDtypeStruct((HALF, 1024), jnp.bfloat16)] * count,
         compiler_params=GRANT,
@@ -331,16 +362,15 @@
     beside = zl_swap(block)
     left = x_shift(block, 1)
     right = x_shift(block, -1)
-    far = zh_swap(near)
-    left, right = lax.optimization_barrier((left, right))
+    left, right, beside = lax.optimization_barrier((left, right, beside))
+    far = zh_swap(after(near, beside))
     beside_left = x_shift(beside, 1)
     beside_right = x_shift(beside, -1)
     opposite = jnp.concatenate([x_shift(left[:128], 1), x_shift(right[128:], -1)], 0)
     beside_opposite = jnp.concatenate(
         [x_shift(beside_left[:128], 1), x_shift(beside_right[128:], -1)], 0
     )
-    far = after(far, (opposite, beside_left, beside_right))
-    weights = (query_weight, near_other, kv_near, far, core_swap(far))
+    weights = (query_weight, near_other, kv_near, far, core_swap(after(far, beside_opposite)))
     gathered = jnp.zeros((4, HALF, 2048), jnp.bfloat16)
     for dz, dx, part in (
         (0, 0, block),

time: 251 us -> 228 us (0.908)
  waiting for transfers between devices: 103 us -> 78.1 us
    ppermute x34, waiting for transfers between devices: 103 us -> 78.1 us  [send(): return lax.ppermute(value, AXES, pairs(change))]
    unnamed x57 -> x67, local copies, waits for them, and re-layouts: 15.4 us -> 16.3 us
  transfers between devices with their start and end apart: 35 -> 35, of which waited for: 17 -> 18; matrix products, arithmetic and copies ran while one was open for 10% -> 10% of each run, Pallas kernels for 11% -> 12%
where the time goes in v9:
time: 228 us; the launch traced here: 226 us
  waiting for transfers between devices  78.1 us (34%)
  starting transfers between devices  55.9 us (25%)
  Pallas kernels  32.2 us (14%)
  local copies, waits for them, and re-layouts  27 us (12%)
  other arithmetic  18.7 us (8%)
  between operations  14.5 us (6%)
    ppermute x34, waiting for transfers between devices, send(): return lax.ppermute(value, AXES, pairs(change))  78.1 us
    ppermute x34, starting transfers between devices, send(): return lax.ppermute(value, AXES, pairs(change))  55.9 us
    unnamed x67, local copies, waits for them, and re-layouts  16.3 us
    pallas_call x2, Pallas kernels, products(): pl.pallas_call(halves_kernel if split else lambda *refs: products_kernel(...  12.8 us
    pallas_call x3, Pallas kernels, project(): pl.pallas_call(project_kernel, grid_spec=pltpu.PrefetchScalarGridSpec(num...  11.9 us
    dynamic_update_slice x4, other arithmetic, add_rows(): lax.dynamic_update_slice(value, value[start:start + rows] + arrived, (sta...  6.43 us
    pallas_call x2, Pallas kernels, attention(): pl.pallas_call(attention_kernel, grid=(1,), in_specs=[pl.BlockSpec((HALF,...  5.46 us
  transfers between devices with their start and end apart: 35, of which 18 were waited for; matrix products, arithmetic and copies ran while one was open for 10% of the time, Pallas kernels for 12%

profile of v9, /device:TPU:3, one launch (start us, length us, event | category | flops | bytes accessed | tf_op | source)
XLA Modules:
  0.0 226.4 jit_solution(14122660220103168464)
XLA Ops:
  20.0 8.3 %collective-permute-start.3 = (bf16[256,1024]{1,0:T(8,128)(2,1)S(1)}, bf16[256,1024]{1,0:T(8,128)(2,1)S(1)}, u32[]{:S(2)}, u32[]{:S(2)}) collective-permute-start(bf16[256,1024]{1,0:T(8,128)(2,1)S(1)} %maximum_select_fusion), channel_id=1, source_target_pairs={{0,16},{1,17},{2,18},{3,19},{4,20},{5,21},{6,22},{7,23},{8,24},{9,... | collective-permute-start | bytes 1572872 | tf_op jit(solution)/shard_map/ppermute | solution.py:41
  28.3 3.7 %collective-permute-start.5 = (bf16[256,1024]{1,0:T(8,128)(2,1)S(1)}, bf16[256,1024]{1,0:T(8,128)(2,1)}, u32[]{:S(2)}, u32[]{:S(2)}) collective-permute-start(bf16[256,1024]{1,0:T(8,128)(2,1)S(1)} %maximum_select_fusion), channel_id=1, source_target_pairs={{0,64},{1,65},{2,66},{3,67},{4,68},{5,69},{6,70},{7,71},{8,72},{9,... | collective-permute-start | bytes 1572872 | tf_op jit(solution)/shard_map/ppermute | solution.py:41
  32.1 7.1 %collective-permute-done.3 = bf16[256,1024]{1,0:T(8,128)(2,1)S(1)} collective-permute-done((bf16[256,1024]{1,0:T(8,128)(2,1)S(1)}, bf16[256,1024]{1,0:T(8,128)(2,1)S(1)}, u32[]{:S(2)}, u32[]{:S(2)}) %collective-permute-start.3) | collective-permute-done | bytes 524320 | tf_op jit(solution)/shard_map/ppermute | solution.py:41
  43.8 3.3 %collective-permute-start.12 = (bf16[1024,640]{1,0:T(8,128)(2,1)}, bf16[1024,640]{1,0:T(8,128)(2,1)S(1)}, u32[]{:S(2)}, u32[]{:S(2)}) collective-permute-start(bf16[1024,640]{1,0:T(8,128)(2,1)} %pad_maximum_fusion), channel_id=1, source_target_pairs={{0,1},{1,0},{2,3},{3,2},{4,5},{5,4},{6,7},{7,6},{8,9},{9,8},{10,11... | collective-permute-start | bytes 3932168 | tf_op jit(solution)/shard_map/ppermute | solution.py:41
  48.8 10.8 %collective-permute-done.8 = bf16[256,1024]{1,0:T(8,128)(2,1)} collective-permute-done((bf16[256,1024]{1,0:T(8,128)(2,1)}, bf16[256,1024]{1,0:T(8,128)(2,1)}, u32[]{:S(2)}, u32[]{:S(2)}) %collective-permute-start.8) | collective-permute-done | bytes 524320 | tf_op jit(solution)/shard_map/ppermute | solution.py:41
  67.8 6.3 %collective-permute-done.11 = bf16[128,1024]{1,0:T(8,128)(2,1)S(1)} collective-permute-done((bf16[128,1024]{1,0:T(8,128)(2,1)S(1)}, bf16[128,1024]{1,0:T(8,128)(2,1)S(1)}, u32[]{:S(2)}, u32[]{:S(2)}) %collective-permute-start.11) | collective-permute-done | bytes 262176 | tf_op jit(solution)/shard_map/ppermute | solution.py:41
  80.6 3.2 %shard_map.64 = (bf16[128,1280]{1,0:T(8,128)(2,1)}, bf16[128,1280]{1,0:T(8,128)(2,1)}) custom-call(s32[3]{0:T(128)S(1)} %pad_add_fusion.3.at_ref, bf16[4,256,2048]{2,1,0:T(8,128)(2,1)S(1)} %bitcast_dynamic-update-slice_fusion.rows_ref, bf16[1024,512]{1,0:T(8,128)(2,1)S(1)} %copy-done.3, bf16[1024,512]{1,0:T(8,128)(2,1)S(1)} %collective-permute-done.2.near_other, ...), custom_call_target="tpu_custom_call" | custom-call | tf_op jit(solution)/shard_map/pallas_call | solution.py:219
  91.2 6.3 %shard_map.65 = (bf16[256,1280]{1,0:T(8,128)(2,1)}, bf16[256,1280]{1,0:T(8,128)(2,1)}) custom-call(s32[4]{0:T(128)S(1)} %pad_add_fusion.4.at_ref, bf16[4,256,2048]{2,1,0:T(8,128)(2,1)S(1)} %copy-done.1, bf16[1024,512]{1,0:T(8,128)(2,1)S(1)} %copy-done.3, bf16[1024,512]{1,0:T(8,128)(2,1)S(1)} %collective-permute-done.2.near_other, ...), custom_call_target="tpu_custom_call" | custom-call | tf_op jit(solution)/shard_map/pallas_call | solution.py:219
  110.1 7.4 %collective-permute-done.20 = f32[256]{0:T(256)S(1)} collective-permute-done((f32[256]{0:T(256)S(1)}, f32[256]{0:T(256)S(1)}, u32[]{:S(2)}, u32[]{:S(2)}) %collective-permute-start.20) | collective-permute-done | bytes 1056 | tf_op jit(solution)/shard_map/ppermute | solution.py:41
  127.4 2.7 %shard_map.68.refs_1_.own_a = bf16[256,512]{1,0:T(8,128)(2,1)S(1)} custom-call(bf16[256,1280]{1,0:T(8,128)(2,1)S(1)} %copy-done.7, bf16[256,1280]{1,0:T(8,128)(2,1)S(1)} %copy-done.12, bf16[256,1280]{1,0:T(8,128)(2,1)} %collective-permute-done.17.k2.v2.s2, f32[256,1]{1,0:T(8,128)S(1)} %copy-done.20, f32[256,128]{1,0:T(8,128)S(1)} %copy-done.18, ...), custom_call_target="tpu_custom_call" | custom-call | tf_op jit(solution)/shard_map/pallas_call | solution.py:168
  130.1 3.0 %collective-permute-start.22 = (bf16[256,512]{1,0:T(8,128)(2,1)S(1)}, bf16[256,512]{1,0:T(8,128)(2,1)}, u32[]{:S(2)}, u32[]{:S(2)}) collective-permute-start(bf16[256,512]{1,0:T(8,128)(2,1)S(1)} %shard_map.68.refs_1_.own_a), channel_id=1, source_target_pairs={{0,1},{1,0},{2,3},{3,2},{4,5},{5,4},{6,7},{7,6},{8,9},{9,8},{10,11... | collective-permute-start | bytes 786440 | tf_op jit(solution)/shard_map/ppermute | solution.py:41
  139.6 6.3 %collective-permute-done.23.refs_4_.far_b = bf16[256,512]{1,0:T(8,128)(2,1)S(1)} collective-permute-done((bf16[256,512]{1,0:T(8,128)(2,1)S(1)}, bf16[256,512]{1,0:T(8,128)(2,1)S(1)}, u32[]{:S(2)}, u32[]{:S(2)}) %collective-permute-start.23) | collective-permute-done | bytes 262176 | tf_op jit(solution)/shard_map/ppermute | solution.py:41
  148.1 5.2 %shard_map.71 = (bf16[256,1024]{1,0:T(8,128)(2,1)}, bf16[256,1024]{1,0:T(8,128)(2,1)}) custom-call(s32[4]{0:T(128)S(1)} %pad_add_fusion.5.at_ref, bf16[256,512]{1,0:T(8,128)(2,1)S(1)} %shard_map.68.refs_1_.own_a, bf16[256,512]{1,0:T(8,128)(2,1)S(1)} %shard_map.69.refs_2_.own_b, bf16[256,512]{1,0:T(8,128)(2,1)} %collective-permute-done.22.refs_3_.far_a, ...), custom_call_target="tpu_custom_call" | custom-call | tf_op jit(solution)/shard_map/pallas_call | solution.py:296
  158.3 7.6 %shard_map.70 = (bf16[256,1024]{1,0:T(8,128)(2,1)S(1)}, bf16[256,1024]{1,0:T(8,128)(2,1)S(1)}, bf16[256,1024]{1,0:T(8,128)(2,1)S(1)}, bf16[256,1024]{1,0:T(8,128...) custom-call(s32[12]{0:T(128)S(1)} %stack.101.refs_0_, ...), custom_call_target="tpu_custom_call" | custom-call | tf_op jit(solution)/shard_map/pallas_call | solution.py:296
  168.0 3.2 %collective-permute-start.30 = (bf16[256,1024]{1,0:T(8,128)(2,1)S(1)}, bf16[256,1024]{1,0:T(8,128)(2,1)S(1)}, u32[]{:S(2)}, u32[]{:S(2)}) collective-permute-start(bf16[256,1024]{1,0:T(8,128)(2,1)S(1)} %get-tuple-element.80), channel_id=1, source_target_pairs={{0,48},{1,49},{2,50},{3,51},{4,52},{5,53},{6,54},{7,55},{8,56},{9,... | collective-permute-start | bytes 1572872 | tf_op jit(solution)/shard_map/ppermute | solution.py:41
  172.6 2.8 %collective-permute-start.28 = (bf16[256,1024]{1,0:T(8,128)(2,1)S(1)}, bf16[256,1024]{1,0:T(8,128)(2,1)}, u32[]{:S(2)}, u32[]{:S(2)}) collective-permute-start(bf16[256,1024]{1,0:T(8,128)(2,1)S(1)} %get-tuple-element.79), channel_id=1, source_target_pairs={{0,48},{1,49},{2,50},{3,51},{4,52},{5,53},{6,54},{7,55},{8,56},{9,... | collective-permute-start | bytes 1572872 | tf_op jit(solution)/shard_map/ppermute | solution.py:41
  175.3 6.6 %collective-permute-done.30 = bf16[256,1024]{1,0:T(8,128)(2,1)S(1)} collective-permute-done((bf16[256,1024]{1,0:T(8,128)(2,1)S(1)}, bf16[256,1024]{1,0:T(8,128)(2,1)S(1)}, u32[]{:S(2)}, u32[]{:S(2)}) %collective-permute-start.30) | collective-permute-done | bytes 524320 | tf_op jit(solution)/shard_map/ppermute | solution.py:41
  182.0 3.8 %collective-permute-done.29 = bf16[256,1024]{1,0:T(8,128)(2,1)S(1)} collective-permute-done((bf16[256,1024]{1,0:T(8,128)(2,1)S(1)}, bf16[256,1024]{1,0:T(8,128)(2,1)S(1)}, u32[]{:S(2)}, u32[]{:S(2)}) %collective-permute-start.29) | collective-permute-done | bytes 524320 | tf_op jit(solution)/shard_map/ppermute | solution.py:41
  186.7 6.6 %collective-permute-done.28 = bf16[256,1024]{1,0:T(8,128)(2,1)} collective-permute-done((bf16[256,1024]{1,0:T(8,128)(2,1)S(1)}, bf16[256,1024]{1,0:T(8,128)(2,1)}, u32[]{:S(2)}, u32[]{:S(2)}) %collective-permute-start.28) | collective-permute-done | bytes 524320 | tf_op jit(solution)/shard_map/ppermute | solution.py:41
  193.3 3.7 %collective-permute-done.26 = bf16[256,1024]{1,0:T(8,128)(2,1)} collective-permute-done((bf16[256,1024]{1,0:T(8,128)(2,1)S(1)}, bf16[256,1024]{1,0:T(8,128)(2,1)}, u32[]{:S(2)}, u32[]{:S(2)}) %collective-permute-start.26) | collective-permute-done | bytes 524320 | tf_op jit(solution)/shard_map/ppermute | solution.py:41
  198.6 6.4 %collective-permute-start.33 = (bf16[256,512]{1,0:T(8,128)(2,1)S(1)}, bf16[256,512]{1,0:T(8,128)(2,1)S(1)}, u32[]{:S(2)}, u32[]{:S(2)}) collective-permute-start(bf16[256,512]{1,0:T(8,128)(2,1)S(1)} %get-tuple-element.76), channel_id=1, source_target_pairs={{0,8},{1,24},{2,10},{3,26},{4,12},{5,28},{6,14},{7,30},{8,0},{9,16... | collective-permute-start | bytes 786440 | tf_op jit(solution)/shard_map/ppermute | solution.py:41
  205.0 2.8 %collective-permute-start.32 = (bf16[256,512]{1,0:T(8,128)(2,1)S(1)}, bf16[256,512]{1,0:T(8,128)(2,1)S(1)}, u32[]{:S(2)}, u32[]{:S(2)}) collective-permute-start(bf16[256,512]{1,0:T(8,128)(2,1)S(1)} %get-tuple-element.75), channel_id=1, source_target_pairs={{0,0},{1,16},{2,2},{3,18},{4,4},{5,20},{6,6},{7,22},{8,8},{9,24},{... | collective-permute-start | bytes 786440 | tf_op jit(solution)/shard_map/ppermute | solution.py:41
  207.8 3.8 %collective-permute-done.33 = bf16[256,512]{1,0:T(8,128)(2,1)S(1)} collective-permute-done((bf16[256,512]{1,0:T(8,128)(2,1)S(1)}, bf16[256,512]{1,0:T(8,128)(2,1)S(1)}, u32[]{:S(2)}, u32[]{:S(2)}) %collective-permute-start.33) | collective-permute-done | bytes 262176 | tf_op jit(solution)/shard_map/ppermute | solution.py:41
  211.6 5.9 %collective-permute-done.32 = bf16[256,512]{1,0:T(8,128)(2,1)S(1)} collective-permute-done((bf16[256,512]{1,0:T(8,128)(2,1)S(1)}, bf16[256,512]{1,0:T(8,128)(2,1)S(1)}, u32[]{:S(2)}, u32[]{:S(2)}) %collective-permute-start.32) | collective-permute-done | bytes 262176 | tf_op jit(solution)/shard_map/ppermute | solution.py:41
  (170 shorter events, 84.9 us)
Async XLA Ops:
  6.5 118.5 %all-gather.3.cloned.1.call-start = ((), (), s32[]{:S(2)}) async-start(), calls=%async_computation | async-start | bytes 5242880 | tf_op jit(solution)/shard_map/all_gather | solution.py:390
  20.0 19.2 %collective-permute-start.3 = (bf16[256,1024]{1,0:T(8,128)(2,1)S(1)}, bf16[256,1024]{1,0:T(8,128)(2,1)S(1)}, u32[]{:S(2)}, u32[]{:S(2)}) collective-permute-start(bf16[256,1024]{1,0:T(8,128)(2,1)S(1)} %maximum_select_fusion), channel_id=1, source_target_pairs={{0,16},{1,17},{2,18},{3,19},{4,20},{5,21},{6,22},{7,23},{8,24},{9,... | collective-permute-start | bytes 1572872 | tf_op jit(solution)/shard_map/ppermute | solution.py:41
  28.3 12.9 %collective-permute-start.4 = (bf16[256,1024]{1,0:T(8,128)(2,1)S(1)}, bf16[256,1024]{1,0:T(8,128)(2,1)S(1)}, u32[]{:S(2)}, u32[]{:S(2)}) collective-permute-start(bf16[256,1024]{1,0:T(8,128)(2,1)S(1)} %maximum_select_fusion), channel_id=1, source_target_pairs={{0,48},{1,49},{2,50},{3,51},{4,52},{5,53},{6,54},{7,55},{8,56},{9,... | collective-permute-start | bytes 1572872 | tf_op jit(solution)/shard_map/ppermute | solution.py:41
  28.3 15.5 %collective-permute-start.5 = (bf16[256,1024]{1,0:T(8,128)(2,1)S(1)}, bf16[256,1024]{1,0:T(8,128)(2,1)}, u32[]{:S(2)}, u32[]{:S(2)}) collective-permute-start(bf16[256,1024]{1,0:T(8,128)(2,1)S(1)} %maximum_select_fusion), channel_id=1, source_target_pairs={{0,64},{1,65},{2,66},{3,67},{4,68},{5,69},{6,70},{7,71},{8,72},{9,... | collective-permute-start | bytes 1572872 | tf_op jit(solution)/shard_map/ppermute | solution.py:41
  43.8 31.4 %collective-permute-start.12 = (bf16[1024,640]{1,0:T(8,128)(2,1)}, bf16[1024,640]{1,0:T(8,128)(2,1)S(1)}, u32[]{:S(2)}, u32[]{:S(2)}) collective-permute-start(bf16[1024,640]{1,0:T(8,128)(2,1)} %pad_maximum_fusion), channel_id=1, source_target_pairs={{0,1},{1,0},{2,3},{3,2},{4,5},{5,4},{6,7},{7,6},{8,9},{9,8},{10,11... | collective-permute-start | bytes 3932168 | tf_op jit(solution)/shard_map/ppermute | solution.py:41
  47.1 12.5 %collective-permute-start.8 = (bf16[256,1024]{1,0:T(8,128)(2,1)}, bf16[256,1024]{1,0:T(8,128)(2,1)}, u32[]{:S(2)}, u32[]{:S(2)}) collective-permute-start(bf16[256,1024]{1,0:T(8,128)(2,1)} %collective-permute-done.5), channel_id=1, source_target_pairs={{0,16},{1,17},{2,18},{3,19},{4,20},{5,21},{6,22},{7,23},{8,24},{9,... | collective-permute-start | bytes 1572872 | tf_op jit(solution)/shard_map/ppermute | solution.py:41
  48.3 15.7 %collective-permute-start.9 = (bf16[256,1024]{1,0:T(8,128)(2,1)}, bf16[256,1024]{1,0:T(8,128)(2,1)}, u32[]{:S(2)}, u32[]{:S(2)}) collective-permute-start(bf16[256,1024]{1,0:T(8,128)(2,1)} %collective-permute-done.5), channel_id=1, source_target_pairs={{0,48},{1,49},{2,50},{3,51},{4,52},{5,53},{6,54},{7,55},{8,56},{9,... | collective-permute-start | bytes 1572872 | tf_op jit(solution)/shard_map/ppermute | solution.py:41
  61.8 16.4 %collective-permute-start.7 = (bf16[128,1024]{1,0:T(8,128)(2,1)S(1)}, bf16[128,1024]{1,0:T(8,128)(2,1)S(1)}, u32[]{:S(2)}, u32[]{:S(2)}) collective-permute-start(bf16[128,1024]{1,0:T(8,128)(2,1)S(1)} %slice.43), channel_id=1, source_target_pairs={{0,48},{1,49},{2,50},{3,51},{4,52},{5,53},{6,54},{7,55},{8,56},{9,... | collective-permute-start | bytes 786440 | tf_op jit(solution)/shard_map/ppermute | solution.py:41
  63.9 14.3 %collective-permute-start.6 = (bf16[128,1024]{1,0:T(8,128)(2,1)S(1)}, bf16[128,1024]{1,0:T(8,128)(2,1)S(1)}, u32[]{:S(2)}, u32[]{:S(2)}) collective-permute-start(bf16[128,1024]{1,0:T(8,128)(2,1)S(1)} %slice.42), channel_id=1, source_target_pairs={{0,16},{1,17},{2,18},{3,19},{4,20},{5,21},{6,22},{7,23},{8,24},{9,... | collective-permute-start | bytes 786440 | tf_op jit(solution)/shard_map/ppermute | solution.py:41
  83.8 13.7 %collective-permute-start.14 = (bf16[128,1280]{1,0:T(8,128)(2,1)}, bf16[128,1280]{1,0:T(8,128)(2,1)}, u32[]{:S(2)}, u32[]{:S(2)}) collective-permute-start(bf16[128,1280]{1,0:T(8,128)(2,1)} %get-tuple-element.50), channel_id=1, source_target_pairs={{0,2},{1,3},{2,4},{3,5},{4,6},{5,7},{6,0},{7,1},{8,10},{9,11},{10,... | collective-permute-start | bytes 983048 | tf_op jit(solution)/shard_map/ppermute | solution.py:41
  83.8 13.6 %collective-permute-start.15 = (bf16[128,1280]{1,0:T(8,128)(2,1)}, bf16[128,1280]{1,0:T(8,128)(2,1)}, u32[]{:S(2)}, u32[]{:S(2)}) collective-permute-start(bf16[128,1280]{1,0:T(8,128)(2,1)} %get-tuple-element.51), channel_id=1, source_target_pairs={{0,6},{1,7},{2,0},{3,1},{4,2},{5,3},{6,4},{7,5},{8,14},{9,15},{10,... | collective-permute-start | bytes 983048 | tf_op jit(solution)/shard_map/ppermute | solution.py:41
  101.4 18.0 %collective-permute-start.16 = (bf16[256,1280]{1,0:T(8,128)(2,1)}, bf16[256,1280]{1,0:T(8,128)(2,1)S(1)}, u32[]{:S(2)}, u32[]{:S(2)}) collective-permute-start(bf16[256,1280]{1,0:T(8,128)(2,1)} %add_dynamic-update-slice_fusion.1), channel_id=1, source_target_pairs={{0,2},{1,3},{2,4},{3,5},{4,6},{5,7},{6,0},{7,1},{8,10},{9,11},{10,... | collective-permute-start | bytes 1966088 | tf_op jit(solution)/shard_map/ppermute | solution.py:41
  101.4 18.0 %collective-permute-start.17 = (bf16[256,1280]{1,0:T(8,128)(2,1)}, bf16[256,1280]{1,0:T(8,128)(2,1)}, u32[]{:S(2)}, u32[]{:S(2)}) collective-permute-start(bf16[256,1280]{1,0:T(8,128)(2,1)} %add_dynamic-update-slice_fusion), channel_id=1, source_target_pairs={{0,6},{1,7},{2,0},{3,1},{4,2},{5,3},{6,4},{7,5},{8,14},{9,15},{10,... | collective-permute-start | bytes 1966088 | tf_op jit(solution)/shard_map/ppermute | solution.py:41
  105.5 12.7 %collective-permute-start.19 = (f32[256]{0:T(256)S(1)}, f32[256]{0:T(256)S(1)}, u32[]{:S(2)}, u32[]{:S(2)}) collective-permute-start(f32[256]{0:T(256)S(1)} %bitcast.50), channel_id=1, source_target_pairs={{0,4},{1,5},{2,6},{3,7},{4,0},{5,1},{6,2},{7,3},{8,12},{9,13},{10,... | collective-permute-start | bytes 3080 | tf_op jit(solution)/shard_map/ppermute | solution.py:41
  105.9 12.7 %collective-permute-start.18 = (f32[256]{0:T(256)S(1)}, f32[256]{0:T(256)S(1)}, u32[]{:S(2)}, u32[]{:S(2)}) collective-permute-start(f32[256]{0:T(256)S(1)} %bitcast.49), channel_id=1, source_target_pairs={{0,2},{1,3},{2,4},{3,5},{4,6},{5,7},{6,0},{7,1},{8,10},{9,11},{10,... | collective-permute-start | bytes 3080 | tf_op jit(solution)/shard_map/ppermute | solution.py:41
  125.0 20.8 %collective-permute-start.24 = (bf16[4,512,1024]{2,1,0:T(8,128)(2,1)}, bf16[4,512,1024]{2,1,0:T(8,128)(2,1)}, u32[]{:S(2)}, u32[]{:S(2)}) collective-permute-start(bf16[4,512,1024]{2,1,0:T(8,128)(2,1)} %bitcast.44), channel_id=1, source_target_pairs={{0,8},{1,9},{2,10},{3,11},{4,12},{5,13},{6,14},{7,15},{8,0},{9,1},... | collective-permute-start | bytes 12582920 | tf_op jit(solution)/shard_map/ppermute | solution.py:41
  153.4 13.4 %collective-permute-start.27 = (bf16[256,1024]{1,0:T(8,128)(2,1)}, bf16[256,1024]{1,0:T(8,128)(2,1)}, u32[]{:S(2)}, u32[]{:S(2)}) collective-permute-start(bf16[256,1024]{1,0:T(8,128)(2,1)} %get-tuple-element.71), channel_id=1, source_target_pairs={{0,48},{1,49},{2,50},{3,51},{4,52},{5,53},{6,54},{7,55},{8,56},{9,... | collective-permute-start | bytes 1572872 | tf_op jit(solution)/shard_map/ppermute | solution.py:41
  155.0 16.2 %collective-permute-start.25 = (bf16[256,1024]{1,0:T(8,128)(2,1)}, bf16[256,1024]{1,0:T(8,128)(2,1)}, u32[]{:S(2)}, u32[]{:S(2)}) collective-permute-start(bf16[256,1024]{1,0:T(8,128)(2,1)} %get-tuple-element.69), channel_id=1, source_target_pairs={{0,16},{1,17},{2,18},{3,19},{4,20},{5,21},{6,22},{7,23},{8,24},{9,... | collective-permute-start | bytes 1572872 | tf_op jit(solution)/shard_map/ppermute | solution.py:41
  168.0 13.9 %collective-permute-start.30 = (bf16[256,1024]{1,0:T(8,128)(2,1)S(1)}, bf16[256,1024]{1,0:T(8,128)(2,1)S(1)}, u32[]{:S(2)}, u32[]{:S(2)}) collective-permute-start(bf16[256,1024]{1,0:T(8,128)(2,1)S(1)} %get-tuple-element.80), channel_id=1, source_target_pairs={{0,48},{1,49},{2,50},{3,51},{4,52},{5,53},{6,54},{7,55},{8,56},{9,... | collective-permute-start | bytes 1572872 | tf_op jit(solution)/shard_map/ppermute | solution.py:41
  172.5 13.3 %collective-permute-start.29 = (bf16[256,1024]{1,0:T(8,128)(2,1)S(1)}, bf16[256,1024]{1,0:T(8,128)(2,1)S(1)}, u32[]{:S(2)}, u32[]{:S(2)}) collective-permute-start(bf16[256,1024]{1,0:T(8,128)(2,1)S(1)} %get-tuple-element.78), channel_id=1, source_target_pairs={{0,16},{1,17},{2,18},{3,19},{4,20},{5,21},{6,22},{7,23},{8,24},{9,... | collective-permute-start | bytes 1572872 | tf_op jit(solution)/shard_map/ppermute | solution.py:41
  172.6 20.7 %collective-permute-start.28 = (bf16[256,1024]{1,0:T(8,128)(2,1)S(1)}, bf16[256,1024]{1,0:T(8,128)(2,1)}, u32[]{:S(2)}, u32[]{:S(2)}) collective-permute-start(bf16[256,1024]{1,0:T(8,128)(2,1)S(1)} %get-tuple-element.79), channel_id=1, source_target_pairs={{0,48},{1,49},{2,50},{3,51},{4,52},{5,53},{6,54},{7,55},{8,56},{9,... | collective-permute-start | bytes 1572872 | tf_op jit(solution)/shard_map/ppermute | solution.py:41
  175.3 21.7 %collective-permute-start.26 = (bf16[256,1024]{1,0:T(8,128)(2,1)S(1)}, bf16[256,1024]{1,0:T(8,128)(2,1)}, u32[]{:S(2)}, u32[]{:S(2)}) collective-permute-start(bf16[256,1024]{1,0:T(8,128)(2,1)S(1)} %get-tuple-element.77), channel_id=1, source_target_pairs={{0,16},{1,17},{2,18},{3,19},{4,20},{5,21},{6,22},{7,23},{8,24},{9,... | collective-permute-start | bytes 1572872 | tf_op jit(solution)/shard_map/ppermute | solution.py:41
  198.6 13.0 %collective-permute-start.33 = (bf16[256,512]{1,0:T(8,128)(2,1)S(1)}, bf16[256,512]{1,0:T(8,128)(2,1)S(1)}, u32[]{:S(2)}, u32[]{:S(2)}) collective-permute-start(bf16[256,512]{1,0:T(8,128)(2,1)S(1)} %get-tuple-element.76), channel_id=1, source_target_pairs={{0,8},{1,24},{2,10},{3,26},{4,12},{5,28},{6,14},{7,30},{8,0},{9,16... | collective-permute-start | bytes 786440 | tf_op jit(solution)/shard_map/ppermute | solution.py:41
  205.0 12.5 %collective-permute-start.32 = (bf16[256,512]{1,0:T(8,128)(2,1)S(1)}, bf16[256,512]{1,0:T(8,128)(2,1)S(1)}, u32[]{:S(2)}, u32[]{:S(2)}) collective-permute-start(bf16[256,512]{1,0:T(8,128)(2,1)S(1)} %get-tuple-element.75), channel_id=1, source_target_pairs={{0,0},{1,16},{2,2},{3,18},{4,4},{5,20},{6,6},{7,22},{8,8},{9,24},{... | collective-permute-start | bytes 786440 | tf_op jit(solution)/shard_map/ppermute | solution.py:41
  (44 other events, 405.8 us)
Sparse Core Ops, SparseCore 0:
  20.1 58.1 all-gather.2

commit v10 on v8

--- a/solution.py
+++ b/solution.py
@@ -103,30 +103,44 @@
 
 
 def total_of(refs, cols=slice(None)):
-    total = refs[0][:, cols].astype(jnp.float32)
-    for ref in refs[1:]:
-        total += ref[:, cols].astype(jnp.float32)
-    return total
-
-
-def key_value_kernel(core_ref, k0, k1, k2, v0, v1, v2, scale_ref, cos_ref, sin_ref, out_ref):
+    whole, *halves = (ref[:, cols].astype(jnp.float32) for ref in refs)
+    a_top, a_bottom, b_top, b_bottom = halves
+    return whole + jnp.concatenate([a_top + b_top, a_bottom + b_bottom], axis=0)
+
+
+def total_kernel(*refs):
+    refs[-1][...] = total_of(refs[:-1]).astype(jnp.bfloat16)
+
+
+def summed_up(*values):
+    return pl.pallas_call(
+        total_kernel, out_shape=jax.ShapeDtypeStruct(values[0].shape, jnp.bfloat16)
+    )(*values)
+
+
+def key_value_kernel(core_ref, *refs):
+    scale_ref, cos_ref, sin_ref, out_ref = refs[10:]
     scale = scale_ref[...]
-    keys = rotated(total_of((k0, k1, k2)) * scale, cos_ref[...], sin_ref[...])
+    keys = rotated(total_of(refs[:5]) * scale, cos_ref[...], sin_ref[...])
     out_ref[:, :HEAD_SIZE] = keys.astype(jnp.bfloat16)
-    out_ref[:, HEAD_SIZE:] = (total_of((v0, v1, v2)) * scale).astype(jnp.bfloat16)
+    out_ref[:, HEAD_SIZE:] = (total_of(refs[5:10]) * scale).astype(jnp.bfloat16)
 
 
 def key_value_rows(core, sums, scale, cosine, sine):
-    keys = pl.BlockSpec((HALF, HEAD_SIZE), lambda i, c: (0, 4 + 5 * c[0]))
-    values = pl.BlockSpec((HALF, HEAD_SIZE), lambda i, c: (0, 9 - 5 * c[0]))
+    keys = [
+        pl.BlockSpec((v.shape[0], HEAD_SIZE), lambda i, c: (0, 4 + 5 * c[0])) for v in sums
+    ]
+    values = [
+        pl.BlockSpec((v.shape[0], HEAD_SIZE), lambda i, c: (0, 9 - 5 * c[0])) for v in sums
+    ]
     table = pl.BlockSpec((HALF, HEAD_SIZE), lambda i, c: (0, 0))
     return pl.pallas_call(
         key_value_kernel,
         grid_spec=pltpu.PrefetchScalarGridSpec(
             num_scalar_prefetch=1,
             grid=(1,),
-            in_specs=[keys] * 3
-            + [values] * 3
+            in_specs=keys
+            + values
             + [pl.BlockSpec((HALF, 1), lambda i, c: (0, 0)), table, table],
             out_specs=pl.BlockSpec((HALF, 2 * HEAD_SIZE), lambda i, c: (0, 0)),
         ),
@@ -134,13 +148,12 @@
     )(core.reshape(1), *sums, *sums, scale, cosine, sine)
 
 
-def attention_kernel(
-    s0, s1, s2, scale_ref, cos_ref, sin_ref, bias_ref, own_ref, other_ref, out_ref
-):
+def attention_kernel(*refs):
+    scale_ref, cos_ref, sin_ref, bias_ref, own_ref, other_ref, out_ref = refs[5:]
     contract = (((1,), (1,)), ((), ()))
     for head in range(4):
         cols = slice(head * HEAD_SIZE, (head + 1) * HEAD_SIZE)
-        rows = total_of((s0, s1, s2), cols) * scale_ref[...]
+        rows = total_of(refs[:5], cols) * scale_ref[...]
         queries = rotated(rows, cos_ref[...], sin_ref[...]).astype(jnp.bfloat16)
 
         def scores_of(ref, first):
@@ -168,7 +181,7 @@
     return pl.pallas_call(
         attention_kernel,
         grid=(1,),
-        in_specs=[pl.BlockSpec((HALF, WIDE), lambda i: (0, part))] * 3
+        in_specs=[pl.BlockSpec((v.shape[0], WIDE), lambda i: (0, part)) for v in sums]
         + [
             fixed((HALF, 1)),
             fixed((HALF, HEAD_SIZE)),
@@ -192,17 +205,15 @@
     def put(start, near_part, far_part):
         cols = slice(start, start + near_part.shape[1])
         value = (dot(near_rows, near_part) + dot(far_rows, far_part)).astype(jnp.bfloat16)
-        if outs[0].shape[0] == 128:
-            outs[0][:, cols] = value[:128]
-            outs[1][:, cols] = value[128:]
-        elif len(outs) == 1:
+        if len(outs) == 1:
             outs[0][:, cols] = value
-        else:
-            for i, out in enumerate(outs):
-
-                @pl.when(step == i)
-                def _():
-                    out[:, cols] = value
+            return
+        for i in range(len(outs) // 2):
+
+            @pl.when(step == i)
+            def _():
+                outs[2 * i][:, cols] = value[:128]
+                outs[2 * i + 1][:, cols] = value[128:]
 
     def kv_cols(which):
         return near_kv[:, pl.ds(pl.multiple_of(which * HEAD_SIZE, HEAD_SIZE), HEAD_SIZE)]
@@ -215,7 +226,7 @@
 
 def project(which, zh, core, gathered, weights, halves=False):
     steps = len(which)
-    rows, outs = (128, 2) if halves else (HALF, steps)
+    rows, outs = (128, 2 * steps) if halves else (HALF, 1)
     return pl.pallas_call(
         project_kernel,
         grid_spec=pltpu.PrefetchScalarGridSpec(
@@ -230,7 +241,7 @@
     )(jnp.stack([zh, core, *which]).astype(jnp.int32), gathered, *weights)
 
 
-def products_kernel(split, steps, at_ref, own_a, own_b, far_a, far_b, near, other, *outs):
+def products_kernel(form, steps, at_ref, own_a, own_b, far_a, far_b, near, other, *outs):
     step = pl.program_id(0)
 
     def put(left, right):
@@ -240,9 +251,12 @@
 
             @pl.when(step == i)
             def _():
-                if split:
+                if form == "joined":
                     outs[0][i * 128 : i * 128 + 128] = product[:128]
                     outs[1][i * 128 : i * 128 + 128] = product[128:]
+                elif form == "halves":
+                    outs[2 * i][...] = product[:128]
+                    outs[2 * i + 1][...] = product[128:]
                 else:
                     outs[i][...] = product
 
@@ -255,23 +269,24 @@
         put(far_a, far_b)
 
 
-def products(targets, zh, attended, near, other, split=False):
+def products(targets, zh, attended, near, other, form="whole"):
     steps = len(targets)
     blocks = [zt * 2 + xt // 2 for zt, xt in targets]
     owns = [xt % 2 == zh for _, xt in targets]
     at = jnp.stack([v.astype(jnp.int32) for v in blocks + owns])
     rows = pl.BlockSpec((HALF, 512), lambda i, at: (0, 0))
     block = pl.BlockSpec((1, 512, 1024), lambda i, at: (at[i], 0, 0))
-    count = 2 if split else steps
+    count = {"joined": 2, "halves": 2 * steps, "whole": steps}[form]
+    size = 128 if form == "halves" else HALF
     return pl.pallas_call(
-        lambda *refs: products_kernel(split, steps, *refs),
+        lambda *refs: products_kernel(form, steps, *refs),
         grid_spec=pltpu.PrefetchScalarGridSpec(
             num_scalar_prefetch=1,
             grid=(steps,),
             in_specs=[rows] * 4 + [block] * 2,
-            out_specs=[pl.BlockSpec((HALF, 1024), lambda i, at: (0, 0))] * count,
+            out_specs=[pl.BlockSpec((size, 1024), lambda i, at: (0, 0))] * count,
         ),
-        out_shape=[jax.ShapeDtypeStruct((HALF, 1024), jnp.bfloat16)] * count,
+        out_shape=[jax.ShapeDtypeStruct((size, 1024), jnp.bfloat16)] * count,
         compiler_params=GRANT,
     )(at, *attended, near, other)
 
@@ -331,16 +346,15 @@
     beside = zl_swap(block)
     left = x_shift(block, 1)
     right = x_shift(block, -1)
-    far = zh_swap(near)
-    left, right = lax.optimization_barrier((left, right))
+    left, right, beside = lax.optimization_barrier((left, right, beside))
+    far = zh_swap(after(near, beside))
     beside_left = x_shift(beside, 1)
     beside_right = x_shift(beside, -1)
     opposite = jnp.concatenate([x_shift(left[:128], 1), x_shift(right[128:], -1)], 0)
     beside_opposite = jnp.concatenate(
         [x_shift(beside_left[:128], 1), x_shift(beside_right[128:], -1)], 0
     )
-    far = after(far, (opposite, beside_left, beside_right))
-    weights = (query_weight, near_other, kv_near, far, core_swap(far))
+    weights = (query_weight, near_other, kv_near, far, core_swap(after(far, beside_opposite)))
     gathered = jnp.zeros((4, HALF, 2048), jnp.bfloat16)
     for dz, dx, part in (
         (0, 0, block),
@@ -359,21 +373,24 @@
 
     out_near = lax.all_gather(after(out_weight, block), "y", axis=0, tiled=False)
 
+    squares = jnp.sum(jnp.square(gathered.astype(jnp.float32) * slice_gain), axis=-1)
+    gathered, squares = lax.optimization_barrier((gathered, squares))
     low, high = project([(y + 2) % 4], zh, core, gathered, weights, True)
     from_below = y_shift(low, 1)
     from_above = y_shift(high, -1)
-    upper, lower = project([(y + 1) % 4, (y + 3) % 4], zh, core, gathered, weights)
-    from_below, from_above, upper, lower = lax.optimization_barrier(
-        (from_below, from_above, upper, lower)
-    )
-    upper = add_rows(upper, from_below, 0)
-    lower = add_rows(lower, from_above, 128)
-    gathered, upper, lower = lax.optimization_barrier((gathered, upper, lower))
+    a_top, a_bottom, b_top, b_bottom = project(
+        [(y + 1) % 4, (y + 3) % 4], zh, core, gathered, weights, True
+    )
+    from_below, from_above, a_top, b_bottom = lax.optimization_barrier(
+        (from_below, from_above, a_top, b_bottom)
+    )
+    a_bottom, b_top = y_shift(a_bottom, 1), y_shift(b_top, -1)
+    a_top, b_bottom = a_top + from_below, b_bottom + from_above
+    gathered = after(gathered, (a_top, b_bottom, a_bottom, b_top))
     (kept,) = project([y], zh, core, gathered, weights)
-    sums = (kept, y_shift(upper, 1), y_shift(lower, -1))
-
-    plain = gathered.astype(jnp.float32) * slice_gain
-    squares = jnp.sum(plain * plain, axis=-1)
+    sums = (kept, y_shift(a_top, 1), a_bottom, b_top, y_shift(b_bottom, -1))
+
+    squares, a_top, b_bottom = lax.optimization_barrier((squares, a_top, b_bottom))
     total = lax.dynamic_index_in_dim(squares, y, 0, keepdims=False)
     for k in (1, 2, 3):
         total += y_shift(lax.dynamic_index_in_dim(squares, (y + k) % 4, 0, keepdims=False), k)
@@ -388,24 +405,27 @@
     far_b = zh_swap(own_b)
     attended = (own_a, own_b, far_a, far_b)
 
-    def made(moves, split=False):
+    def made(moves, form="whole"):
         targets = [(zl ^ dz, (x + dx) % 4) for dz, dx in moves]
-        return products(targets, zh, attended, out_near, out_other, split)
-
-    low, high = made([(1, 2), (0, 2)], True)
+        return products(targets, zh, attended, out_near, out_other, form)
+
+    low, high = made([(1, 2), (0, 2)], "joined")
     from_left, from_right = x_shift(low, 1), x_shift(high, -1)
-    beside_a, beside_b, here_a, here_b, beside, mixed = made(
-        [(1, 1), (1, 3), (0, 1), (0, 3), (1, 0), (0, 0)]
-    )
-    beside_a = x_shift(add_rows(beside_a, from_left[:128], 0), 1)
-    beside_b = x_shift(add_rows(beside_b, from_right[:128], 128), -1)
+    a_top, a_bottom, b_top, b_bottom = made([(1, 1), (1, 3)], "halves")
+    here_a, here_b, beside, mixed = made([(0, 1), (0, 3), (1, 0), (0, 0)])
+    from_left, from_right, here_a, here_b = lax.optimization_barrier(
+        (from_left, from_right, here_a, here_b)
+    )
+    a_bottom, b_top = x_shift(a_bottom, 1), x_shift(b_top, -1)
+    a_top = x_shift(a_top + from_left[:128], 1)
+    b_bottom = x_shift(b_bottom + from_right[:128], -1)
     here_a = x_shift(add_rows(here_a, from_left[128:], 0), 1)
     here_b = x_shift(add_rows(here_b, from_right[128:], 128), -1)
 
     def sum_of(*values):
         return sum(v.astype(jnp.float32) for v in values).astype(jnp.bfloat16)
 
-    across = zl_swap(sum_of(beside, beside_a, beside_b))
+    across = zl_swap(summed_up(beside, a_top, a_bottom, b_top, b_bottom))
     mixed = sum_of(mixed, here_a, here_b, across)
     keep = send(half_of(mixed, core, 1), to_home(0))
     got = send(half_of(mixed, 1 - core, 1), to_home(1))

time: 251 us -> 223 us (0.89)
  waiting for transfers between devices: 103 us -> 58.4 us
  starting transfers between devices: 55.6 us -> 65.4 us
  local copies, waits for them, and re-layouts: 26 us -> 30.6 us
  Pallas kernels: 31.3 us -> 34.8 us
    ppermute x34 -> x38, waiting for transfers between devices: 103 us -> 58.4 us  [send(): return lax.ppermute(value, AXES, pairs(change))]
    ppermute x34 -> x38, starting transfers between devices: 55.6 us -> 65.4 us  [send(): return lax.ppermute(value, AXES, pairs(change))]
    unnamed x57 -> x71, local copies, waits for them, and re-layouts: 15.4 us -> 19.9 us
    dynamic_update_slice x4 -> x2, other arithmetic: 6.42 us -> 2.63 us  [add_rows(): lax.dynamic_update_slice(value, value[start:start + rows] + arrived, (sta...]
    pallas_call x4 -> x6, Pallas kernels: 17.4 us -> 21.2 us  [the longest x3 13.1 us: products(): pl.pallas_call(lambda *refs: products_kernel(form, steps, *refs), grid_sp...]
    add x0 -> x2, other arithmetic: none -> 3.75 us  [local(): a_top, b_bottom = (a_top + from_below, b_bottom + from_above)]
  transfers between devices with their start and end apart: 35 -> 39, of which waited for: 17 -> 17; matrix products, arithmetic and copies ran while one was open for 10% -> 11% of each run, Pallas kernels for 11% -> 14%
where the time goes in v10:
time: 223 us; the launch traced here: 221 us
  starting transfers between devices  65.4 us (29%)
  waiting for transfers between devices  58.4 us (26%)
  Pallas kernels  34.8 us (16%)
  local copies, waits for them, and re-layouts  30.6 us (14%)
  other arithmetic  17.3 us (8%)
  between operations  14.7 us (7%)
    ppermute x38, starting transfers between devices, send(): return lax.ppermute(value, AXES, pairs(change))  65.4 us
    ppermute x38, waiting for transfers between devices, send(): return lax.ppermute(value, AXES, pairs(change))  58.4 us
    unnamed x71, local copies, waits for them, and re-layouts  19.9 us
    pallas_call x3, Pallas kernels, products(): pl.pallas_call(lambda *refs: products_kernel(form, steps, *refs), grid_sp...  13.1 us
    pallas_call x3, Pallas kernels, project(): pl.pallas_call(project_kernel, grid_spec=pltpu.PrefetchScalarGridSpec(num...  11.5 us
    pallas_call x2, Pallas kernels, attention(): pl.pallas_call(attention_kernel, grid=(1,), in_specs=[pl.BlockSpec((v.sha...  5.76 us
  transfers between devices with their start and end apart: 39, of which 17 were waited for; matrix products, arithmetic and copies ran while one was open for 11% of the time, Pallas kernels for 14%

profile of v10, /device:TPU:3, one launch (start us, length us, event | category | flops | bytes accessed | tf_op | source)
XLA Modules:
  0.0 221.2 jit_solution(8611446063953805063)
XLA Ops:
  19.9 8.4 %collective-permute-start.3 = (bf16[256,1024]{1,0:T(8,128)(2,1)S(1)}, bf16[256,1024]{1,0:T(8,128)(2,1)S(1)}, u32[]{:S(2)}, u32[]{:S(2)}) collective-permute-start(bf16[256,1024]{1,0:T(8,128)(2,1)S(1)} %maximum_select_fusion), channel_id=1, source_target_pairs={{0,16},{1,17},{2,18},{3,19},{4,20},{5,21},{6,22},{7,23},{8,24},{9,... | collective-permute-start | bytes 1572872 | tf_op jit(solution)/shard_map/ppermute | solution.py:41
  28.3 3.7 %collective-permute-start.5 = (bf16[256,1024]{1,0:T(8,128)(2,1)S(1)}, bf16[256,1024]{1,0:T(8,128)(2,1)}, u32[]{:S(2)}, u32[]{:S(2)}) collective-permute-start(bf16[256,1024]{1,0:T(8,128)(2,1)S(1)} %maximum_select_fusion), channel_id=1, source_target_pairs={{0,64},{1,65},{2,66},{3,67},{4,68},{5,69},{6,70},{7,71},{8,72},{9,... | collective-permute-start | bytes 1572872 | tf_op jit(solution)/shard_map/ppermute | solution.py:41
  32.1 7.1 %collective-permute-done.3 = bf16[256,1024]{1,0:T(8,128)(2,1)S(1)} collective-permute-done((bf16[256,1024]{1,0:T(8,128)(2,1)S(1)}, bf16[256,1024]{1,0:T(8,128)(2,1)S(1)}, u32[]{:S(2)}, u32[]{:S(2)}) %collective-permute-start.3) | collective-permute-done | bytes 524320 | tf_op jit(solution)/shard_map/ppermute | solution.py:41
  43.8 3.3 %collective-permute-start.12 = (bf16[1024,640]{1,0:T(8,128)(2,1)}, bf16[1024,640]{1,0:T(8,128)(2,1)S(1)}, u32[]{:S(2)}, u32[]{:S(2)}) collective-permute-start(bf16[1024,640]{1,0:T(8,128)(2,1)} %pad_maximum_fusion), channel_id=1, source_target_pairs={{0,1},{1,0},{2,3},{3,2},{4,5},{5,4},{6,7},{7,6},{8,9},{9,8},{10,11... | collective-permute-start | bytes 3932168 | tf_op jit(solution)/shard_map/ppermute | solution.py:41
  50.2 2.8 %collective-permute-start.7 = (bf16[128,1024]{1,0:T(8,128)(2,1)S(1)}, bf16[128,1024]{1,0:T(8,128)(2,1)S(1)}, u32[]{:S(2)}, u32[]{:S(2)}) collective-permute-start(bf16[128,1024]{1,0:T(8,128)(2,1)S(1)} %slice.31), channel_id=1, source_target_pairs={{0,48},{1,49},{2,50},{3,51},{4,52},{5,53},{6,54},{7,55},{8,56},{9,... | collective-permute-start | bytes 786440 | tf_op jit(solution)/shard_map/ppermute | solution.py:41
  53.1 6.6 %collective-permute-done.8 = bf16[256,1024]{1,0:T(8,128)(2,1)} collective-permute-done((bf16[256,1024]{1,0:T(8,128)(2,1)}, bf16[256,1024]{1,0:T(8,128)(2,1)}, u32[]{:S(2)}, u32[]{:S(2)}) %collective-permute-start.8) | collective-permute-done | bytes 524320 | tf_op jit(solution)/shard_map/ppermute | solution.py:41
  64.4 6.2 %collective-permute-done.10 = bf16[128,1024]{1,0:T(8,128)(2,1)S(1)} collective-permute-done((bf16[128,1024]{1,0:T(8,128)(2,1)S(1)}, bf16[128,1024]{1,0:T(8,128)(2,1)S(1)}, u32[]{:S(2)}, u32[]{:S(2)}) %collective-permute-start.10) | collective-permute-done | bytes 262176 | tf_op jit(solution)/shard_map/ppermute | solution.py:41
  71.0 4.2 %collective-permute-done.12.far = bf16[1024,640]{1,0:T(8,128)(2,1)S(1)} collective-permute-done((bf16[1024,640]{1,0:T(8,128)(2,1)}, bf16[1024,640]{1,0:T(8,128)(2,1)S(1)}, u32[]{:S(2)}, u32[]{:S(2)}) %collective-permute-start.12) | collective-permute-done | bytes 1310752 | tf_op jit(solution)/shard_map/ppermute | solution.py:41
  81.8 3.1 %shard_map.64 = (bf16[128,1280]{1,0:T(8,128)(2,1)}, bf16[128,1280]{1,0:T(8,128)(2,1)}) custom-call(s32[3]{0:T(128)S(1)} %pad_add_fusion.3.at_ref, bf16[4,256,2048]{2,1,0:T(8,128)(2,1)S(1)} %bitcast_dynamic-update-slice_fusion.rows_ref, bf16[1024,512]{1,0:T(8,128)(2,1)S(1)} %copy-done.5, bf16[1024,512]{1,0:T(8,128)(2,1)S(1)} %collective-permute-done.2.near_other, ...), custom_call_target="tpu_custom_call" | custom-call | tf_op jit(solution)/shard_map/pallas_call | solution.py:230
  84.9 2.9 %collective-permute-start.15 = (bf16[128,1280]{1,0:T(8,128)(2,1)}, bf16[128,1280]{1,0:T(8,128)(2,1)}, u32[]{:S(2)}, u32[]{:S(2)}) collective-permute-start(bf16[128,1280]{1,0:T(8,128)(2,1)} %get-tuple-element.62), channel_id=1, source_target_pairs={{0,6},{1,7},{2,0},{3,1},{4,2},{5,3},{6,4},{7,5},{8,14},{9,15},{10,... | collective-permute-start | bytes 983048 | tf_op jit(solution)/shard_map/ppermute | solution.py:41
  92.4 6.0 %shard_map.65 = (bf16[128,1280]{1,0:T(8,128)(2,1)S(1)}, bf16[128,1280]{1,0:T(8,128)(2,1)}, bf16[128,1280]{1,0:T(8,128)(2,1)}, bf16[128,1280]{1,0:T(8,128)(2,1)S(1)}) custom-call(s32[4]{0:T(128)S(1)} %pad_add_fusion.4.at_ref, bf16[4,256,2048]{2,1,0:T(8,128)(2,1)S(1)} %copy-done.1, bf16[1024,512]{1,0:T(8,128)(2,1)S(1)} %copy-done.5, ...), custom_call_target="tpu_custom_call" | custom-call | tf_op jit(solution)/shard_map/pallas_call | solution.py:230
  121.5 3.0 %collective-permute-start.23 = (bf16[256,256]{1,0:T(8,128)(2,1)}, bf16[256,256]{1,0:T(8,128)(2,1)S(1)}, u32[]{:S(2)}, u32[]{:S(2)}) collective-permute-start(bf16[256,256]{1,0:T(8,128)(2,1)} %shard_map.67.refs_9_), channel_id=1, source_target_pairs={{0,8},{1,9},{2,10},{3,11},{4,12},{5,13},{6,14},{7,15},{8,0},{9,1},... | collective-permute-start | bytes 393224 | tf_op jit(solution)/shard_map/ppermute | solution.py:41
  127.0 2.9 %shard_map.68.refs_1_ = bf16[256,512]{1,0:T(8,128)(2,1)S(1)} custom-call(bf16[256,1280]{1,0:T(8,128)(2,1)S(1)} %copy-done.7, bf16[128,1280]{1,0:T(8,128)(2,1)} %collective-permute-done.18.refs_1_.refs_6_, bf16[128,1280]{1,0:T(8,128)(2,1)} %collective-permute-done.16.refs_2_.refs_7_, bf16[128,1280]{1,0:T(8,128)(2,1)} %collective-permute-done.17.refs_3_.refs_8_, ...), custom_call_target="tpu_custom_call" | custom-call | tf_op jit(solution)/shard_map/pallas_call | solution.py:181
  129.9 3.0 %collective-permute-start.24 = (bf16[256,512]{1,0:T(8,128)(2,1)S(1)}, bf16[256,512]{1,0:T(8,128)(2,1)S(1)}, u32[]{:S(2)}, u32[]{:S(2)}) collective-permute-start(bf16[256,512]{1,0:T(8,128)(2,1)S(1)} %shard_map.68.refs_1_), channel_id=1, source_target_pairs={{0,1},{1,0},{2,3},{3,2},{4,5},{5,4},{6,7},{7,6},{8,9},{9,8},{10,11... | collective-permute-start | bytes 786440 | tf_op jit(solution)/shard_map/ppermute | solution.py:41
  133.9 2.9 %shard_map.69.refs_2_ = bf16[256,512]{1,0:T(8,128)(2,1)S(1)} custom-call(bf16[256,1280]{1,0:T(8,128)(2,1)S(1)} %copy-done.7, bf16[128,1280]{1,0:T(8,128)(2,1)} %collective-permute-done.18.refs_1_.refs_6_, bf16[128,1280]{1,0:T(8,128)(2,1)} %collective-permute-done.16.refs_2_.refs_7_, bf16[128,1280]{1,0:T(8,128)(2,1)} %collective-permute-done.17.refs_3_.refs_8_, ...), custom_call_target="tpu_custom_call" | custom-call | tf_op jit(solution)/shard_map/pallas_call | solution.py:181
  139.3 6.5 %collective-permute-done.25.refs_4_ = bf16[256,512]{1,0:T(8,128)(2,1)S(1)} collective-permute-done((bf16[256,512]{1,0:T(8,128)(2,1)S(1)}, bf16[256,512]{1,0:T(8,128)(2,1)S(1)}, u32[]{:S(2)}, u32[]{:S(2)}) %collective-permute-start.25) | collective-permute-done | bytes 262176 | tf_op jit(solution)/shard_map/ppermute | solution.py:41
  148.0 4.3 %shard_map.71 = (bf16[256,1024]{1,0:T(8,128)(2,1)}, bf16[256,1024]{1,0:T(8,128)(2,1)}) custom-call(s32[4]{0:T(128)S(1)} %get-tuple-element.108.refs_0_, bf16[256,512]{1,0:T(8,128)(2,1)S(1)} %shard_map.68.refs_1_, bf16[256,512]{1,0:T(8,128)(2,1)S(1)} %shard_map.69.refs_2_, bf16[256,512]{1,0:T(8,128)(2,1)S(1)} %collective-permute-done.24.refs_3_, ...), custom_call_target="tpu_custom_call" | custom-call | tf_op jit(solution)/shard_map/pallas_call | solution.py:281
  156.0 3.3 %shard_map.72 = (bf16[128,1024]{1,0:T(8,128)(2,1)S(1)}, bf16[128,1024]{1,0:T(8,128)(2,1)S(1)}, bf16[128,1024]{1,0:T(8,128)(2,1)S(1)}, bf16[128,1024]{1,0:T(8,128)(2,1)S(1)}) custom-call(s32[4]{0:T(128)S(1)} %get-tuple-element.109.refs_0_, bf16[256,512]{1,0:T(8,128)(2,1)S(1)} %shard_map.68.refs_1_, bf16[256,512]{1,0:T(8,128)(2,1)S(1)} %shard_map.69.refs_2_, ...), custom_call_target="tpu_custom_call" | custom-call | tf_op jit(solution)/shard_map/pallas_call | solution.py:281
  162.0 5.4 %shard_map.70 = (bf16[256,1024]{1,0:T(8,128)(2,1)S(1)}, bf16[256,1024]{1,0:T(8,128)(2,1)S(1)}, bf16[256,1024]{1,0:T(8,128)(2,1)S(1)}, bf16[256,1024]{1,0:T(8,128)(2,1)S(1)}) custom-call(s32[8]{0:T(128)S(1)} %stack.102.refs_0_, bf16[256,512]{1,0:T(8,128)(2,1)S(1)} %shard_map.68.refs_1_, bf16[256,512]{1,0:T(8,128)(2,1)S(1)} %shard_map.69.refs_2_, ...), custom_call_target="tpu_custom_call" | custom-call | tf_op jit(solution)/shard_map/pallas_call | solution.py:281
  179.6 7.8 %collective-permute-done.30 = bf16[256,1024]{1,0:T(8,128)(2,1)S(1)} collective-permute-done((bf16[256,1024]{1,0:T(8,128)(2,1)S(1)}, bf16[256,1024]{1,0:T(8,128)(2,1)S(1)}, u32[]{:S(2)}, u32[]{:S(2)}) %collective-permute-start.30) | collective-permute-done | bytes 524320 | tf_op jit(solution)/shard_map/ppermute | solution.py:41
  189.8 11.0 %collective-permute-start.37 = (bf16[256,512]{1,0:T(8,128)(2,1)S(1)}, bf16[256,512]{1,0:T(8,128)(2,1)S(1)}, u32[]{:S(2)}, u32[]{:S(2)}) collective-permute-start(bf16[256,512]{1,0:T(8,128)(2,1)S(1)} %get-tuple-element.94), channel_id=1, source_target_pairs={{0,8},{1,24},{2,10},{3,26},{4,12},{5,28},{6,14},{7,30},{8,0},{9,16... | collective-permute-start | bytes 786440 | tf_op jit(solution)/shard_map/ppermute | solution.py:41
  200.8 3.1 %collective-permute-start.36 = (bf16[256,512]{1,0:T(8,128)(2,1)S(1)}, bf16[256,512]{1,0:T(8,128)(2,1)S(1)}, u32[]{:S(2)}, u32[]{:S(2)}) collective-permute-start(bf16[256,512]{1,0:T(8,128)(2,1)S(1)} %get-tuple-element.93), channel_id=1, source_target_pairs={{0,0},{1,16},{2,2},{3,18},{4,4},{5,20},{6,6},{7,22},{8,8},{9,24},{... | collective-permute-start | bytes 786440 | tf_op jit(solution)/shard_map/ppermute | solution.py:41
  203.9 3.2 %collective-permute-done.37 = bf16[256,512]{1,0:T(8,128)(2,1)S(1)} collective-permute-done((bf16[256,512]{1,0:T(8,128)(2,1)S(1)}, bf16[256,512]{1,0:T(8,128)(2,1)S(1)}, u32[]{:S(2)}, u32[]{:S(2)}) %collective-permute-start.37) | collective-permute-done | bytes 262176 | tf_op jit(solution)/shard_map/ppermute | solution.py:41
  207.1 6.2 %collective-permute-done.36 = bf16[256,512]{1,0:T(8,128)(2,1)S(1)} collective-permute-done((bf16[256,512]{1,0:T(8,128)(2,1)S(1)}, bf16[256,512]{1,0:T(8,128)(2,1)S(1)}, u32[]{:S(2)}, u32[]{:S(2)}) %collective-permute-start.36) | collective-permute-done | bytes 262176 | tf_op jit(solution)/shard_map/ppermute | solution.py:41
  (183 shorter events, 89.4 us)
Async XLA Ops:
  6.5 119.2 %all-gather.3.cloned.1.call-start = ((), (), s32[]{:S(2)}) async-start(), calls=%async_computation | async-start | bytes 5242880 | tf_op jit(solution)/shard_map/all_gather | solution.py:374
  19.9 19.3 %collective-permute-start.3 = (bf16[256,1024]{1,0:T(8,128)(2,1)S(1)}, bf16[256,1024]{1,0:T(8,128)(2,1)S(1)}, u32[]{:S(2)}, u32[]{:S(2)}) collective-permute-start(bf16[256,1024]{1,0:T(8,128)(2,1)S(1)} %maximum_select_fusion), channel_id=1, source_target_pairs={{0,16},{1,17},{2,18},{3,19},{4,20},{5,21},{6,22},{7,23},{8,24},{9,... | collective-permute-start | bytes 1572872 | tf_op jit(solution)/shard_map/ppermute | solution.py:41
  28.3 12.9 %collective-permute-start.4 = (bf16[256,1024]{1,0:T(8,128)(2,1)S(1)}, bf16[256,1024]{1,0:T(8,128)(2,1)S(1)}, u32[]{:S(2)}, u32[]{:S(2)}) collective-permute-start(bf16[256,1024]{1,0:T(8,128)(2,1)S(1)} %maximum_select_fusion), channel_id=1, source_target_pairs={{0,48},{1,49},{2,50},{3,51},{4,52},{5,53},{6,54},{7,55},{8,56},{9,... | collective-permute-start | bytes 1572872 | tf_op jit(solution)/shard_map/ppermute | solution.py:41
  28.3 15.5 %collective-permute-start.5 = (bf16[256,1024]{1,0:T(8,128)(2,1)S(1)}, bf16[256,1024]{1,0:T(8,128)(2,1)}, u32[]{:S(2)}, u32[]{:S(2)}) collective-permute-start(bf16[256,1024]{1,0:T(8,128)(2,1)S(1)} %maximum_select_fusion), channel_id=1, source_target_pairs={{0,64},{1,65},{2,66},{3,67},{4,68},{5,69},{6,70},{7,71},{8,72},{9,... | collective-permute-start | bytes 1572872 | tf_op jit(solution)/shard_map/ppermute | solution.py:41
  43.8 31.4 %collective-permute-start.12 = (bf16[1024,640]{1,0:T(8,128)(2,1)}, bf16[1024,640]{1,0:T(8,128)(2,1)S(1)}, u32[]{:S(2)}, u32[]{:S(2)}) collective-permute-start(bf16[1024,640]{1,0:T(8,128)(2,1)} %pad_maximum_fusion), channel_id=1, source_target_pairs={{0,1},{1,0},{2,3},{3,2},{4,5},{5,4},{6,7},{7,6},{8,9},{9,8},{10,11... | collective-permute-start | bytes 3932168 | tf_op jit(solution)/shard_map/ppermute | solution.py:41
  47.1 12.5 %collective-permute-start.8 = (bf16[256,1024]{1,0:T(8,128)(2,1)}, bf16[256,1024]{1,0:T(8,128)(2,1)}, u32[]{:S(2)}, u32[]{:S(2)}) collective-permute-start(bf16[256,1024]{1,0:T(8,128)(2,1)} %collective-permute-done.5), channel_id=1, source_target_pairs={{0,16},{1,17},{2,18},{3,19},{4,20},{5,21},{6,22},{7,23},{8,24},{9,... | collective-permute-start | bytes 1572872 | tf_op jit(solution)/shard_map/ppermute | solution.py:41
  48.3 13.0 %collective-permute-start.9 = (bf16[256,1024]{1,0:T(8,128)(2,1)}, bf16[256,1024]{1,0:T(8,128)(2,1)}, u32[]{:S(2)}, u32[]{:S(2)}) collective-permute-start(bf16[256,1024]{1,0:T(8,128)(2,1)} %collective-permute-done.5), channel_id=1, source_target_pairs={{0,48},{1,49},{2,50},{3,51},{4,52},{5,53},{6,54},{7,55},{8,56},{9,... | collective-permute-start | bytes 1572872 | tf_op jit(solution)/shard_map/ppermute | solution.py:41
  50.2 28.0 %collective-permute-start.7 = (bf16[128,1024]{1,0:T(8,128)(2,1)S(1)}, bf16[128,1024]{1,0:T(8,128)(2,1)S(1)}, u32[]{:S(2)}, u32[]{:S(2)}) collective-permute-start(bf16[128,1024]{1,0:T(8,128)(2,1)S(1)} %slice.31), channel_id=1, source_target_pairs={{0,48},{1,49},{2,50},{3,51},{4,52},{5,53},{6,54},{7,55},{8,56},{9,... | collective-permute-start | bytes 786440 | tf_op jit(solution)/shard_map/ppermute | solution.py:41
  53.0 25.2 %collective-permute-start.6 = (bf16[128,1024]{1,0:T(8,128)(2,1)S(1)}, bf16[128,1024]{1,0:T(8,128)(2,1)S(1)}, u32[]{:S(2)}, u32[]{:S(2)}) collective-permute-start(bf16[128,1024]{1,0:T(8,128)(2,1)S(1)} %slice.30), channel_id=1, source_target_pairs={{0,16},{1,17},{2,18},{3,19},{4,20},{5,21},{6,22},{7,23},{8,24},{9,... | collective-permute-start | bytes 786440 | tf_op jit(solution)/shard_map/ppermute | solution.py:41
  84.9 17.7 %collective-permute-start.14 = (bf16[128,1280]{1,0:T(8,128)(2,1)}, bf16[128,1280]{1,0:T(8,128)(2,1)}, u32[]{:S(2)}, u32[]{:S(2)}) collective-permute-start(bf16[128,1280]{1,0:T(8,128)(2,1)} %get-tuple-element.61), channel_id=1, source_target_pairs={{0,2},{1,3},{2,4},{3,5},{4,6},{5,7},{6,0},{7,1},{8,10},{9,11},{10,... | collective-permute-start | bytes 983048 | tf_op jit(solution)/shard_map/ppermute | solution.py:41
  84.9 17.7 %collective-permute-start.15 = (bf16[128,1280]{1,0:T(8,128)(2,1)}, bf16[128,1280]{1,0:T(8,128)(2,1)}, u32[]{:S(2)}, u32[]{:S(2)}) collective-permute-start(bf16[128,1280]{1,0:T(8,128)(2,1)} %get-tuple-element.62), channel_id=1, source_target_pairs={{0,6},{1,7},{2,0},{3,1},{4,2},{5,3},{6,4},{7,5},{8,14},{9,15},{10,... | collective-permute-start | bytes 983048 | tf_op jit(solution)/shard_map/ppermute | solution.py:41
  99.9 10.5 %collective-permute-start.16 = (bf16[128,1280]{1,0:T(8,128)(2,1)}, bf16[128,1280]{1,0:T(8,128)(2,1)}, u32[]{:S(2)}, u32[]{:S(2)}) collective-permute-start(bf16[128,1280]{1,0:T(8,128)(2,1)} %get-tuple-element.69), channel_id=1, source_target_pairs={{0,2},{1,3},{2,4},{3,5},{4,6},{5,7},{6,0},{7,1},{8,10},{9,11},{10,... | collective-permute-start | bytes 983048 | tf_op jit(solution)/shard_map/ppermute | solution.py:41
  99.9 10.5 %collective-permute-start.17 = (bf16[128,1280]{1,0:T(8,128)(2,1)}, bf16[128,1280]{1,0:T(8,128)(2,1)}, u32[]{:S(2)}, u32[]{:S(2)}) collective-permute-start(bf16[128,1280]{1,0:T(8,128)(2,1)} %get-tuple-element.70), channel_id=1, source_target_pairs={{0,6},{1,7},{2,0},{3,1},{4,2},{5,3},{6,4},{7,5},{8,14},{9,15},{10,... | collective-permute-start | bytes 983048 | tf_op jit(solution)/shard_map/ppermute | solution.py:41
  104.5 14.9 %collective-permute-start.18 = (bf16[128,1280]{1,0:T(8,128)(2,1)}, bf16[128,1280]{1,0:T(8,128)(2,1)}, u32[]{:S(2)}, u32[]{:S(2)}) collective-permute-start(bf16[128,1280]{1,0:T(8,128)(2,1)} %add.331), channel_id=1, source_target_pairs={{0,2},{1,3},{2,4},{3,5},{4,6},{5,7},{6,0},{7,1},{8,10},{9,11},{10,... | collective-permute-start | bytes 983048 | tf_op jit(solution)/shard_map/ppermute | solution.py:41
  106.4 13.1 %collective-permute-start.19 = (bf16[128,1280]{1,0:T(8,128)(2,1)}, bf16[128,1280]{1,0:T(8,128)(2,1)}, u32[]{:S(2)}, u32[]{:S(2)}) collective-permute-start(bf16[128,1280]{1,0:T(8,128)(2,1)} %add.332), channel_id=1, source_target_pairs={{0,6},{1,7},{2,0},{3,1},{4,2},{5,3},{6,4},{7,5},{8,14},{9,15},{10,... | collective-permute-start | bytes 983048 | tf_op jit(solution)/shard_map/ppermute | solution.py:41
  125.7 20.0 %collective-permute-start.26 = (bf16[4,512,1024]{2,1,0:T(8,128)(2,1)}, bf16[4,512,1024]{2,1,0:T(8,128)(2,1)}, u32[]{:S(2)}, u32[]{:S(2)}) collective-permute-start(bf16[4,512,1024]{2,1,0:T(8,128)(2,1)} %bitcast.44), channel_id=1, source_target_pairs={{0,8},{1,9},{2,10},{3,11},{4,12},{5,13},{6,14},{7,15},{8,0},{9,1},... | collective-permute-start | bytes 12582920 | tf_op jit(solution)/shard_map/ppermute | solution.py:41
  152.3 15.2 %collective-permute-start.27 = (bf16[256,1024]{1,0:T(8,128)(2,1)}, bf16[256,1024]{1,0:T(8,128)(2,1)}, u32[]{:S(2)}, u32[]{:S(2)}) collective-permute-start(bf16[256,1024]{1,0:T(8,128)(2,1)} %get-tuple-element.80), channel_id=1, source_target_pairs={{0,16},{1,17},{2,18},{3,19},{4,20},{5,21},{6,22},{7,23},{8,24},{9,... | collective-permute-start | bytes 1572872 | tf_op jit(solution)/shard_map/ppermute | solution.py:41
  152.8 14.7 %collective-permute-start.28 = (bf16[256,1024]{1,0:T(8,128)(2,1)}, bf16[256,1024]{1,0:T(8,128)(2,1)}, u32[]{:S(2)}, u32[]{:S(2)}) collective-permute-start(bf16[256,1024]{1,0:T(8,128)(2,1)} %get-tuple-element.81), channel_id=1, source_target_pairs={{0,48},{1,49},{2,50},{3,51},{4,52},{5,53},{6,54},{7,55},{8,56},{9,... | collective-permute-start | bytes 1572872 | tf_op jit(solution)/shard_map/ppermute | solution.py:41
  159.4 16.2 %collective-permute-start.32 = (bf16[128,1024]{1,0:T(8,128)(2,1)S(1)}, bf16[128,1024]{1,0:T(8,128)(2,1)S(1)}, u32[]{:S(2)}, u32[]{:S(2)}) collective-permute-start(bf16[128,1024]{1,0:T(8,128)(2,1)S(1)} %get-tuple-element.90), channel_id=1, source_target_pairs={{0,16},{1,17},{2,18},{3,19},{4,20},{5,21},{6,22},{7,23},{8,24},{9,... | collective-permute-start | bytes 786440 | tf_op jit(solution)/shard_map/ppermute | solution.py:41
  160.9 14.7 %collective-permute-start.33 = (bf16[128,1024]{1,0:T(8,128)(2,1)S(1)}, bf16[128,1024]{1,0:T(8,128)(2,1)S(1)}, u32[]{:S(2)}, u32[]{:S(2)}) collective-permute-start(bf16[128,1024]{1,0:T(8,128)(2,1)S(1)} %get-tuple-element.91), channel_id=1, source_target_pairs={{0,48},{1,49},{2,50},{3,51},{4,52},{5,53},{6,54},{7,55},{8,56},{9,... | collective-permute-start | bytes 786440 | tf_op jit(solution)/shard_map/ppermute | solution.py:41
  172.9 14.4 %collective-permute-start.30 = (bf16[256,1024]{1,0:T(8,128)(2,1)S(1)}, bf16[256,1024]{1,0:T(8,128)(2,1)S(1)}, u32[]{:S(2)}, u32[]{:S(2)}) collective-permute-start(bf16[256,1024]{1,0:T(8,128)(2,1)S(1)} %get-tuple-element.97), channel_id=1, source_target_pairs={{0,48},{1,49},{2,50},{3,51},{4,52},{5,53},{6,54},{7,55},{8,56},{9,... | collective-permute-start | bytes 1572872 | tf_op jit(solution)/shard_map/ppermute | solution.py:41
  175.6 11.8 %collective-permute-start.29 = (bf16[256,1024]{1,0:T(8,128)(2,1)S(1)}, bf16[256,1024]{1,0:T(8,128)(2,1)}, u32[]{:S(2)}, u32[]{:S(2)}) collective-permute-start(bf16[256,1024]{1,0:T(8,128)(2,1)S(1)} %get-tuple-element.95), channel_id=1, source_target_pairs={{0,16},{1,17},{2,18},{3,19},{4,20},{5,21},{6,22},{7,23},{8,24},{9,... | collective-permute-start | bytes 1572872 | tf_op jit(solution)/shard_map/ppermute | solution.py:41
  189.8 17.3 %collective-permute-start.37 = (bf16[256,512]{1,0:T(8,128)(2,1)S(1)}, bf16[256,512]{1,0:T(8,128)(2,1)S(1)}, u32[]{:S(2)}, u32[]{:S(2)}) collective-permute-start(bf16[256,512]{1,0:T(8,128)(2,1)S(1)} %get-tuple-element.94), channel_id=1, source_target_pairs={{0,8},{1,24},{2,10},{3,26},{4,12},{5,28},{6,14},{7,30},{8,0},{9,16... | collective-permute-start | bytes 786440 | tf_op jit(solution)/shard_map/ppermute | solution.py:41
  200.8 12.5 %collective-permute-start.36 = (bf16[256,512]{1,0:T(8,128)(2,1)S(1)}, bf16[256,512]{1,0:T(8,128)(2,1)S(1)}, u32[]{:S(2)}, u32[]{:S(2)}) collective-permute-start(bf16[256,512]{1,0:T(8,128)(2,1)S(1)} %get-tuple-element.93), channel_id=1, source_target_pairs={{0,0},{1,16},{2,2},{3,18},{4,4},{5,20},{6,6},{7,22},{8,8},{9,24},{... | collective-permute-start | bytes 786440 | tf_op jit(solution)/shard_map/ppermute | solution.py:41
  (50 other events, 290.9 us)
Sparse Core Ops, SparseCore 0:
  20.0 58.2 all-gather.2

commit v11 on v10

--- a/solution.py
+++ b/solution.py
@@ -205,16 +205,17 @@
     def put(start, near_part, far_part):
         cols = slice(start, start + near_part.shape[1])
         value = (dot(near_rows, near_part) + dot(far_rows, far_part)).astype(jnp.bfloat16)
-        if len(outs) == 1:
-            outs[0][:, cols] = value
-            return
-        for i in range(len(outs) // 2):
+        for i in range(3):
 
             @pl.when(step == i)
             def _():
                 outs[2 * i][:, cols] = value[:128]
                 outs[2 * i + 1][:, cols] = value[128:]
 
+        @pl.when(step == 3)
+        def _():
+            outs[6][:, cols] = value
+
     def kv_cols(which):
         return near_kv[:, pl.ds(pl.multiple_of(which * HEAD_SIZE, HEAD_SIZE), HEAD_SIZE)]
 
@@ -224,21 +225,32 @@
     put(WIDE + 512, kv_cols(1 - core), far_other[:, 512:])
 
 
-def project(which, zh, core, gathered, weights, halves=False):
-    steps = len(which)
-    rows, outs = (128, 2 * steps) if halves else (HALF, 1)
+def project(which, zh, core, gathered, weights):
+    rows = [128] * 6 + [HALF]
     return pl.pallas_call(
         project_kernel,
         grid_spec=pltpu.PrefetchScalarGridSpec(
             num_scalar_prefetch=1,
-            grid=(steps,),
+            grid=(4,),
             in_specs=[pl.BlockSpec((1, HALF, 2048), lambda i, at: (at[2 + i], 0, 0))]
             + [pl.BlockSpec(w.shape, lambda i, at: (0, 0)) for w in weights],
-            out_specs=[pl.BlockSpec((rows, 2 * WIDE), lambda i, at: (0, 0))] * outs,
+            out_specs=[pl.BlockSpec((r, 2 * WIDE), lambda i, at: (0, 0)) for r in rows],
         ),
-        out_shape=[jax.ShapeDtypeStruct((rows, 2 * WIDE), jnp.bfloat16)] * outs,
+        out_shape=[jax.ShapeDtypeStruct((r, 2 * WIDE), jnp.bfloat16) for r in rows],
         compiler_params=GRANT,
     )(jnp.stack([zh, core, *which]).astype(jnp.int32), gathered, *weights)
+
+
+def two_sums_kernel(a, b, c, d, first, second):
+    for left, right, out in ((a, b, first), (c, d, second)):
+        out[...] = (left[...].astype(jnp.float32) + right[...].astype(jnp.float32)).astype(
+            jnp.bfloat16
+        )
+
+
+def two_sums(a, b, c, d):
+    shape = jax.ShapeDtypeStruct(a.shape, jnp.bfloat16)
+    return pl.pallas_call(two_sums_kernel, out_shape=[shape, shape])(a, b, c, d)
 
 
 def products_kernel(form, steps, at_ref, own_a, own_b, far_a, far_b, near, other, *outs):
@@ -351,51 +363,53 @@
     beside_left = x_shift(beside, 1)
     beside_right = x_shift(beside, -1)
     opposite = jnp.concatenate([x_shift(left[:128], 1), x_shift(right[128:], -1)], 0)
-    beside_opposite = jnp.concatenate(
-        [x_shift(beside_left[:128], 1), x_shift(beside_right[128:], -1)], 0
-    )
-    weights = (query_weight, near_other, kv_near, far, core_swap(after(far, beside_opposite)))
-    gathered = jnp.zeros((4, HALF, 2048), jnp.bfloat16)
-    for dz, dx, part in (
+
+    def placed(whole, *parts):
+        for dz, dx, part in parts:
+            zs, xs = zl ^ dz, (x + dx) % 4
+            whole = lax.dynamic_update_slice(
+                whole, part[None], (zs * 2 + xs // 2, 0, (xs % 2) * 1024)
+            )
+        return whole
+
+    gathered = placed(
+        jnp.zeros((4, HALF, 2048), jnp.bfloat16),
         (0, 0, block),
         (0, 3, left),
         (0, 1, right),
         (1, 0, beside),
-        (0, 2, opposite),
-        (1, 3, beside_left),
-        (1, 1, beside_right),
-        (1, 2, beside_opposite),
-    ):
-        zs, xs = zl ^ dz, (x + dx) % 4
-        gathered = lax.dynamic_update_slice(
-            gathered, part[None], (zs * 2 + xs // 2, 0, (xs % 2) * 1024)
-        )
+    )
+    gathered, beside_left, beside_right = lax.optimization_barrier(
+        (gathered, beside_left, beside_right)
+    )
+    beside_opposite = (x_shift(beside_left[:128], 1), x_shift(beside_right[128:], -1))
+    gathered = placed(
+        gathered, (0, 2, opposite), (1, 3, beside_left), (1, 1, beside_right)
+    )
+    gathered = placed(gathered, (1, 2, jnp.concatenate(beside_opposite, 0)))
+    far_other = core_swap(after(far, beside_opposite))
+    weights = (query_weight, near_other, kv_near, far, far_other)
 
     out_near = lax.all_gather(after(out_weight, block), "y", axis=0, tiled=False)
 
     squares = jnp.sum(jnp.square(gathered.astype(jnp.float32) * slice_gain), axis=-1)
-    gathered, squares = lax.optimization_barrier((gathered, squares))
-    low, high = project([(y + 2) % 4], zh, core, gathered, weights, True)
+    square_total = lax.dynamic_index_in_dim(squares, y, 0, keepdims=False)
+    arrived = [
+        y_shift(lax.dynamic_index_in_dim(squares, (y + k) % 4, 0, keepdims=False), k)
+        for k in (1, 2, 3)
+    ]
+    gathered, arrived = lax.optimization_barrier((gathered, arrived))
+    low, high, a_top, a_bottom, b_top, b_bottom, kept = project(
+        [(y + 2) % 4, (y + 1) % 4, (y + 3) % 4, y], zh, core, gathered, weights
+    )
     from_below = y_shift(low, 1)
     from_above = y_shift(high, -1)
-    a_top, a_bottom, b_top, b_bottom = project(
-        [(y + 1) % 4, (y + 3) % 4], zh, core, gathered, weights, True
-    )
-    from_below, from_above, a_top, b_bottom = lax.optimization_barrier(
-        (from_below, from_above, a_top, b_bottom)
-    )
     a_bottom, b_top = y_shift(a_bottom, 1), y_shift(b_top, -1)
-    a_top, b_bottom = a_top + from_below, b_bottom + from_above
-    gathered = after(gathered, (a_top, b_bottom, a_bottom, b_top))
-    (kept,) = project([y], zh, core, gathered, weights)
+    a_top, b_bottom = two_sums(a_top, from_below, b_bottom, from_above)
     sums = (kept, y_shift(a_top, 1), a_bottom, b_top, y_shift(b_bottom, -1))
 
-    squares, a_top, b_bottom = lax.optimization_barrier((squares, a_top, b_bottom))
-    total = lax.dynamic_index_in_dim(squares, y, 0, keepdims=False)
-    for k in (1, 2, 3):
-        total += y_shift(lax.dynamic_index_in_dim(squares, (y + k) % 4, 0, keepdims=False), k)
-    scale = lax.rsqrt(total / 8192.0 + norm_eps)[:, None]
-
+    square_total += arrived[0] + arrived[1] + arrived[2]
+    scale = lax.rsqrt(square_total / 8192.0 + norm_eps)[:, None]
     kv_rows = key_value_rows(core, sums, scale, cosine, sine)
     kv_other = core_swap(kv_rows)
     out_other = core_swap(after(out_near, kv_other))

time: 223 us -> 245 us (1.099)
  waiting for transfers between devices: 58.4 us -> 67.3 us
  local copies, waits for them, and re-layouts: 30.6 us -> 37 us
  starting transfers between devices: 65.4 us -> 69.8 us
    ppermute x38, waiting for transfers between devices: 58.4 us -> 67.3 us  [send(): return lax.ppermute(value, AXES, pairs(change))]
    dynamic_update_slice x7 -> x6, local copies, waits for them, and re-layouts: 3.51 us -> 10.4 us  [placed(): lax.dynamic_update_slice(whole, part[None], (zs * 2 + xs // 2, 0, xs % 2...]
    ppermute x38, starting transfers between devices: 65.4 us -> 69.8 us  [send(): return lax.ppermute(value, AXES, pairs(change))]
    unnamed x71 -> x64, local copies, waits for them, and re-layouts: 19.9 us -> 15.9 us
    add x2 -> x0, other arithmetic: 3.75 us -> none  [local(): a_top, b_bottom = (a_top + from_below, b_bottom + from_above)]
    dynamic_update_slice x1 -> x2, other arithmetic: 0.05 us -> 3.7 us  [placed(): lax.dynamic_update_slice(whole, part[None], (zs * 2 + xs // 2, 0, xs % 2...]
    pallas_call x3 -> x1, Pallas kernels: 11.5 us -> 12.9 us  [project(): pl.pallas_call(project_kernel, grid_spec=pltpu.PrefetchScalarGridSpec(num...]
  transfers between devices with their start and end apart: 39 -> 39, of which waited for: 17 -> 22; matrix products, arithmetic and copies ran while one was open for 11% -> 14% of each run, Pallas kernels for 14% -> 13%
where the time goes in v11:
time: 245 us; the launch traced here: 243 us
  starting transfers between devices  69.8 us (28%)
  waiting for transfers between devices  67.3 us (27%)
  local copies, waits for them, and re-layouts  37 us (15%)
  Pallas kernels  35.8 us (15%)
  other arithmetic  19 us (8%)
  between operations  14.3 us (6%)
    ppermute x38, starting transfers between devices, send(): return lax.ppermute(value, AXES, pairs(change))  69.8 us
    ppermute x38, waiting for transfers between devices, send(): return lax.ppermute(value, AXES, pairs(change))  67.3 us
    unnamed x64, local copies, waits for them, and re-layouts  15.9 us
    pallas_call x3, Pallas kernels, products(): pl.pallas_call(lambda *refs: products_kernel(form, steps, *refs), grid_sp...  12.9 us
    pallas_call x1, Pallas kernels, project(): pl.pallas_call(project_kernel, grid_spec=pltpu.PrefetchScalarGridSpec(num...  12.9 us
    dynamic_update_slice x6, local copies, waits for them, and re-layouts, placed(): lax.dynamic_update_slice(whole, part[None], (zs * 2 + xs // 2, 0, xs % 2...  10.4 us
  transfers between devices with their start and end apart: 39, of which 22 were waited for; matrix products, arithmetic and copies ran while one was open for 14% of the time, Pallas kernels for 13%

profile of v11, /device:TPU:3, one launch (start us, length us, event | category | flops | bytes accessed | tf_op | source)
XLA Modules:
  0.0 243.2 jit_solution(7390356671414212871)
XLA Ops:
  9.3 3.6 %collective-permute-start = (bf16[256,512]{1,0:T(8,128)(2,1)}, bf16[256,512]{1,0:T(8,128)(2,1)}, u32[]{:S(2)}, u32[]{:S(2)}) collective-permute-start(bf16[256,512]{1,0:T(8,128)(2,1)} %get-tuple-element.103), channel_id=1, source_target_pairs={{0,0},{1,1},{2,32},{3,33},{4,64},{5,65},{6,96},{7,97},{8,8},{9,9},... | collective-permute-start | bytes 786440 | tf_op jit(solution)/shard_map/ppermute | solution.py:41
  21.9 9.1 %collective-permute-start.3 = (bf16[256,1024]{1,0:T(8,128)(2,1)}, bf16[256,1024]{1,0:T(8,128)(2,1)}, u32[]{:S(2)}, u32[]{:S(2)}) collective-permute-start(bf16[256,1024]{1,0:T(8,128)(2,1)} %maximum_select_fusion), channel_id=1, source_target_pairs={{0,16},{1,17},{2,18},{3,19},{4,20},{5,21},{6,22},{7,23},{8,24},{9,... | collective-permute-start | bytes 1572872 | tf_op jit(solution)/shard_map/ppermute | solution.py:41
  31.0 3.7 %collective-permute-start.5 = (bf16[256,1024]{1,0:T(8,128)(2,1)}, bf16[256,1024]{1,0:T(8,128)(2,1)}, u32[]{:S(2)}, u32[]{:S(2)}) collective-permute-start(bf16[256,1024]{1,0:T(8,128)(2,1)} %maximum_select_fusion), channel_id=1, source_target_pairs={{0,64},{1,65},{2,66},{3,67},{4,68},{5,69},{6,70},{7,71},{8,72},{9,... | collective-permute-start | bytes 1572872 | tf_op jit(solution)/shard_map/ppermute | solution.py:41
  34.7 8.3 %collective-permute-done.3 = bf16[256,1024]{1,0:T(8,128)(2,1)} collective-permute-done((bf16[256,1024]{1,0:T(8,128)(2,1)}, bf16[256,1024]{1,0:T(8,128)(2,1)}, u32[]{:S(2)}, u32[]{:S(2)}) %collective-permute-start.3) | collective-permute-done | bytes 524320 | tf_op jit(solution)/shard_map/ppermute | solution.py:41
  47.6 3.3 %collective-permute-start.15 = (bf16[1024,640]{1,0:T(8,128)(2,1)}, bf16[1024,640]{1,0:T(8,128)(2,1)}, u32[]{:S(2)}, u32[]{:S(2)}) collective-permute-start(bf16[1024,640]{1,0:T(8,128)(2,1)} %pad_maximum_fusion), channel_id=1, source_target_pairs={{0,1},{1,0},{2,3},{3,2},{4,5},{5,4},{6,7},{7,6},{8,9},{9,8},{10,11... | collective-permute-start | bytes 3932168 | tf_op jit(solution)/shard_map/ppermute | solution.py:41
  61.6 6.0 %collective-permute-done.6 = bf16[256,1024]{1,0:T(8,128)(2,1)S(1)} collective-permute-done((bf16[256,1024]{1,0:T(8,128)(2,1)}, bf16[256,1024]{1,0:T(8,128)(2,1)S(1)}, u32[]{:S(2)}, u32[]{:S(2)}) %collective-permute-start.6) | collective-permute-done | bytes 524320 | tf_op jit(solution)/shard_map/ppermute | solution.py:41
  76.8 3.2 %collective-permute-done.15.far = bf16[1024,640]{1,0:T(8,128)(2,1)} collective-permute-done((bf16[1024,640]{1,0:T(8,128)(2,1)}, bf16[1024,640]{1,0:T(8,128)(2,1)}, u32[]{:S(2)}, u32[]{:S(2)}) %collective-permute-start.15) | collective-permute-done | bytes 1310752 | tf_op jit(solution)/shard_map/ppermute | solution.py:41
  90.0 3.3 %multiply_reduce_fusion = f32[4,256]{1,0:T(4,128)S(1)} fusion(bf16[4,256,2048]{2,1,0:T(8,128)(2,1)} %fusion.3.rows_ref, f32[2048]{0:T(1024)S(1)} %dynamic-slice_divide_fusion), kind=kLoop, calls=%fused_computation | loop fusion | flops 8387584 | bytes 4206592 | tf_op jit(solution)/shard_map/reduce_sum | solution.py:395
  93.5 2.7 %collective-permute-start.13 = (f32[256]{0:T(256)S(1)}, f32[256]{0:T(256)S(1)}, u32[]{:S(2)}, u32[]{:S(2)}) collective-permute-start(f32[256]{0:T(256)S(1)} %bitcast.53), channel_id=1, source_target_pairs={{0,4},{1,5},{2,6},{3,7},{4,0},{5,1},{6,2},{7,3},{8,12},{9,13},{10,... | collective-permute-start | bytes 3080 | tf_op jit(solution)/shard_map/ppermute | solution.py:41
  98.6 12.9 %shard_map.64 = (bf16[128,1280]{1,0:T(8,128)(2,1)S(1)}, bf16[128,1280]{1,0:T(8,128)(2,1)S(1)}, bf16[128,1280]{1,0:T(8,128)(2,1)S(1)}, bf16[128,1280]{1,0:T(8,128...) custom-call(s32[6]{0:T(128)S(1)} %stack.99.at_ref, ...), custom_call_target="tpu_custom_call" | custom-call | tf_op jit(solution)/shard_map/pallas_call | solution.py:230
  116.4 2.7 %collective-permute-start.21 = (bf16[128,1280]{1,0:T(8,128)(2,1)}, bf16[128,1280]{1,0:T(8,128)(2,1)S(1)}, u32[]{:S(2)}, u32[]{:S(2)}) collective-permute-start(bf16[128,1280]{1,0:T(8,128)(2,1)} %get-tuple-element.73), channel_id=1, source_target_pairs={{0,6},{1,7},{2,0},{3,1},{4,2},{5,3},{6,4},{7,5},{8,14},{9,15},{10,... | collective-permute-start | bytes 983048 | tf_op jit(solution)/shard_map/ppermute | solution.py:41
  123.9 2.7 %collective-permute-start.22 = (bf16[128,1280]{1,0:T(8,128)(2,1)}, bf16[128,1280]{1,0:T(8,128)(2,1)S(1)}, u32[]{:S(2)}, u32[]{:S(2)}) collective-permute-start(bf16[128,1280]{1,0:T(8,128)(2,1)} %get-tuple-element.74), channel_id=1, source_target_pairs={{0,6},{1,7},{2,0},{3,1},{4,2},{5,3},{6,4},{7,5},{8,14},{9,15},{10,... | collective-permute-start | bytes 983048 | tf_op jit(solution)/shard_map/ppermute | solution.py:41
  127.4 7.7 %collective-permute-done.19.refs_1_.refs_6_ = bf16[128,1280]{1,0:T(8,128)(2,1)S(1)} collective-permute-done((bf16[128,1280]{1,0:T(8,128)(2,1)}, bf16[128,1280]{1,0:T(8,128)(2,1)S(1)}, u32[]{:S(2)}, u32[]{:S(2)}) %collective-permute-start.19) | collective-permute-done | bytes 327712 | tf_op jit(solution)/shard_map/ppermute | solution.py:41
  138.0 5.1 %collective-permute-start.23 = (bf16[256,256]{1,0:T(8,128)(2,1)}, bf16[256,256]{1,0:T(8,128)(2,1)S(1)}, u32[]{:S(2)}, u32[]{:S(2)}) collective-permute-start(bf16[256,256]{1,0:T(8,128)(2,1)} %shard_map.66.refs_9_), channel_id=1, source_target_pairs={{0,8},{1,9},{2,10},{3,11},{4,12},{5,13},{6,14},{7,15},{8,0},{9,1},... | collective-permute-start | bytes 393224 | tf_op jit(solution)/shard_map/ppermute | solution.py:41
  157.1 3.5 %collective-permute-done.25.refs_4_ = bf16[256,512]{1,0:T(8,128)(2,1)S(1)} collective-permute-done((bf16[256,512]{1,0:T(8,128)(2,1)S(1)}, bf16[256,512]{1,0:T(8,128)(2,1)S(1)}, u32[]{:S(2)}, u32[]{:S(2)}) %collective-permute-start.25) | collective-permute-done | bytes 262176 | tf_op jit(solution)/shard_map/ppermute | solution.py:41
  160.5 5.6 %collective-permute-done.24.refs_3_ = bf16[256,512]{1,0:T(8,128)(2,1)S(1)} collective-permute-done((bf16[256,512]{1,0:T(8,128)(2,1)S(1)}, bf16[256,512]{1,0:T(8,128)(2,1)S(1)}, u32[]{:S(2)}, u32[]{:S(2)}) %collective-permute-start.24) | collective-permute-done | bytes 262176 | tf_op jit(solution)/shard_map/ppermute | solution.py:41
  168.4 4.1 %shard_map.70 = (bf16[256,1024]{1,0:T(8,128)(2,1)}, bf16[256,1024]{1,0:T(8,128)(2,1)S(1)}) custom-call(s32[4]{0:T(128)S(1)} %get-tuple-element.112.refs_0_, bf16[256,512]{1,0:T(8,128)(2,1)S(1)} %shard_map.67.refs_1_, bf16[256,512]{1,0:T(8,128)(2,1)S(1)} %shard_map.68.refs_2_, bf16[256,512]{1,0:T(8,128)(2,1)S(1)} %collective-permute-done.24.refs_3_, ...), custom_call_target="tpu_custom_call" | custom-call | tf_op jit(solution)/shard_map/pallas_call | solution.py:293
  176.6 3.3 %shard_map.71 = (bf16[128,1024]{1,0:T(8,128)(2,1)S(1)}, bf16[128,1024]{1,0:T(8,128)(2,1)S(1)}, bf16[128,1024]{1,0:T(8,128)(2,1)S(1)}, bf16[128,1024]{1,0:T(8,128)(2,1)S(1)}) custom-call(s32[4]{0:T(128)S(1)} %get-tuple-element.113.refs_0_, bf16[256,512]{1,0:T(8,128)(2,1)S(1)} %shard_map.67.refs_1_, bf16[256,512]{1,0:T(8,128)(2,1)S(1)} %shard_map.68.refs_2_, ...), custom_call_target="tpu_custom_call" | custom-call | tf_op jit(solution)/shard_map/pallas_call | solution.py:293
  182.8 5.4 %shard_map.69 = (bf16[256,1024]{1,0:T(8,128)(2,1)S(1)}, bf16[256,1024]{1,0:T(8,128)(2,1)S(1)}, bf16[256,1024]{1,0:T(8,128)(2,1)S(1)}, bf16[256,1024]{1,0:T(8,128)(2,1)S(1)}) custom-call(s32[8]{0:T(128)S(1)} %stack.92.refs_0_, bf16[256,512]{1,0:T(8,128)(2,1)S(1)} %shard_map.67.refs_1_, bf16[256,512]{1,0:T(8,128)(2,1)S(1)} %shard_map.68.refs_2_, ...), custom_call_target="tpu_custom_call" | custom-call | tf_op jit(solution)/shard_map/pallas_call | solution.py:293
  190.3 2.7 %collective-permute-start.34 = (bf16[128,1024]{1,0:T(8,128)(2,1)S(1)}, bf16[128,1024]{1,0:T(8,128)(2,1)S(1)}, u32[]{:S(2)}, u32[]{:S(2)}) collective-permute-start(bf16[128,1024]{1,0:T(8,128)(2,1)S(1)} %get-tuple-element.102), channel_id=1, source_target_pairs={{0,48},{1,49},{2,50},{3,51},{4,52},{5,53},{6,54},{7,55},{8,56},{9,... | collective-permute-start | bytes 786440 | tf_op jit(solution)/shard_map/ppermute | solution.py:41
  203.1 6.8 %collective-permute-done.30 = bf16[256,1024]{1,0:T(8,128)(2,1)S(1)} collective-permute-done((bf16[256,1024]{1,0:T(8,128)(2,1)S(1)}, bf16[256,1024]{1,0:T(8,128)(2,1)S(1)}, u32[]{:S(2)}, u32[]{:S(2)}) %collective-permute-start.30) | collective-permute-done | bytes 524320 | tf_op jit(solution)/shard_map/ppermute | solution.py:41
  213.6 4.4 %collective-permute-start.36 = (bf16[256,512]{1,0:T(8,128)(2,1)S(1)}, bf16[256,512]{1,0:T(8,128)(2,1)S(1)}, u32[]{:S(2)}, u32[]{:S(2)}) collective-permute-start(bf16[256,512]{1,0:T(8,128)(2,1)S(1)} %get-tuple-element.97), channel_id=1, source_target_pairs={{0,0},{1,16},{2,2},{3,18},{4,4},{5,20},{6,6},{7,22},{8,8},{9,24},{... | collective-permute-start | bytes 786440 | tf_op jit(solution)/shard_map/ppermute | solution.py:41
  218.0 8.3 %collective-permute-start.37 = (bf16[256,512]{1,0:T(8,128)(2,1)S(1)}, bf16[256,512]{1,0:T(8,128)(2,1)S(1)}, u32[]{:S(2)}, u32[]{:S(2)}) collective-permute-start(bf16[256,512]{1,0:T(8,128)(2,1)S(1)} %get-tuple-element.98), channel_id=1, source_target_pairs={{0,8},{1,24},{2,10},{3,26},{4,12},{5,28},{6,14},{7,30},{8,0},{9,16... | collective-permute-start | bytes 786440 | tf_op jit(solution)/shard_map/ppermute | solution.py:41
  226.3 9.0 %collective-permute-done.37 = bf16[256,512]{1,0:T(8,128)(2,1)S(1)} collective-permute-done((bf16[256,512]{1,0:T(8,128)(2,1)S(1)}, bf16[256,512]{1,0:T(8,128)(2,1)S(1)}, u32[]{:S(2)}, u32[]{:S(2)}) %collective-permute-start.37) | collective-permute-done | bytes 262176 | tf_op jit(solution)/shard_map/ppermute | solution.py:41
  (170 shorter events, 101.4 us)
Async XLA Ops:
  6.5 137.7 %all-gather.3.cloned.1.call-start = ((), (), s32[]{:S(2)}) async-start(), calls=%async_computation | async-start | bytes 5242880 | tf_op jit(solution)/shard_map/all_gather | solution.py:393
  9.3 10.4 %collective-permute-start = (bf16[256,512]{1,0:T(8,128)(2,1)}, bf16[256,512]{1,0:T(8,128)(2,1)}, u32[]{:S(2)}, u32[]{:S(2)}) collective-permute-start(bf16[256,512]{1,0:T(8,128)(2,1)} %get-tuple-element.103), channel_id=1, source_target_pairs={{0,0},{1,1},{2,32},{3,33},{4,64},{5,65},{6,96},{7,97},{8,8},{9,9},... | collective-permute-start | bytes 786440 | tf_op jit(solution)/shard_map/ppermute | solution.py:41
  21.9 21.1 %collective-permute-start.3 = (bf16[256,1024]{1,0:T(8,128)(2,1)}, bf16[256,1024]{1,0:T(8,128)(2,1)}, u32[]{:S(2)}, u32[]{:S(2)}) collective-permute-start(bf16[256,1024]{1,0:T(8,128)(2,1)} %maximum_select_fusion), channel_id=1, source_target_pairs={{0,16},{1,17},{2,18},{3,19},{4,20},{5,21},{6,22},{7,23},{8,24},{9,... | collective-permute-start | bytes 1572872 | tf_op jit(solution)/shard_map/ppermute | solution.py:41
  31.0 14.0 %collective-permute-start.4 = (bf16[256,1024]{1,0:T(8,128)(2,1)}, bf16[256,1024]{1,0:T(8,128)(2,1)}, u32[]{:S(2)}, u32[]{:S(2)}) collective-permute-start(bf16[256,1024]{1,0:T(8,128)(2,1)} %maximum_select_fusion), channel_id=1, source_target_pairs={{0,48},{1,49},{2,50},{3,51},{4,52},{5,53},{6,54},{7,55},{8,56},{9,... | collective-permute-start | bytes 1572872 | tf_op jit(solution)/shard_map/ppermute | solution.py:41
  31.0 16.6 %collective-permute-start.5 = (bf16[256,1024]{1,0:T(8,128)(2,1)}, bf16[256,1024]{1,0:T(8,128)(2,1)}, u32[]{:S(2)}, u32[]{:S(2)}) collective-permute-start(bf16[256,1024]{1,0:T(8,128)(2,1)} %maximum_select_fusion), channel_id=1, source_target_pairs={{0,64},{1,65},{2,66},{3,67},{4,68},{5,69},{6,70},{7,71},{8,72},{9,... | collective-permute-start | bytes 1572872 | tf_op jit(solution)/shard_map/ppermute | solution.py:41
  47.6 32.4 %collective-permute-start.15 = (bf16[1024,640]{1,0:T(8,128)(2,1)}, bf16[1024,640]{1,0:T(8,128)(2,1)}, u32[]{:S(2)}, u32[]{:S(2)}) collective-permute-start(bf16[1024,640]{1,0:T(8,128)(2,1)} %pad_maximum_fusion), channel_id=1, source_target_pairs={{0,1},{1,0},{2,3},{3,2},{4,5},{5,4},{6,7},{7,6},{8,9},{9,8},{10,11... | collective-permute-start | bytes 3932168 | tf_op jit(solution)/shard_map/ppermute | solution.py:41
  54.3 13.4 %collective-permute-start.6 = (bf16[256,1024]{1,0:T(8,128)(2,1)}, bf16[256,1024]{1,0:T(8,128)(2,1)S(1)}, u32[]{:S(2)}, u32[]{:S(2)}) collective-permute-start(bf16[256,1024]{1,0:T(8,128)(2,1)} %collective-permute-done.5), channel_id=1, source_target_pairs={{0,16},{1,17},{2,18},{3,19},{4,20},{5,21},{6,22},{7,23},{8,24},{9,... | collective-permute-start | bytes 1572872 | tf_op jit(solution)/shard_map/ppermute | solution.py:41
  55.5 12.5 %collective-permute-start.7 = (bf16[256,1024]{1,0:T(8,128)(2,1)}, bf16[256,1024]{1,0:T(8,128)(2,1)S(1)}, u32[]{:S(2)}, u32[]{:S(2)}) collective-permute-start(bf16[256,1024]{1,0:T(8,128)(2,1)} %collective-permute-done.5), channel_id=1, source_target_pairs={{0,48},{1,49},{2,50},{3,51},{4,52},{5,53},{6,54},{7,55},{8,56},{9,... | collective-permute-start | bytes 1572872 | tf_op jit(solution)/shard_map/ppermute | solution.py:41
  80.0 18.5 %collective-permute-start.16 = (bf16[1024,640]{1,0:T(8,128)(2,1)}, bf16[1024,640]{1,0:T(8,128)(2,1)}, u32[]{:S(2)}, u32[]{:S(2)}) collective-permute-start(bf16[1024,640]{1,0:T(8,128)(2,1)} %collective-permute-done.15.far), channel_id=1, source_target_pairs={{0,8},{1,9},{2,10},{3,11},{4,12},{5,13},{6,14},{7,15},{8,0},{9,1},... | collective-permute-start | bytes 3932168 | tf_op jit(solution)/shard_map/ppermute | solution.py:41
  116.4 11.0 %collective-permute-start.20 = (bf16[128,1280]{1,0:T(8,128)(2,1)}, bf16[128,1280]{1,0:T(8,128)(2,1)S(1)}, u32[]{:S(2)}, u32[]{:S(2)}) collective-permute-start(bf16[128,1280]{1,0:T(8,128)(2,1)} %get-tuple-element.72), channel_id=1, source_target_pairs={{0,2},{1,3},{2,4},{3,5},{4,6},{5,7},{6,0},{7,1},{8,10},{9,11},{10,... | collective-permute-start | bytes 983048 | tf_op jit(solution)/shard_map/ppermute | solution.py:41
  116.4 11.0 %collective-permute-start.21 = (bf16[128,1280]{1,0:T(8,128)(2,1)}, bf16[128,1280]{1,0:T(8,128)(2,1)S(1)}, u32[]{:S(2)}, u32[]{:S(2)}) collective-permute-start(bf16[128,1280]{1,0:T(8,128)(2,1)} %get-tuple-element.73), channel_id=1, source_target_pairs={{0,6},{1,7},{2,0},{3,1},{4,2},{5,3},{6,4},{7,5},{8,14},{9,15},{10,... | collective-permute-start | bytes 983048 | tf_op jit(solution)/shard_map/ppermute | solution.py:41
  123.9 11.2 %collective-permute-start.19 = (bf16[128,1280]{1,0:T(8,128)(2,1)}, bf16[128,1280]{1,0:T(8,128)(2,1)S(1)}, u32[]{:S(2)}, u32[]{:S(2)}) collective-permute-start(bf16[128,1280]{1,0:T(8,128)(2,1)} %get-tuple-element.71), channel_id=1, source_target_pairs={{0,2},{1,3},{2,4},{3,5},{4,6},{5,7},{6,0},{7,1},{8,10},{9,11},{10,... | collective-permute-start | bytes 983048 | tf_op jit(solution)/shard_map/ppermute | solution.py:41
  123.9 11.2 %collective-permute-start.22 = (bf16[128,1280]{1,0:T(8,128)(2,1)}, bf16[128,1280]{1,0:T(8,128)(2,1)S(1)}, u32[]{:S(2)}, u32[]{:S(2)}) collective-permute-start(bf16[128,1280]{1,0:T(8,128)(2,1)} %get-tuple-element.74), channel_id=1, source_target_pairs={{0,6},{1,7},{2,0},{3,1},{4,2},{5,3},{6,4},{7,5},{8,14},{9,15},{10,... | collective-permute-start | bytes 983048 | tf_op jit(solution)/shard_map/ppermute | solution.py:41
  144.3 21.9 %collective-permute-start.26 = (bf16[4,512,1024]{2,1,0:T(8,128)(2,1)}, bf16[4,512,1024]{2,1,0:T(8,128)(2,1)}, u32[]{:S(2)}, u32[]{:S(2)}) collective-permute-start(bf16[4,512,1024]{2,1,0:T(8,128)(2,1)} %bitcast.46), channel_id=1, source_target_pairs={{0,8},{1,9},{2,10},{3,11},{4,12},{5,13},{6,14},{7,15},{8,0},{9,1},... | collective-permute-start | bytes 12582920 | tf_op jit(solution)/shard_map/ppermute | solution.py:41
  151.2 9.3 %collective-permute-start.25 = (bf16[256,512]{1,0:T(8,128)(2,1)S(1)}, bf16[256,512]{1,0:T(8,128)(2,1)S(1)}, u32[]{:S(2)}, u32[]{:S(2)}) collective-permute-start(bf16[256,512]{1,0:T(8,128)(2,1)S(1)} %shard_map.68.refs_2_), channel_id=1, source_target_pairs={{0,1},{1,0},{2,3},{3,2},{4,5},{5,4},{6,7},{7,6},{8,9},{9,8},{10,11... | collective-permute-start | bytes 786440 | tf_op jit(solution)/shard_map/ppermute | solution.py:41
  156.0 10.2 %collective-permute-start.24 = (bf16[256,512]{1,0:T(8,128)(2,1)S(1)}, bf16[256,512]{1,0:T(8,128)(2,1)S(1)}, u32[]{:S(2)}, u32[]{:S(2)}) collective-permute-start(bf16[256,512]{1,0:T(8,128)(2,1)S(1)} %shard_map.67.refs_1_), channel_id=1, source_target_pairs={{0,1},{1,0},{2,3},{3,2},{4,5},{5,4},{6,7},{7,6},{8,9},{9,8},{10,11... | collective-permute-start | bytes 786440 | tf_op jit(solution)/shard_map/ppermute | solution.py:41
  172.5 16.5 %collective-permute-start.27 = (bf16[256,1024]{1,0:T(8,128)(2,1)}, bf16[256,1024]{1,0:T(8,128)(2,1)}, u32[]{:S(2)}, u32[]{:S(2)}) collective-permute-start(bf16[256,1024]{1,0:T(8,128)(2,1)} %get-tuple-element.84), channel_id=1, source_target_pairs={{0,16},{1,17},{2,18},{3,19},{4,20},{5,21},{6,22},{7,23},{8,24},{9,... | collective-permute-start | bytes 1572872 | tf_op jit(solution)/shard_map/ppermute | solution.py:41
  174.1 14.9 %collective-permute-start.28 = (bf16[256,1024]{1,0:T(8,128)(2,1)S(1)}, bf16[256,1024]{1,0:T(8,128)(2,1)}, u32[]{:S(2)}, u32[]{:S(2)}) collective-permute-start(bf16[256,1024]{1,0:T(8,128)(2,1)S(1)} %get-tuple-element.85), channel_id=1, source_target_pairs={{0,48},{1,49},{2,50},{3,51},{4,52},{5,53},{6,54},{7,55},{8,56},{9,... | collective-permute-start | bytes 1572872 | tf_op jit(solution)/shard_map/ppermute | solution.py:41
  180.0 16.0 %collective-permute-start.32 = (bf16[128,1024]{1,0:T(8,128)(2,1)S(1)}, bf16[128,1024]{1,0:T(8,128)(2,1)S(1)}, u32[]{:S(2)}, u32[]{:S(2)}) collective-permute-start(bf16[128,1024]{1,0:T(8,128)(2,1)S(1)} %get-tuple-element.94), channel_id=1, source_target_pairs={{0,16},{1,17},{2,18},{3,19},{4,20},{5,21},{6,22},{7,23},{8,24},{9,... | collective-permute-start | bytes 786440 | tf_op jit(solution)/shard_map/ppermute | solution.py:41
  181.8 14.2 %collective-permute-start.33 = (bf16[128,1024]{1,0:T(8,128)(2,1)S(1)}, bf16[128,1024]{1,0:T(8,128)(2,1)S(1)}, u32[]{:S(2)}, u32[]{:S(2)}) collective-permute-start(bf16[128,1024]{1,0:T(8,128)(2,1)S(1)} %get-tuple-element.95), channel_id=1, source_target_pairs={{0,48},{1,49},{2,50},{3,51},{4,52},{5,53},{6,54},{7,55},{8,56},{9,... | collective-permute-start | bytes 786440 | tf_op jit(solution)/shard_map/ppermute | solution.py:41
  194.5 15.4 %collective-permute-start.30 = (bf16[256,1024]{1,0:T(8,128)(2,1)S(1)}, bf16[256,1024]{1,0:T(8,128)(2,1)S(1)}, u32[]{:S(2)}, u32[]{:S(2)}) collective-permute-start(bf16[256,1024]{1,0:T(8,128)(2,1)S(1)} %get-tuple-element.101), channel_id=1, source_target_pairs={{0,48},{1,49},{2,50},{3,51},{4,52},{5,53},{6,54},{7,55},{8,56},{9,... | collective-permute-start | bytes 1572872 | tf_op jit(solution)/shard_map/ppermute | solution.py:41
  196.0 15.2 %collective-permute-start.29 = (bf16[256,1024]{1,0:T(8,128)(2,1)S(1)}, bf16[256,1024]{1,0:T(8,128)(2,1)S(1)}, u32[]{:S(2)}, u32[]{:S(2)}) collective-permute-start(bf16[256,1024]{1,0:T(8,128)(2,1)S(1)} %get-tuple-element.99), channel_id=1, source_target_pairs={{0,16},{1,17},{2,18},{3,19},{4,20},{5,21},{6,22},{7,23},{8,24},{9,... | collective-permute-start | bytes 1572872 | tf_op jit(solution)/shard_map/ppermute | solution.py:41
  213.6 12.7 %collective-permute-start.36 = (bf16[256,512]{1,0:T(8,128)(2,1)S(1)}, bf16[256,512]{1,0:T(8,128)(2,1)S(1)}, u32[]{:S(2)}, u32[]{:S(2)}) collective-permute-start(bf16[256,512]{1,0:T(8,128)(2,1)S(1)} %get-tuple-element.97), channel_id=1, source_target_pairs={{0,0},{1,16},{2,2},{3,18},{4,4},{5,20},{6,6},{7,22},{8,8},{9,24},{... | collective-permute-start | bytes 786440 | tf_op jit(solution)/shard_map/ppermute | solution.py:41
  218.0 17.3 %collective-permute-start.37 = (bf16[256,512]{1,0:T(8,128)(2,1)S(1)}, bf16[256,512]{1,0:T(8,128)(2,1)S(1)}, u32[]{:S(2)}, u32[]{:S(2)}) collective-permute-start(bf16[256,512]{1,0:T(8,128)(2,1)S(1)} %get-tuple-element.98), channel_id=1, source_target_pairs={{0,8},{1,24},{2,10},{3,26},{4,12},{5,28},{6,14},{7,30},{8,0},{9,16... | collective-permute-start | bytes 786440 | tf_op jit(solution)/shard_map/ppermute | solution.py:41
  (47 other events, 315.5 us)
Sparse Core Ops, SparseCore 0:
  22.0 58.6 all-gather.2

commit v12 on v10

--- a/solution.py
+++ b/solution.py
@@ -205,9 +205,6 @@
     def put(start, near_part, far_part):
         cols = slice(start, start + near_part.shape[1])
         value = (dot(near_rows, near_part) + dot(far_rows, far_part)).astype(jnp.bfloat16)
-        if len(outs) == 1:
-            outs[0][:, cols] = value
-            return
         for i in range(len(outs) // 2):
 
             @pl.when(step == i)
@@ -215,6 +212,12 @@
                 outs[2 * i][:, cols] = value[:128]
                 outs[2 * i + 1][:, cols] = value[128:]
 
+        if len(outs) % 2:
+
+            @pl.when(step == len(outs) // 2)
+            def _():
+                outs[-1][:, cols] = value
+
     def kv_cols(which):
         return near_kv[:, pl.ds(pl.multiple_of(which * HEAD_SIZE, HEAD_SIZE), HEAD_SIZE)]
 
@@ -224,9 +227,9 @@
     put(WIDE + 512, kv_cols(1 - core), far_other[:, 512:])
 
 
-def project(which, zh, core, gathered, weights, halves=False):
+def project(which, zh, core, gathered, weights, whole_last=False):
     steps = len(which)
-    rows, outs = (128, 2 * steps) if halves else (HALF, 1)
+    rows = [128] * 2 * steps if not whole_last else [128] * 2 * (steps - 1) + [HALF]
     return pl.pallas_call(
         project_kernel,
         grid_spec=pltpu.PrefetchScalarGridSpec(
@@ -234,11 +237,23 @@
             grid=(steps,),
             in_specs=[pl.BlockSpec((1, HALF, 2048), lambda i, at: (at[2 + i], 0, 0))]
             + [pl.BlockSpec(w.shape, lambda i, at: (0, 0)) for w in weights],
-            out_specs=[pl.BlockSpec((rows, 2 * WIDE), lambda i, at: (0, 0))] * outs,
+            out_specs=[pl.BlockSpec((r, 2 * WIDE), lambda i, at: (0, 0)) for r in rows],
         ),
-        out_shape=[jax.ShapeDtypeStruct((rows, 2 * WIDE), jnp.bfloat16)] * outs,
+        out_shape=[jax.ShapeDtypeStruct((r, 2 * WIDE), jnp.bfloat16) for r in rows],
         compiler_params=GRANT,
     )(jnp.stack([zh, core, *which]).astype(jnp.int32), gathered, *weights)
+
+
+def two_sums_kernel(a, b, c, d, first, second):
+    for left, right, out in ((a, b, first), (c, d, second)):
+        out[...] = (left[...].astype(jnp.float32) + right[...].astype(jnp.float32)).astype(
+            jnp.bfloat16
+        )
+
+
+def two_sums(a, b, c, d):
+    shape = jax.ShapeDtypeStruct(a.shape, jnp.bfloat16)
+    return pl.pallas_call(two_sums_kernel, out_shape=[shape, shape])(a, b, c, d)
 
 
 def products_kernel(form, steps, at_ref, own_a, own_b, far_a, far_b, near, other, *outs):
@@ -375,19 +390,18 @@
 
     squares = jnp.sum(jnp.square(gathered.astype(jnp.float32) * slice_gain), axis=-1)
     gathered, squares = lax.optimization_barrier((gathered, squares))
-    low, high = project([(y + 2) % 4], zh, core, gathered, weights, True)
+    low, high = project([(y + 2) % 4], zh, core, gathered, weights)
     from_below = y_shift(low, 1)
     from_above = y_shift(high, -1)
-    a_top, a_bottom, b_top, b_bottom = project(
-        [(y + 1) % 4, (y + 3) % 4], zh, core, gathered, weights, True
+    a_top, a_bottom, b_top, b_bottom, kept = project(
+        [(y + 1) % 4, (y + 3) % 4, y], zh, core, gathered, weights, True
     )
     from_below, from_above, a_top, b_bottom = lax.optimization_barrier(
         (from_below, from_above, a_top, b_bottom)
     )
     a_bottom, b_top = y_shift(a_bottom, 1), y_shift(b_top, -1)
-    a_top, b_bottom = a_top + from_below, b_bottom + from_above
-    gathered = after(gathered, (a_top, b_bottom, a_bottom, b_top))
-    (kept,) = project([y], zh, core, gathered, weights)
+    a_top, b_bottom = two_sums(a_top, from_below, b_bottom, from_above)
+    squares, a_bottom, b_top = lax.optimization_barrier((squares, a_bottom, b_top))
     sums = (kept, y_shift(a_top, 1), a_bottom, b_top, y_shift(b_bottom, -1))
 
     squares, a_top, b_bottom = lax.optimization_barrier((squares, a_top, b_bottom))

time: 223 us -> 231 us (1.036)
  waiting for transfers between devices: 58.4 us -> 67.6 us
  other arithmetic: 17.3 us -> 13.2 us
  starting transfers between devices: 65.4 us -> 69.1 us
    ppermute x38, waiting for transfers between devices: 58.4 us -> 67.6 us  [send(): return lax.ppermute(value, AXES, pairs(change))]
    ppermute x38, starting transfers between devices: 65.4 us -> 69.1 us  [send(): return lax.ppermute(value, AXES, pairs(change))]
    add x2 -> x0, other arithmetic: 3.75 us -> none  [local(): a_top, b_bottom = (a_top + from_below, b_bottom + from_above)]
    unnamed x71 -> x77, local copies, waits for them, and re-layouts: 19.9 us -> 19.4 us
    pallas_call x3 -> x2, Pallas kernels: 11.5 us -> 11.6 us  [project(): pl.pallas_call(project_kernel, grid_spec=pltpu.PrefetchScalarGridSpec(num...]
  transfers between devices with their start and end apart: 39 -> 39, of which waited for: 17 -> 18; matrix products, arithmetic and copies ran while one was open for 11% -> 8% of each run, Pallas kernels for 14% -> 13%
where the time goes in v12:
time: 231 us; the launch traced here: 230 us
  starting transfers between devices  69.1 us (30%)
  waiting for transfers between devices  67.6 us (29%)
  Pallas kernels  34.8 us (15%)
  local copies, waits for them, and re-layouts  30.3 us (13%)
  between operations  14.7 us (6%)
  other arithmetic  13.2 us (6%)
    ppermute x38, starting transfers between devices, send(): return lax.ppermute(value, AXES, pairs(change))  69.1 us
    ppermute x38, waiting for transfers between devices, send(): return lax.ppermute(value, AXES, pairs(change))  67.6 us
    unnamed x77, local copies, waits for them, and re-layouts  19.4 us
    pallas_call x3, Pallas kernels, products(): pl.pallas_call(lambda *refs: products_kernel(form, steps, *refs), grid_sp...  13.1 us
    pallas_call x2, Pallas kernels, project(): pl.pallas_call(project_kernel, grid_spec=pltpu.PrefetchScalarGridSpec(num...  11.6 us
  transfers between devices with their start and end apart: 39, of which 18 were waited for; matrix products, arithmetic and copies ran while one was open for 8% of the time, Pallas kernels for 13%

profile of v12, /device:TPU:3, one launch (start us, length us, event | category | flops | bytes accessed | tf_op | source)
XLA Modules:
  0.0 229.7 jit_solution(16859499338264296406)
XLA Ops:
  10.0 3.6 %collective-permute-start = (bf16[256,512]{1,0:T(8,128)(2,1)}, bf16[256,512]{1,0:T(8,128)(2,1)}, u32[]{:S(2)}, u32[]{:S(2)}) collective-permute-start(bf16[256,512]{1,0:T(8,128)(2,1)} %get-tuple-element.109), channel_id=1, source_target_pairs={{0,0},{1,1},{2,32},{3,33},{4,64},{5,65},{6,96},{7,97},{8,8},{9,9},... | collective-permute-start | bytes 786440 | tf_op jit(solution)/shard_map/ppermute | solution.py:41
  22.1 8.0 %collective-permute-start.3 = (bf16[256,1024]{1,0:T(8,128)(2,1)}, bf16[256,1024]{1,0:T(8,128)(2,1)S(1)}, u32[]{:S(2)}, u32[]{:S(2)}) collective-permute-start(bf16[256,1024]{1,0:T(8,128)(2,1)} %maximum_select_fusion), channel_id=1, source_target_pairs={{0,16},{1,17},{2,18},{3,19},{4,20},{5,21},{6,22},{7,23},{8,24},{9,... | collective-permute-start | bytes 1572872 | tf_op jit(solution)/shard_map/ppermute | solution.py:41
  30.0 3.7 %collective-permute-start.5 = (bf16[256,1024]{1,0:T(8,128)(2,1)}, bf16[256,1024]{1,0:T(8,128)(2,1)}, u32[]{:S(2)}, u32[]{:S(2)}) collective-permute-start(bf16[256,1024]{1,0:T(8,128)(2,1)} %maximum_select_fusion), channel_id=1, source_target_pairs={{0,64},{1,65},{2,66},{3,67},{4,68},{5,69},{6,70},{7,71},{8,72},{9,... | collective-permute-start | bytes 1572872 | tf_op jit(solution)/shard_map/ppermute | solution.py:41
  33.8 7.5 %collective-permute-done.3 = bf16[256,1024]{1,0:T(8,128)(2,1)S(1)} collective-permute-done((bf16[256,1024]{1,0:T(8,128)(2,1)}, bf16[256,1024]{1,0:T(8,128)(2,1)S(1)}, u32[]{:S(2)}, u32[]{:S(2)}) %collective-permute-start.3) | collective-permute-done | bytes 524320 | tf_op jit(solution)/shard_map/ppermute | solution.py:41
  45.8 3.3 %collective-permute-start.12 = (bf16[1024,640]{1,0:T(8,128)(2,1)}, bf16[1024,640]{1,0:T(8,128)(2,1)S(1)}, u32[]{:S(2)}, u32[]{:S(2)}) collective-permute-start(bf16[1024,640]{1,0:T(8,128)(2,1)} %pad_maximum_fusion), channel_id=1, source_target_pairs={{0,1},{1,0},{2,3},{3,2},{4,5},{5,4},{6,7},{7,6},{8,9},{9,8},{10,11... | collective-permute-start | bytes 3932168 | tf_op jit(solution)/shard_map/ppermute | solution.py:41
  55.0 6.5 %collective-permute-done.8 = bf16[256,1024]{1,0:T(8,128)(2,1)} collective-permute-done((bf16[256,1024]{1,0:T(8,128)(2,1)}, bf16[256,1024]{1,0:T(8,128)(2,1)}, u32[]{:S(2)}, u32[]{:S(2)}) %collective-permute-start.8) | collective-permute-done | bytes 524320 | tf_op jit(solution)/shard_map/ppermute | solution.py:41
  66.3 6.2 %collective-permute-done.10 = bf16[128,1024]{1,0:T(8,128)(2,1)S(1)} collective-permute-done((bf16[128,1024]{1,0:T(8,128)(2,1)S(1)}, bf16[128,1024]{1,0:T(8,128)(2,1)S(1)}, u32[]{:S(2)}, u32[]{:S(2)}) %collective-permute-start.10) | collective-permute-done | bytes 262176 | tf_op jit(solution)/shard_map/ppermute | solution.py:41
  72.9 4.2 %collective-permute-done.12.far = bf16[1024,640]{1,0:T(8,128)(2,1)S(1)} collective-permute-done((bf16[1024,640]{1,0:T(8,128)(2,1)}, bf16[1024,640]{1,0:T(8,128)(2,1)S(1)}, u32[]{:S(2)}, u32[]{:S(2)}) %collective-permute-start.12) | collective-permute-done | bytes 1310752 | tf_op jit(solution)/shard_map/ppermute | solution.py:41
  83.8 3.2 %shard_map.65 = (bf16[128,1280]{1,0:T(8,128)(2,1)}, bf16[128,1280]{1,0:T(8,128)(2,1)}) custom-call(s32[3]{0:T(128)S(1)} %pad_add_fusion.1.at_ref, bf16[4,256,2048]{2,1,0:T(8,128)(2,1)S(1)} %bitcast_dynamic-update-slice_fusion.rows_ref, bf16[1024,512]{1,0:T(8,128)(2,1)S(1)} %copy-done.6, bf16[1024,512]{1,0:T(8,128)(2,1)S(1)} %copy-done.18, ...), custom_call_target="tpu_custom_call" | custom-call | tf_op jit(solution)/shard_map/pallas_call | solution.py:233
  87.0 2.9 %collective-permute-start.15 = (bf16[128,1280]{1,0:T(8,128)(2,1)}, bf16[128,1280]{1,0:T(8,128)(2,1)}, u32[]{:S(2)}, u32[]{:S(2)}) collective-permute-start(bf16[128,1280]{1,0:T(8,128)(2,1)} %get-tuple-element.68), channel_id=1, source_target_pairs={{0,6},{1,7},{2,0},{3,1},{4,2},{5,3},{6,4},{7,5},{8,14},{9,15},{10,... | collective-permute-start | bytes 983048 | tf_op jit(solution)/shard_map/ppermute | solution.py:41
  94.7 8.4 %shard_map.64 = (bf16[128,1280]{1,0:T(8,128)(2,1)S(1)}, bf16[128,1280]{1,0:T(8,128)(2,1)}, bf16[128,1280]{1,0:T(8,128)(2,1)}, bf16[128,1280]{1,0:T(8,128)(2,1)S(1)}, bf16[256,1280]{1,0:T(8,128)(2,1)S(1)}) custom-call(s32[5]{0:T(128)S(1)} %stack.103.at_ref, bf16[4,256,2048]{2,1,0:T(8,128)(2,1)S(1)} %copy-done.1, bf16[1024,512]{1,0:T(8,128)(2,1)S(1)} %copy-done.6, ...), custom_call_target="tpu_custom_call" | custom-call | tf_op jit(solution)/shard_map/pallas_call | solution.py:233
  110.2 5.5 %collective-permute-done.17.refs_2_.refs_7_ = bf16[128,1280]{1,0:T(8,128)(2,1)S(1)} collective-permute-done((bf16[128,1280]{1,0:T(8,128)(2,1)}, bf16[128,1280]{1,0:T(8,128)(2,1)S(1)}, u32[]{:S(2)}, u32[]{:S(2)}) %collective-permute-start.17) | collective-permute-done | bytes 327712 | tf_op jit(solution)/shard_map/ppermute | solution.py:41
  119.7 4.3 %collective-permute-done.22 = f32[256]{0:T(256)S(1)} collective-permute-done((f32[256]{0:T(256)S(1)}, f32[256]{0:T(256)S(1)}, u32[]{:S(2)}, u32[]{:S(2)}) %collective-permute-start.22) | collective-permute-done | bytes 1056 | tf_op jit(solution)/shard_map/ppermute | solution.py:41
  127.7 2.8 %collective-permute-start.23 = (bf16[256,256]{1,0:T(8,128)(2,1)}, bf16[256,256]{1,0:T(8,128)(2,1)S(1)}, u32[]{:S(2)}, u32[]{:S(2)}) collective-permute-start(bf16[256,256]{1,0:T(8,128)(2,1)} %shard_map.67.refs_9_), channel_id=1, source_target_pairs={{0,8},{1,9},{2,10},{3,11},{4,12},{5,13},{6,14},{7,15},{8,0},{9,1},... | collective-permute-start | bytes 393224 | tf_op jit(solution)/shard_map/ppermute | solution.py:41
  138.6 3.0 %collective-permute-start.24 = (bf16[256,512]{1,0:T(8,128)(2,1)S(1)}, bf16[256,512]{1,0:T(8,128)(2,1)S(1)}, u32[]{:S(2)}, u32[]{:S(2)}) collective-permute-start(bf16[256,512]{1,0:T(8,128)(2,1)S(1)} %shard_map.68.refs_1_), channel_id=1, source_target_pairs={{0,1},{1,0},{2,3},{3,2},{4,5},{5,4},{6,7},{7,6},{8,9},{9,8},{10,11... | collective-permute-start | bytes 786440 | tf_op jit(solution)/shard_map/ppermute | solution.py:41
  144.5 3.5 %collective-permute-done.24.refs_3_ = bf16[256,512]{1,0:T(8,128)(2,1)S(1)} collective-permute-done((bf16[256,512]{1,0:T(8,128)(2,1)S(1)}, bf16[256,512]{1,0:T(8,128)(2,1)S(1)}, u32[]{:S(2)}, u32[]{:S(2)}) %collective-permute-start.24) | collective-permute-done | bytes 262176 | tf_op jit(solution)/shard_map/ppermute | solution.py:41
  147.9 5.4 %collective-permute-done.25.refs_4_ = bf16[256,512]{1,0:T(8,128)(2,1)S(1)} collective-permute-done((bf16[256,512]{1,0:T(8,128)(2,1)S(1)}, bf16[256,512]{1,0:T(8,128)(2,1)S(1)}, u32[]{:S(2)}, u32[]{:S(2)}) %collective-permute-start.25) | collective-permute-done | bytes 262176 | tf_op jit(solution)/shard_map/ppermute | solution.py:41
  155.5 4.3 %shard_map.71 = (bf16[256,1024]{1,0:T(8,128)(2,1)}, bf16[256,1024]{1,0:T(8,128)(2,1)}) custom-call(s32[4]{0:T(128)S(1)} %get-tuple-element.118.refs_0_, bf16[256,512]{1,0:T(8,128)(2,1)S(1)} %shard_map.68.refs_1_, bf16[256,512]{1,0:T(8,128)(2,1)S(1)} %shard_map.69.refs_2_, bf16[256,512]{1,0:T(8,128)(2,1)S(1)} %collective-permute-done.24.refs_3_, ...), custom_call_target="tpu_custom_call" | custom-call | tf_op jit(solution)/shard_map/pallas_call | solution.py:296
  163.7 3.3 %shard_map.72 = (bf16[128,1024]{1,0:T(8,128)(2,1)S(1)}, bf16[128,1024]{1,0:T(8,128)(2,1)S(1)}, bf16[128,1024]{1,0:T(8,128)(2,1)S(1)}, bf16[128,1024]{1,0:T(8,128)(2,1)S(1)}) custom-call(s32[4]{0:T(128)S(1)} %get-tuple-element.119.refs_0_, bf16[256,512]{1,0:T(8,128)(2,1)S(1)} %shard_map.68.refs_1_, bf16[256,512]{1,0:T(8,128)(2,1)S(1)} %shard_map.69.refs_2_, ...), custom_call_target="tpu_custom_call" | custom-call | tf_op jit(solution)/shard_map/pallas_call | solution.py:296
  170.1 5.4 %shard_map.70 = (bf16[256,1024]{1,0:T(8,128)(2,1)S(1)}, bf16[256,1024]{1,0:T(8,128)(2,1)S(1)}, bf16[256,1024]{1,0:T(8,128)(2,1)S(1)}, bf16[256,1024]{1,0:T(8,128)(2,1)S(1)}) custom-call(s32[8]{0:T(128)S(1)} %stack.97.refs_0_, bf16[256,512]{1,0:T(8,128)(2,1)S(1)} %shard_map.68.refs_1_, bf16[256,512]{1,0:T(8,128)(2,1)S(1)} %shard_map.69.refs_2_, ...), custom_call_target="tpu_custom_call" | custom-call | tf_op jit(solution)/shard_map/pallas_call | solution.py:296
  188.7 6.7 %collective-permute-done.30 = bf16[256,1024]{1,0:T(8,128)(2,1)S(1)} collective-permute-done((bf16[256,1024]{1,0:T(8,128)(2,1)S(1)}, bf16[256,1024]{1,0:T(8,128)(2,1)S(1)}, u32[]{:S(2)}, u32[]{:S(2)}) %collective-permute-start.30) | collective-permute-done | bytes 524320 | tf_op jit(solution)/shard_map/ppermute | solution.py:41
  197.7 12.1 %collective-permute-start.37 = (bf16[256,512]{1,0:T(8,128)(2,1)S(1)}, bf16[256,512]{1,0:T(8,128)(2,1)S(1)}, u32[]{:S(2)}, u32[]{:S(2)}) collective-permute-start(bf16[256,512]{1,0:T(8,128)(2,1)S(1)} %get-tuple-element.104), channel_id=1, source_target_pairs={{0,8},{1,24},{2,10},{3,26},{4,12},{5,28},{6,14},{7,30},{8,0},{9,16... | collective-permute-start | bytes 786440 | tf_op jit(solution)/shard_map/ppermute | solution.py:41
  211.7 4.4 %collective-permute-done.37 = bf16[256,512]{1,0:T(8,128)(2,1)S(1)} collective-permute-done((bf16[256,512]{1,0:T(8,128)(2,1)S(1)}, bf16[256,512]{1,0:T(8,128)(2,1)S(1)}, u32[]{:S(2)}, u32[]{:S(2)}) %collective-permute-start.37) | collective-permute-done | bytes 262176 | tf_op jit(solution)/shard_map/ppermute | solution.py:41
  216.2 5.6 %collective-permute-done.36 = bf16[256,512]{1,0:T(8,128)(2,1)S(1)} collective-permute-done((bf16[256,512]{1,0:T(8,128)(2,1)S(1)}, bf16[256,512]{1,0:T(8,128)(2,1)S(1)}, u32[]{:S(2)}, u32[]{:S(2)}) %collective-permute-start.36) | collective-permute-done | bytes 262176 | tf_op jit(solution)/shard_map/ppermute | solution.py:41
  (186 shorter events, 90.9 us)
Async XLA Ops:
  6.5 125.1 %all-gather.3.cloned.1.call-start = ((), (), s32[]{:S(2)}) async-start(), calls=%async_computation | async-start | bytes 5242880 | tf_op jit(solution)/shard_map/all_gather | solution.py:389
  9.4 10.5 %collective-permute-start.1 = (bf16[256,512]{1,0:T(8,128)(2,1)}, bf16[256,512]{1,0:T(8,128)(2,1)}, u32[]{:S(2)}, u32[]{:S(2)}) collective-permute-start(bf16[256,512]{1,0:T(8,128)(2,1)} %get-tuple-element.110), channel_id=1, source_target_pairs={{0,8},{1,9},{2,40},{3,41},{4,72},{5,73},{6,104},{7,105},{8,0},{9,1... | collective-permute-start | bytes 786440 | tf_op jit(solution)/shard_map/ppermute | solution.py:41
  22.1 19.2 %collective-permute-start.3 = (bf16[256,1024]{1,0:T(8,128)(2,1)}, bf16[256,1024]{1,0:T(8,128)(2,1)S(1)}, u32[]{:S(2)}, u32[]{:S(2)}) collective-permute-start(bf16[256,1024]{1,0:T(8,128)(2,1)} %maximum_select_fusion), channel_id=1, source_target_pairs={{0,16},{1,17},{2,18},{3,19},{4,20},{5,21},{6,22},{7,23},{8,24},{9,... | collective-permute-start | bytes 1572872 | tf_op jit(solution)/shard_map/ppermute | solution.py:41
  30.0 13.1 %collective-permute-start.4 = (bf16[256,1024]{1,0:T(8,128)(2,1)}, bf16[256,1024]{1,0:T(8,128)(2,1)S(1)}, u32[]{:S(2)}, u32[]{:S(2)}) collective-permute-start(bf16[256,1024]{1,0:T(8,128)(2,1)} %maximum_select_fusion), channel_id=1, source_target_pairs={{0,48},{1,49},{2,50},{3,51},{4,52},{5,53},{6,54},{7,55},{8,56},{9,... | collective-permute-start | bytes 1572872 | tf_op jit(solution)/shard_map/ppermute | solution.py:41
  30.0 15.8 %collective-permute-start.5 = (bf16[256,1024]{1,0:T(8,128)(2,1)}, bf16[256,1024]{1,0:T(8,128)(2,1)}, u32[]{:S(2)}, u32[]{:S(2)}) collective-permute-start(bf16[256,1024]{1,0:T(8,128)(2,1)} %maximum_select_fusion), channel_id=1, source_target_pairs={{0,64},{1,65},{2,66},{3,67},{4,68},{5,69},{6,70},{7,71},{8,72},{9,... | collective-permute-start | bytes 1572872 | tf_op jit(solution)/shard_map/ppermute | solution.py:41
  45.8 31.4 %collective-permute-start.12 = (bf16[1024,640]{1,0:T(8,128)(2,1)}, bf16[1024,640]{1,0:T(8,128)(2,1)S(1)}, u32[]{:S(2)}, u32[]{:S(2)}) collective-permute-start(bf16[1024,640]{1,0:T(8,128)(2,1)} %pad_maximum_fusion), channel_id=1, source_target_pairs={{0,1},{1,0},{2,3},{3,2},{4,5},{5,4},{6,7},{7,6},{8,9},{9,8},{10,11... | collective-permute-start | bytes 3932168 | tf_op jit(solution)/shard_map/ppermute | solution.py:41
  49.1 12.4 %collective-permute-start.8 = (bf16[256,1024]{1,0:T(8,128)(2,1)}, bf16[256,1024]{1,0:T(8,128)(2,1)}, u32[]{:S(2)}, u32[]{:S(2)}) collective-permute-start(bf16[256,1024]{1,0:T(8,128)(2,1)} %collective-permute-done.5), channel_id=1, source_target_pairs={{0,16},{1,17},{2,18},{3,19},{4,20},{5,21},{6,22},{7,23},{8,24},{9,... | collective-permute-start | bytes 1572872 | tf_op jit(solution)/shard_map/ppermute | solution.py:41
  50.2 13.0 %collective-permute-start.9 = (bf16[256,1024]{1,0:T(8,128)(2,1)}, bf16[256,1024]{1,0:T(8,128)(2,1)}, u32[]{:S(2)}, u32[]{:S(2)}) collective-permute-start(bf16[256,1024]{1,0:T(8,128)(2,1)} %collective-permute-done.5), channel_id=1, source_target_pairs={{0,48},{1,49},{2,50},{3,51},{4,52},{5,53},{6,54},{7,55},{8,56},{9,... | collective-permute-start | bytes 1572872 | tf_op jit(solution)/shard_map/ppermute | solution.py:41
  52.1 28.0 %collective-permute-start.7 = (bf16[128,1024]{1,0:T(8,128)(2,1)S(1)}, bf16[128,1024]{1,0:T(8,128)(2,1)S(1)}, u32[]{:S(2)}, u32[]{:S(2)}) collective-permute-start(bf16[128,1024]{1,0:T(8,128)(2,1)S(1)} %slice.31), channel_id=1, source_target_pairs={{0,48},{1,49},{2,50},{3,51},{4,52},{5,53},{6,54},{7,55},{8,56},{9,... | collective-permute-start | bytes 786440 | tf_op jit(solution)/shard_map/ppermute | solution.py:41
  54.9 25.2 %collective-permute-start.6 = (bf16[128,1024]{1,0:T(8,128)(2,1)S(1)}, bf16[128,1024]{1,0:T(8,128)(2,1)S(1)}, u32[]{:S(2)}, u32[]{:S(2)}) collective-permute-start(bf16[128,1024]{1,0:T(8,128)(2,1)S(1)} %slice.30), channel_id=1, source_target_pairs={{0,16},{1,17},{2,18},{3,19},{4,20},{5,21},{6,22},{7,23},{8,24},{9,... | collective-permute-start | bytes 786440 | tf_op jit(solution)/shard_map/ppermute | solution.py:41
  87.0 21.1 %collective-permute-start.14 = (bf16[128,1280]{1,0:T(8,128)(2,1)}, bf16[128,1280]{1,0:T(8,128)(2,1)}, u32[]{:S(2)}, u32[]{:S(2)}) collective-permute-start(bf16[128,1280]{1,0:T(8,128)(2,1)} %get-tuple-element.67), channel_id=1, source_target_pairs={{0,2},{1,3},{2,4},{3,5},{4,6},{5,7},{6,0},{7,1},{8,10},{9,11},{10,... | collective-permute-start | bytes 983048 | tf_op jit(solution)/shard_map/ppermute | solution.py:41
  87.0 21.1 %collective-permute-start.15 = (bf16[128,1280]{1,0:T(8,128)(2,1)}, bf16[128,1280]{1,0:T(8,128)(2,1)}, u32[]{:S(2)}, u32[]{:S(2)}) collective-permute-start(bf16[128,1280]{1,0:T(8,128)(2,1)} %get-tuple-element.68), channel_id=1, source_target_pairs={{0,6},{1,7},{2,0},{3,1},{4,2},{5,3},{6,4},{7,5},{8,14},{9,15},{10,... | collective-permute-start | bytes 983048 | tf_op jit(solution)/shard_map/ppermute | solution.py:41
  105.4 10.4 %collective-permute-start.17 = (bf16[128,1280]{1,0:T(8,128)(2,1)}, bf16[128,1280]{1,0:T(8,128)(2,1)S(1)}, u32[]{:S(2)}, u32[]{:S(2)}) collective-permute-start(bf16[128,1280]{1,0:T(8,128)(2,1)} %get-tuple-element.77), channel_id=1, source_target_pairs={{0,2},{1,3},{2,4},{3,5},{4,6},{5,7},{6,0},{7,1},{8,10},{9,11},{10,... | collective-permute-start | bytes 983048 | tf_op jit(solution)/shard_map/ppermute | solution.py:41
  105.4 10.4 %collective-permute-start.18 = (bf16[128,1280]{1,0:T(8,128)(2,1)}, bf16[128,1280]{1,0:T(8,128)(2,1)S(1)}, u32[]{:S(2)}, u32[]{:S(2)}) collective-permute-start(bf16[128,1280]{1,0:T(8,128)(2,1)} %get-tuple-element.78), channel_id=1, source_target_pairs={{0,6},{1,7},{2,0},{3,1},{4,2},{5,3},{6,4},{7,5},{8,14},{9,15},{10,... | collective-permute-start | bytes 983048 | tf_op jit(solution)/shard_map/ppermute | solution.py:41
  110.2 14.5 %collective-permute-start.16 = (bf16[128,1280]{1,0:T(8,128)(2,1)}, bf16[128,1280]{1,0:T(8,128)(2,1)S(1)}, u32[]{:S(2)}, u32[]{:S(2)}) collective-permute-start(bf16[128,1280]{1,0:T(8,128)(2,1)} %get-tuple-element.75), channel_id=1, source_target_pairs={{0,2},{1,3},{2,4},{3,5},{4,6},{5,7},{6,0},{7,1},{8,10},{9,11},{10,... | collective-permute-start | bytes 983048 | tf_op jit(solution)/shard_map/ppermute | solution.py:41
  131.7 21.6 %collective-permute-start.26 = (bf16[4,512,1024]{2,1,0:T(8,128)(2,1)}, bf16[4,512,1024]{2,1,0:T(8,128)(2,1)}, u32[]{:S(2)}, u32[]{:S(2)}) collective-permute-start(bf16[4,512,1024]{2,1,0:T(8,128)(2,1)} %bitcast.44), channel_id=1, source_target_pairs={{0,8},{1,9},{2,10},{3,11},{4,12},{5,13},{6,14},{7,15},{8,0},{9,1},... | collective-permute-start | bytes 12582920 | tf_op jit(solution)/shard_map/ppermute | solution.py:41
  159.8 15.7 %collective-permute-start.27 = (bf16[256,1024]{1,0:T(8,128)(2,1)}, bf16[256,1024]{1,0:T(8,128)(2,1)}, u32[]{:S(2)}, u32[]{:S(2)}) collective-permute-start(bf16[256,1024]{1,0:T(8,128)(2,1)} %get-tuple-element.90), channel_id=1, source_target_pairs={{0,16},{1,17},{2,18},{3,19},{4,20},{5,21},{6,22},{7,23},{8,24},{9,... | collective-permute-start | bytes 1572872 | tf_op jit(solution)/shard_map/ppermute | solution.py:41
  160.9 14.6 %collective-permute-start.28 = (bf16[256,1024]{1,0:T(8,128)(2,1)}, bf16[256,1024]{1,0:T(8,128)(2,1)}, u32[]{:S(2)}, u32[]{:S(2)}) collective-permute-start(bf16[256,1024]{1,0:T(8,128)(2,1)} %get-tuple-element.91), channel_id=1, source_target_pairs={{0,48},{1,49},{2,50},{3,51},{4,52},{5,53},{6,54},{7,55},{8,56},{9,... | collective-permute-start | bytes 1572872 | tf_op jit(solution)/shard_map/ppermute | solution.py:41
  167.0 16.6 %collective-permute-start.32 = (bf16[128,1024]{1,0:T(8,128)(2,1)S(1)}, bf16[128,1024]{1,0:T(8,128)(2,1)S(1)}, u32[]{:S(2)}, u32[]{:S(2)}) collective-permute-start(bf16[128,1024]{1,0:T(8,128)(2,1)S(1)} %get-tuple-element.100), channel_id=1, source_target_pairs={{0,16},{1,17},{2,18},{3,19},{4,20},{5,21},{6,22},{7,23},{8,24},{9,... | collective-permute-start | bytes 786440 | tf_op jit(solution)/shard_map/ppermute | solution.py:41
  168.5 15.2 %collective-permute-start.33 = (bf16[128,1024]{1,0:T(8,128)(2,1)S(1)}, bf16[128,1024]{1,0:T(8,128)(2,1)S(1)}, u32[]{:S(2)}, u32[]{:S(2)}) collective-permute-start(bf16[128,1024]{1,0:T(8,128)(2,1)S(1)} %get-tuple-element.101), channel_id=1, source_target_pairs={{0,48},{1,49},{2,50},{3,51},{4,52},{5,53},{6,54},{7,55},{8,56},{9,... | collective-permute-start | bytes 786440 | tf_op jit(solution)/shard_map/ppermute | solution.py:41
  181.0 14.4 %collective-permute-start.30 = (bf16[256,1024]{1,0:T(8,128)(2,1)S(1)}, bf16[256,1024]{1,0:T(8,128)(2,1)S(1)}, u32[]{:S(2)}, u32[]{:S(2)}) collective-permute-start(bf16[256,1024]{1,0:T(8,128)(2,1)S(1)} %get-tuple-element.107), channel_id=1, source_target_pairs={{0,48},{1,49},{2,50},{3,51},{4,52},{5,53},{6,54},{7,55},{8,56},{9,... | collective-permute-start | bytes 1572872 | tf_op jit(solution)/shard_map/ppermute | solution.py:41
  183.6 11.8 %collective-permute-start.29 = (bf16[256,1024]{1,0:T(8,128)(2,1)S(1)}, bf16[256,1024]{1,0:T(8,128)(2,1)}, u32[]{:S(2)}, u32[]{:S(2)}) collective-permute-start(bf16[256,1024]{1,0:T(8,128)(2,1)S(1)} %get-tuple-element.105), channel_id=1, source_target_pairs={{0,16},{1,17},{2,18},{3,19},{4,20},{5,21},{6,22},{7,23},{8,24},{9,... | collective-permute-start | bytes 1572872 | tf_op jit(solution)/shard_map/ppermute | solution.py:41
  197.7 18.5 %collective-permute-start.37 = (bf16[256,512]{1,0:T(8,128)(2,1)S(1)}, bf16[256,512]{1,0:T(8,128)(2,1)S(1)}, u32[]{:S(2)}, u32[]{:S(2)}) collective-permute-start(bf16[256,512]{1,0:T(8,128)(2,1)S(1)} %get-tuple-element.104), channel_id=1, source_target_pairs={{0,8},{1,24},{2,10},{3,26},{4,12},{5,28},{6,14},{7,30},{8,0},{9,16... | collective-permute-start | bytes 786440 | tf_op jit(solution)/shard_map/ppermute | solution.py:41
  209.8 12.0 %collective-permute-start.36 = (bf16[256,512]{1,0:T(8,128)(2,1)S(1)}, bf16[256,512]{1,0:T(8,128)(2,1)S(1)}, u32[]{:S(2)}, u32[]{:S(2)}) collective-permute-start(bf16[256,512]{1,0:T(8,128)(2,1)S(1)} %get-tuple-element.103), channel_id=1, source_target_pairs={{0,0},{1,16},{2,2},{3,18},{4,4},{5,20},{6,6},{7,22},{8,8},{9,24},{... | collective-permute-start | bytes 786440 | tf_op jit(solution)/shard_map/ppermute | solution.py:41
  (53 other events, 356.8 us)
Sparse Core Ops, SparseCore 0:
  22.2 57.7 all-gather.2

commit v13 on v10

--- a/solution.py
+++ b/solution.py
@@ -289,6 +289,40 @@
         out_shape=[jax.ShapeDtypeStruct((size, 1024), jnp.bfloat16)] * count,
         compiler_params=GRANT,
     )(at, *attended, near, other)
+
+
+def two_sums_kernel(a, b, c, d, first, second):
+    for left, right, out in ((a, b, first), (c, d, second)):
+        out[...] = (left[...].astype(jnp.float32) + right[...].astype(jnp.float32)).astype(
+            jnp.bfloat16
+        )
+
+
+def two_sums(a, b, c, d):
+    shape = jax.ShapeDtypeStruct(a.shape, jnp.bfloat16)
+    return pl.pallas_call(two_sums_kernel, out_shape=[shape, shape])(a, b, c, d)
+
+
+def final_kernel(core_ref, a, b, c, d, keep, give):
+    core = core_ref[0]
+    for which, out in ((core, keep), (1 - core, give)):
+        cols = pl.ds(pl.multiple_of(which * 512, 512), 512)
+        value = a[:, cols].astype(jnp.float32) + b[:, cols].astype(jnp.float32)
+        value += c[:, cols].astype(jnp.float32) + d[:, cols].astype(jnp.float32)
+        out[...] = value.astype(jnp.bfloat16)
+
+
+def final_sums(core, *values):
+    whole = pl.BlockSpec((HALF, 1024), lambda i, c: (0, 0))
+    half = pl.BlockSpec((HALF, 512), lambda i, c: (0, 0))
+    shape = jax.ShapeDtypeStruct((HALF, 512), jnp.bfloat16)
+    return pl.pallas_call(
+        final_kernel,
+        grid_spec=pltpu.PrefetchScalarGridSpec(
+            num_scalar_prefetch=1, grid=(1,), in_specs=[whole] * 4, out_specs=[half, half]
+        ),
+        out_shape=[shape, shape],
+    )(core.reshape(1), *values)
 
 
 def add_rows(value, arrived, start):
@@ -385,7 +419,7 @@
         (from_below, from_above, a_top, b_bottom)
     )
     a_bottom, b_top = y_shift(a_bottom, 1), y_shift(b_top, -1)
-    a_top, b_bottom = a_top + from_below, b_bottom + from_above
+    a_top, b_bottom = two_sums(a_top, from_below, b_bottom, from_above)
     gathered = after(gathered, (a_top, b_bottom, a_bottom, b_top))
     (kept,) = project([y], zh, core, gathered, weights)
     sums = (kept, y_shift(a_top, 1), a_bottom, b_top, y_shift(b_bottom, -1))
@@ -422,13 +456,9 @@
     here_a = x_shift(add_rows(here_a, from_left[128:], 0), 1)
     here_b = x_shift(add_rows(here_b, from_right[128:], 128), -1)
 
-    def sum_of(*values):
-        return sum(v.astype(jnp.float32) for v in values).astype(jnp.bfloat16)
-
     across = zl_swap(summed_up(beside, a_top, a_bottom, b_top, b_bottom))
-    mixed = sum_of(mixed, here_a, here_b, across)
-    keep = send(half_of(mixed, core, 1), to_home(0))
-    got = send(half_of(mixed, 1 - core, 1), to_home(1))
+    keep, give = final_sums(core, mixed, here_a, here_b, across)
+    keep, got = send(keep, to_home(0)), send(give, to_home(1))
     return (wide + ordered(is_first, keep, got, 0).astype(jnp.float32)).astype(jnp.bfloat16)
 
 

time: 223 us -> 225 us (level)
  other arithmetic: 17.3 us -> 12.2 us
  Pallas kernels: 34.8 us -> 39.6 us
    pallas_call x0 -> x2, Pallas kernels: none -> 4.68 us  [the longest x1 2.48 us: final_sums(): pl.pallas_call(final_kernel, grid_spec=pltpu.PrefetchScalarGridSpec(num_s...]
    dynamic_update_slice x2 -> x0, other arithmetic: 2.63 us -> none  [add_rows(): lax.dynamic_update_slice(value, value[start:start + rows] + arrived, (sta...]
    unnamed x71 -> x75, local copies, waits for them, and re-layouts: 19.9 us -> 20.9 us
  transfers between devices with their start and end apart: 39 -> 39, of which waited for: 17 -> 16; matrix products, arithmetic and copies ran while one was open for 11% -> 9% of each run, Pallas kernels for 14% -> 15%
where the time goes in v13:
time: 225 us; the launch traced here: 223 us
  starting transfers between devices  64.9 us (29%)
  waiting for transfers between devices  60.4 us (27%)
  Pallas kernels  39.6 us (18%)
  local copies, waits for them, and re-layouts  31.5 us (14%)
  between operations  14.7 us (7%)
  other arithmetic  12.2 us (5%)
    ppermute x38, starting transfers between devices, send(): return lax.ppermute(value, AXES, pairs(change))  64.9 us
    ppermute x38, waiting for transfers between devices, send(): return lax.ppermute(value, AXES, pairs(change))  60.4 us
    unnamed x75, local copies, waits for them, and re-layouts  20.9 us
    pallas_call x3, Pallas kernels, products(): pl.pallas_call(lambda *refs: products_kernel(form, steps, *refs), grid_sp...  13.1 us
    pallas_call x3, Pallas kernels, project(): pl.pallas_call(project_kernel, grid_spec=pltpu.PrefetchScalarGridSpec(num...  11.6 us
    pallas_call x2, Pallas kernels, attention(): pl.pallas_call(attention_kernel, grid=(1,), in_specs=[pl.BlockSpec((v.sha...  5.76 us
  transfers between devices with their start and end apart: 39, of which 16 were waited for; matrix products, arithmetic and copies ran while one was open for 9% of the time, Pallas kernels for 15%

profile of v13, /device:TPU:3, one launch (start us, length us, event | category | flops | bytes accessed | tf_op | source)
XLA Modules:
  0.0 223.4 jit_solution(2630893618428619669)
XLA Ops:
  19.9 8.4 %collective-permute-start.3 = (bf16[256,1024]{1,0:T(8,128)(2,1)S(1)}, bf16[256,1024]{1,0:T(8,128)(2,1)S(1)}, u32[]{:S(2)}, u32[]{:S(2)}) collective-permute-start(bf16[256,1024]{1,0:T(8,128)(2,1)S(1)} %maximum_select_fusion), channel_id=1, source_target_pairs={{0,16},{1,17},{2,18},{3,19},{4,20},{5,21},{6,22},{7,23},{8,24},{9,... | collective-permute-start | bytes 1572872 | tf_op jit(solution)/shard_map/ppermute | solution.py:41
  28.4 3.7 %collective-permute-start.5 = (bf16[256,1024]{1,0:T(8,128)(2,1)S(1)}, bf16[256,1024]{1,0:T(8,128)(2,1)}, u32[]{:S(2)}, u32[]{:S(2)}) collective-permute-start(bf16[256,1024]{1,0:T(8,128)(2,1)S(1)} %maximum_select_fusion), channel_id=1, source_target_pairs={{0,64},{1,65},{2,66},{3,67},{4,68},{5,69},{6,70},{7,71},{8,72},{9,... | collective-permute-start | bytes 1572872 | tf_op jit(solution)/shard_map/ppermute | solution.py:41
  32.1 7.1 %collective-permute-done.3 = bf16[256,1024]{1,0:T(8,128)(2,1)S(1)} collective-permute-done((bf16[256,1024]{1,0:T(8,128)(2,1)S(1)}, bf16[256,1024]{1,0:T(8,128)(2,1)S(1)}, u32[]{:S(2)}, u32[]{:S(2)}) %collective-permute-start.3) | collective-permute-done | bytes 524320 | tf_op jit(solution)/shard_map/ppermute | solution.py:41
  43.9 3.3 %collective-permute-start.12 = (bf16[1024,640]{1,0:T(8,128)(2,1)}, bf16[1024,640]{1,0:T(8,128)(2,1)S(1)}, u32[]{:S(2)}, u32[]{:S(2)}) collective-permute-start(bf16[1024,640]{1,0:T(8,128)(2,1)} %pad_maximum_fusion), channel_id=1, source_target_pairs={{0,1},{1,0},{2,3},{3,2},{4,5},{5,4},{6,7},{7,6},{8,9},{9,8},{10,11... | collective-permute-start | bytes 3932168 | tf_op jit(solution)/shard_map/ppermute | solution.py:41
  53.1 6.6 %collective-permute-done.8 = bf16[256,1024]{1,0:T(8,128)(2,1)} collective-permute-done((bf16[256,1024]{1,0:T(8,128)(2,1)}, bf16[256,1024]{1,0:T(8,128)(2,1)}, u32[]{:S(2)}, u32[]{:S(2)}) %collective-permute-start.8) | collective-permute-done | bytes 524320 | tf_op jit(solution)/shard_map/ppermute | solution.py:41
  64.4 6.2 %collective-permute-done.10 = bf16[128,1024]{1,0:T(8,128)(2,1)S(1)} collective-permute-done((bf16[128,1024]{1,0:T(8,128)(2,1)S(1)}, bf16[128,1024]{1,0:T(8,128)(2,1)S(1)}, u32[]{:S(2)}, u32[]{:S(2)}) %collective-permute-start.10) | collective-permute-done | bytes 262176 | tf_op jit(solution)/shard_map/ppermute | solution.py:41
  71.0 4.2 %collective-permute-done.12.far = bf16[1024,640]{1,0:T(8,128)(2,1)S(1)} collective-permute-done((bf16[1024,640]{1,0:T(8,128)(2,1)}, bf16[1024,640]{1,0:T(8,128)(2,1)S(1)}, u32[]{:S(2)}, u32[]{:S(2)}) %collective-permute-start.12) | collective-permute-done | bytes 1310752 | tf_op jit(solution)/shard_map/ppermute | solution.py:41
  81.8 3.2 %shard_map.64 = (bf16[128,1280]{1,0:T(8,128)(2,1)}, bf16[128,1280]{1,0:T(8,128)(2,1)}) custom-call(s32[3]{0:T(128)S(1)} %pad_add_fusion.3.at_ref, bf16[4,256,2048]{2,1,0:T(8,128)(2,1)S(1)} %bitcast_dynamic-update-slice_fusion.rows_ref, bf16[1024,512]{1,0:T(8,128)(2,1)S(1)} %copy-done.5, bf16[1024,512]{1,0:T(8,128)(2,1)S(1)} %collective-permute-done.2.near_other, ...), custom_call_target="tpu_custom_call" | custom-call | tf_op jit(solution)/shard_map/pallas_call | solution.py:230
  85.0 2.9 %collective-permute-start.15 = (bf16[128,1280]{1,0:T(8,128)(2,1)}, bf16[128,1280]{1,0:T(8,128)(2,1)}, u32[]{:S(2)}, u32[]{:S(2)}) collective-permute-start(bf16[128,1280]{1,0:T(8,128)(2,1)} %get-tuple-element.66), channel_id=1, source_target_pairs={{0,6},{1,7},{2,0},{3,1},{4,2},{5,3},{6,4},{7,5},{8,14},{9,15},{10,... | collective-permute-start | bytes 983048 | tf_op jit(solution)/shard_map/ppermute | solution.py:41
  92.5 6.1 %shard_map.65 = (bf16[128,1280]{1,0:T(8,128)(2,1)S(1)}, bf16[128,1280]{1,0:T(8,128)(2,1)}, bf16[128,1280]{1,0:T(8,128)(2,1)}, bf16[128,1280]{1,0:T(8,128)(2,1)S(1)}) custom-call(s32[4]{0:T(128)S(1)} %pad_add_fusion.4.at_ref, bf16[4,256,2048]{2,1,0:T(8,128)(2,1)S(1)} %copy-done.1, bf16[1024,512]{1,0:T(8,128)(2,1)S(1)} %copy-done.5, ...), custom_call_target="tpu_custom_call" | custom-call | tf_op jit(solution)/shard_map/pallas_call | solution.py:230
  107.7 2.8 %collective-permute-done.16.refs_2_.refs_7_ = bf16[128,1280]{1,0:T(8,128)(2,1)} collective-permute-done((bf16[128,1280]{1,0:T(8,128)(2,1)}, bf16[128,1280]{1,0:T(8,128)(2,1)}, u32[]{:S(2)}, u32[]{:S(2)}) %collective-permute-start.16) | collective-permute-done | bytes 327712 | tf_op jit(solution)/shard_map/ppermute | solution.py:41
  121.7 3.0 %collective-permute-start.23 = (bf16[256,256]{1,0:T(8,128)(2,1)}, bf16[256,256]{1,0:T(8,128)(2,1)S(1)}, u32[]{:S(2)}, u32[]{:S(2)}) collective-permute-start(bf16[256,256]{1,0:T(8,128)(2,1)} %shard_map.68.refs_9_), channel_id=1, source_target_pairs={{0,8},{1,9},{2,10},{3,11},{4,12},{5,13},{6,14},{7,15},{8,0},{9,1},... | collective-permute-start | bytes 393224 | tf_op jit(solution)/shard_map/ppermute | solution.py:41
  127.2 2.9 %shard_map.69.refs_1_ = bf16[256,512]{1,0:T(8,128)(2,1)S(1)} custom-call(bf16[256,1280]{1,0:T(8,128)(2,1)S(1)} %copy-done.7, bf16[128,1280]{1,0:T(8,128)(2,1)} %collective-permute-done.18.refs_1_.refs_6_, bf16[128,1280]{1,0:T(8,128)(2,1)} %collective-permute-done.16.refs_2_.refs_7_, bf16[128,1280]{1,0:T(8,128)(2,1)} %collective-permute-done.17.refs_3_.refs_8_, ...), custom_call_target="tpu_custom_call" | custom-call | tf_op jit(solution)/shard_map/pallas_call | solution.py:181
  130.1 3.1 %collective-permute-start.24 = (bf16[256,512]{1,0:T(8,128)(2,1)S(1)}, bf16[256,512]{1,0:T(8,128)(2,1)S(1)}, u32[]{:S(2)}, u32[]{:S(2)}) collective-permute-start(bf16[256,512]{1,0:T(8,128)(2,1)S(1)} %shard_map.69.refs_1_), channel_id=1, source_target_pairs={{0,1},{1,0},{2,3},{3,2},{4,5},{5,4},{6,7},{7,6},{8,9},{9,8},{10,11... | collective-permute-start | bytes 786440 | tf_op jit(solution)/shard_map/ppermute | solution.py:41
  134.0 2.9 %shard_map.70.refs_2_ = bf16[256,512]{1,0:T(8,128)(2,1)S(1)} custom-call(bf16[256,1280]{1,0:T(8,128)(2,1)S(1)} %copy-done.7, bf16[128,1280]{1,0:T(8,128)(2,1)} %collective-permute-done.18.refs_1_.refs_6_, bf16[128,1280]{1,0:T(8,128)(2,1)} %collective-permute-done.16.refs_2_.refs_7_, bf16[128,1280]{1,0:T(8,128)(2,1)} %collective-permute-done.17.refs_3_.refs_8_, ...), custom_call_target="tpu_custom_call" | custom-call | tf_op jit(solution)/shard_map/pallas_call | solution.py:181
  139.4 6.5 %collective-permute-done.25.refs_4_ = bf16[256,512]{1,0:T(8,128)(2,1)S(1)} collective-permute-done((bf16[256,512]{1,0:T(8,128)(2,1)S(1)}, bf16[256,512]{1,0:T(8,128)(2,1)S(1)}, u32[]{:S(2)}, u32[]{:S(2)}) %collective-permute-start.25) | collective-permute-done | bytes 262176 | tf_op jit(solution)/shard_map/ppermute | solution.py:41
  148.1 4.3 %shard_map.72 = (bf16[256,1024]{1,0:T(8,128)(2,1)}, bf16[256,1024]{1,0:T(8,128)(2,1)}) custom-call(s32[4]{0:T(128)S(1)} %get-tuple-element.114.refs_0_, bf16[256,512]{1,0:T(8,128)(2,1)S(1)} %shard_map.69.refs_1_, bf16[256,512]{1,0:T(8,128)(2,1)S(1)} %shard_map.70.refs_2_, bf16[256,512]{1,0:T(8,128)(2,1)S(1)} %collective-permute-done.24.refs_3_, ...), custom_call_target="tpu_custom_call" | custom-call | tf_op jit(solution)/shard_map/pallas_call | solution.py:281
  156.2 3.3 %shard_map.73 = (bf16[128,1024]{1,0:T(8,128)(2,1)S(1)}, bf16[128,1024]{1,0:T(8,128)(2,1)S(1)}, bf16[128,1024]{1,0:T(8,128)(2,1)S(1)}, bf16[128,1024]{1,0:T(8,128)(2,1)S(1)}) custom-call(s32[4]{0:T(128)S(1)} %get-tuple-element.115.refs_0_, bf16[256,512]{1,0:T(8,128)(2,1)S(1)} %shard_map.69.refs_1_, bf16[256,512]{1,0:T(8,128)(2,1)S(1)} %shard_map.70.refs_2_, ...), custom_call_target="tpu_custom_call" | custom-call | tf_op jit(solution)/shard_map/pallas_call | solution.py:281
  162.2 5.4 %shard_map.71 = (bf16[256,1024]{1,0:T(8,128)(2,1)S(1)}, bf16[256,1024]{1,0:T(8,128)(2,1)S(1)}, bf16[256,1024]{1,0:T(8,128)(2,1)S(1)}, bf16[256,1024]{1,0:T(8,128)(2,1)S(1)}) custom-call(s32[8]{0:T(128)S(1)} %stack.100.refs_0_, bf16[256,512]{1,0:T(8,128)(2,1)S(1)} %shard_map.69.refs_1_, bf16[256,512]{1,0:T(8,128)(2,1)S(1)} %shard_map.70.refs_2_, ...), custom_call_target="tpu_custom_call" | custom-call | tf_op jit(solution)/shard_map/pallas_call | solution.py:281
  179.9 8.7 %collective-permute-done.29.b = bf16[256,1024]{1,0:T(8,128)(2,1)S(1)} collective-permute-done((bf16[256,1024]{1,0:T(8,128)(2,1)S(1)}, bf16[256,1024]{1,0:T(8,128)(2,1)S(1)}, u32[]{:S(2)}, u32[]{:S(2)}) %collective-permute-start.29) | collective-permute-done | bytes 524320 | tf_op jit(solution)/shard_map/ppermute | solution.py:41
  192.1 10.7 %collective-permute-start.37 = (bf16[256,512]{1,0:T(8,128)(2,1)}, bf16[256,512]{1,0:T(8,128)(2,1)S(1)}, u32[]{:S(2)}, u32[]{:S(2)}) collective-permute-start(bf16[256,512]{1,0:T(8,128)(2,1)} %get-tuple-element.100), channel_id=1, source_target_pairs={{0,8},{1,24},{2,10},{3,26},{4,12},{5,28},{6,14},{7,30},{8,0},{9,16... | collective-permute-start | bytes 786440 | tf_op jit(solution)/shard_map/ppermute | solution.py:41
  202.8 2.8 %collective-permute-start.36 = (bf16[256,512]{1,0:T(8,128)(2,1)}, bf16[256,512]{1,0:T(8,128)(2,1)S(1)}, u32[]{:S(2)}, u32[]{:S(2)}) collective-permute-start(bf16[256,512]{1,0:T(8,128)(2,1)} %get-tuple-element.99), channel_id=1, source_target_pairs={{0,0},{1,16},{2,2},{3,18},{4,4},{5,20},{6,6},{7,22},{8,8},{9,24},{... | collective-permute-start | bytes 786440 | tf_op jit(solution)/shard_map/ppermute | solution.py:41
  205.5 4.1 %collective-permute-done.37 = bf16[256,512]{1,0:T(8,128)(2,1)S(1)} collective-permute-done((bf16[256,512]{1,0:T(8,128)(2,1)}, bf16[256,512]{1,0:T(8,128)(2,1)S(1)}, u32[]{:S(2)}, u32[]{:S(2)}) %collective-permute-start.37) | collective-permute-done | bytes 262176 | tf_op jit(solution)/shard_map/ppermute | solution.py:41
  209.6 5.8 %collective-permute-done.36 = bf16[256,512]{1,0:T(8,128)(2,1)S(1)} collective-permute-done((bf16[256,512]{1,0:T(8,128)(2,1)}, bf16[256,512]{1,0:T(8,128)(2,1)S(1)}, u32[]{:S(2)}, u32[]{:S(2)}) %collective-permute-start.36) | collective-permute-done | bytes 262176 | tf_op jit(solution)/shard_map/ppermute | solution.py:41
  (185 shorter events, 90.6 us)
Async XLA Ops:
  6.5 119.3 %all-gather.3.cloned.1.call-start = ((), (), s32[]{:S(2)}) async-start(), calls=%async_computation | async-start | bytes 5242880 | tf_op jit(solution)/shard_map/all_gather | solution.py:408
  19.9 19.3 %collective-permute-start.3 = (bf16[256,1024]{1,0:T(8,128)(2,1)S(1)}, bf16[256,1024]{1,0:T(8,128)(2,1)S(1)}, u32[]{:S(2)}, u32[]{:S(2)}) collective-permute-start(bf16[256,1024]{1,0:T(8,128)(2,1)S(1)} %maximum_select_fusion), channel_id=1, source_target_pairs={{0,16},{1,17},{2,18},{3,19},{4,20},{5,21},{6,22},{7,23},{8,24},{9,... | collective-permute-start | bytes 1572872 | tf_op jit(solution)/shard_map/ppermute | solution.py:41
  28.4 12.9 %collective-permute-start.4 = (bf16[256,1024]{1,0:T(8,128)(2,1)S(1)}, bf16[256,1024]{1,0:T(8,128)(2,1)S(1)}, u32[]{:S(2)}, u32[]{:S(2)}) collective-permute-start(bf16[256,1024]{1,0:T(8,128)(2,1)S(1)} %maximum_select_fusion), channel_id=1, source_target_pairs={{0,48},{1,49},{2,50},{3,51},{4,52},{5,53},{6,54},{7,55},{8,56},{9,... | collective-permute-start | bytes 1572872 | tf_op jit(solution)/shard_map/ppermute | solution.py:41
  28.4 15.5 %collective-permute-start.5 = (bf16[256,1024]{1,0:T(8,128)(2,1)S(1)}, bf16[256,1024]{1,0:T(8,128)(2,1)}, u32[]{:S(2)}, u32[]{:S(2)}) collective-permute-start(bf16[256,1024]{1,0:T(8,128)(2,1)S(1)} %maximum_select_fusion), channel_id=1, source_target_pairs={{0,64},{1,65},{2,66},{3,67},{4,68},{5,69},{6,70},{7,71},{8,72},{9,... | collective-permute-start | bytes 1572872 | tf_op jit(solution)/shard_map/ppermute | solution.py:41
  43.9 31.4 %collective-permute-start.12 = (bf16[1024,640]{1,0:T(8,128)(2,1)}, bf16[1024,640]{1,0:T(8,128)(2,1)S(1)}, u32[]{:S(2)}, u32[]{:S(2)}) collective-permute-start(bf16[1024,640]{1,0:T(8,128)(2,1)} %pad_maximum_fusion), channel_id=1, source_target_pairs={{0,1},{1,0},{2,3},{3,2},{4,5},{5,4},{6,7},{7,6},{8,9},{9,8},{10,11... | collective-permute-start | bytes 3932168 | tf_op jit(solution)/shard_map/ppermute | solution.py:41
  47.2 12.5 %collective-permute-start.8 = (bf16[256,1024]{1,0:T(8,128)(2,1)}, bf16[256,1024]{1,0:T(8,128)(2,1)}, u32[]{:S(2)}, u32[]{:S(2)}) collective-permute-start(bf16[256,1024]{1,0:T(8,128)(2,1)} %collective-permute-done.5), channel_id=1, source_target_pairs={{0,16},{1,17},{2,18},{3,19},{4,20},{5,21},{6,22},{7,23},{8,24},{9,... | collective-permute-start | bytes 1572872 | tf_op jit(solution)/shard_map/ppermute | solution.py:41
  48.3 13.0 %collective-permute-start.9 = (bf16[256,1024]{1,0:T(8,128)(2,1)}, bf16[256,1024]{1,0:T(8,128)(2,1)}, u32[]{:S(2)}, u32[]{:S(2)}) collective-permute-start(bf16[256,1024]{1,0:T(8,128)(2,1)} %collective-permute-done.5), channel_id=1, source_target_pairs={{0,48},{1,49},{2,50},{3,51},{4,52},{5,53},{6,54},{7,55},{8,56},{9,... | collective-permute-start | bytes 1572872 | tf_op jit(solution)/shard_map/ppermute | solution.py:41
  50.2 28.0 %collective-permute-start.7 = (bf16[128,1024]{1,0:T(8,128)(2,1)S(1)}, bf16[128,1024]{1,0:T(8,128)(2,1)S(1)}, u32[]{:S(2)}, u32[]{:S(2)}) collective-permute-start(bf16[128,1024]{1,0:T(8,128)(2,1)S(1)} %slice.31), channel_id=1, source_target_pairs={{0,48},{1,49},{2,50},{3,51},{4,52},{5,53},{6,54},{7,55},{8,56},{9,... | collective-permute-start | bytes 786440 | tf_op jit(solution)/shard_map/ppermute | solution.py:41
  53.0 25.2 %collective-permute-start.6 = (bf16[128,1024]{1,0:T(8,128)(2,1)S(1)}, bf16[128,1024]{1,0:T(8,128)(2,1)S(1)}, u32[]{:S(2)}, u32[]{:S(2)}) collective-permute-start(bf16[128,1024]{1,0:T(8,128)(2,1)S(1)} %slice.30), channel_id=1, source_target_pairs={{0,16},{1,17},{2,18},{3,19},{4,20},{5,21},{6,22},{7,23},{8,24},{9,... | collective-permute-start | bytes 786440 | tf_op jit(solution)/shard_map/ppermute | solution.py:41
  85.0 17.8 %collective-permute-start.14 = (bf16[128,1280]{1,0:T(8,128)(2,1)}, bf16[128,1280]{1,0:T(8,128)(2,1)}, u32[]{:S(2)}, u32[]{:S(2)}) collective-permute-start(bf16[128,1280]{1,0:T(8,128)(2,1)} %get-tuple-element.65), channel_id=1, source_target_pairs={{0,2},{1,3},{2,4},{3,5},{4,6},{5,7},{6,0},{7,1},{8,10},{9,11},{10,... | collective-permute-start | bytes 983048 | tf_op jit(solution)/shard_map/ppermute | solution.py:41
  85.0 17.8 %collective-permute-start.15 = (bf16[128,1280]{1,0:T(8,128)(2,1)}, bf16[128,1280]{1,0:T(8,128)(2,1)}, u32[]{:S(2)}, u32[]{:S(2)}) collective-permute-start(bf16[128,1280]{1,0:T(8,128)(2,1)} %get-tuple-element.66), channel_id=1, source_target_pairs={{0,6},{1,7},{2,0},{3,1},{4,2},{5,3},{6,4},{7,5},{8,14},{9,15},{10,... | collective-permute-start | bytes 983048 | tf_op jit(solution)/shard_map/ppermute | solution.py:41
  100.1 10.5 %collective-permute-start.17 = (bf16[128,1280]{1,0:T(8,128)(2,1)}, bf16[128,1280]{1,0:T(8,128)(2,1)}, u32[]{:S(2)}, u32[]{:S(2)}) collective-permute-start(bf16[128,1280]{1,0:T(8,128)(2,1)} %get-tuple-element.76), channel_id=1, source_target_pairs={{0,6},{1,7},{2,0},{3,1},{4,2},{5,3},{6,4},{7,5},{8,14},{9,15},{10,... | collective-permute-start | bytes 983048 | tf_op jit(solution)/shard_map/ppermute | solution.py:41
  105.0 14.6 %collective-permute-start.18 = (bf16[128,1280]{1,0:T(8,128)(2,1)}, bf16[128,1280]{1,0:T(8,128)(2,1)}, u32[]{:S(2)}, u32[]{:S(2)}) collective-permute-start(bf16[128,1280]{1,0:T(8,128)(2,1)} %get-tuple-element.73), channel_id=1, source_target_pairs={{0,2},{1,3},{2,4},{3,5},{4,6},{5,7},{6,0},{7,1},{8,10},{9,11},{10,... | collective-permute-start | bytes 983048 | tf_op jit(solution)/shard_map/ppermute | solution.py:41
  105.0 14.6 %collective-permute-start.19 = (bf16[128,1280]{1,0:T(8,128)(2,1)}, bf16[128,1280]{1,0:T(8,128)(2,1)}, u32[]{:S(2)}, u32[]{:S(2)}) collective-permute-start(bf16[128,1280]{1,0:T(8,128)(2,1)} %get-tuple-element.74), channel_id=1, source_target_pairs={{0,6},{1,7},{2,0},{3,1},{4,2},{5,3},{6,4},{7,5},{8,14},{9,15},{10,... | collective-permute-start | bytes 983048 | tf_op jit(solution)/shard_map/ppermute | solution.py:41
  107.6 11.1 %collective-permute-start.22 = (f32[256]{0:T(256)S(1)}, f32[256]{0:T(256)S(1)}, u32[]{:S(2)}, u32[]{:S(2)}) collective-permute-start(f32[256]{0:T(256)S(1)} %bitcast.52), channel_id=1, source_target_pairs={{0,6},{1,7},{2,0},{3,1},{4,2},{5,3},{6,4},{7,5},{8,14},{9,15},{10,... | collective-permute-start | bytes 3080 | tf_op jit(solution)/shard_map/ppermute | solution.py:41
  125.9 20.1 %collective-permute-start.26 = (bf16[4,512,1024]{2,1,0:T(8,128)(2,1)}, bf16[4,512,1024]{2,1,0:T(8,128)(2,1)}, u32[]{:S(2)}, u32[]{:S(2)}) collective-permute-start(bf16[4,512,1024]{2,1,0:T(8,128)(2,1)} %bitcast.44), channel_id=1, source_target_pairs={{0,8},{1,9},{2,10},{3,11},{4,12},{5,13},{6,14},{7,15},{8,0},{9,1},... | collective-permute-start | bytes 12582920 | tf_op jit(solution)/shard_map/ppermute | solution.py:41
  152.4 15.3 %collective-permute-start.27 = (bf16[256,1024]{1,0:T(8,128)(2,1)}, bf16[256,1024]{1,0:T(8,128)(2,1)}, u32[]{:S(2)}, u32[]{:S(2)}) collective-permute-start(bf16[256,1024]{1,0:T(8,128)(2,1)} %get-tuple-element.86), channel_id=1, source_target_pairs={{0,16},{1,17},{2,18},{3,19},{4,20},{5,21},{6,22},{7,23},{8,24},{9,... | collective-permute-start | bytes 1572872 | tf_op jit(solution)/shard_map/ppermute | solution.py:41
  153.0 14.7 %collective-permute-start.28 = (bf16[256,1024]{1,0:T(8,128)(2,1)}, bf16[256,1024]{1,0:T(8,128)(2,1)}, u32[]{:S(2)}, u32[]{:S(2)}) collective-permute-start(bf16[256,1024]{1,0:T(8,128)(2,1)} %get-tuple-element.87), channel_id=1, source_target_pairs={{0,48},{1,49},{2,50},{3,51},{4,52},{5,53},{6,54},{7,55},{8,56},{9,... | collective-permute-start | bytes 1572872 | tf_op jit(solution)/shard_map/ppermute | solution.py:41
  159.5 13.8 %collective-permute-start.32 = (bf16[128,1024]{1,0:T(8,128)(2,1)S(1)}, bf16[128,1024]{1,0:T(8,128)(2,1)S(1)}, u32[]{:S(2)}, u32[]{:S(2)}) collective-permute-start(bf16[128,1024]{1,0:T(8,128)(2,1)S(1)} %get-tuple-element.96), channel_id=1, source_target_pairs={{0,16},{1,17},{2,18},{3,19},{4,20},{5,21},{6,22},{7,23},{8,24},{9,... | collective-permute-start | bytes 786440 | tf_op jit(solution)/shard_map/ppermute | solution.py:41
  161.0 15.0 %collective-permute-start.33 = (bf16[128,1024]{1,0:T(8,128)(2,1)S(1)}, bf16[128,1024]{1,0:T(8,128)(2,1)S(1)}, u32[]{:S(2)}, u32[]{:S(2)}) collective-permute-start(bf16[128,1024]{1,0:T(8,128)(2,1)S(1)} %get-tuple-element.97), channel_id=1, source_target_pairs={{0,48},{1,49},{2,50},{3,51},{4,52},{5,53},{6,54},{7,55},{8,56},{9,... | collective-permute-start | bytes 786440 | tf_op jit(solution)/shard_map/ppermute | solution.py:41
  173.3 15.3 %collective-permute-start.29 = (bf16[256,1024]{1,0:T(8,128)(2,1)S(1)}, bf16[256,1024]{1,0:T(8,128)(2,1)S(1)}, u32[]{:S(2)}, u32[]{:S(2)}) collective-permute-start(bf16[256,1024]{1,0:T(8,128)(2,1)S(1)} %get-tuple-element.104), channel_id=1, source_target_pairs={{0,16},{1,17},{2,18},{3,19},{4,20},{5,21},{6,22},{7,23},{8,24},{9,... | collective-permute-start | bytes 1572872 | tf_op jit(solution)/shard_map/ppermute | solution.py:41
  173.3 15.3 %collective-permute-start.30 = (bf16[256,1024]{1,0:T(8,128)(2,1)S(1)}, bf16[256,1024]{1,0:T(8,128)(2,1)}, u32[]{:S(2)}, u32[]{:S(2)}) collective-permute-start(bf16[256,1024]{1,0:T(8,128)(2,1)S(1)} %get-tuple-element.102), channel_id=1, source_target_pairs={{0,48},{1,49},{2,50},{3,51},{4,52},{5,53},{6,54},{7,55},{8,56},{9,... | collective-permute-start | bytes 1572872 | tf_op jit(solution)/shard_map/ppermute | solution.py:41
  192.1 17.5 %collective-permute-start.37 = (bf16[256,512]{1,0:T(8,128)(2,1)}, bf16[256,512]{1,0:T(8,128)(2,1)S(1)}, u32[]{:S(2)}, u32[]{:S(2)}) collective-permute-start(bf16[256,512]{1,0:T(8,128)(2,1)} %get-tuple-element.100), channel_id=1, source_target_pairs={{0,8},{1,24},{2,10},{3,26},{4,12},{5,28},{6,14},{7,30},{8,0},{9,16... | collective-permute-start | bytes 786440 | tf_op jit(solution)/shard_map/ppermute | solution.py:41
  202.8 12.7 %collective-permute-start.36 = (bf16[256,512]{1,0:T(8,128)(2,1)}, bf16[256,512]{1,0:T(8,128)(2,1)S(1)}, u32[]{:S(2)}, u32[]{:S(2)}) collective-permute-start(bf16[256,512]{1,0:T(8,128)(2,1)} %get-tuple-element.99), channel_id=1, source_target_pairs={{0,0},{1,16},{2,2},{3,18},{4,4},{5,20},{6,6},{7,22},{8,8},{9,24},{... | collective-permute-start | bytes 786440 | tf_op jit(solution)/shard_map/ppermute | solution.py:41
  (52 other events, 318.7 us)
Sparse Core Ops, SparseCore 0:
  20.1 58.2 all-gather.2

commit v14 on v12

--- a/solution.py
+++ b/solution.py
@@ -389,25 +389,33 @@
     out_near = lax.all_gather(after(out_weight, block), "y", axis=0, tiled=False)
 
     squares = jnp.sum(jnp.square(gathered.astype(jnp.float32) * slice_gain), axis=-1)
-    gathered, squares = lax.optimization_barrier((gathered, squares))
-    low, high = project([(y + 2) % 4], zh, core, gathered, weights)
+    low, high, kept = project([(y + 2) % 4, y], zh, core, gathered, weights, True)
     from_below = y_shift(low, 1)
     from_above = y_shift(high, -1)
-    a_top, a_bottom, b_top, b_bottom, kept = project(
-        [(y + 1) % 4, (y + 3) % 4, y], zh, core, gathered, weights, True
+    a_top, a_bottom, b_top, b_bottom = project(
+        [(y + 1) % 4, (y + 3) % 4], zh, core, gathered, weights
+    )
+
+    squares, a_bottom, b_top = lax.optimization_barrier((squares, a_bottom, b_top))
+
+    def squares_of(which):
+        return lax.dynamic_index_in_dim(squares, which, 0, keepdims=False)
+
+    squares_in = send(
+        jnp.stack([squares_of(y ^ 1), squares_of(y ^ 3)]), lambda c: dict(y=c["y"] ^ 1)
     )
     from_below, from_above, a_top, b_bottom = lax.optimization_barrier(
         (from_below, from_above, a_top, b_bottom)
     )
     a_bottom, b_top = y_shift(a_bottom, 1), y_shift(b_top, -1)
     a_top, b_bottom = two_sums(a_top, from_below, b_bottom, from_above)
-    squares, a_bottom, b_top = lax.optimization_barrier((squares, a_bottom, b_top))
+    squares_here, squares_beyond = squares_of(y) + squares_in[0], squares_of(y ^ 2) + squares_in[1]
+    squares_here, squares_beyond, a_top, b_bottom = lax.optimization_barrier(
+        (squares_here, squares_beyond, a_top, b_bottom)
+    )
     sums = (kept, y_shift(a_top, 1), a_bottom, b_top, y_shift(b_bottom, -1))
 
-    squares, a_top, b_bottom = lax.optimization_barrier((squares, a_top, b_bottom))
-    total = lax.dynamic_index_in_dim(squares, y, 0, keepdims=False)
-    for k in (1, 2, 3):
-        total += y_shift(lax.dynamic_index_in_dim(squares, (y + k) % 4, 0, keepdims=False), k)
+    total = squares_here + y_shift(squares_beyond, 2)
     scale = lax.rsqrt(total / 8192.0 + norm_eps)[:, None]
 
     kv_rows = key_value_rows(core, sums, scale, cosine, sine)

time: 231 us -> 230 us (level)
  waiting for transfers between devices: 67.6 us -> 70.5 us
  local copies, waits for them, and re-layouts: 30.3 us -> 27.9 us
    ppermute x38 -> x37, waiting for transfers between devices: 67.6 us -> 70.5 us  [send(): return lax.ppermute(value, AXES, pairs(change))]
    unnamed x77 -> x75, local copies, waits for them, and re-layouts: 19.4 us -> 17.1 us
    ppermute x38 -> x37, starting transfers between devices: 69.1 us -> 67.9 us  [send(): return lax.ppermute(value, AXES, pairs(change))]
  transfers between devices with their start and end apart: 39 -> 38, of which waited for: 18 -> 19; matrix products, arithmetic and copies ran while one was open for 8% -> 8% of each run, Pallas kernels for 13% -> 13%
where the time goes in v14:
time: 230 us; the launch traced here: 229 us
  waiting for transfers between devices  70.5 us (31%)
  starting transfers between devices  67.9 us (30%)
  Pallas kernels  34.4 us (15%)
  local copies, waits for them, and re-layouts  27.9 us (12%)
  between operations  14.7 us (6%)
  other arithmetic  13.2 us (6%)
    ppermute x37, waiting for transfers between devices, send(): return lax.ppermute(value, AXES, pairs(change))  70.5 us
    ppermute x37, starting transfers between devices, send(): return lax.ppermute(value, AXES, pairs(change))  67.9 us
    unnamed x75, local copies, waits for them, and re-layouts  17.1 us
    pallas_call x3, Pallas kernels, products(): pl.pallas_call(lambda *refs: products_kernel(form, steps, *refs), grid_sp...  13.1 us
    pallas_call x2, Pallas kernels, project(): pl.pallas_call(project_kernel, grid_spec=pltpu.PrefetchScalarGridSpec(num...  11.2 us
  transfers between devices with their start and end apart: 38, of which 19 were waited for; matrix products, arithmetic and copies ran while one was open for 8% of the time, Pallas kernels for 13%

profile of v14, /device:TPU:3, one launch (start us, length us, event | category | flops | bytes accessed | tf_op | source)
XLA Modules:
  0.0 228.6 jit_solution(15464134792242824981)
XLA Ops:
  10.0 3.6 %collective-permute-start = (bf16[256,512]{1,0:T(8,128)(2,1)}, bf16[256,512]{1,0:T(8,128)(2,1)}, u32[]{:S(2)}, u32[]{:S(2)}) collective-permute-start(bf16[256,512]{1,0:T(8,128)(2,1)} %get-tuple-element.111), channel_id=1, source_target_pairs={{0,0},{1,1},{2,32},{3,33},{4,64},{5,65},{6,96},{7,97},{8,8},{9,9},... | collective-permute-start | bytes 786440 | tf_op jit(solution)/shard_map/ppermute | solution.py:41
  22.1 8.0 %collective-permute-start.3 = (bf16[256,1024]{1,0:T(8,128)(2,1)}, bf16[256,1024]{1,0:T(8,128)(2,1)S(1)}, u32[]{:S(2)}, u32[]{:S(2)}) collective-permute-start(bf16[256,1024]{1,0:T(8,128)(2,1)} %maximum_select_fusion), channel_id=1, source_target_pairs={{0,16},{1,17},{2,18},{3,19},{4,20},{5,21},{6,22},{7,23},{8,24},{9,... | collective-permute-start | bytes 1572872 | tf_op jit(solution)/shard_map/ppermute | solution.py:41
  30.0 3.7 %collective-permute-start.5 = (bf16[256,1024]{1,0:T(8,128)(2,1)}, bf16[256,1024]{1,0:T(8,128)(2,1)}, u32[]{:S(2)}, u32[]{:S(2)}) collective-permute-start(bf16[256,1024]{1,0:T(8,128)(2,1)} %maximum_select_fusion), channel_id=1, source_target_pairs={{0,64},{1,65},{2,66},{3,67},{4,68},{5,69},{6,70},{7,71},{8,72},{9,... | collective-permute-start | bytes 1572872 | tf_op jit(solution)/shard_map/ppermute | solution.py:41
  33.8 7.5 %collective-permute-done.3 = bf16[256,1024]{1,0:T(8,128)(2,1)S(1)} collective-permute-done((bf16[256,1024]{1,0:T(8,128)(2,1)}, bf16[256,1024]{1,0:T(8,128)(2,1)S(1)}, u32[]{:S(2)}, u32[]{:S(2)}) %collective-permute-start.3) | collective-permute-done | bytes 524320 | tf_op jit(solution)/shard_map/ppermute | solution.py:41
  45.8 3.3 %collective-permute-start.12 = (bf16[1024,640]{1,0:T(8,128)(2,1)}, bf16[1024,640]{1,0:T(8,128)(2,1)S(1)}, u32[]{:S(2)}, u32[]{:S(2)}) collective-permute-start(bf16[1024,640]{1,0:T(8,128)(2,1)} %pad_maximum_fusion), channel_id=1, source_target_pairs={{0,1},{1,0},{2,3},{3,2},{4,5},{5,4},{6,7},{7,6},{8,9},{9,8},{10,11... | collective-permute-start | bytes 3932168 | tf_op jit(solution)/shard_map/ppermute | solution.py:41
  52.1 2.7 %collective-permute-start.7 = (bf16[128,1024]{1,0:T(8,128)(2,1)S(1)}, bf16[128,1024]{1,0:T(8,128)(2,1)S(1)}, u32[]{:S(2)}, u32[]{:S(2)}) collective-permute-start(bf16[128,1024]{1,0:T(8,128)(2,1)S(1)} %slice.37), channel_id=1, source_target_pairs={{0,48},{1,49},{2,50},{3,51},{4,52},{5,53},{6,54},{7,55},{8,56},{9,... | collective-permute-start | bytes 786440 | tf_op jit(solution)/shard_map/ppermute | solution.py:41
  55.0 6.5 %collective-permute-done.8 = bf16[256,1024]{1,0:T(8,128)(2,1)} collective-permute-done((bf16[256,1024]{1,0:T(8,128)(2,1)}, bf16[256,1024]{1,0:T(8,128)(2,1)}, u32[]{:S(2)}, u32[]{:S(2)}) %collective-permute-start.8) | collective-permute-done | bytes 524320 | tf_op jit(solution)/shard_map/ppermute | solution.py:41
  66.3 6.2 %collective-permute-done.10 = bf16[128,1024]{1,0:T(8,128)(2,1)S(1)} collective-permute-done((bf16[128,1024]{1,0:T(8,128)(2,1)S(1)}, bf16[128,1024]{1,0:T(8,128)(2,1)S(1)}, u32[]{:S(2)}, u32[]{:S(2)}) %collective-permute-start.10) | collective-permute-done | bytes 262176 | tf_op jit(solution)/shard_map/ppermute | solution.py:41
  72.9 4.2 %collective-permute-done.12.far = bf16[1024,640]{1,0:T(8,128)(2,1)S(1)} collective-permute-done((bf16[1024,640]{1,0:T(8,128)(2,1)}, bf16[1024,640]{1,0:T(8,128)(2,1)S(1)}, u32[]{:S(2)}, u32[]{:S(2)}) %collective-permute-start.12) | collective-permute-done | bytes 1310752 | tf_op jit(solution)/shard_map/ppermute | solution.py:41
  83.7 5.2 %shard_map.65 = (bf16[128,1280]{1,0:T(8,128)(2,1)S(1)}, bf16[128,1280]{1,0:T(8,128)(2,1)S(1)}, bf16[128,1280]{1,0:T(8,128)(2,1)S(1)}, bf16[128,1280]{1,0:T(8,128)(2,1)S(1)}) custom-call(s32[4]{0:T(128)S(1)} %get-tuple-element.121.at_ref, bf16[4,256,2048]{2,1,0:T(8,128)(2,1)S(1)} %bitcast_dynamic-update-slice_fusion.rows_ref, ...), custom_call_target="tpu_custom_call" | custom-call | tf_op jit(solution)/shard_map/pallas_call | solution.py:233
  91.9 6.0 %shard_map.64 = (bf16[128,1280]{1,0:T(8,128)(2,1)}, bf16[128,1280]{1,0:T(8,128)(2,1)}, bf16[256,1280]{1,0:T(8,128)(2,1)S(1)}) custom-call(s32[4]{0:T(128)S(1)} %get-tuple-element.120.at_ref, bf16[4,256,2048]{2,1,0:T(8,128)(2,1)S(1)} %bitcast_dynamic-update-slice_fusion.rows_ref, bf16[1024,512]{1,0:T(8,128)(2,1)S(1)} %copy-done.4, ...), custom_call_target="tpu_custom_call" | custom-call | tf_op jit(solution)/shard_map/pallas_call | solution.py:233
  98.8 2.7 %collective-permute-start.16 = (bf16[128,1280]{1,0:T(8,128)(2,1)}, bf16[128,1280]{1,0:T(8,128)(2,1)S(1)}, u32[]{:S(2)}, u32[]{:S(2)}) collective-permute-start(bf16[128,1280]{1,0:T(8,128)(2,1)} %get-tuple-element.71), channel_id=1, source_target_pairs={{0,6},{1,7},{2,0},{3,1},{4,2},{5,3},{6,4},{7,5},{8,14},{9,15},{10,... | collective-permute-start | bytes 983048 | tf_op jit(solution)/shard_map/ppermute | solution.py:41
  104.3 4.5 %collective-permute-done.14 = f32[2,256]{1,0:T(2,128)S(1)} collective-permute-done((f32[2,256]{1,0:T(2,128)S(1)}, f32[2,256]{1,0:T(2,128)S(1)}, u32[]{:S(2)}, u32[]{:S(2)}) %collective-permute-start.14) | collective-permute-done | bytes 2080 | tf_op jit(solution)/shard_map/ppermute | solution.py:41
  116.2 6.8 %collective-permute-done.21 = f32[256]{0:T(256)S(1)} collective-permute-done((f32[256]{0:T(256)S(1)}, f32[256]{0:T(256)S(1)}, u32[]{:S(2)}, u32[]{:S(2)}) %collective-permute-start.21) | collective-permute-done | bytes 1056 | tf_op jit(solution)/shard_map/ppermute | solution.py:41
  137.5 3.0 %collective-permute-start.23 = (bf16[256,512]{1,0:T(8,128)(2,1)S(1)}, bf16[256,512]{1,0:T(8,128)(2,1)S(1)}, u32[]{:S(2)}, u32[]{:S(2)}) collective-permute-start(bf16[256,512]{1,0:T(8,128)(2,1)S(1)} %shard_map.68.refs_1_), channel_id=1, source_target_pairs={{0,1},{1,0},{2,3},{3,2},{4,5},{5,4},{6,7},{7,6},{8,9},{9,8},{10,11... | collective-permute-start | bytes 786440 | tf_op jit(solution)/shard_map/ppermute | solution.py:41
  143.4 3.5 %collective-permute-done.23.refs_3_ = bf16[256,512]{1,0:T(8,128)(2,1)S(1)} collective-permute-done((bf16[256,512]{1,0:T(8,128)(2,1)S(1)}, bf16[256,512]{1,0:T(8,128)(2,1)S(1)}, u32[]{:S(2)}, u32[]{:S(2)}) %collective-permute-start.23) | collective-permute-done | bytes 262176 | tf_op jit(solution)/shard_map/ppermute | solution.py:41
  146.8 5.4 %collective-permute-done.24.refs_4_ = bf16[256,512]{1,0:T(8,128)(2,1)S(1)} collective-permute-done((bf16[256,512]{1,0:T(8,128)(2,1)S(1)}, bf16[256,512]{1,0:T(8,128)(2,1)S(1)}, u32[]{:S(2)}, u32[]{:S(2)}) %collective-permute-start.24) | collective-permute-done | bytes 262176 | tf_op jit(solution)/shard_map/ppermute | solution.py:41
  154.4 4.3 %shard_map.71 = (bf16[256,1024]{1,0:T(8,128)(2,1)}, bf16[256,1024]{1,0:T(8,128)(2,1)}) custom-call(s32[4]{0:T(128)S(1)} %get-tuple-element.122.refs_0_, bf16[256,512]{1,0:T(8,128)(2,1)S(1)} %shard_map.68.refs_1_, bf16[256,512]{1,0:T(8,128)(2,1)S(1)} %shard_map.69.refs_2_, bf16[256,512]{1,0:T(8,128)(2,1)S(1)} %collective-permute-done.23.refs_3_, ...), custom_call_target="tpu_custom_call" | custom-call | tf_op jit(solution)/shard_map/pallas_call | solution.py:296
  162.5 3.3 %shard_map.72 = (bf16[128,1024]{1,0:T(8,128)(2,1)S(1)}, bf16[128,1024]{1,0:T(8,128)(2,1)S(1)}, bf16[128,1024]{1,0:T(8,128)(2,1)S(1)}, bf16[128,1024]{1,0:T(8,128)(2,1)S(1)}) custom-call(s32[4]{0:T(128)S(1)} %get-tuple-element.123.refs_0_, bf16[256,512]{1,0:T(8,128)(2,1)S(1)} %shard_map.68.refs_1_, bf16[256,512]{1,0:T(8,128)(2,1)S(1)} %shard_map.69.refs_2_, ...), custom_call_target="tpu_custom_call" | custom-call | tf_op jit(solution)/shard_map/pallas_call | solution.py:296
  168.6 5.4 %shard_map.70 = (bf16[256,1024]{1,0:T(8,128)(2,1)S(1)}, bf16[256,1024]{1,0:T(8,128)(2,1)S(1)}, bf16[256,1024]{1,0:T(8,128)(2,1)S(1)}, bf16[256,1024]{1,0:T(8,128)(2,1)S(1)}) custom-call(s32[8]{0:T(128)S(1)} %stack.102.refs_0_, bf16[256,512]{1,0:T(8,128)(2,1)S(1)} %shard_map.68.refs_1_, bf16[256,512]{1,0:T(8,128)(2,1)S(1)} %shard_map.69.refs_2_, ...), custom_call_target="tpu_custom_call" | custom-call | tf_op jit(solution)/shard_map/pallas_call | solution.py:296
  186.8 6.9 %collective-permute-done.29 = bf16[256,1024]{1,0:T(8,128)(2,1)S(1)} collective-permute-done((bf16[256,1024]{1,0:T(8,128)(2,1)S(1)}, bf16[256,1024]{1,0:T(8,128)(2,1)S(1)}, u32[]{:S(2)}, u32[]{:S(2)}) %collective-permute-start.29) | collective-permute-done | bytes 524320 | tf_op jit(solution)/shard_map/ppermute | solution.py:41
  196.0 12.1 %collective-permute-start.36 = (bf16[256,512]{1,0:T(8,128)(2,1)S(1)}, bf16[256,512]{1,0:T(8,128)(2,1)S(1)}, u32[]{:S(2)}, u32[]{:S(2)}) collective-permute-start(bf16[256,512]{1,0:T(8,128)(2,1)S(1)} %get-tuple-element.106), channel_id=1, source_target_pairs={{0,8},{1,24},{2,10},{3,26},{4,12},{5,28},{6,14},{7,30},{8,0},{9,16... | collective-permute-start | bytes 786440 | tf_op jit(solution)/shard_map/ppermute | solution.py:41
  210.2 4.8 %collective-permute-done.36 = bf16[256,512]{1,0:T(8,128)(2,1)S(1)} collective-permute-done((bf16[256,512]{1,0:T(8,128)(2,1)S(1)}, bf16[256,512]{1,0:T(8,128)(2,1)S(1)}, u32[]{:S(2)}, u32[]{:S(2)}) %collective-permute-start.36) | collective-permute-done | bytes 262176 | tf_op jit(solution)/shard_map/ppermute | solution.py:41
  215.0 5.7 %collective-permute-done.35 = bf16[256,512]{1,0:T(8,128)(2,1)S(1)} collective-permute-done((bf16[256,512]{1,0:T(8,128)(2,1)S(1)}, bf16[256,512]{1,0:T(8,128)(2,1)S(1)}, u32[]{:S(2)}, u32[]{:S(2)}) %collective-permute-start.35) | collective-permute-done | bytes 262176 | tf_op jit(solution)/shard_map/ppermute | solution.py:41
  (183 shorter events, 88.3 us)
Async XLA Ops:
  6.5 124.1 %all-gather.3.cloned.1.call-start = ((), (), s32[]{:S(2)}) async-start(), calls=%async_computation | async-start | bytes 5242880 | tf_op jit(solution)/shard_map/all_gather | solution.py:389
  22.1 19.2 %collective-permute-start.3 = (bf16[256,1024]{1,0:T(8,128)(2,1)}, bf16[256,1024]{1,0:T(8,128)(2,1)S(1)}, u32[]{:S(2)}, u32[]{:S(2)}) collective-permute-start(bf16[256,1024]{1,0:T(8,128)(2,1)} %maximum_select_fusion), channel_id=1, source_target_pairs={{0,16},{1,17},{2,18},{3,19},{4,20},{5,21},{6,22},{7,23},{8,24},{9,... | collective-permute-start | bytes 1572872 | tf_op jit(solution)/shard_map/ppermute | solution.py:41
  30.0 13.1 %collective-permute-start.4 = (bf16[256,1024]{1,0:T(8,128)(2,1)}, bf16[256,1024]{1,0:T(8,128)(2,1)S(1)}, u32[]{:S(2)}, u32[]{:S(2)}) collective-permute-start(bf16[256,1024]{1,0:T(8,128)(2,1)} %maximum_select_fusion), channel_id=1, source_target_pairs={{0,48},{1,49},{2,50},{3,51},{4,52},{5,53},{6,54},{7,55},{8,56},{9,... | collective-permute-start | bytes 1572872 | tf_op jit(solution)/shard_map/ppermute | solution.py:41
  30.0 15.8 %collective-permute-start.5 = (bf16[256,1024]{1,0:T(8,128)(2,1)}, bf16[256,1024]{1,0:T(8,128)(2,1)}, u32[]{:S(2)}, u32[]{:S(2)}) collective-permute-start(bf16[256,1024]{1,0:T(8,128)(2,1)} %maximum_select_fusion), channel_id=1, source_target_pairs={{0,64},{1,65},{2,66},{3,67},{4,68},{5,69},{6,70},{7,71},{8,72},{9,... | collective-permute-start | bytes 1572872 | tf_op jit(solution)/shard_map/ppermute | solution.py:41
  45.8 31.4 %collective-permute-start.12 = (bf16[1024,640]{1,0:T(8,128)(2,1)}, bf16[1024,640]{1,0:T(8,128)(2,1)S(1)}, u32[]{:S(2)}, u32[]{:S(2)}) collective-permute-start(bf16[1024,640]{1,0:T(8,128)(2,1)} %pad_maximum_fusion), channel_id=1, source_target_pairs={{0,1},{1,0},{2,3},{3,2},{4,5},{5,4},{6,7},{7,6},{8,9},{9,8},{10,11... | collective-permute-start | bytes 3932168 | tf_op jit(solution)/shard_map/ppermute | solution.py:41
  49.1 12.4 %collective-permute-start.8 = (bf16[256,1024]{1,0:T(8,128)(2,1)}, bf16[256,1024]{1,0:T(8,128)(2,1)}, u32[]{:S(2)}, u32[]{:S(2)}) collective-permute-start(bf16[256,1024]{1,0:T(8,128)(2,1)} %collective-permute-done.5), channel_id=1, source_target_pairs={{0,16},{1,17},{2,18},{3,19},{4,20},{5,21},{6,22},{7,23},{8,24},{9,... | collective-permute-start | bytes 1572872 | tf_op jit(solution)/shard_map/ppermute | solution.py:41
  50.2 13.0 %collective-permute-start.9 = (bf16[256,1024]{1,0:T(8,128)(2,1)}, bf16[256,1024]{1,0:T(8,128)(2,1)}, u32[]{:S(2)}, u32[]{:S(2)}) collective-permute-start(bf16[256,1024]{1,0:T(8,128)(2,1)} %collective-permute-done.5), channel_id=1, source_target_pairs={{0,48},{1,49},{2,50},{3,51},{4,52},{5,53},{6,54},{7,55},{8,56},{9,... | collective-permute-start | bytes 1572872 | tf_op jit(solution)/shard_map/ppermute | solution.py:41
  52.1 28.0 %collective-permute-start.7 = (bf16[128,1024]{1,0:T(8,128)(2,1)S(1)}, bf16[128,1024]{1,0:T(8,128)(2,1)S(1)}, u32[]{:S(2)}, u32[]{:S(2)}) collective-permute-start(bf16[128,1024]{1,0:T(8,128)(2,1)S(1)} %slice.37), channel_id=1, source_target_pairs={{0,48},{1,49},{2,50},{3,51},{4,52},{5,53},{6,54},{7,55},{8,56},{9,... | collective-permute-start | bytes 786440 | tf_op jit(solution)/shard_map/ppermute | solution.py:41
  54.9 25.2 %collective-permute-start.6 = (bf16[128,1024]{1,0:T(8,128)(2,1)S(1)}, bf16[128,1024]{1,0:T(8,128)(2,1)S(1)}, u32[]{:S(2)}, u32[]{:S(2)}) collective-permute-start(bf16[128,1024]{1,0:T(8,128)(2,1)S(1)} %slice.36), channel_id=1, source_target_pairs={{0,16},{1,17},{2,18},{3,19},{4,20},{5,21},{6,22},{7,23},{8,24},{9,... | collective-permute-start | bytes 786440 | tf_op jit(solution)/shard_map/ppermute | solution.py:41
  98.8 10.8 %collective-permute-start.15 = (bf16[128,1280]{1,0:T(8,128)(2,1)}, bf16[128,1280]{1,0:T(8,128)(2,1)S(1)}, u32[]{:S(2)}, u32[]{:S(2)}) collective-permute-start(bf16[128,1280]{1,0:T(8,128)(2,1)} %get-tuple-element.70), channel_id=1, source_target_pairs={{0,2},{1,3},{2,4},{3,5},{4,6},{5,7},{6,0},{7,1},{8,10},{9,11},{10,... | collective-permute-start | bytes 983048 | tf_op jit(solution)/shard_map/ppermute | solution.py:41
  98.8 10.8 %collective-permute-start.16 = (bf16[128,1280]{1,0:T(8,128)(2,1)}, bf16[128,1280]{1,0:T(8,128)(2,1)S(1)}, u32[]{:S(2)}, u32[]{:S(2)}) collective-permute-start(bf16[128,1280]{1,0:T(8,128)(2,1)} %get-tuple-element.71), channel_id=1, source_target_pairs={{0,6},{1,7},{2,0},{3,1},{4,2},{5,3},{6,4},{7,5},{8,14},{9,15},{10,... | collective-permute-start | bytes 983048 | tf_op jit(solution)/shard_map/ppermute | solution.py:41
  101.6 22.3 %collective-permute-start.18 = (bf16[128,1280]{1,0:T(8,128)(2,1)}, bf16[128,1280]{1,0:T(8,128)(2,1)S(1)}, u32[]{:S(2)}, u32[]{:S(2)}) collective-permute-start(bf16[128,1280]{1,0:T(8,128)(2,1)} %copy-done.24), channel_id=1, source_target_pairs={{0,2},{1,3},{2,4},{3,5},{4,6},{5,7},{6,0},{7,1},{8,10},{9,11},{10,... | collective-permute-start | bytes 983048 | tf_op jit(solution)/shard_map/ppermute | solution.py:41
  103.0 20.9 %collective-permute-start.19 = (bf16[128,1280]{1,0:T(8,128)(2,1)}, bf16[128,1280]{1,0:T(8,128)(2,1)S(1)}, u32[]{:S(2)}, u32[]{:S(2)}) collective-permute-start(bf16[128,1280]{1,0:T(8,128)(2,1)} %copy-done.23), channel_id=1, source_target_pairs={{0,6},{1,7},{2,0},{3,1},{4,2},{5,3},{6,4},{7,5},{8,14},{9,15},{10,... | collective-permute-start | bytes 983048 | tf_op jit(solution)/shard_map/ppermute | solution.py:41
  112.5 11.4 %collective-permute-start.17 = (bf16[128,1280]{1,0:T(8,128)(2,1)}, bf16[128,1280]{1,0:T(8,128)(2,1)S(1)}, u32[]{:S(2)}, u32[]{:S(2)}) collective-permute-start(bf16[128,1280]{1,0:T(8,128)(2,1)} %get-tuple-element.80), channel_id=1, source_target_pairs={{0,2},{1,3},{2,4},{3,5},{4,6},{5,7},{6,0},{7,1},{8,10},{9,11},{10,... | collective-permute-start | bytes 983048 | tf_op jit(solution)/shard_map/ppermute | solution.py:41
  112.8 11.1 %collective-permute-start.20 = (bf16[128,1280]{1,0:T(8,128)(2,1)}, bf16[128,1280]{1,0:T(8,128)(2,1)S(1)}, u32[]{:S(2)}, u32[]{:S(2)}) collective-permute-start(bf16[128,1280]{1,0:T(8,128)(2,1)} %get-tuple-element.83), channel_id=1, source_target_pairs={{0,6},{1,7},{2,0},{3,1},{4,2},{5,3},{6,4},{7,5},{8,14},{9,15},{10,... | collective-permute-start | bytes 983048 | tf_op jit(solution)/shard_map/ppermute | solution.py:41
  130.6 21.6 %collective-permute-start.25 = (bf16[4,512,1024]{2,1,0:T(8,128)(2,1)}, bf16[4,512,1024]{2,1,0:T(8,128)(2,1)}, u32[]{:S(2)}, u32[]{:S(2)}) collective-permute-start(bf16[4,512,1024]{2,1,0:T(8,128)(2,1)} %bitcast.42), channel_id=1, source_target_pairs={{0,8},{1,9},{2,10},{3,11},{4,12},{5,13},{6,14},{7,15},{8,0},{9,1},... | collective-permute-start | bytes 12582920 | tf_op jit(solution)/shard_map/ppermute | solution.py:41
  158.7 15.3 %collective-permute-start.26 = (bf16[256,1024]{1,0:T(8,128)(2,1)}, bf16[256,1024]{1,0:T(8,128)(2,1)}, u32[]{:S(2)}, u32[]{:S(2)}) collective-permute-start(bf16[256,1024]{1,0:T(8,128)(2,1)} %get-tuple-element.92), channel_id=1, source_target_pairs={{0,16},{1,17},{2,18},{3,19},{4,20},{5,21},{6,22},{7,23},{8,24},{9,... | collective-permute-start | bytes 1572872 | tf_op jit(solution)/shard_map/ppermute | solution.py:41
  159.3 14.7 %collective-permute-start.27 = (bf16[256,1024]{1,0:T(8,128)(2,1)}, bf16[256,1024]{1,0:T(8,128)(2,1)}, u32[]{:S(2)}, u32[]{:S(2)}) collective-permute-start(bf16[256,1024]{1,0:T(8,128)(2,1)} %get-tuple-element.93), channel_id=1, source_target_pairs={{0,48},{1,49},{2,50},{3,51},{4,52},{5,53},{6,54},{7,55},{8,56},{9,... | collective-permute-start | bytes 1572872 | tf_op jit(solution)/shard_map/ppermute | solution.py:41
  165.8 16.1 %collective-permute-start.31 = (bf16[128,1024]{1,0:T(8,128)(2,1)S(1)}, bf16[128,1024]{1,0:T(8,128)(2,1)S(1)}, u32[]{:S(2)}, u32[]{:S(2)}) collective-permute-start(bf16[128,1024]{1,0:T(8,128)(2,1)S(1)} %get-tuple-element.102), channel_id=1, source_target_pairs={{0,16},{1,17},{2,18},{3,19},{4,20},{5,21},{6,22},{7,23},{8,24},{9,... | collective-permute-start | bytes 786440 | tf_op jit(solution)/shard_map/ppermute | solution.py:41
  167.3 14.6 %collective-permute-start.32 = (bf16[128,1024]{1,0:T(8,128)(2,1)S(1)}, bf16[128,1024]{1,0:T(8,128)(2,1)S(1)}, u32[]{:S(2)}, u32[]{:S(2)}) collective-permute-start(bf16[128,1024]{1,0:T(8,128)(2,1)S(1)} %get-tuple-element.103), channel_id=1, source_target_pairs={{0,48},{1,49},{2,50},{3,51},{4,52},{5,53},{6,54},{7,55},{8,56},{9,... | collective-permute-start | bytes 786440 | tf_op jit(solution)/shard_map/ppermute | solution.py:41
  179.3 14.4 %collective-permute-start.29 = (bf16[256,1024]{1,0:T(8,128)(2,1)S(1)}, bf16[256,1024]{1,0:T(8,128)(2,1)S(1)}, u32[]{:S(2)}, u32[]{:S(2)}) collective-permute-start(bf16[256,1024]{1,0:T(8,128)(2,1)S(1)} %get-tuple-element.109), channel_id=1, source_target_pairs={{0,48},{1,49},{2,50},{3,51},{4,52},{5,53},{6,54},{7,55},{8,56},{9,... | collective-permute-start | bytes 1572872 | tf_op jit(solution)/shard_map/ppermute | solution.py:41
  181.9 11.8 %collective-permute-start.28 = (bf16[256,1024]{1,0:T(8,128)(2,1)S(1)}, bf16[256,1024]{1,0:T(8,128)(2,1)}, u32[]{:S(2)}, u32[]{:S(2)}) collective-permute-start(bf16[256,1024]{1,0:T(8,128)(2,1)S(1)} %get-tuple-element.107), channel_id=1, source_target_pairs={{0,16},{1,17},{2,18},{3,19},{4,20},{5,21},{6,22},{7,23},{8,24},{9,... | collective-permute-start | bytes 1572872 | tf_op jit(solution)/shard_map/ppermute | solution.py:41
  196.0 19.0 %collective-permute-start.36 = (bf16[256,512]{1,0:T(8,128)(2,1)S(1)}, bf16[256,512]{1,0:T(8,128)(2,1)S(1)}, u32[]{:S(2)}, u32[]{:S(2)}) collective-permute-start(bf16[256,512]{1,0:T(8,128)(2,1)S(1)} %get-tuple-element.106), channel_id=1, source_target_pairs={{0,8},{1,24},{2,10},{3,26},{4,12},{5,28},{6,14},{7,30},{8,0},{9,16... | collective-permute-start | bytes 786440 | tf_op jit(solution)/shard_map/ppermute | solution.py:41
  208.1 12.6 %collective-permute-start.35 = (bf16[256,512]{1,0:T(8,128)(2,1)S(1)}, bf16[256,512]{1,0:T(8,128)(2,1)S(1)}, u32[]{:S(2)}, u32[]{:S(2)}) collective-permute-start(bf16[256,512]{1,0:T(8,128)(2,1)S(1)} %get-tuple-element.105), channel_id=1, source_target_pairs={{0,0},{1,16},{2,2},{3,18},{4,4},{5,20},{6,6},{7,22},{8,8},{9,24},{... | collective-permute-start | bytes 786440 | tf_op jit(solution)/shard_map/ppermute | solution.py:41
  (51 other events, 346.8 us)
Sparse Core Ops, SparseCore 0:
  22.2 57.7 all-gather.2

commit v15 on v10

--- a/solution.py
+++ b/solution.py
@@ -374,7 +374,6 @@
     out_near = lax.all_gather(after(out_weight, block), "y", axis=0, tiled=False)
 
     squares = jnp.sum(jnp.square(gathered.astype(jnp.float32) * slice_gain), axis=-1)
-    gathered, squares = lax.optimization_barrier((gathered, squares))
     low, high = project([(y + 2) % 4], zh, core, gathered, weights, True)
     from_below = y_shift(low, 1)
     from_above = y_shift(high, -1)

time: 223 us -> 210 us (0.942)
  local copies, waits for them, and re-layouts: 30.6 us -> 19.6 us
  waiting for transfers between devices: 58.4 us -> 61.6 us
    unnamed x71 -> x59, local copies, waits for them, and re-layouts: 19.9 us -> 8.89 us
    ppermute x38, waiting for transfers between devices: 58.4 us -> 61.6 us  [send(): return lax.ppermute(value, AXES, pairs(change))]
  transfers between devices with their start and end apart: 39 -> 39, of which waited for: 17 -> 18; matrix products, arithmetic and copies ran while one was open for 11% -> 10% of each run, Pallas kernels for 14% -> 14%
where the time goes in v15:
time: 210 us; the launch traced here: 209 us
  starting transfers between devices  65.4 us (31%)
  waiting for transfers between devices  61.6 us (29%)
  Pallas kernels  32.9 us (16%)
  local copies, waits for them, and re-layouts  19.6 us (9%)
  other arithmetic  15.2 us (7%)
  between operations  14.6 us (7%)
    ppermute x38, starting transfers between devices, send(): return lax.ppermute(value, AXES, pairs(change))  65.4 us
    ppermute x38, waiting for transfers between devices, send(): return lax.ppermute(value, AXES, pairs(change))  61.6 us
    pallas_call x3, Pallas kernels, products(): pl.pallas_call(lambda *refs: products_kernel(form, steps, *refs), grid_sp...  13.1 us
    pallas_call x3, Pallas kernels, project(): pl.pallas_call(project_kernel, grid_spec=pltpu.PrefetchScalarGridSpec(num...  9.87 us
    unnamed x59, local copies, waits for them, and re-layouts  8.89 us
    pallas_call x2, Pallas kernels, attention(): pl.pallas_call(attention_kernel, grid=(1,), in_specs=[pl.BlockSpec((v.sha...  5.48 us
  transfers between devices with their start and end apart: 39, of which 18 were waited for; matrix products, arithmetic and copies ran while one was open for 10% of the time, Pallas kernels for 14%

profile of v15, /device:TPU:3, one launch (start us, length us, event | category | flops | bytes accessed | tf_op | source)
XLA Modules:
  0.0 209.3 jit_solution(2500090071792020279)
XLA Ops:
  20.0 8.4 %collective-permute-start.3 = (bf16[256,1024]{1,0:T(8,128)(2,1)S(1)}, bf16[256,1024]{1,0:T(8,128)(2,1)S(1)}, u32[]{:S(2)}, u32[]{:S(2)}) collective-permute-start(bf16[256,1024]{1,0:T(8,128)(2,1)S(1)} %maximum_select_fusion), channel_id=1, source_target_pairs={{0,16},{1,17},{2,18},{3,19},{4,20},{5,21},{6,22},{7,23},{8,24},{9,... | collective-permute-start | bytes 1572872 | tf_op jit(solution)/shard_map/ppermute | solution.py:41
  28.4 3.7 %collective-permute-start.5 = (bf16[256,1024]{1,0:T(8,128)(2,1)S(1)}, bf16[256,1024]{1,0:T(8,128)(2,1)}, u32[]{:S(2)}, u32[]{:S(2)}) collective-permute-start(bf16[256,1024]{1,0:T(8,128)(2,1)S(1)} %maximum_select_fusion), channel_id=1, source_target_pairs={{0,64},{1,65},{2,66},{3,67},{4,68},{5,69},{6,70},{7,71},{8,72},{9,... | collective-permute-start | bytes 1572872 | tf_op jit(solution)/shard_map/ppermute | solution.py:41
  32.1 7.1 %collective-permute-done.3 = bf16[256,1024]{1,0:T(8,128)(2,1)S(1)} collective-permute-done((bf16[256,1024]{1,0:T(8,128)(2,1)S(1)}, bf16[256,1024]{1,0:T(8,128)(2,1)S(1)}, u32[]{:S(2)}, u32[]{:S(2)}) %collective-permute-start.3) | collective-permute-done | bytes 524320 | tf_op jit(solution)/shard_map/ppermute | solution.py:41
  43.9 3.3 %collective-permute-start.12 = (bf16[1024,640]{1,0:T(8,128)(2,1)}, bf16[1024,640]{1,0:T(8,128)(2,1)S(1)}, u32[]{:S(2)}, u32[]{:S(2)}) collective-permute-start(bf16[1024,640]{1,0:T(8,128)(2,1)} %pad_maximum_fusion), channel_id=1, source_target_pairs={{0,1},{1,0},{2,3},{3,2},{4,5},{5,4},{6,7},{7,6},{8,9},{9,8},{10,11... | collective-permute-start | bytes 3932168 | tf_op jit(solution)/shard_map/ppermute | solution.py:41
  48.9 10.7 %collective-permute-done.8 = bf16[256,1024]{1,0:T(8,128)(2,1)} collective-permute-done((bf16[256,1024]{1,0:T(8,128)(2,1)}, bf16[256,1024]{1,0:T(8,128)(2,1)}, u32[]{:S(2)}, u32[]{:S(2)}) %collective-permute-start.8) | collective-permute-done | bytes 524320 | tf_op jit(solution)/shard_map/ppermute | solution.py:41
  65.0 2.7 %collective-permute-start.11 = (bf16[128,1024]{1,0:T(8,128)(2,1)S(1)}, bf16[128,1024]{1,0:T(8,128)(2,1)S(1)}, u32[]{:S(2)}, u32[]{:S(2)}) collective-permute-start(bf16[128,1024]{1,0:T(8,128)(2,1)S(1)} %slice.41), channel_id=1, source_target_pairs={{0,48},{1,49},{2,50},{3,51},{4,52},{5,53},{6,54},{7,55},{8,56},{9,... | collective-permute-start | bytes 786440 | tf_op jit(solution)/shard_map/ppermute | solution.py:41
  67.9 6.3 %collective-permute-done.11 = bf16[128,1024]{1,0:T(8,128)(2,1)S(1)} collective-permute-done((bf16[128,1024]{1,0:T(8,128)(2,1)S(1)}, bf16[128,1024]{1,0:T(8,128)(2,1)S(1)}, u32[]{:S(2)}, u32[]{:S(2)}) %collective-permute-start.11) | collective-permute-done | bytes 262176 | tf_op jit(solution)/shard_map/ppermute | solution.py:41
  83.0 2.7 %collective-permute-start.15 = (bf16[128,1280]{1,0:T(8,128)(2,1)S(1)}, bf16[128,1280]{1,0:T(8,128)(2,1)S(1)}, u32[]{:S(2)}, u32[]{:S(2)}) collective-permute-start(bf16[128,1280]{1,0:T(8,128)(2,1)S(1)} %get-tuple-element.58), channel_id=1, source_target_pairs={{0,6},{1,7},{2,0},{3,1},{4,2},{5,3},{6,4},{7,5},{8,14},{9,15},{10,... | collective-permute-start | bytes 983048 | tf_op jit(solution)/shard_map/ppermute | solution.py:41
  85.8 5.2 %shard_map.65 = (bf16[128,1280]{1,0:T(8,128)(2,1)S(1)}, bf16[128,1280]{1,0:T(8,128)(2,1)S(1)}, bf16[128,1280]{1,0:T(8,128)(2,1)S(1)}, bf16[128,1280]{1,0:T(8,128)(2,1)S(1)}) custom-call(s32[4]{0:T(128)S(1)} %pad_add_fusion.4.at_ref, bf16[4,256,2048]{2,1,0:T(8,128)(2,1)S(1)} %bitcast_dynamic-update-slice_fusion.rows_ref, bf16[1024,512]{1,0:T(8,128)(2,1)S(1)} %copy-done.2, ...), custom_call_target="tpu_custom_call" | custom-call | tf_op jit(solution)/shard_map/pallas_call | solution.py:230
  91.1 2.7 %collective-permute-start.17 = (bf16[128,1280]{1,0:T(8,128)(2,1)S(1)}, bf16[128,1280]{1,0:T(8,128)(2,1)S(1)}, u32[]{:S(2)}, u32[]{:S(2)}) collective-permute-start(bf16[128,1280]{1,0:T(8,128)(2,1)S(1)} %get-tuple-element.66), channel_id=1, source_target_pairs={{0,6},{1,7},{2,0},{3,1},{4,2},{5,3},{6,4},{7,5},{8,14},{9,15},{10,... | collective-permute-start | bytes 983048 | tf_op jit(solution)/shard_map/ppermute | solution.py:41
  96.5 2.7 %collective-permute-start.19 = (bf16[128,1280]{1,0:T(8,128)(2,1)}, bf16[128,1280]{1,0:T(8,128)(2,1)}, u32[]{:S(2)}, u32[]{:S(2)}) collective-permute-start(bf16[128,1280]{1,0:T(8,128)(2,1)} %add.332), channel_id=1, source_target_pairs={{0,6},{1,7},{2,0},{3,1},{4,2},{5,3},{6,4},{7,5},{8,14},{9,15},{10,... | collective-permute-start | bytes 983048 | tf_op jit(solution)/shard_map/ppermute | solution.py:41
  115.1 2.7 %shard_map.68.refs_1_ = bf16[256,512]{1,0:T(8,128)(2,1)S(1)} custom-call(bf16[256,1280]{1,0:T(8,128)(2,1)S(1)} %copy-done.4, bf16[128,1280]{1,0:T(8,128)(2,1)} %collective-permute-done.18.refs_1_.refs_6_, bf16[128,1280]{1,0:T(8,128)(2,1)S(1)} %copy-done.7, bf16[128,1280]{1,0:T(8,128)(2,1)S(1)} %copy-done.9, ...), custom_call_target="tpu_custom_call" | custom-call | tf_op jit(solution)/shard_map/pallas_call | solution.py:181
  117.8 3.0 %collective-permute-start.24 = (bf16[256,512]{1,0:T(8,128)(2,1)S(1)}, bf16[256,512]{1,0:T(8,128)(2,1)S(1)}, u32[]{:S(2)}, u32[]{:S(2)}) collective-permute-start(bf16[256,512]{1,0:T(8,128)(2,1)S(1)} %shard_map.68.refs_1_), channel_id=1, source_target_pairs={{0,1},{1,0},{2,3},{3,2},{4,5},{5,4},{6,7},{7,6},{8,9},{9,8},{10,11... | collective-permute-start | bytes 786440 | tf_op jit(solution)/shard_map/ppermute | solution.py:41
  121.7 2.7 %shard_map.69.refs_2_ = bf16[256,512]{1,0:T(8,128)(2,1)S(1)} custom-call(bf16[256,1280]{1,0:T(8,128)(2,1)S(1)} %copy-done.4, bf16[128,1280]{1,0:T(8,128)(2,1)} %collective-permute-done.18.refs_1_.refs_6_, bf16[128,1280]{1,0:T(8,128)(2,1)S(1)} %copy-done.7, bf16[128,1280]{1,0:T(8,128)(2,1)S(1)} %copy-done.9, ...), custom_call_target="tpu_custom_call" | custom-call | tf_op jit(solution)/shard_map/pallas_call | solution.py:181
  127.1 6.4 %collective-permute-done.25.refs_4_ = bf16[256,512]{1,0:T(8,128)(2,1)S(1)} collective-permute-done((bf16[256,512]{1,0:T(8,128)(2,1)S(1)}, bf16[256,512]{1,0:T(8,128)(2,1)S(1)}, u32[]{:S(2)}, u32[]{:S(2)}) %collective-permute-start.25) | collective-permute-done | bytes 262176 | tf_op jit(solution)/shard_map/ppermute | solution.py:41
  135.7 4.3 %shard_map.71 = (bf16[256,1024]{1,0:T(8,128)(2,1)}, bf16[256,1024]{1,0:T(8,128)(2,1)}) custom-call(s32[4]{0:T(128)S(1)} %get-tuple-element.104.refs_0_, bf16[256,512]{1,0:T(8,128)(2,1)S(1)} %shard_map.68.refs_1_, bf16[256,512]{1,0:T(8,128)(2,1)S(1)} %shard_map.69.refs_2_, bf16[256,512]{1,0:T(8,128)(2,1)S(1)} %collective-permute-done.24.refs_3_, ...), custom_call_target="tpu_custom_call" | custom-call | tf_op jit(solution)/shard_map/pallas_call | solution.py:281
  143.8 3.3 %shard_map.72 = (bf16[128,1024]{1,0:T(8,128)(2,1)S(1)}, bf16[128,1024]{1,0:T(8,128)(2,1)S(1)}, bf16[128,1024]{1,0:T(8,128)(2,1)S(1)}, bf16[128,1024]{1,0:T(8,128)(2,1)S(1)}) custom-call(s32[4]{0:T(128)S(1)} %get-tuple-element.105.refs_0_, bf16[256,512]{1,0:T(8,128)(2,1)S(1)} %shard_map.68.refs_1_, bf16[256,512]{1,0:T(8,128)(2,1)S(1)} %shard_map.69.refs_2_, ...), custom_call_target="tpu_custom_call" | custom-call | tf_op jit(solution)/shard_map/pallas_call | solution.py:281
  147.1 2.6 %collective-permute-start.32 = (bf16[128,1024]{1,0:T(8,128)(2,1)S(1)}, bf16[128,1024]{1,0:T(8,128)(2,1)S(1)}, u32[]{:S(2)}, u32[]{:S(2)}) collective-permute-start(bf16[128,1024]{1,0:T(8,128)(2,1)S(1)} %get-tuple-element.86), channel_id=1, source_target_pairs={{0,16},{1,17},{2,18},{3,19},{4,20},{5,21},{6,22},{7,23},{8,24},{9,... | collective-permute-start | bytes 786440 | tf_op jit(solution)/shard_map/ppermute | solution.py:41
  150.4 5.4 %shard_map.70 = (bf16[256,1024]{1,0:T(8,128)(2,1)S(1)}, bf16[256,1024]{1,0:T(8,128)(2,1)S(1)}, bf16[256,1024]{1,0:T(8,128)(2,1)S(1)}, bf16[256,1024]{1,0:T(8,128)(2,1)S(1)}) custom-call(s32[8]{0:T(128)S(1)} %stack.102.refs_0_, bf16[256,512]{1,0:T(8,128)(2,1)S(1)} %shard_map.68.refs_1_, bf16[256,512]{1,0:T(8,128)(2,1)S(1)} %shard_map.69.refs_2_, ...), custom_call_target="tpu_custom_call" | custom-call | tf_op jit(solution)/shard_map/pallas_call | solution.py:281
  161.3 2.7 %collective-permute-start.30 = (bf16[256,1024]{1,0:T(8,128)(2,1)S(1)}, bf16[256,1024]{1,0:T(8,128)(2,1)S(1)}, u32[]{:S(2)}, u32[]{:S(2)}) collective-permute-start(bf16[256,1024]{1,0:T(8,128)(2,1)S(1)} %get-tuple-element.93), channel_id=1, source_target_pairs={{0,48},{1,49},{2,50},{3,51},{4,52},{5,53},{6,54},{7,55},{8,56},{9,... | collective-permute-start | bytes 1572872 | tf_op jit(solution)/shard_map/ppermute | solution.py:41
  169.0 7.2 %collective-permute-done.30 = bf16[256,1024]{1,0:T(8,128)(2,1)S(1)} collective-permute-done((bf16[256,1024]{1,0:T(8,128)(2,1)S(1)}, bf16[256,1024]{1,0:T(8,128)(2,1)S(1)}, u32[]{:S(2)}, u32[]{:S(2)}) %collective-permute-start.30) | collective-permute-done | bytes 524320 | tf_op jit(solution)/shard_map/ppermute | solution.py:41
  178.8 10.1 %collective-permute-start.37 = (bf16[256,512]{1,0:T(8,128)(2,1)S(1)}, bf16[256,512]{1,0:T(8,128)(2,1)S(1)}, u32[]{:S(2)}, u32[]{:S(2)}) collective-permute-start(bf16[256,512]{1,0:T(8,128)(2,1)S(1)} %get-tuple-element.90), channel_id=1, source_target_pairs={{0,8},{1,24},{2,10},{3,26},{4,12},{5,28},{6,14},{7,30},{8,0},{9,16... | collective-permute-start | bytes 786440 | tf_op jit(solution)/shard_map/ppermute | solution.py:41
  188.9 3.6 %collective-permute-start.36 = (bf16[256,512]{1,0:T(8,128)(2,1)S(1)}, bf16[256,512]{1,0:T(8,128)(2,1)S(1)}, u32[]{:S(2)}, u32[]{:S(2)}) collective-permute-start(bf16[256,512]{1,0:T(8,128)(2,1)S(1)} %get-tuple-element.89), channel_id=1, source_target_pairs={{0,0},{1,16},{2,2},{3,18},{4,4},{5,20},{6,6},{7,22},{8,8},{9,24},{... | collective-permute-start | bytes 786440 | tf_op jit(solution)/shard_map/ppermute | solution.py:41
  194.6 6.8 %collective-permute-done.36 = bf16[256,512]{1,0:T(8,128)(2,1)S(1)} collective-permute-done((bf16[256,512]{1,0:T(8,128)(2,1)S(1)}, bf16[256,512]{1,0:T(8,128)(2,1)S(1)}, u32[]{:S(2)}, u32[]{:S(2)}) %collective-permute-start.36) | collective-permute-done | bytes 262176 | tf_op jit(solution)/shard_map/ppermute | solution.py:41
  (171 shorter events, 78.1 us)
Async XLA Ops:
  6.5 107.2 %all-gather.3.cloned.1.call-start = ((), (), s32[]{:S(2)}) async-start(), calls=%async_computation | async-start | bytes 5242880 | tf_op jit(solution)/shard_map/all_gather | solution.py:374
  20.0 19.3 %collective-permute-start.3 = (bf16[256,1024]{1,0:T(8,128)(2,1)S(1)}, bf16[256,1024]{1,0:T(8,128)(2,1)S(1)}, u32[]{:S(2)}, u32[]{:S(2)}) collective-permute-start(bf16[256,1024]{1,0:T(8,128)(2,1)S(1)} %maximum_select_fusion), channel_id=1, source_target_pairs={{0,16},{1,17},{2,18},{3,19},{4,20},{5,21},{6,22},{7,23},{8,24},{9,... | collective-permute-start | bytes 1572872 | tf_op jit(solution)/shard_map/ppermute | solution.py:41
  28.4 12.9 %collective-permute-start.4 = (bf16[256,1024]{1,0:T(8,128)(2,1)S(1)}, bf16[256,1024]{1,0:T(8,128)(2,1)S(1)}, u32[]{:S(2)}, u32[]{:S(2)}) collective-permute-start(bf16[256,1024]{1,0:T(8,128)(2,1)S(1)} %maximum_select_fusion), channel_id=1, source_target_pairs={{0,48},{1,49},{2,50},{3,51},{4,52},{5,53},{6,54},{7,55},{8,56},{9,... | collective-permute-start | bytes 1572872 | tf_op jit(solution)/shard_map/ppermute | solution.py:41
  28.4 15.5 %collective-permute-start.5 = (bf16[256,1024]{1,0:T(8,128)(2,1)S(1)}, bf16[256,1024]{1,0:T(8,128)(2,1)}, u32[]{:S(2)}, u32[]{:S(2)}) collective-permute-start(bf16[256,1024]{1,0:T(8,128)(2,1)S(1)} %maximum_select_fusion), channel_id=1, source_target_pairs={{0,64},{1,65},{2,66},{3,67},{4,68},{5,69},{6,70},{7,71},{8,72},{9,... | collective-permute-start | bytes 1572872 | tf_op jit(solution)/shard_map/ppermute | solution.py:41
  43.9 31.4 %collective-permute-start.12 = (bf16[1024,640]{1,0:T(8,128)(2,1)}, bf16[1024,640]{1,0:T(8,128)(2,1)S(1)}, u32[]{:S(2)}, u32[]{:S(2)}) collective-permute-start(bf16[1024,640]{1,0:T(8,128)(2,1)} %pad_maximum_fusion), channel_id=1, source_target_pairs={{0,1},{1,0},{2,3},{3,2},{4,5},{5,4},{6,7},{7,6},{8,9},{9,8},{10,11... | collective-permute-start | bytes 3932168 | tf_op jit(solution)/shard_map/ppermute | solution.py:41
  47.2 12.5 %collective-permute-start.8 = (bf16[256,1024]{1,0:T(8,128)(2,1)}, bf16[256,1024]{1,0:T(8,128)(2,1)}, u32[]{:S(2)}, u32[]{:S(2)}) collective-permute-start(bf16[256,1024]{1,0:T(8,128)(2,1)} %collective-permute-done.5), channel_id=1, source_target_pairs={{0,16},{1,17},{2,18},{3,19},{4,20},{5,21},{6,22},{7,23},{8,24},{9,... | collective-permute-start | bytes 1572872 | tf_op jit(solution)/shard_map/ppermute | solution.py:41
  48.3 15.7 %collective-permute-start.9 = (bf16[256,1024]{1,0:T(8,128)(2,1)}, bf16[256,1024]{1,0:T(8,128)(2,1)}, u32[]{:S(2)}, u32[]{:S(2)}) collective-permute-start(bf16[256,1024]{1,0:T(8,128)(2,1)} %collective-permute-done.5), channel_id=1, source_target_pairs={{0,48},{1,49},{2,50},{3,51},{4,52},{5,53},{6,54},{7,55},{8,56},{9,... | collective-permute-start | bytes 1572872 | tf_op jit(solution)/shard_map/ppermute | solution.py:41
  61.9 16.4 %collective-permute-start.7 = (bf16[128,1024]{1,0:T(8,128)(2,1)S(1)}, bf16[128,1024]{1,0:T(8,128)(2,1)S(1)}, u32[]{:S(2)}, u32[]{:S(2)}) collective-permute-start(bf16[128,1024]{1,0:T(8,128)(2,1)S(1)} %slice.31), channel_id=1, source_target_pairs={{0,48},{1,49},{2,50},{3,51},{4,52},{5,53},{6,54},{7,55},{8,56},{9,... | collective-permute-start | bytes 786440 | tf_op jit(solution)/shard_map/ppermute | solution.py:41
  64.0 14.3 %collective-permute-start.6 = (bf16[128,1024]{1,0:T(8,128)(2,1)S(1)}, bf16[128,1024]{1,0:T(8,128)(2,1)S(1)}, u32[]{:S(2)}, u32[]{:S(2)}) collective-permute-start(bf16[128,1024]{1,0:T(8,128)(2,1)S(1)} %slice.30), channel_id=1, source_target_pairs={{0,16},{1,17},{2,18},{3,19},{4,20},{5,21},{6,22},{7,23},{8,24},{9,... | collective-permute-start | bytes 786440 | tf_op jit(solution)/shard_map/ppermute | solution.py:41
  83.0 11.9 %collective-permute-start.14 = (bf16[128,1280]{1,0:T(8,128)(2,1)S(1)}, bf16[128,1280]{1,0:T(8,128)(2,1)S(1)}, u32[]{:S(2)}, u32[]{:S(2)}) collective-permute-start(bf16[128,1280]{1,0:T(8,128)(2,1)S(1)} %get-tuple-element.57), channel_id=1, source_target_pairs={{0,2},{1,3},{2,4},{3,5},{4,6},{5,7},{6,0},{7,1},{8,10},{9,11},{10,... | collective-permute-start | bytes 983048 | tf_op jit(solution)/shard_map/ppermute | solution.py:41
  83.0 11.9 %collective-permute-start.15 = (bf16[128,1280]{1,0:T(8,128)(2,1)S(1)}, bf16[128,1280]{1,0:T(8,128)(2,1)S(1)}, u32[]{:S(2)}, u32[]{:S(2)}) collective-permute-start(bf16[128,1280]{1,0:T(8,128)(2,1)S(1)} %get-tuple-element.58), channel_id=1, source_target_pairs={{0,6},{1,7},{2,0},{3,1},{4,2},{5,3},{6,4},{7,5},{8,14},{9,15},{10,... | collective-permute-start | bytes 983048 | tf_op jit(solution)/shard_map/ppermute | solution.py:41
  91.0 10.1 %collective-permute-start.16 = (bf16[128,1280]{1,0:T(8,128)(2,1)S(1)}, bf16[128,1280]{1,0:T(8,128)(2,1)S(1)}, u32[]{:S(2)}, u32[]{:S(2)}) collective-permute-start(bf16[128,1280]{1,0:T(8,128)(2,1)S(1)} %get-tuple-element.65), channel_id=1, source_target_pairs={{0,2},{1,3},{2,4},{3,5},{4,6},{5,7},{6,0},{7,1},{8,10},{9,11},{10,... | collective-permute-start | bytes 983048 | tf_op jit(solution)/shard_map/ppermute | solution.py:41
  91.1 10.3 %collective-permute-start.17 = (bf16[128,1280]{1,0:T(8,128)(2,1)S(1)}, bf16[128,1280]{1,0:T(8,128)(2,1)S(1)}, u32[]{:S(2)}, u32[]{:S(2)}) collective-permute-start(bf16[128,1280]{1,0:T(8,128)(2,1)S(1)} %get-tuple-element.66), channel_id=1, source_target_pairs={{0,6},{1,7},{2,0},{3,1},{4,2},{5,3},{6,4},{7,5},{8,14},{9,15},{10,... | collective-permute-start | bytes 983048 | tf_op jit(solution)/shard_map/ppermute | solution.py:41
  95.7 13.3 %collective-permute-start.18 = (bf16[128,1280]{1,0:T(8,128)(2,1)}, bf16[128,1280]{1,0:T(8,128)(2,1)}, u32[]{:S(2)}, u32[]{:S(2)}) collective-permute-start(bf16[128,1280]{1,0:T(8,128)(2,1)} %add.331), channel_id=1, source_target_pairs={{0,2},{1,3},{2,4},{3,5},{4,6},{5,7},{6,0},{7,1},{8,10},{9,11},{10,... | collective-permute-start | bytes 983048 | tf_op jit(solution)/shard_map/ppermute | solution.py:41
  96.5 12.5 %collective-permute-start.19 = (bf16[128,1280]{1,0:T(8,128)(2,1)}, bf16[128,1280]{1,0:T(8,128)(2,1)}, u32[]{:S(2)}, u32[]{:S(2)}) collective-permute-start(bf16[128,1280]{1,0:T(8,128)(2,1)} %add.332), channel_id=1, source_target_pairs={{0,6},{1,7},{2,0},{3,1},{4,2},{5,3},{6,4},{7,5},{8,14},{9,15},{10,... | collective-permute-start | bytes 983048 | tf_op jit(solution)/shard_map/ppermute | solution.py:41
  113.7 19.8 %collective-permute-start.26 = (bf16[4,512,1024]{2,1,0:T(8,128)(2,1)}, bf16[4,512,1024]{2,1,0:T(8,128)(2,1)}, u32[]{:S(2)}, u32[]{:S(2)}) collective-permute-start(bf16[4,512,1024]{2,1,0:T(8,128)(2,1)} %bitcast.44), channel_id=1, source_target_pairs={{0,8},{1,9},{2,10},{3,11},{4,12},{5,13},{6,14},{7,15},{8,0},{9,1},... | collective-permute-start | bytes 12582920 | tf_op jit(solution)/shard_map/ppermute | solution.py:41
  140.0 15.9 %collective-permute-start.27 = (bf16[256,1024]{1,0:T(8,128)(2,1)}, bf16[256,1024]{1,0:T(8,128)(2,1)}, u32[]{:S(2)}, u32[]{:S(2)}) collective-permute-start(bf16[256,1024]{1,0:T(8,128)(2,1)} %get-tuple-element.76), channel_id=1, source_target_pairs={{0,16},{1,17},{2,18},{3,19},{4,20},{5,21},{6,22},{7,23},{8,24},{9,... | collective-permute-start | bytes 1572872 | tf_op jit(solution)/shard_map/ppermute | solution.py:41
  141.0 14.9 %collective-permute-start.28 = (bf16[256,1024]{1,0:T(8,128)(2,1)}, bf16[256,1024]{1,0:T(8,128)(2,1)}, u32[]{:S(2)}, u32[]{:S(2)}) collective-permute-start(bf16[256,1024]{1,0:T(8,128)(2,1)} %get-tuple-element.77), channel_id=1, source_target_pairs={{0,48},{1,49},{2,50},{3,51},{4,52},{5,53},{6,54},{7,55},{8,56},{9,... | collective-permute-start | bytes 1572872 | tf_op jit(solution)/shard_map/ppermute | solution.py:41
  147.1 16.9 %collective-permute-start.32 = (bf16[128,1024]{1,0:T(8,128)(2,1)S(1)}, bf16[128,1024]{1,0:T(8,128)(2,1)S(1)}, u32[]{:S(2)}, u32[]{:S(2)}) collective-permute-start(bf16[128,1024]{1,0:T(8,128)(2,1)S(1)} %get-tuple-element.86), channel_id=1, source_target_pairs={{0,16},{1,17},{2,18},{3,19},{4,20},{5,21},{6,22},{7,23},{8,24},{9,... | collective-permute-start | bytes 786440 | tf_op jit(solution)/shard_map/ppermute | solution.py:41
  149.7 14.2 %collective-permute-start.33 = (bf16[128,1024]{1,0:T(8,128)(2,1)S(1)}, bf16[128,1024]{1,0:T(8,128)(2,1)S(1)}, u32[]{:S(2)}, u32[]{:S(2)}) collective-permute-start(bf16[128,1024]{1,0:T(8,128)(2,1)S(1)} %get-tuple-element.87), channel_id=1, source_target_pairs={{0,48},{1,49},{2,50},{3,51},{4,52},{5,53},{6,54},{7,55},{8,56},{9,... | collective-permute-start | bytes 786440 | tf_op jit(solution)/shard_map/ppermute | solution.py:41
  161.3 14.9 %collective-permute-start.30 = (bf16[256,1024]{1,0:T(8,128)(2,1)S(1)}, bf16[256,1024]{1,0:T(8,128)(2,1)S(1)}, u32[]{:S(2)}, u32[]{:S(2)}) collective-permute-start(bf16[256,1024]{1,0:T(8,128)(2,1)S(1)} %get-tuple-element.93), channel_id=1, source_target_pairs={{0,48},{1,49},{2,50},{3,51},{4,52},{5,53},{6,54},{7,55},{8,56},{9,... | collective-permute-start | bytes 1572872 | tf_op jit(solution)/shard_map/ppermute | solution.py:41
  164.0 12.3 %collective-permute-start.29 = (bf16[256,1024]{1,0:T(8,128)(2,1)S(1)}, bf16[256,1024]{1,0:T(8,128)(2,1)}, u32[]{:S(2)}, u32[]{:S(2)}) collective-permute-start(bf16[256,1024]{1,0:T(8,128)(2,1)S(1)} %get-tuple-element.91), channel_id=1, source_target_pairs={{0,16},{1,17},{2,18},{3,19},{4,20},{5,21},{6,22},{7,23},{8,24},{9,... | collective-permute-start | bytes 1572872 | tf_op jit(solution)/shard_map/ppermute | solution.py:41
  178.8 15.8 %collective-permute-start.37 = (bf16[256,512]{1,0:T(8,128)(2,1)S(1)}, bf16[256,512]{1,0:T(8,128)(2,1)S(1)}, u32[]{:S(2)}, u32[]{:S(2)}) collective-permute-start(bf16[256,512]{1,0:T(8,128)(2,1)S(1)} %get-tuple-element.90), channel_id=1, source_target_pairs={{0,8},{1,24},{2,10},{3,26},{4,12},{5,28},{6,14},{7,30},{8,0},{9,16... | collective-permute-start | bytes 786440 | tf_op jit(solution)/shard_map/ppermute | solution.py:41
  188.9 12.5 %collective-permute-start.36 = (bf16[256,512]{1,0:T(8,128)(2,1)S(1)}, bf16[256,512]{1,0:T(8,128)(2,1)S(1)}, u32[]{:S(2)}, u32[]{:S(2)}) collective-permute-start(bf16[256,512]{1,0:T(8,128)(2,1)S(1)} %get-tuple-element.89), channel_id=1, source_target_pairs={{0,0},{1,16},{2,2},{3,18},{4,4},{5,20},{6,6},{7,22},{8,8},{9,24},{... | collective-permute-start | bytes 786440 | tf_op jit(solution)/shard_map/ppermute | solution.py:41
  (44 other events, 334.0 us)
Sparse Core Ops, SparseCore 0:
  20.1 58.1 all-gather.2

commit v16 on v15

--- a/solution.py
+++ b/solution.py
@@ -100,6 +100,7 @@
 
 WIDE = 640
 GRANT = pltpu.CompilerParams(vmem_limit_bytes=24 * 1024 * 1024)
+WIDE_GRANT = pltpu.CompilerParams(vmem_limit_bytes=52 * 1024 * 1024)
 
 
 def total_of(refs, cols=slice(None)):
@@ -287,7 +288,7 @@
             out_specs=[pl.BlockSpec((size, 1024), lambda i, at: (0, 0))] * count,
         ),
         out_shape=[jax.ShapeDtypeStruct((size, 1024), jnp.bfloat16)] * count,
-        compiler_params=GRANT,
+        compiler_params=WIDE_GRANT if form == "joined" else GRANT,
     )(at, *attended, near, other)
 
 

time: 210 us -> 208 us (level)
  local copies, waits for them, and re-layouts: 19.6 us -> 17.4 us
    unnamed x59 -> x57, local copies, waits for them, and re-layouts: 8.89 us -> 6.68 us
where the time goes in v16:
time: 208 us; the launch traced here: 207 us
  starting transfers between devices  65.4 us (31%)
  waiting for transfers between devices  61.6 us (30%)
  Pallas kernels  33.2 us (16%)
  local copies, waits for them, and re-layouts  17.4 us (8%)
  other arithmetic  15.2 us (7%)
  between operations  14.6 us (7%)
    ppermute x38, starting transfers between devices, send(): return lax.ppermute(value, AXES, pairs(change))  65.4 us
    ppermute x38, waiting for transfers between devices, send(): return lax.ppermute(value, AXES, pairs(change))  61.6 us
    pallas_call x3, Pallas kernels, products(): pl.pallas_call(lambda *refs: products_kernel(form, steps, *refs), grid_sp...  13.4 us
    pallas_call x3, Pallas kernels, project(): pl.pallas_call(project_kernel, grid_spec=pltpu.PrefetchScalarGridSpec(num...  9.87 us
    unnamed x57, local copies, waits for them, and re-layouts  6.68 us
    pallas_call x2, Pallas kernels, attention(): pl.pallas_call(attention_kernel, grid=(1,), in_specs=[pl.BlockSpec((v.sha...  5.48 us
  transfers between devices with their start and end apart: 39, of which 18 were waited for; matrix products, arithmetic and copies ran while one was open for 10% of the time, Pallas kernels for 14%

profile of v16, /device:TPU:3, one launch (start us, length us, event | category | flops | bytes accessed | tf_op | source)
XLA Modules:
  0.0 207.4 jit_solution(895693170103058574)
XLA Ops:
  20.0 8.4 %collective-permute-start.3 = (bf16[256,1024]{1,0:T(8,128)(2,1)S(1)}, bf16[256,1024]{1,0:T(8,128)(2,1)S(1)}, u32[]{:S(2)}, u32[]{:S(2)}) collective-permute-start(bf16[256,1024]{1,0:T(8,128)(2,1)S(1)} %maximum_select_fusion), channel_id=1, source_target_pairs={{0,16},{1,17},{2,18},{3,19},{4,20},{5,21},{6,22},{7,23},{8,24},{9,... | collective-permute-start | bytes 1572872 | tf_op jit(solution)/shard_map/ppermute | solution.py:41
  28.4 3.7 %collective-permute-start.5 = (bf16[256,1024]{1,0:T(8,128)(2,1)S(1)}, bf16[256,1024]{1,0:T(8,128)(2,1)}, u32[]{:S(2)}, u32[]{:S(2)}) collective-permute-start(bf16[256,1024]{1,0:T(8,128)(2,1)S(1)} %maximum_select_fusion), channel_id=1, source_target_pairs={{0,64},{1,65},{2,66},{3,67},{4,68},{5,69},{6,70},{7,71},{8,72},{9,... | collective-permute-start | bytes 1572872 | tf_op jit(solution)/shard_map/ppermute | solution.py:41
  32.1 7.1 %collective-permute-done.3 = bf16[256,1024]{1,0:T(8,128)(2,1)S(1)} collective-permute-done((bf16[256,1024]{1,0:T(8,128)(2,1)S(1)}, bf16[256,1024]{1,0:T(8,128)(2,1)S(1)}, u32[]{:S(2)}, u32[]{:S(2)}) %collective-permute-start.3) | collective-permute-done | bytes 524320 | tf_op jit(solution)/shard_map/ppermute | solution.py:41
  43.9 3.3 %collective-permute-start.12 = (bf16[1024,640]{1,0:T(8,128)(2,1)}, bf16[1024,640]{1,0:T(8,128)(2,1)S(1)}, u32[]{:S(2)}, u32[]{:S(2)}) collective-permute-start(bf16[1024,640]{1,0:T(8,128)(2,1)} %pad_maximum_fusion), channel_id=1, source_target_pairs={{0,1},{1,0},{2,3},{3,2},{4,5},{5,4},{6,7},{7,6},{8,9},{9,8},{10,11... | collective-permute-start | bytes 3932168 | tf_op jit(solution)/shard_map/ppermute | solution.py:41
  48.9 10.7 %collective-permute-done.8 = bf16[256,1024]{1,0:T(8,128)(2,1)} collective-permute-done((bf16[256,1024]{1,0:T(8,128)(2,1)}, bf16[256,1024]{1,0:T(8,128)(2,1)}, u32[]{:S(2)}, u32[]{:S(2)}) %collective-permute-start.8) | collective-permute-done | bytes 524320 | tf_op jit(solution)/shard_map/ppermute | solution.py:41
  65.0 2.7 %collective-permute-start.11 = (bf16[128,1024]{1,0:T(8,128)(2,1)S(1)}, bf16[128,1024]{1,0:T(8,128)(2,1)S(1)}, u32[]{:S(2)}, u32[]{:S(2)}) collective-permute-start(bf16[128,1024]{1,0:T(8,128)(2,1)S(1)} %slice.41), channel_id=1, source_target_pairs={{0,48},{1,49},{2,50},{3,51},{4,52},{5,53},{6,54},{7,55},{8,56},{9,... | collective-permute-start | bytes 786440 | tf_op jit(solution)/shard_map/ppermute | solution.py:41
  67.9 6.3 %collective-permute-done.11 = bf16[128,1024]{1,0:T(8,128)(2,1)S(1)} collective-permute-done((bf16[128,1024]{1,0:T(8,128)(2,1)S(1)}, bf16[128,1024]{1,0:T(8,128)(2,1)S(1)}, u32[]{:S(2)}, u32[]{:S(2)}) %collective-permute-start.11) | collective-permute-done | bytes 262176 | tf_op jit(solution)/shard_map/ppermute | solution.py:41
  83.0 2.7 %collective-permute-start.15 = (bf16[128,1280]{1,0:T(8,128)(2,1)S(1)}, bf16[128,1280]{1,0:T(8,128)(2,1)S(1)}, u32[]{:S(2)}, u32[]{:S(2)}) collective-permute-start(bf16[128,1280]{1,0:T(8,128)(2,1)S(1)} %get-tuple-element.58), channel_id=1, source_target_pairs={{0,6},{1,7},{2,0},{3,1},{4,2},{5,3},{6,4},{7,5},{8,14},{9,15},{10,... | collective-permute-start | bytes 983048 | tf_op jit(solution)/shard_map/ppermute | solution.py:41
  85.8 5.2 %shard_map.65 = (bf16[128,1280]{1,0:T(8,128)(2,1)S(1)}, bf16[128,1280]{1,0:T(8,128)(2,1)S(1)}, bf16[128,1280]{1,0:T(8,128)(2,1)S(1)}, bf16[128,1280]{1,0:T(8,128)(2,1)S(1)}) custom-call(s32[4]{0:T(128)S(1)} %pad_add_fusion.4.at_ref, bf16[4,256,2048]{2,1,0:T(8,128)(2,1)S(1)} %bitcast_dynamic-update-slice_fusion.rows_ref, bf16[1024,512]{1,0:T(8,128)(2,1)S(1)} %copy-done.1, ...), custom_call_target="tpu_custom_call" | custom-call | tf_op jit(solution)/shard_map/pallas_call | solution.py:231
  91.1 2.7 %collective-permute-start.17 = (bf16[128,1280]{1,0:T(8,128)(2,1)S(1)}, bf16[128,1280]{1,0:T(8,128)(2,1)S(1)}, u32[]{:S(2)}, u32[]{:S(2)}) collective-permute-start(bf16[128,1280]{1,0:T(8,128)(2,1)S(1)} %get-tuple-element.66), channel_id=1, source_target_pairs={{0,6},{1,7},{2,0},{3,1},{4,2},{5,3},{6,4},{7,5},{8,14},{9,15},{10,... | collective-permute-start | bytes 983048 | tf_op jit(solution)/shard_map/ppermute | solution.py:41
  96.5 2.7 %collective-permute-start.19 = (bf16[128,1280]{1,0:T(8,128)(2,1)}, bf16[128,1280]{1,0:T(8,128)(2,1)}, u32[]{:S(2)}, u32[]{:S(2)}) collective-permute-start(bf16[128,1280]{1,0:T(8,128)(2,1)} %add.332), channel_id=1, source_target_pairs={{0,6},{1,7},{2,0},{3,1},{4,2},{5,3},{6,4},{7,5},{8,14},{9,15},{10,... | collective-permute-start | bytes 983048 | tf_op jit(solution)/shard_map/ppermute | solution.py:41
  115.1 2.7 %shard_map.68.refs_1_ = bf16[256,512]{1,0:T(8,128)(2,1)S(1)} custom-call(bf16[256,1280]{1,0:T(8,128)(2,1)S(1)} %copy-done.3, bf16[128,1280]{1,0:T(8,128)(2,1)} %collective-permute-done.18.refs_1_.refs_6_, bf16[128,1280]{1,0:T(8,128)(2,1)S(1)} %copy-done.6, bf16[128,1280]{1,0:T(8,128)(2,1)S(1)} %copy-done.8, ...), custom_call_target="tpu_custom_call" | custom-call | tf_op jit(solution)/shard_map/pallas_call | solution.py:182
  117.8 3.0 %collective-permute-start.24 = (bf16[256,512]{1,0:T(8,128)(2,1)S(1)}, bf16[256,512]{1,0:T(8,128)(2,1)S(1)}, u32[]{:S(2)}, u32[]{:S(2)}) collective-permute-start(bf16[256,512]{1,0:T(8,128)(2,1)S(1)} %shard_map.68.refs_1_), channel_id=1, source_target_pairs={{0,1},{1,0},{2,3},{3,2},{4,5},{5,4},{6,7},{7,6},{8,9},{9,8},{10,11... | collective-permute-start | bytes 786440 | tf_op jit(solution)/shard_map/ppermute | solution.py:41
  121.8 2.7 %shard_map.69.refs_2_ = bf16[256,512]{1,0:T(8,128)(2,1)S(1)} custom-call(bf16[256,1280]{1,0:T(8,128)(2,1)S(1)} %copy-done.3, bf16[128,1280]{1,0:T(8,128)(2,1)} %collective-permute-done.18.refs_1_.refs_6_, bf16[128,1280]{1,0:T(8,128)(2,1)S(1)} %copy-done.6, bf16[128,1280]{1,0:T(8,128)(2,1)S(1)} %copy-done.8, ...), custom_call_target="tpu_custom_call" | custom-call | tf_op jit(solution)/shard_map/pallas_call | solution.py:182
  127.2 6.4 %collective-permute-done.25.refs_4_ = bf16[256,512]{1,0:T(8,128)(2,1)S(1)} collective-permute-done((bf16[256,512]{1,0:T(8,128)(2,1)S(1)}, bf16[256,512]{1,0:T(8,128)(2,1)S(1)}, u32[]{:S(2)}, u32[]{:S(2)}) %collective-permute-start.25) | collective-permute-done | bytes 262176 | tf_op jit(solution)/shard_map/ppermute | solution.py:41
  133.5 4.6 %shard_map.71 = (bf16[256,1024]{1,0:T(8,128)(2,1)}, bf16[256,1024]{1,0:T(8,128)(2,1)}) custom-call(s32[4]{0:T(128)S(1)} %get-tuple-element.104.refs_0_, bf16[256,512]{1,0:T(8,128)(2,1)S(1)} %shard_map.68.refs_1_, bf16[256,512]{1,0:T(8,128)(2,1)S(1)} %shard_map.69.refs_2_, bf16[256,512]{1,0:T(8,128)(2,1)S(1)} %collective-permute-done.24.refs_3_, ...), custom_call_target="tpu_custom_call" | custom-call | tf_op jit(solution)/shard_map/pallas_call | solution.py:282
  141.9 3.3 %shard_map.72 = (bf16[128,1024]{1,0:T(8,128)(2,1)S(1)}, bf16[128,1024]{1,0:T(8,128)(2,1)S(1)}, bf16[128,1024]{1,0:T(8,128)(2,1)S(1)}, bf16[128,1024]{1,0:T(8,128)(2,1)S(1)}) custom-call(s32[4]{0:T(128)S(1)} %get-tuple-element.105.refs_0_, bf16[256,512]{1,0:T(8,128)(2,1)S(1)} %shard_map.68.refs_1_, bf16[256,512]{1,0:T(8,128)(2,1)S(1)} %shard_map.69.refs_2_, ...), custom_call_target="tpu_custom_call" | custom-call | tf_op jit(solution)/shard_map/pallas_call | solution.py:282
  145.3 2.6 %collective-permute-start.32 = (bf16[128,1024]{1,0:T(8,128)(2,1)S(1)}, bf16[128,1024]{1,0:T(8,128)(2,1)S(1)}, u32[]{:S(2)}, u32[]{:S(2)}) collective-permute-start(bf16[128,1024]{1,0:T(8,128)(2,1)S(1)} %get-tuple-element.86), channel_id=1, source_target_pairs={{0,16},{1,17},{2,18},{3,19},{4,20},{5,21},{6,22},{7,23},{8,24},{9,... | collective-permute-start | bytes 786440 | tf_op jit(solution)/shard_map/ppermute | solution.py:41
  148.6 5.4 %shard_map.70 = (bf16[256,1024]{1,0:T(8,128)(2,1)S(1)}, bf16[256,1024]{1,0:T(8,128)(2,1)S(1)}, bf16[256,1024]{1,0:T(8,128)(2,1)S(1)}, bf16[256,1024]{1,0:T(8,128)(2,1)S(1)}) custom-call(s32[8]{0:T(128)S(1)} %stack.102.refs_0_, bf16[256,512]{1,0:T(8,128)(2,1)S(1)} %shard_map.68.refs_1_, bf16[256,512]{1,0:T(8,128)(2,1)S(1)} %shard_map.69.refs_2_, ...), custom_call_target="tpu_custom_call" | custom-call | tf_op jit(solution)/shard_map/pallas_call | solution.py:282
  159.4 2.7 %collective-permute-start.30 = (bf16[256,1024]{1,0:T(8,128)(2,1)S(1)}, bf16[256,1024]{1,0:T(8,128)(2,1)S(1)}, u32[]{:S(2)}, u32[]{:S(2)}) collective-permute-start(bf16[256,1024]{1,0:T(8,128)(2,1)S(1)} %get-tuple-element.93), channel_id=1, source_target_pairs={{0,48},{1,49},{2,50},{3,51},{4,52},{5,53},{6,54},{7,55},{8,56},{9,... | collective-permute-start | bytes 1572872 | tf_op jit(solution)/shard_map/ppermute | solution.py:41
  167.2 7.2 %collective-permute-done.30 = bf16[256,1024]{1,0:T(8,128)(2,1)S(1)} collective-permute-done((bf16[256,1024]{1,0:T(8,128)(2,1)S(1)}, bf16[256,1024]{1,0:T(8,128)(2,1)S(1)}, u32[]{:S(2)}, u32[]{:S(2)}) %collective-permute-start.30) | collective-permute-done | bytes 524320 | tf_op jit(solution)/shard_map/ppermute | solution.py:41
  176.9 10.1 %collective-permute-start.37 = (bf16[256,512]{1,0:T(8,128)(2,1)S(1)}, bf16[256,512]{1,0:T(8,128)(2,1)S(1)}, u32[]{:S(2)}, u32[]{:S(2)}) collective-permute-start(bf16[256,512]{1,0:T(8,128)(2,1)S(1)} %get-tuple-element.90), channel_id=1, source_target_pairs={{0,8},{1,24},{2,10},{3,26},{4,12},{5,28},{6,14},{7,30},{8,0},{9,16... | collective-permute-start | bytes 786440 | tf_op jit(solution)/shard_map/ppermute | solution.py:41
  187.0 3.6 %collective-permute-start.36 = (bf16[256,512]{1,0:T(8,128)(2,1)S(1)}, bf16[256,512]{1,0:T(8,128)(2,1)S(1)}, u32[]{:S(2)}, u32[]{:S(2)}) collective-permute-start(bf16[256,512]{1,0:T(8,128)(2,1)S(1)} %get-tuple-element.89), channel_id=1, source_target_pairs={{0,0},{1,16},{2,2},{3,18},{4,4},{5,20},{6,6},{7,22},{8,8},{9,24},{... | collective-permute-start | bytes 786440 | tf_op jit(solution)/shard_map/ppermute | solution.py:41
  192.7 6.8 %collective-permute-done.36 = bf16[256,512]{1,0:T(8,128)(2,1)S(1)} collective-permute-done((bf16[256,512]{1,0:T(8,128)(2,1)S(1)}, bf16[256,512]{1,0:T(8,128)(2,1)S(1)}, u32[]{:S(2)}, u32[]{:S(2)}) %collective-permute-start.36) | collective-permute-done | bytes 262176 | tf_op jit(solution)/shard_map/ppermute | solution.py:41
  (169 shorter events, 76.0 us)
Async XLA Ops:
  6.5 107.2 %all-gather.3.cloned.1.call-start = ((), (), s32[]{:S(2)}) async-start(), calls=%async_computation | async-start | bytes 5242880 | tf_op jit(solution)/shard_map/all_gather | solution.py:375
  20.0 19.3 %collective-permute-start.3 = (bf16[256,1024]{1,0:T(8,128)(2,1)S(1)}, bf16[256,1024]{1,0:T(8,128)(2,1)S(1)}, u32[]{:S(2)}, u32[]{:S(2)}) collective-permute-start(bf16[256,1024]{1,0:T(8,128)(2,1)S(1)} %maximum_select_fusion), channel_id=1, source_target_pairs={{0,16},{1,17},{2,18},{3,19},{4,20},{5,21},{6,22},{7,23},{8,24},{9,... | collective-permute-start | bytes 1572872 | tf_op jit(solution)/shard_map/ppermute | solution.py:41
  28.4 12.9 %collective-permute-start.4 = (bf16[256,1024]{1,0:T(8,128)(2,1)S(1)}, bf16[256,1024]{1,0:T(8,128)(2,1)S(1)}, u32[]{:S(2)}, u32[]{:S(2)}) collective-permute-start(bf16[256,1024]{1,0:T(8,128)(2,1)S(1)} %maximum_select_fusion), channel_id=1, source_target_pairs={{0,48},{1,49},{2,50},{3,51},{4,52},{5,53},{6,54},{7,55},{8,56},{9,... | collective-permute-start | bytes 1572872 | tf_op jit(solution)/shard_map/ppermute | solution.py:41
  28.4 15.5 %collective-permute-start.5 = (bf16[256,1024]{1,0:T(8,128)(2,1)S(1)}, bf16[256,1024]{1,0:T(8,128)(2,1)}, u32[]{:S(2)}, u32[]{:S(2)}) collective-permute-start(bf16[256,1024]{1,0:T(8,128)(2,1)S(1)} %maximum_select_fusion), channel_id=1, source_target_pairs={{0,64},{1,65},{2,66},{3,67},{4,68},{5,69},{6,70},{7,71},{8,72},{9,... | collective-permute-start | bytes 1572872 | tf_op jit(solution)/shard_map/ppermute | solution.py:41
  43.9 31.4 %collective-permute-start.12 = (bf16[1024,640]{1,0:T(8,128)(2,1)}, bf16[1024,640]{1,0:T(8,128)(2,1)S(1)}, u32[]{:S(2)}, u32[]{:S(2)}) collective-permute-start(bf16[1024,640]{1,0:T(8,128)(2,1)} %pad_maximum_fusion), channel_id=1, source_target_pairs={{0,1},{1,0},{2,3},{3,2},{4,5},{5,4},{6,7},{7,6},{8,9},{9,8},{10,11... | collective-permute-start | bytes 3932168 | tf_op jit(solution)/shard_map/ppermute | solution.py:41
  47.2 12.5 %collective-permute-start.8 = (bf16[256,1024]{1,0:T(8,128)(2,1)}, bf16[256,1024]{1,0:T(8,128)(2,1)}, u32[]{:S(2)}, u32[]{:S(2)}) collective-permute-start(bf16[256,1024]{1,0:T(8,128)(2,1)} %collective-permute-done.5), channel_id=1, source_target_pairs={{0,16},{1,17},{2,18},{3,19},{4,20},{5,21},{6,22},{7,23},{8,24},{9,... | collective-permute-start | bytes 1572872 | tf_op jit(solution)/shard_map/ppermute | solution.py:41
  48.3 15.7 %collective-permute-start.9 = (bf16[256,1024]{1,0:T(8,128)(2,1)}, bf16[256,1024]{1,0:T(8,128)(2,1)}, u32[]{:S(2)}, u32[]{:S(2)}) collective-permute-start(bf16[256,1024]{1,0:T(8,128)(2,1)} %collective-permute-done.5), channel_id=1, source_target_pairs={{0,48},{1,49},{2,50},{3,51},{4,52},{5,53},{6,54},{7,55},{8,56},{9,... | collective-permute-start | bytes 1572872 | tf_op jit(solution)/shard_map/ppermute | solution.py:41
  61.9 16.4 %collective-permute-start.7 = (bf16[128,1024]{1,0:T(8,128)(2,1)S(1)}, bf16[128,1024]{1,0:T(8,128)(2,1)S(1)}, u32[]{:S(2)}, u32[]{:S(2)}) collective-permute-start(bf16[128,1024]{1,0:T(8,128)(2,1)S(1)} %slice.31), channel_id=1, source_target_pairs={{0,48},{1,49},{2,50},{3,51},{4,52},{5,53},{6,54},{7,55},{8,56},{9,... | collective-permute-start | bytes 786440 | tf_op jit(solution)/shard_map/ppermute | solution.py:41
  64.0 14.3 %collective-permute-start.6 = (bf16[128,1024]{1,0:T(8,128)(2,1)S(1)}, bf16[128,1024]{1,0:T(8,128)(2,1)S(1)}, u32[]{:S(2)}, u32[]{:S(2)}) collective-permute-start(bf16[128,1024]{1,0:T(8,128)(2,1)S(1)} %slice.30), channel_id=1, source_target_pairs={{0,16},{1,17},{2,18},{3,19},{4,20},{5,21},{6,22},{7,23},{8,24},{9,... | collective-permute-start | bytes 786440 | tf_op jit(solution)/shard_map/ppermute | solution.py:41
  82.9 11.9 %collective-permute-start.14 = (bf16[128,1280]{1,0:T(8,128)(2,1)S(1)}, bf16[128,1280]{1,0:T(8,128)(2,1)S(1)}, u32[]{:S(2)}, u32[]{:S(2)}) collective-permute-start(bf16[128,1280]{1,0:T(8,128)(2,1)S(1)} %get-tuple-element.57), channel_id=1, source_target_pairs={{0,2},{1,3},{2,4},{3,5},{4,6},{5,7},{6,0},{7,1},{8,10},{9,11},{10,... | collective-permute-start | bytes 983048 | tf_op jit(solution)/shard_map/ppermute | solution.py:41
  83.0 11.9 %collective-permute-start.15 = (bf16[128,1280]{1,0:T(8,128)(2,1)S(1)}, bf16[128,1280]{1,0:T(8,128)(2,1)S(1)}, u32[]{:S(2)}, u32[]{:S(2)}) collective-permute-start(bf16[128,1280]{1,0:T(8,128)(2,1)S(1)} %get-tuple-element.58), channel_id=1, source_target_pairs={{0,6},{1,7},{2,0},{3,1},{4,2},{5,3},{6,4},{7,5},{8,14},{9,15},{10,... | collective-permute-start | bytes 983048 | tf_op jit(solution)/shard_map/ppermute | solution.py:41
  91.0 10.1 %collective-permute-start.16 = (bf16[128,1280]{1,0:T(8,128)(2,1)S(1)}, bf16[128,1280]{1,0:T(8,128)(2,1)S(1)}, u32[]{:S(2)}, u32[]{:S(2)}) collective-permute-start(bf16[128,1280]{1,0:T(8,128)(2,1)S(1)} %get-tuple-element.65), channel_id=1, source_target_pairs={{0,2},{1,3},{2,4},{3,5},{4,6},{5,7},{6,0},{7,1},{8,10},{9,11},{10,... | collective-permute-start | bytes 983048 | tf_op jit(solution)/shard_map/ppermute | solution.py:41
  91.1 10.3 %collective-permute-start.17 = (bf16[128,1280]{1,0:T(8,128)(2,1)S(1)}, bf16[128,1280]{1,0:T(8,128)(2,1)S(1)}, u32[]{:S(2)}, u32[]{:S(2)}) collective-permute-start(bf16[128,1280]{1,0:T(8,128)(2,1)S(1)} %get-tuple-element.66), channel_id=1, source_target_pairs={{0,6},{1,7},{2,0},{3,1},{4,2},{5,3},{6,4},{7,5},{8,14},{9,15},{10,... | collective-permute-start | bytes 983048 | tf_op jit(solution)/shard_map/ppermute | solution.py:41
  95.7 13.3 %collective-permute-start.18 = (bf16[128,1280]{1,0:T(8,128)(2,1)}, bf16[128,1280]{1,0:T(8,128)(2,1)}, u32[]{:S(2)}, u32[]{:S(2)}) collective-permute-start(bf16[128,1280]{1,0:T(8,128)(2,1)} %add.331), channel_id=1, source_target_pairs={{0,2},{1,3},{2,4},{3,5},{4,6},{5,7},{6,0},{7,1},{8,10},{9,11},{10,... | collective-permute-start | bytes 983048 | tf_op jit(solution)/shard_map/ppermute | solution.py:41
  96.5 12.5 %collective-permute-start.19 = (bf16[128,1280]{1,0:T(8,128)(2,1)}, bf16[128,1280]{1,0:T(8,128)(2,1)}, u32[]{:S(2)}, u32[]{:S(2)}) collective-permute-start(bf16[128,1280]{1,0:T(8,128)(2,1)} %add.332), channel_id=1, source_target_pairs={{0,6},{1,7},{2,0},{3,1},{4,2},{5,3},{6,4},{7,5},{8,14},{9,15},{10,... | collective-permute-start | bytes 983048 | tf_op jit(solution)/shard_map/ppermute | solution.py:41
  113.8 19.8 %collective-permute-start.26 = (bf16[4,512,1024]{2,1,0:T(8,128)(2,1)}, bf16[4,512,1024]{2,1,0:T(8,128)(2,1)}, u32[]{:S(2)}, u32[]{:S(2)}) collective-permute-start(bf16[4,512,1024]{2,1,0:T(8,128)(2,1)} %bitcast.44), channel_id=1, source_target_pairs={{0,8},{1,9},{2,10},{3,11},{4,12},{5,13},{6,14},{7,15},{8,0},{9,1},... | collective-permute-start | bytes 12582920 | tf_op jit(solution)/shard_map/ppermute | solution.py:41
  138.2 15.9 %collective-permute-start.27 = (bf16[256,1024]{1,0:T(8,128)(2,1)}, bf16[256,1024]{1,0:T(8,128)(2,1)}, u32[]{:S(2)}, u32[]{:S(2)}) collective-permute-start(bf16[256,1024]{1,0:T(8,128)(2,1)} %get-tuple-element.76), channel_id=1, source_target_pairs={{0,16},{1,17},{2,18},{3,19},{4,20},{5,21},{6,22},{7,23},{8,24},{9,... | collective-permute-start | bytes 1572872 | tf_op jit(solution)/shard_map/ppermute | solution.py:41
  139.2 14.9 %collective-permute-start.28 = (bf16[256,1024]{1,0:T(8,128)(2,1)}, bf16[256,1024]{1,0:T(8,128)(2,1)}, u32[]{:S(2)}, u32[]{:S(2)}) collective-permute-start(bf16[256,1024]{1,0:T(8,128)(2,1)} %get-tuple-element.77), channel_id=1, source_target_pairs={{0,48},{1,49},{2,50},{3,51},{4,52},{5,53},{6,54},{7,55},{8,56},{9,... | collective-permute-start | bytes 1572872 | tf_op jit(solution)/shard_map/ppermute | solution.py:41
  145.3 16.8 %collective-permute-start.32 = (bf16[128,1024]{1,0:T(8,128)(2,1)S(1)}, bf16[128,1024]{1,0:T(8,128)(2,1)S(1)}, u32[]{:S(2)}, u32[]{:S(2)}) collective-permute-start(bf16[128,1024]{1,0:T(8,128)(2,1)S(1)} %get-tuple-element.86), channel_id=1, source_target_pairs={{0,16},{1,17},{2,18},{3,19},{4,20},{5,21},{6,22},{7,23},{8,24},{9,... | collective-permute-start | bytes 786440 | tf_op jit(solution)/shard_map/ppermute | solution.py:41
  147.9 14.2 %collective-permute-start.33 = (bf16[128,1024]{1,0:T(8,128)(2,1)S(1)}, bf16[128,1024]{1,0:T(8,128)(2,1)S(1)}, u32[]{:S(2)}, u32[]{:S(2)}) collective-permute-start(bf16[128,1024]{1,0:T(8,128)(2,1)S(1)} %get-tuple-element.87), channel_id=1, source_target_pairs={{0,48},{1,49},{2,50},{3,51},{4,52},{5,53},{6,54},{7,55},{8,56},{9,... | collective-permute-start | bytes 786440 | tf_op jit(solution)/shard_map/ppermute | solution.py:41
  159.4 14.9 %collective-permute-start.30 = (bf16[256,1024]{1,0:T(8,128)(2,1)S(1)}, bf16[256,1024]{1,0:T(8,128)(2,1)S(1)}, u32[]{:S(2)}, u32[]{:S(2)}) collective-permute-start(bf16[256,1024]{1,0:T(8,128)(2,1)S(1)} %get-tuple-element.93), channel_id=1, source_target_pairs={{0,48},{1,49},{2,50},{3,51},{4,52},{5,53},{6,54},{7,55},{8,56},{9,... | collective-permute-start | bytes 1572872 | tf_op jit(solution)/shard_map/ppermute | solution.py:41
  162.1 12.3 %collective-permute-start.29 = (bf16[256,1024]{1,0:T(8,128)(2,1)S(1)}, bf16[256,1024]{1,0:T(8,128)(2,1)}, u32[]{:S(2)}, u32[]{:S(2)}) collective-permute-start(bf16[256,1024]{1,0:T(8,128)(2,1)S(1)} %get-tuple-element.91), channel_id=1, source_target_pairs={{0,16},{1,17},{2,18},{3,19},{4,20},{5,21},{6,22},{7,23},{8,24},{9,... | collective-permute-start | bytes 1572872 | tf_op jit(solution)/shard_map/ppermute | solution.py:41
  176.9 15.8 %collective-permute-start.37 = (bf16[256,512]{1,0:T(8,128)(2,1)S(1)}, bf16[256,512]{1,0:T(8,128)(2,1)S(1)}, u32[]{:S(2)}, u32[]{:S(2)}) collective-permute-start(bf16[256,512]{1,0:T(8,128)(2,1)S(1)} %get-tuple-element.90), channel_id=1, source_target_pairs={{0,8},{1,24},{2,10},{3,26},{4,12},{5,28},{6,14},{7,30},{8,0},{9,16... | collective-permute-start | bytes 786440 | tf_op jit(solution)/shard_map/ppermute | solution.py:41
  187.0 12.5 %collective-permute-start.36 = (bf16[256,512]{1,0:T(8,128)(2,1)S(1)}, bf16[256,512]{1,0:T(8,128)(2,1)S(1)}, u32[]{:S(2)}, u32[]{:S(2)}) collective-permute-start(bf16[256,512]{1,0:T(8,128)(2,1)S(1)} %get-tuple-element.89), channel_id=1, source_target_pairs={{0,0},{1,16},{2,2},{3,18},{4,4},{5,20},{6,6},{7,22},{8,8},{9,24},{... | collective-permute-start | bytes 786440 | tf_op jit(solution)/shard_map/ppermute | solution.py:41
  (43 other events, 331.8 us)
Sparse Core Ops, SparseCore 0:
  20.1 58.1 all-gather.2

commit v17 on v16

--- a/solution.py
+++ b/solution.py
@@ -115,7 +115,9 @@
 
 def summed_up(*values):
     return pl.pallas_call(
-        total_kernel, out_shape=jax.ShapeDtypeStruct(values[0].shape, jnp.bfloat16)
+        total_kernel,
+        out_shape=jax.ShapeDtypeStruct(values[0].shape, jnp.bfloat16),
+        compiler_params=WIDE_GRANT,
     )(*values)
 
 

time: 208 us -> 208 us (level)
    unnamed x57 -> x47, local copies, waits for them, and re-layouts: 6.68 us -> 5.72 us
  transfers between devices with their start and end apart: 39 -> 39, of which waited for: 18 -> 17; matrix products, arithmetic and copies ran while one was open for 10% -> 11% of each run, Pallas kernels for 14% -> 14%
where the time goes in v17:
time: 208 us; the launch traced here: 207 us
  waiting for transfers between devices  63.6 us (31%)
  starting transfers between devices  63.5 us (31%)
  Pallas kernels  32.8 us (16%)
  local copies, waits for them, and re-layouts  16.4 us (8%)
  other arithmetic  16 us (8%)
  between operations  14.5 us (7%)
    ppermute x38, waiting for transfers between devices, send(): return lax.ppermute(value, AXES, pairs(change))  63.6 us
    ppermute x38, starting transfers between devices, send(): return lax.ppermute(value, AXES, pairs(change))  63.5 us
    pallas_call x3, Pallas kernels, products(): pl.pallas_call(lambda *refs: products_kernel(form, steps, *refs), grid_sp...  14.2 us
    pallas_call x3, Pallas kernels, project(): pl.pallas_call(project_kernel, grid_spec=pltpu.PrefetchScalarGridSpec(num...  9.87 us
    unnamed x47, local copies, waits for them, and re-layouts  5.72 us
    pallas_call x2, Pallas kernels, attention(): pl.pallas_call(attention_kernel, grid=(1,), in_specs=[pl.BlockSpec((v.sha...  5.48 us
  transfers between devices with their start and end apart: 39, of which 17 were waited for; matrix products, arithmetic and copies ran while one was open for 11% of the time, Pallas kernels for 14%

profile of v17, /device:TPU:3, one launch (start us, length us, event | category | flops | bytes accessed | tf_op | source)
XLA Modules:
  0.0 206.8 jit_solution(18136967699246358781)
XLA Ops:
  20.0 8.4 %collective-permute-start.3 = (bf16[256,1024]{1,0:T(8,128)(2,1)S(1)}, bf16[256,1024]{1,0:T(8,128)(2,1)S(1)}, u32[]{:S(2)}, u32[]{:S(2)}) collective-permute-start(bf16[256,1024]{1,0:T(8,128)(2,1)S(1)} %maximum_select_fusion), channel_id=1, source_target_pairs={{0,16},{1,17},{2,18},{3,19},{4,20},{5,21},{6,22},{7,23},{8,24},{9,... | collective-permute-start | bytes 1572872 | tf_op jit(solution)/shard_map/ppermute | solution.py:41
  28.3 3.7 %collective-permute-start.5 = (bf16[256,1024]{1,0:T(8,128)(2,1)S(1)}, bf16[256,1024]{1,0:T(8,128)(2,1)}, u32[]{:S(2)}, u32[]{:S(2)}) collective-permute-start(bf16[256,1024]{1,0:T(8,128)(2,1)S(1)} %maximum_select_fusion), channel_id=1, source_target_pairs={{0,64},{1,65},{2,66},{3,67},{4,68},{5,69},{6,70},{7,71},{8,72},{9,... | collective-permute-start | bytes 1572872 | tf_op jit(solution)/shard_map/ppermute | solution.py:41
  32.1 7.1 %collective-permute-done.3 = bf16[256,1024]{1,0:T(8,128)(2,1)S(1)} collective-permute-done((bf16[256,1024]{1,0:T(8,128)(2,1)S(1)}, bf16[256,1024]{1,0:T(8,128)(2,1)S(1)}, u32[]{:S(2)}, u32[]{:S(2)}) %collective-permute-start.3) | collective-permute-done | bytes 524320 | tf_op jit(solution)/shard_map/ppermute | solution.py:41
  43.8 3.3 %collective-permute-start.12 = (bf16[1024,640]{1,0:T(8,128)(2,1)}, bf16[1024,640]{1,0:T(8,128)(2,1)S(1)}, u32[]{:S(2)}, u32[]{:S(2)}) collective-permute-start(bf16[1024,640]{1,0:T(8,128)(2,1)} %pad_maximum_fusion), channel_id=1, source_target_pairs={{0,1},{1,0},{2,3},{3,2},{4,5},{5,4},{6,7},{7,6},{8,9},{9,8},{10,11... | collective-permute-start | bytes 3932168 | tf_op jit(solution)/shard_map/ppermute | solution.py:41
  48.9 10.7 %collective-permute-done.8 = bf16[256,1024]{1,0:T(8,128)(2,1)} collective-permute-done((bf16[256,1024]{1,0:T(8,128)(2,1)}, bf16[256,1024]{1,0:T(8,128)(2,1)}, u32[]{:S(2)}, u32[]{:S(2)}) %collective-permute-start.8) | collective-permute-done | bytes 524320 | tf_op jit(solution)/shard_map/ppermute | solution.py:41
  65.0 2.7 %collective-permute-start.11 = (bf16[128,1024]{1,0:T(8,128)(2,1)S(1)}, bf16[128,1024]{1,0:T(8,128)(2,1)S(1)}, u32[]{:S(2)}, u32[]{:S(2)}) collective-permute-start(bf16[128,1024]{1,0:T(8,128)(2,1)S(1)} %slice.41), channel_id=1, source_target_pairs={{0,48},{1,49},{2,50},{3,51},{4,52},{5,53},{6,54},{7,55},{8,56},{9,... | collective-permute-start | bytes 786440 | tf_op jit(solution)/shard_map/ppermute | solution.py:41
  67.8 6.3 %collective-permute-done.11 = bf16[128,1024]{1,0:T(8,128)(2,1)S(1)} collective-permute-done((bf16[128,1024]{1,0:T(8,128)(2,1)S(1)}, bf16[128,1024]{1,0:T(8,128)(2,1)S(1)}, u32[]{:S(2)}, u32[]{:S(2)}) %collective-permute-start.11) | collective-permute-done | bytes 262176 | tf_op jit(solution)/shard_map/ppermute | solution.py:41
  83.0 2.8 %collective-permute-start.15 = (bf16[128,1280]{1,0:T(8,128)(2,1)S(1)}, bf16[128,1280]{1,0:T(8,128)(2,1)S(1)}, u32[]{:S(2)}, u32[]{:S(2)}) collective-permute-start(bf16[128,1280]{1,0:T(8,128)(2,1)S(1)} %get-tuple-element.58), channel_id=1, source_target_pairs={{0,6},{1,7},{2,0},{3,1},{4,2},{5,3},{6,4},{7,5},{8,14},{9,15},{10,... | collective-permute-start | bytes 983048 | tf_op jit(solution)/shard_map/ppermute | solution.py:41
  85.8 5.2 %shard_map.65 = (bf16[128,1280]{1,0:T(8,128)(2,1)S(1)}, bf16[128,1280]{1,0:T(8,128)(2,1)S(1)}, bf16[128,1280]{1,0:T(8,128)(2,1)S(1)}, bf16[128,1280]{1,0:T(8,128)(2,1)S(1)}) custom-call(s32[4]{0:T(128)S(1)} %pad_add_fusion.4.at_ref, bf16[4,256,2048]{2,1,0:T(8,128)(2,1)S(1)} %bitcast_dynamic-update-slice_fusion.rows_ref, bf16[1024,512]{1,0:T(8,128)(2,1)S(1)} %copy-done.1, ...), custom_call_target="tpu_custom_call" | custom-call | tf_op jit(solution)/shard_map/pallas_call | solution.py:233
  91.1 2.7 %collective-permute-start.17 = (bf16[128,1280]{1,0:T(8,128)(2,1)S(1)}, bf16[128,1280]{1,0:T(8,128)(2,1)S(1)}, u32[]{:S(2)}, u32[]{:S(2)}) collective-permute-start(bf16[128,1280]{1,0:T(8,128)(2,1)S(1)} %get-tuple-element.66), channel_id=1, source_target_pairs={{0,6},{1,7},{2,0},{3,1},{4,2},{5,3},{6,4},{7,5},{8,14},{9,15},{10,... | collective-permute-start | bytes 983048 | tf_op jit(solution)/shard_map/ppermute | solution.py:41
  96.5 2.7 %collective-permute-start.19 = (bf16[128,1280]{1,0:T(8,128)(2,1)}, bf16[128,1280]{1,0:T(8,128)(2,1)}, u32[]{:S(2)}, u32[]{:S(2)}) collective-permute-start(bf16[128,1280]{1,0:T(8,128)(2,1)} %add.332), channel_id=1, source_target_pairs={{0,6},{1,7},{2,0},{3,1},{4,2},{5,3},{6,4},{7,5},{8,14},{9,15},{10,... | collective-permute-start | bytes 983048 | tf_op jit(solution)/shard_map/ppermute | solution.py:41
  115.1 2.7 %shard_map.68.refs_1_ = bf16[256,512]{1,0:T(8,128)(2,1)S(1)} custom-call(bf16[256,1280]{1,0:T(8,128)(2,1)S(1)} %copy-done.3, bf16[128,1280]{1,0:T(8,128)(2,1)} %collective-permute-done.18.refs_1_.refs_6_, bf16[128,1280]{1,0:T(8,128)(2,1)S(1)} %copy-done.6, bf16[128,1280]{1,0:T(8,128)(2,1)S(1)} %copy-done.8, ...), custom_call_target="tpu_custom_call" | custom-call | tf_op jit(solution)/shard_map/pallas_call | solution.py:184
  117.8 3.0 %collective-permute-start.24 = (bf16[256,512]{1,0:T(8,128)(2,1)S(1)}, bf16[256,512]{1,0:T(8,128)(2,1)S(1)}, u32[]{:S(2)}, u32[]{:S(2)}) collective-permute-start(bf16[256,512]{1,0:T(8,128)(2,1)S(1)} %shard_map.68.refs_1_), channel_id=1, source_target_pairs={{0,1},{1,0},{2,3},{3,2},{4,5},{5,4},{6,7},{7,6},{8,9},{9,8},{10,11... | collective-permute-start | bytes 786440 | tf_op jit(solution)/shard_map/ppermute | solution.py:41
  121.8 2.7 %shard_map.69.refs_2_ = bf16[256,512]{1,0:T(8,128)(2,1)S(1)} custom-call(bf16[256,1280]{1,0:T(8,128)(2,1)S(1)} %copy-done.3, bf16[128,1280]{1,0:T(8,128)(2,1)} %collective-permute-done.18.refs_1_.refs_6_, bf16[128,1280]{1,0:T(8,128)(2,1)S(1)} %copy-done.6, bf16[128,1280]{1,0:T(8,128)(2,1)S(1)} %copy-done.8, ...), custom_call_target="tpu_custom_call" | custom-call | tf_op jit(solution)/shard_map/pallas_call | solution.py:184
  127.1 6.4 %collective-permute-done.25.refs_4_ = bf16[256,512]{1,0:T(8,128)(2,1)S(1)} collective-permute-done((bf16[256,512]{1,0:T(8,128)(2,1)S(1)}, bf16[256,512]{1,0:T(8,128)(2,1)S(1)}, u32[]{:S(2)}, u32[]{:S(2)}) %collective-permute-start.25) | collective-permute-done | bytes 262176 | tf_op jit(solution)/shard_map/ppermute | solution.py:41
  133.5 4.6 %shard_map.71 = (bf16[256,1024]{1,0:T(8,128)(2,1)}, bf16[256,1024]{1,0:T(8,128)(2,1)}) custom-call(s32[4]{0:T(128)S(1)} %get-tuple-element.104.refs_0_, bf16[256,512]{1,0:T(8,128)(2,1)S(1)} %shard_map.68.refs_1_, bf16[256,512]{1,0:T(8,128)(2,1)S(1)} %shard_map.69.refs_2_, bf16[256,512]{1,0:T(8,128)(2,1)S(1)} %collective-permute-done.24.refs_3_, ...), custom_call_target="tpu_custom_call" | custom-call | tf_op jit(solution)/shard_map/pallas_call | solution.py:284
  141.9 3.3 %shard_map.72 = (bf16[128,1024]{1,0:T(8,128)(2,1)S(1)}, bf16[128,1024]{1,0:T(8,128)(2,1)S(1)}, bf16[128,1024]{1,0:T(8,128)(2,1)S(1)}, bf16[128,1024]{1,0:T(8,128)(2,1)S(1)}) custom-call(s32[4]{0:T(128)S(1)} %get-tuple-element.105.refs_0_, bf16[256,512]{1,0:T(8,128)(2,1)S(1)} %shard_map.68.refs_1_, bf16[256,512]{1,0:T(8,128)(2,1)S(1)} %shard_map.69.refs_2_, ...), custom_call_target="tpu_custom_call" | custom-call | tf_op jit(solution)/shard_map/pallas_call | solution.py:284
  148.5 6.2 %shard_map.70 = (bf16[256,1024]{1,0:T(8,128)(2,1)S(1)}, bf16[256,1024]{1,0:T(8,128)(2,1)}, bf16[256,1024]{1,0:T(8,128)(2,1)S(1)}, bf16[256,1024]{1,0:T(8,128)(2,1)S(1)}) custom-call(s32[8]{0:T(128)S(1)} %stack.102.refs_0_, bf16[256,512]{1,0:T(8,128)(2,1)S(1)} %shard_map.68.refs_1_, bf16[256,512]{1,0:T(8,128)(2,1)S(1)} %shard_map.69.refs_2_, ...), custom_call_target="tpu_custom_call" | custom-call | tf_op jit(solution)/shard_map/pallas_call | solution.py:284
  160.9 2.7 %collective-permute-start.30 = (bf16[256,1024]{1,0:T(8,128)(2,1)}, bf16[256,1024]{1,0:T(8,128)(2,1)}, u32[]{:S(2)}, u32[]{:S(2)}) collective-permute-start(bf16[256,1024]{1,0:T(8,128)(2,1)} %get-tuple-element.93), channel_id=1, source_target_pairs={{0,48},{1,49},{2,50},{3,51},{4,52},{5,53},{6,54},{7,55},{8,56},{9,... | collective-permute-start | bytes 1572872 | tf_op jit(solution)/shard_map/ppermute | solution.py:41
  166.5 9.4 %collective-permute-done.30 = bf16[256,1024]{1,0:T(8,128)(2,1)} collective-permute-done((bf16[256,1024]{1,0:T(8,128)(2,1)}, bf16[256,1024]{1,0:T(8,128)(2,1)}, u32[]{:S(2)}, u32[]{:S(2)}) %collective-permute-start.30) | collective-permute-done | bytes 524320 | tf_op jit(solution)/shard_map/ppermute | solution.py:41
  177.5 8.9 %collective-permute-start.37 = (bf16[256,512]{1,0:T(8,128)(2,1)S(1)}, bf16[256,512]{1,0:T(8,128)(2,1)S(1)}, u32[]{:S(2)}, u32[]{:S(2)}) collective-permute-start(bf16[256,512]{1,0:T(8,128)(2,1)S(1)} %get-tuple-element.90), channel_id=1, source_target_pairs={{0,8},{1,24},{2,10},{3,26},{4,12},{5,28},{6,14},{7,30},{8,0},{9,16... | collective-permute-start | bytes 786440 | tf_op jit(solution)/shard_map/ppermute | solution.py:41
  186.4 2.8 %collective-permute-start.36 = (bf16[256,512]{1,0:T(8,128)(2,1)S(1)}, bf16[256,512]{1,0:T(8,128)(2,1)S(1)}, u32[]{:S(2)}, u32[]{:S(2)}) collective-permute-start(bf16[256,512]{1,0:T(8,128)(2,1)S(1)} %get-tuple-element.89), channel_id=1, source_target_pairs={{0,0},{1,16},{2,2},{3,18},{4,4},{5,20},{6,6},{7,22},{8,8},{9,24},{... | collective-permute-start | bytes 786440 | tf_op jit(solution)/shard_map/ppermute | solution.py:41
  189.3 3.7 %collective-permute-done.37 = bf16[256,512]{1,0:T(8,128)(2,1)S(1)} collective-permute-done((bf16[256,512]{1,0:T(8,128)(2,1)S(1)}, bf16[256,512]{1,0:T(8,128)(2,1)S(1)}, u32[]{:S(2)}, u32[]{:S(2)}) %collective-permute-start.37) | collective-permute-done | bytes 262176 | tf_op jit(solution)/shard_map/ppermute | solution.py:41
  193.0 5.9 %collective-permute-done.36 = bf16[256,512]{1,0:T(8,128)(2,1)S(1)} collective-permute-done((bf16[256,512]{1,0:T(8,128)(2,1)S(1)}, bf16[256,512]{1,0:T(8,128)(2,1)S(1)}, u32[]{:S(2)}, u32[]{:S(2)}) %collective-permute-start.36) | collective-permute-done | bytes 262176 | tf_op jit(solution)/shard_map/ppermute | solution.py:41
  (159 shorter events, 74.2 us)
Async XLA Ops:
  6.5 107.2 %all-gather.3.cloned.1.call-start = ((), (), s32[]{:S(2)}) async-start(), calls=%async_computation | async-start | bytes 5242880 | tf_op jit(solution)/shard_map/all_gather | solution.py:377
  20.0 19.3 %collective-permute-start.3 = (bf16[256,1024]{1,0:T(8,128)(2,1)S(1)}, bf16[256,1024]{1,0:T(8,128)(2,1)S(1)}, u32[]{:S(2)}, u32[]{:S(2)}) collective-permute-start(bf16[256,1024]{1,0:T(8,128)(2,1)S(1)} %maximum_select_fusion), channel_id=1, source_target_pairs={{0,16},{1,17},{2,18},{3,19},{4,20},{5,21},{6,22},{7,23},{8,24},{9,... | collective-permute-start | bytes 1572872 | tf_op jit(solution)/shard_map/ppermute | solution.py:41
  28.3 12.9 %collective-permute-start.4 = (bf16[256,1024]{1,0:T(8,128)(2,1)S(1)}, bf16[256,1024]{1,0:T(8,128)(2,1)S(1)}, u32[]{:S(2)}, u32[]{:S(2)}) collective-permute-start(bf16[256,1024]{1,0:T(8,128)(2,1)S(1)} %maximum_select_fusion), channel_id=1, source_target_pairs={{0,48},{1,49},{2,50},{3,51},{4,52},{5,53},{6,54},{7,55},{8,56},{9,... | collective-permute-start | bytes 1572872 | tf_op jit(solution)/shard_map/ppermute | solution.py:41
  28.3 15.5 %collective-permute-start.5 = (bf16[256,1024]{1,0:T(8,128)(2,1)S(1)}, bf16[256,1024]{1,0:T(8,128)(2,1)}, u32[]{:S(2)}, u32[]{:S(2)}) collective-permute-start(bf16[256,1024]{1,0:T(8,128)(2,1)S(1)} %maximum_select_fusion), channel_id=1, source_target_pairs={{0,64},{1,65},{2,66},{3,67},{4,68},{5,69},{6,70},{7,71},{8,72},{9,... | collective-permute-start | bytes 1572872 | tf_op jit(solution)/shard_map/ppermute | solution.py:41
  43.8 31.4 %collective-permute-start.12 = (bf16[1024,640]{1,0:T(8,128)(2,1)}, bf16[1024,640]{1,0:T(8,128)(2,1)S(1)}, u32[]{:S(2)}, u32[]{:S(2)}) collective-permute-start(bf16[1024,640]{1,0:T(8,128)(2,1)} %pad_maximum_fusion), channel_id=1, source_target_pairs={{0,1},{1,0},{2,3},{3,2},{4,5},{5,4},{6,7},{7,6},{8,9},{9,8},{10,11... | collective-permute-start | bytes 3932168 | tf_op jit(solution)/shard_map/ppermute | solution.py:41
  47.1 12.5 %collective-permute-start.8 = (bf16[256,1024]{1,0:T(8,128)(2,1)}, bf16[256,1024]{1,0:T(8,128)(2,1)}, u32[]{:S(2)}, u32[]{:S(2)}) collective-permute-start(bf16[256,1024]{1,0:T(8,128)(2,1)} %collective-permute-done.5), channel_id=1, source_target_pairs={{0,16},{1,17},{2,18},{3,19},{4,20},{5,21},{6,22},{7,23},{8,24},{9,... | collective-permute-start | bytes 1572872 | tf_op jit(solution)/shard_map/ppermute | solution.py:41
  48.3 15.7 %collective-permute-start.9 = (bf16[256,1024]{1,0:T(8,128)(2,1)}, bf16[256,1024]{1,0:T(8,128)(2,1)}, u32[]{:S(2)}, u32[]{:S(2)}) collective-permute-start(bf16[256,1024]{1,0:T(8,128)(2,1)} %collective-permute-done.5), channel_id=1, source_target_pairs={{0,48},{1,49},{2,50},{3,51},{4,52},{5,53},{6,54},{7,55},{8,56},{9,... | collective-permute-start | bytes 1572872 | tf_op jit(solution)/shard_map/ppermute | solution.py:41
  61.8 16.4 %collective-permute-start.7 = (bf16[128,1024]{1,0:T(8,128)(2,1)S(1)}, bf16[128,1024]{1,0:T(8,128)(2,1)S(1)}, u32[]{:S(2)}, u32[]{:S(2)}) collective-permute-start(bf16[128,1024]{1,0:T(8,128)(2,1)S(1)} %slice.31), channel_id=1, source_target_pairs={{0,48},{1,49},{2,50},{3,51},{4,52},{5,53},{6,54},{7,55},{8,56},{9,... | collective-permute-start | bytes 786440 | tf_op jit(solution)/shard_map/ppermute | solution.py:41
  63.9 14.3 %collective-permute-start.6 = (bf16[128,1024]{1,0:T(8,128)(2,1)S(1)}, bf16[128,1024]{1,0:T(8,128)(2,1)S(1)}, u32[]{:S(2)}, u32[]{:S(2)}) collective-permute-start(bf16[128,1024]{1,0:T(8,128)(2,1)S(1)} %slice.30), channel_id=1, source_target_pairs={{0,16},{1,17},{2,18},{3,19},{4,20},{5,21},{6,22},{7,23},{8,24},{9,... | collective-permute-start | bytes 786440 | tf_op jit(solution)/shard_map/ppermute | solution.py:41
  82.9 12.0 %collective-permute-start.14 = (bf16[128,1280]{1,0:T(8,128)(2,1)S(1)}, bf16[128,1280]{1,0:T(8,128)(2,1)S(1)}, u32[]{:S(2)}, u32[]{:S(2)}) collective-permute-start(bf16[128,1280]{1,0:T(8,128)(2,1)S(1)} %get-tuple-element.57), channel_id=1, source_target_pairs={{0,2},{1,3},{2,4},{3,5},{4,6},{5,7},{6,0},{7,1},{8,10},{9,11},{10,... | collective-permute-start | bytes 983048 | tf_op jit(solution)/shard_map/ppermute | solution.py:41
  83.0 11.9 %collective-permute-start.15 = (bf16[128,1280]{1,0:T(8,128)(2,1)S(1)}, bf16[128,1280]{1,0:T(8,128)(2,1)S(1)}, u32[]{:S(2)}, u32[]{:S(2)}) collective-permute-start(bf16[128,1280]{1,0:T(8,128)(2,1)S(1)} %get-tuple-element.58), channel_id=1, source_target_pairs={{0,6},{1,7},{2,0},{3,1},{4,2},{5,3},{6,4},{7,5},{8,14},{9,15},{10,... | collective-permute-start | bytes 983048 | tf_op jit(solution)/shard_map/ppermute | solution.py:41
  91.0 10.1 %collective-permute-start.16 = (bf16[128,1280]{1,0:T(8,128)(2,1)S(1)}, bf16[128,1280]{1,0:T(8,128)(2,1)S(1)}, u32[]{:S(2)}, u32[]{:S(2)}) collective-permute-start(bf16[128,1280]{1,0:T(8,128)(2,1)S(1)} %get-tuple-element.65), channel_id=1, source_target_pairs={{0,2},{1,3},{2,4},{3,5},{4,6},{5,7},{6,0},{7,1},{8,10},{9,11},{10,... | collective-permute-start | bytes 983048 | tf_op jit(solution)/shard_map/ppermute | solution.py:41
  91.1 10.2 %collective-permute-start.17 = (bf16[128,1280]{1,0:T(8,128)(2,1)S(1)}, bf16[128,1280]{1,0:T(8,128)(2,1)S(1)}, u32[]{:S(2)}, u32[]{:S(2)}) collective-permute-start(bf16[128,1280]{1,0:T(8,128)(2,1)S(1)} %get-tuple-element.66), channel_id=1, source_target_pairs={{0,6},{1,7},{2,0},{3,1},{4,2},{5,3},{6,4},{7,5},{8,14},{9,15},{10,... | collective-permute-start | bytes 983048 | tf_op jit(solution)/shard_map/ppermute | solution.py:41
  95.7 13.4 %collective-permute-start.18 = (bf16[128,1280]{1,0:T(8,128)(2,1)}, bf16[128,1280]{1,0:T(8,128)(2,1)}, u32[]{:S(2)}, u32[]{:S(2)}) collective-permute-start(bf16[128,1280]{1,0:T(8,128)(2,1)} %add.331), channel_id=1, source_target_pairs={{0,2},{1,3},{2,4},{3,5},{4,6},{5,7},{6,0},{7,1},{8,10},{9,11},{10,... | collective-permute-start | bytes 983048 | tf_op jit(solution)/shard_map/ppermute | solution.py:41
  96.5 12.5 %collective-permute-start.19 = (bf16[128,1280]{1,0:T(8,128)(2,1)}, bf16[128,1280]{1,0:T(8,128)(2,1)}, u32[]{:S(2)}, u32[]{:S(2)}) collective-permute-start(bf16[128,1280]{1,0:T(8,128)(2,1)} %add.332), channel_id=1, source_target_pairs={{0,6},{1,7},{2,0},{3,1},{4,2},{5,3},{6,4},{7,5},{8,14},{9,15},{10,... | collective-permute-start | bytes 983048 | tf_op jit(solution)/shard_map/ppermute | solution.py:41
  113.7 19.8 %collective-permute-start.26 = (bf16[4,512,1024]{2,1,0:T(8,128)(2,1)}, bf16[4,512,1024]{2,1,0:T(8,128)(2,1)}, u32[]{:S(2)}, u32[]{:S(2)}) collective-permute-start(bf16[4,512,1024]{2,1,0:T(8,128)(2,1)} %bitcast.44), channel_id=1, source_target_pairs={{0,8},{1,9},{2,10},{3,11},{4,12},{5,13},{6,14},{7,15},{8,0},{9,1},... | collective-permute-start | bytes 12582920 | tf_op jit(solution)/shard_map/ppermute | solution.py:41
  138.1 16.6 %collective-permute-start.27 = (bf16[256,1024]{1,0:T(8,128)(2,1)}, bf16[256,1024]{1,0:T(8,128)(2,1)}, u32[]{:S(2)}, u32[]{:S(2)}) collective-permute-start(bf16[256,1024]{1,0:T(8,128)(2,1)} %get-tuple-element.76), channel_id=1, source_target_pairs={{0,16},{1,17},{2,18},{3,19},{4,20},{5,21},{6,22},{7,23},{8,24},{9,... | collective-permute-start | bytes 1572872 | tf_op jit(solution)/shard_map/ppermute | solution.py:41
  139.1 15.6 %collective-permute-start.28 = (bf16[256,1024]{1,0:T(8,128)(2,1)}, bf16[256,1024]{1,0:T(8,128)(2,1)}, u32[]{:S(2)}, u32[]{:S(2)}) collective-permute-start(bf16[256,1024]{1,0:T(8,128)(2,1)} %get-tuple-element.77), channel_id=1, source_target_pairs={{0,48},{1,49},{2,50},{3,51},{4,52},{5,53},{6,54},{7,55},{8,56},{9,... | collective-permute-start | bytes 1572872 | tf_op jit(solution)/shard_map/ppermute | solution.py:41
  145.2 18.3 %collective-permute-start.32 = (bf16[128,1024]{1,0:T(8,128)(2,1)S(1)}, bf16[128,1024]{1,0:T(8,128)(2,1)S(1)}, u32[]{:S(2)}, u32[]{:S(2)}) collective-permute-start(bf16[128,1024]{1,0:T(8,128)(2,1)S(1)} %get-tuple-element.86), channel_id=1, source_target_pairs={{0,16},{1,17},{2,18},{3,19},{4,20},{5,21},{6,22},{7,23},{8,24},{9,... | collective-permute-start | bytes 786440 | tf_op jit(solution)/shard_map/ppermute | solution.py:41
  147.8 15.7 %collective-permute-start.33 = (bf16[128,1024]{1,0:T(8,128)(2,1)S(1)}, bf16[128,1024]{1,0:T(8,128)(2,1)S(1)}, u32[]{:S(2)}, u32[]{:S(2)}) collective-permute-start(bf16[128,1024]{1,0:T(8,128)(2,1)S(1)} %get-tuple-element.87), channel_id=1, source_target_pairs={{0,48},{1,49},{2,50},{3,51},{4,52},{5,53},{6,54},{7,55},{8,56},{9,... | collective-permute-start | bytes 786440 | tf_op jit(solution)/shard_map/ppermute | solution.py:41
  160.9 15.0 %collective-permute-start.30 = (bf16[256,1024]{1,0:T(8,128)(2,1)}, bf16[256,1024]{1,0:T(8,128)(2,1)}, u32[]{:S(2)}, u32[]{:S(2)}) collective-permute-start(bf16[256,1024]{1,0:T(8,128)(2,1)} %get-tuple-element.93), channel_id=1, source_target_pairs={{0,48},{1,49},{2,50},{3,51},{4,52},{5,53},{6,54},{7,55},{8,56},{9,... | collective-permute-start | bytes 1572872 | tf_op jit(solution)/shard_map/ppermute | solution.py:41
  163.5 12.4 %collective-permute-start.29 = (bf16[256,1024]{1,0:T(8,128)(2,1)S(1)}, bf16[256,1024]{1,0:T(8,128)(2,1)}, u32[]{:S(2)}, u32[]{:S(2)}) collective-permute-start(bf16[256,1024]{1,0:T(8,128)(2,1)S(1)} %get-tuple-element.91), channel_id=1, source_target_pairs={{0,16},{1,17},{2,18},{3,19},{4,20},{5,21},{6,22},{7,23},{8,24},{9,... | collective-permute-start | bytes 1572872 | tf_op jit(solution)/shard_map/ppermute | solution.py:41
  177.5 15.5 %collective-permute-start.37 = (bf16[256,512]{1,0:T(8,128)(2,1)S(1)}, bf16[256,512]{1,0:T(8,128)(2,1)S(1)}, u32[]{:S(2)}, u32[]{:S(2)}) collective-permute-start(bf16[256,512]{1,0:T(8,128)(2,1)S(1)} %get-tuple-element.90), channel_id=1, source_target_pairs={{0,8},{1,24},{2,10},{3,26},{4,12},{5,28},{6,14},{7,30},{8,0},{9,16... | collective-permute-start | bytes 786440 | tf_op jit(solution)/shard_map/ppermute | solution.py:41
  186.4 12.5 %collective-permute-start.36 = (bf16[256,512]{1,0:T(8,128)(2,1)S(1)}, bf16[256,512]{1,0:T(8,128)(2,1)S(1)}, u32[]{:S(2)}, u32[]{:S(2)}) collective-permute-start(bf16[256,512]{1,0:T(8,128)(2,1)S(1)} %get-tuple-element.89), channel_id=1, source_target_pairs={{0,0},{1,16},{2,2},{3,18},{4,4},{5,20},{6,6},{7,22},{8,8},{9,24},{... | collective-permute-start | bytes 786440 | tf_op jit(solution)/shard_map/ppermute | solution.py:41
  (38 other events, 326.4 us)
Sparse Core Ops, SparseCore 0:
  20.1 58.2 all-gather.2

commit v18 on v17

--- a/solution.py
+++ b/solution.py
@@ -419,8 +419,9 @@
         (from_left, from_right, here_a, here_b)
     )
     a_bottom, b_top = x_shift(a_bottom, 1), x_shift(b_top, -1)
-    a_top = x_shift(a_top + from_left[:128], 1)
-    b_bottom = x_shift(b_bottom + from_right[:128], -1)
+    a_top, b_bottom = a_top + from_left[:128], b_bottom + from_right[:128]
+    here_a, here_b, a_top, b_bottom = lax.optimization_barrier((here_a, here_b, a_top, b_bottom))
+    a_top, b_bottom = x_shift(a_top, 1), x_shift(b_bottom, -1)
     here_a = x_shift(add_rows(here_a, from_left[128:], 0), 1)
     here_b = x_shift(add_rows(here_b, from_right[128:], 128), -1)
 

time: 208 us -> 207 us (level)
    add x0 -> x2, other arithmetic: none -> 2.21 us  [local(): a_top, b_bottom = (a_top + from_left[:128], b_bottom + from_right[:128])]
where the time goes in v18:
time: 207 us; the launch traced here: 206 us
  starting transfers between devices  62.4 us (30%)
  waiting for transfers between devices  61.9 us (30%)
  Pallas kernels  32.9 us (16%)
  other arithmetic  17.6 us (9%)
  local copies, waits for them, and re-layouts  16.4 us (8%)
  between operations  14.6 us (7%)
    ppermute x38, starting transfers between devices, send(): return lax.ppermute(value, AXES, pairs(change))  62.4 us
    ppermute x38, waiting for transfers between devices, send(): return lax.ppermute(value, AXES, pairs(change))  61.9 us
    pallas_call x3, Pallas kernels, products(): pl.pallas_call(lambda *refs: products_kernel(form, steps, *refs), grid_sp...  14.2 us
    pallas_call x3, Pallas kernels, project(): pl.pallas_call(project_kernel, grid_spec=pltpu.PrefetchScalarGridSpec(num...  9.87 us
    unnamed x47, local copies, waits for them, and re-layouts  5.73 us
    pallas_call x2, Pallas kernels, attention(): pl.pallas_call(attention_kernel, grid=(1,), in_specs=[pl.BlockSpec((v.sha...  5.48 us
  transfers between devices with their start and end apart: 39, of which 17 were waited for; matrix products, arithmetic and copies ran while one was open for 11% of the time, Pallas kernels for 14%

profile of v18, /device:TPU:3, one launch (start us, length us, event | category | flops | bytes accessed | tf_op | source)
XLA Modules:
  0.0 205.8 jit_solution(14566427935430216204)
XLA Ops:
  20.0 8.4 %collective-permute-start.3 = (bf16[256,1024]{1,0:T(8,128)(2,1)S(1)}, bf16[256,1024]{1,0:T(8,128)(2,1)S(1)}, u32[]{:S(2)}, u32[]{:S(2)}) collective-permute-start(bf16[256,1024]{1,0:T(8,128)(2,1)S(1)} %maximum_select_fusion), channel_id=1, source_target_pairs={{0,16},{1,17},{2,18},{3,19},{4,20},{5,21},{6,22},{7,23},{8,24},{9,... | collective-permute-start | bytes 1572872 | tf_op jit(solution)/shard_map/ppermute | solution.py:41
  28.3 3.7 %collective-permute-start.5 = (bf16[256,1024]{1,0:T(8,128)(2,1)S(1)}, bf16[256,1024]{1,0:T(8,128)(2,1)}, u32[]{:S(2)}, u32[]{:S(2)}) collective-permute-start(bf16[256,1024]{1,0:T(8,128)(2,1)S(1)} %maximum_select_fusion), channel_id=1, source_target_pairs={{0,64},{1,65},{2,66},{3,67},{4,68},{5,69},{6,70},{7,71},{8,72},{9,... | collective-permute-start | bytes 1572872 | tf_op jit(solution)/shard_map/ppermute | solution.py:41
  32.1 7.1 %collective-permute-done.3 = bf16[256,1024]{1,0:T(8,128)(2,1)S(1)} collective-permute-done((bf16[256,1024]{1,0:T(8,128)(2,1)S(1)}, bf16[256,1024]{1,0:T(8,128)(2,1)S(1)}, u32[]{:S(2)}, u32[]{:S(2)}) %collective-permute-start.3) | collective-permute-done | bytes 524320 | tf_op jit(solution)/shard_map/ppermute | solution.py:41
  43.8 3.3 %collective-permute-start.12 = (bf16[1024,640]{1,0:T(8,128)(2,1)}, bf16[1024,640]{1,0:T(8,128)(2,1)S(1)}, u32[]{:S(2)}, u32[]{:S(2)}) collective-permute-start(bf16[1024,640]{1,0:T(8,128)(2,1)} %pad_maximum_fusion), channel_id=1, source_target_pairs={{0,1},{1,0},{2,3},{3,2},{4,5},{5,4},{6,7},{7,6},{8,9},{9,8},{10,11... | collective-permute-start | bytes 3932168 | tf_op jit(solution)/shard_map/ppermute | solution.py:41
  48.9 10.7 %collective-permute-done.8 = bf16[256,1024]{1,0:T(8,128)(2,1)} collective-permute-done((bf16[256,1024]{1,0:T(8,128)(2,1)}, bf16[256,1024]{1,0:T(8,128)(2,1)}, u32[]{:S(2)}, u32[]{:S(2)}) %collective-permute-start.8) | collective-permute-done | bytes 524320 | tf_op jit(solution)/shard_map/ppermute | solution.py:41
  65.0 2.7 %collective-permute-start.11 = (bf16[128,1024]{1,0:T(8,128)(2,1)S(1)}, bf16[128,1024]{1,0:T(8,128)(2,1)S(1)}, u32[]{:S(2)}, u32[]{:S(2)}) collective-permute-start(bf16[128,1024]{1,0:T(8,128)(2,1)S(1)} %slice.41), channel_id=1, source_target_pairs={{0,48},{1,49},{2,50},{3,51},{4,52},{5,53},{6,54},{7,55},{8,56},{9,... | collective-permute-start | bytes 786440 | tf_op jit(solution)/shard_map/ppermute | solution.py:41
  67.8 6.3 %collective-permute-done.11 = bf16[128,1024]{1,0:T(8,128)(2,1)S(1)} collective-permute-done((bf16[128,1024]{1,0:T(8,128)(2,1)S(1)}, bf16[128,1024]{1,0:T(8,128)(2,1)S(1)}, u32[]{:S(2)}, u32[]{:S(2)}) %collective-permute-start.11) | collective-permute-done | bytes 262176 | tf_op jit(solution)/shard_map/ppermute | solution.py:41
  83.0 2.7 %collective-permute-start.15 = (bf16[128,1280]{1,0:T(8,128)(2,1)S(1)}, bf16[128,1280]{1,0:T(8,128)(2,1)S(1)}, u32[]{:S(2)}, u32[]{:S(2)}) collective-permute-start(bf16[128,1280]{1,0:T(8,128)(2,1)S(1)} %get-tuple-element.62), channel_id=1, source_target_pairs={{0,6},{1,7},{2,0},{3,1},{4,2},{5,3},{6,4},{7,5},{8,14},{9,15},{10,... | collective-permute-start | bytes 983048 | tf_op jit(solution)/shard_map/ppermute | solution.py:41
  85.8 5.2 %shard_map.65 = (bf16[128,1280]{1,0:T(8,128)(2,1)S(1)}, bf16[128,1280]{1,0:T(8,128)(2,1)S(1)}, bf16[128,1280]{1,0:T(8,128)(2,1)S(1)}, bf16[128,1280]{1,0:T(8,128)(2,1)S(1)}) custom-call(s32[4]{0:T(128)S(1)} %pad_add_fusion.4.at_ref, bf16[4,256,2048]{2,1,0:T(8,128)(2,1)S(1)} %bitcast_dynamic-update-slice_fusion.rows_ref, bf16[1024,512]{1,0:T(8,128)(2,1)S(1)} %copy-done.1, ...), custom_call_target="tpu_custom_call" | custom-call | tf_op jit(solution)/shard_map/pallas_call | solution.py:233
  91.0 2.7 %collective-permute-start.17 = (bf16[128,1280]{1,0:T(8,128)(2,1)S(1)}, bf16[128,1280]{1,0:T(8,128)(2,1)S(1)}, u32[]{:S(2)}, u32[]{:S(2)}) collective-permute-start(bf16[128,1280]{1,0:T(8,128)(2,1)S(1)} %get-tuple-element.70), channel_id=1, source_target_pairs={{0,6},{1,7},{2,0},{3,1},{4,2},{5,3},{6,4},{7,5},{8,14},{9,15},{10,... | collective-permute-start | bytes 983048 | tf_op jit(solution)/shard_map/ppermute | solution.py:41
  96.5 2.7 %collective-permute-start.19 = (bf16[128,1280]{1,0:T(8,128)(2,1)}, bf16[128,1280]{1,0:T(8,128)(2,1)}, u32[]{:S(2)}, u32[]{:S(2)}) collective-permute-start(bf16[128,1280]{1,0:T(8,128)(2,1)} %add.332), channel_id=1, source_target_pairs={{0,6},{1,7},{2,0},{3,1},{4,2},{5,3},{6,4},{7,5},{8,14},{9,15},{10,... | collective-permute-start | bytes 983048 | tf_op jit(solution)/shard_map/ppermute | solution.py:41
  115.0 2.7 %shard_map.68.refs_1_ = bf16[256,512]{1,0:T(8,128)(2,1)S(1)} custom-call(bf16[256,1280]{1,0:T(8,128)(2,1)S(1)} %copy-done.3, bf16[128,1280]{1,0:T(8,128)(2,1)} %collective-permute-done.18.refs_1_.refs_6_, bf16[128,1280]{1,0:T(8,128)(2,1)S(1)} %copy-done.6, bf16[128,1280]{1,0:T(8,128)(2,1)S(1)} %copy-done.8, ...), custom_call_target="tpu_custom_call" | custom-call | tf_op jit(solution)/shard_map/pallas_call | solution.py:184
  117.8 3.0 %collective-permute-start.24 = (bf16[256,512]{1,0:T(8,128)(2,1)S(1)}, bf16[256,512]{1,0:T(8,128)(2,1)S(1)}, u32[]{:S(2)}, u32[]{:S(2)}) collective-permute-start(bf16[256,512]{1,0:T(8,128)(2,1)S(1)} %shard_map.68.refs_1_), channel_id=1, source_target_pairs={{0,1},{1,0},{2,3},{3,2},{4,5},{5,4},{6,7},{7,6},{8,9},{9,8},{10,11... | collective-permute-start | bytes 786440 | tf_op jit(solution)/shard_map/ppermute | solution.py:41
  121.7 2.7 %shard_map.69.refs_2_ = bf16[256,512]{1,0:T(8,128)(2,1)S(1)} custom-call(bf16[256,1280]{1,0:T(8,128)(2,1)S(1)} %copy-done.3, bf16[128,1280]{1,0:T(8,128)(2,1)} %collective-permute-done.18.refs_1_.refs_6_, bf16[128,1280]{1,0:T(8,128)(2,1)S(1)} %copy-done.6, bf16[128,1280]{1,0:T(8,128)(2,1)S(1)} %copy-done.8, ...), custom_call_target="tpu_custom_call" | custom-call | tf_op jit(solution)/shard_map/pallas_call | solution.py:184
  127.1 6.4 %collective-permute-done.25.refs_4_ = bf16[256,512]{1,0:T(8,128)(2,1)S(1)} collective-permute-done((bf16[256,512]{1,0:T(8,128)(2,1)S(1)}, bf16[256,512]{1,0:T(8,128)(2,1)S(1)}, u32[]{:S(2)}, u32[]{:S(2)}) %collective-permute-start.25) | collective-permute-done | bytes 262176 | tf_op jit(solution)/shard_map/ppermute | solution.py:41
  133.5 4.7 %shard_map.71 = (bf16[256,1024]{1,0:T(8,128)(2,1)}, bf16[256,1024]{1,0:T(8,128)(2,1)}) custom-call(s32[4]{0:T(128)S(1)} %get-tuple-element.108.refs_0_, bf16[256,512]{1,0:T(8,128)(2,1)S(1)} %shard_map.68.refs_1_, bf16[256,512]{1,0:T(8,128)(2,1)S(1)} %shard_map.69.refs_2_, bf16[256,512]{1,0:T(8,128)(2,1)S(1)} %collective-permute-done.24.refs_3_, ...), custom_call_target="tpu_custom_call" | custom-call | tf_op jit(solution)/shard_map/pallas_call | solution.py:284
  141.9 3.3 %shard_map.72 = (bf16[128,1024]{1,0:T(8,128)(2,1)S(1)}, bf16[128,1024]{1,0:T(8,128)(2,1)S(1)}, bf16[128,1024]{1,0:T(8,128)(2,1)S(1)}, bf16[128,1024]{1,0:T(8,128)(2,1)S(1)}) custom-call(s32[4]{0:T(128)S(1)} %get-tuple-element.109.refs_0_, bf16[256,512]{1,0:T(8,128)(2,1)S(1)} %shard_map.68.refs_1_, bf16[256,512]{1,0:T(8,128)(2,1)S(1)} %shard_map.69.refs_2_, ...), custom_call_target="tpu_custom_call" | custom-call | tf_op jit(solution)/shard_map/pallas_call | solution.py:284
  145.2 2.6 %collective-permute-start.32 = (bf16[128,1024]{1,0:T(8,128)(2,1)S(1)}, bf16[128,1024]{1,0:T(8,128)(2,1)S(1)}, u32[]{:S(2)}, u32[]{:S(2)}) collective-permute-start(bf16[128,1024]{1,0:T(8,128)(2,1)S(1)} %get-tuple-element.94), channel_id=1, source_target_pairs={{0,16},{1,17},{2,18},{3,19},{4,20},{5,21},{6,22},{7,23},{8,24},{9,... | collective-permute-start | bytes 786440 | tf_op jit(solution)/shard_map/ppermute | solution.py:41
  148.5 6.2 %shard_map.70 = (bf16[256,1024]{1,0:T(8,128)(2,1)S(1)}, bf16[256,1024]{1,0:T(8,128)(2,1)}, bf16[256,1024]{1,0:T(8,128)(2,1)S(1)}, bf16[256,1024]{1,0:T(8,128)(2,1)S(1)}) custom-call(s32[8]{0:T(128)S(1)} %stack.102.refs_0_, bf16[256,512]{1,0:T(8,128)(2,1)S(1)} %shard_map.68.refs_1_, bf16[256,512]{1,0:T(8,128)(2,1)S(1)} %shard_map.69.refs_2_, ...), custom_call_target="tpu_custom_call" | custom-call | tf_op jit(solution)/shard_map/pallas_call | solution.py:284
  167.2 8.6 %collective-permute-done.30 = bf16[256,1024]{1,0:T(8,128)(2,1)} collective-permute-done((bf16[256,1024]{1,0:T(8,128)(2,1)}, bf16[256,1024]{1,0:T(8,128)(2,1)}, u32[]{:S(2)}, u32[]{:S(2)}) %collective-permute-start.30) | collective-permute-done | bytes 524320 | tf_op jit(solution)/shard_map/ppermute | solution.py:41
  177.7 7.8 %collective-permute-start.37 = (bf16[256,512]{1,0:T(8,128)(2,1)S(1)}, bf16[256,512]{1,0:T(8,128)(2,1)S(1)}, u32[]{:S(2)}, u32[]{:S(2)}) collective-permute-start(bf16[256,512]{1,0:T(8,128)(2,1)S(1)} %get-tuple-element.98), channel_id=1, source_target_pairs={{0,8},{1,24},{2,10},{3,26},{4,12},{5,28},{6,14},{7,30},{8,0},{9,16... | collective-permute-start | bytes 786440 | tf_op jit(solution)/shard_map/ppermute | solution.py:41
  185.4 2.9 %collective-permute-start.36 = (bf16[256,512]{1,0:T(8,128)(2,1)S(1)}, bf16[256,512]{1,0:T(8,128)(2,1)S(1)}, u32[]{:S(2)}, u32[]{:S(2)}) collective-permute-start(bf16[256,512]{1,0:T(8,128)(2,1)S(1)} %get-tuple-element.97), channel_id=1, source_target_pairs={{0,0},{1,16},{2,2},{3,18},{4,4},{5,20},{6,6},{7,22},{8,8},{9,24},{... | collective-permute-start | bytes 786440 | tf_op jit(solution)/shard_map/ppermute | solution.py:41
  188.3 3.6 %collective-permute-done.37 = bf16[256,512]{1,0:T(8,128)(2,1)S(1)} collective-permute-done((bf16[256,512]{1,0:T(8,128)(2,1)S(1)}, bf16[256,512]{1,0:T(8,128)(2,1)S(1)}, u32[]{:S(2)}, u32[]{:S(2)}) %collective-permute-start.37) | collective-permute-done | bytes 262176 | tf_op jit(solution)/shard_map/ppermute | solution.py:41
  191.9 6.0 %collective-permute-done.36 = bf16[256,512]{1,0:T(8,128)(2,1)S(1)} collective-permute-done((bf16[256,512]{1,0:T(8,128)(2,1)S(1)}, bf16[256,512]{1,0:T(8,128)(2,1)S(1)}, u32[]{:S(2)}, u32[]{:S(2)}) %collective-permute-start.36) | collective-permute-done | bytes 262176 | tf_op jit(solution)/shard_map/ppermute | solution.py:41
  (161 shorter events, 75.1 us)
Async XLA Ops:
  6.5 107.2 %all-gather.3.cloned.1.call-start = ((), (), s32[]{:S(2)}) async-start(), calls=%async_computation | async-start | bytes 5242880 | tf_op jit(solution)/shard_map/all_gather | solution.py:377
  20.0 19.3 %collective-permute-start.3 = (bf16[256,1024]{1,0:T(8,128)(2,1)S(1)}, bf16[256,1024]{1,0:T(8,128)(2,1)S(1)}, u32[]{:S(2)}, u32[]{:S(2)}) collective-permute-start(bf16[256,1024]{1,0:T(8,128)(2,1)S(1)} %maximum_select_fusion), channel_id=1, source_target_pairs={{0,16},{1,17},{2,18},{3,19},{4,20},{5,21},{6,22},{7,23},{8,24},{9,... | collective-permute-start | bytes 1572872 | tf_op jit(solution)/shard_map/ppermute | solution.py:41
  28.3 12.9 %collective-permute-start.4 = (bf16[256,1024]{1,0:T(8,128)(2,1)S(1)}, bf16[256,1024]{1,0:T(8,128)(2,1)S(1)}, u32[]{:S(2)}, u32[]{:S(2)}) collective-permute-start(bf16[256,1024]{1,0:T(8,128)(2,1)S(1)} %maximum_select_fusion), channel_id=1, source_target_pairs={{0,48},{1,49},{2,50},{3,51},{4,52},{5,53},{6,54},{7,55},{8,56},{9,... | collective-permute-start | bytes 1572872 | tf_op jit(solution)/shard_map/ppermute | solution.py:41
  28.3 15.5 %collective-permute-start.5 = (bf16[256,1024]{1,0:T(8,128)(2,1)S(1)}, bf16[256,1024]{1,0:T(8,128)(2,1)}, u32[]{:S(2)}, u32[]{:S(2)}) collective-permute-start(bf16[256,1024]{1,0:T(8,128)(2,1)S(1)} %maximum_select_fusion), channel_id=1, source_target_pairs={{0,64},{1,65},{2,66},{3,67},{4,68},{5,69},{6,70},{7,71},{8,72},{9,... | collective-permute-start | bytes 1572872 | tf_op jit(solution)/shard_map/ppermute | solution.py:41
  43.8 31.4 %collective-permute-start.12 = (bf16[1024,640]{1,0:T(8,128)(2,1)}, bf16[1024,640]{1,0:T(8,128)(2,1)S(1)}, u32[]{:S(2)}, u32[]{:S(2)}) collective-permute-start(bf16[1024,640]{1,0:T(8,128)(2,1)} %pad_maximum_fusion), channel_id=1, source_target_pairs={{0,1},{1,0},{2,3},{3,2},{4,5},{5,4},{6,7},{7,6},{8,9},{9,8},{10,11... | collective-permute-start | bytes 3932168 | tf_op jit(solution)/shard_map/ppermute | solution.py:41
  47.1 12.5 %collective-permute-start.8 = (bf16[256,1024]{1,0:T(8,128)(2,1)}, bf16[256,1024]{1,0:T(8,128)(2,1)}, u32[]{:S(2)}, u32[]{:S(2)}) collective-permute-start(bf16[256,1024]{1,0:T(8,128)(2,1)} %collective-permute-done.5), channel_id=1, source_target_pairs={{0,16},{1,17},{2,18},{3,19},{4,20},{5,21},{6,22},{7,23},{8,24},{9,... | collective-permute-start | bytes 1572872 | tf_op jit(solution)/shard_map/ppermute | solution.py:41
  48.3 15.7 %collective-permute-start.9 = (bf16[256,1024]{1,0:T(8,128)(2,1)}, bf16[256,1024]{1,0:T(8,128)(2,1)}, u32[]{:S(2)}, u32[]{:S(2)}) collective-permute-start(bf16[256,1024]{1,0:T(8,128)(2,1)} %collective-permute-done.5), channel_id=1, source_target_pairs={{0,48},{1,49},{2,50},{3,51},{4,52},{5,53},{6,54},{7,55},{8,56},{9,... | collective-permute-start | bytes 1572872 | tf_op jit(solution)/shard_map/ppermute | solution.py:41
  61.8 16.4 %collective-permute-start.7 = (bf16[128,1024]{1,0:T(8,128)(2,1)S(1)}, bf16[128,1024]{1,0:T(8,128)(2,1)S(1)}, u32[]{:S(2)}, u32[]{:S(2)}) collective-permute-start(bf16[128,1024]{1,0:T(8,128)(2,1)S(1)} %slice.31), channel_id=1, source_target_pairs={{0,48},{1,49},{2,50},{3,51},{4,52},{5,53},{6,54},{7,55},{8,56},{9,... | collective-permute-start | bytes 786440 | tf_op jit(solution)/shard_map/ppermute | solution.py:41
  63.9 14.3 %collective-permute-start.6 = (bf16[128,1024]{1,0:T(8,128)(2,1)S(1)}, bf16[128,1024]{1,0:T(8,128)(2,1)S(1)}, u32[]{:S(2)}, u32[]{:S(2)}) collective-permute-start(bf16[128,1024]{1,0:T(8,128)(2,1)S(1)} %slice.30), channel_id=1, source_target_pairs={{0,16},{1,17},{2,18},{3,19},{4,20},{5,21},{6,22},{7,23},{8,24},{9,... | collective-permute-start | bytes 786440 | tf_op jit(solution)/shard_map/ppermute | solution.py:41
  82.9 12.0 %collective-permute-start.14 = (bf16[128,1280]{1,0:T(8,128)(2,1)S(1)}, bf16[128,1280]{1,0:T(8,128)(2,1)S(1)}, u32[]{:S(2)}, u32[]{:S(2)}) collective-permute-start(bf16[128,1280]{1,0:T(8,128)(2,1)S(1)} %get-tuple-element.61), channel_id=1, source_target_pairs={{0,2},{1,3},{2,4},{3,5},{4,6},{5,7},{6,0},{7,1},{8,10},{9,11},{10,... | collective-permute-start | bytes 983048 | tf_op jit(solution)/shard_map/ppermute | solution.py:41
  83.0 11.9 %collective-permute-start.15 = (bf16[128,1280]{1,0:T(8,128)(2,1)S(1)}, bf16[128,1280]{1,0:T(8,128)(2,1)S(1)}, u32[]{:S(2)}, u32[]{:S(2)}) collective-permute-start(bf16[128,1280]{1,0:T(8,128)(2,1)S(1)} %get-tuple-element.62), channel_id=1, source_target_pairs={{0,6},{1,7},{2,0},{3,1},{4,2},{5,3},{6,4},{7,5},{8,14},{9,15},{10,... | collective-permute-start | bytes 983048 | tf_op jit(solution)/shard_map/ppermute | solution.py:41
  91.0 10.1 %collective-permute-start.16 = (bf16[128,1280]{1,0:T(8,128)(2,1)S(1)}, bf16[128,1280]{1,0:T(8,128)(2,1)S(1)}, u32[]{:S(2)}, u32[]{:S(2)}) collective-permute-start(bf16[128,1280]{1,0:T(8,128)(2,1)S(1)} %get-tuple-element.69), channel_id=1, source_target_pairs={{0,2},{1,3},{2,4},{3,5},{4,6},{5,7},{6,0},{7,1},{8,10},{9,11},{10,... | collective-permute-start | bytes 983048 | tf_op jit(solution)/shard_map/ppermute | solution.py:41
  91.0 10.3 %collective-permute-start.17 = (bf16[128,1280]{1,0:T(8,128)(2,1)S(1)}, bf16[128,1280]{1,0:T(8,128)(2,1)S(1)}, u32[]{:S(2)}, u32[]{:S(2)}) collective-permute-start(bf16[128,1280]{1,0:T(8,128)(2,1)S(1)} %get-tuple-element.70), channel_id=1, source_target_pairs={{0,6},{1,7},{2,0},{3,1},{4,2},{5,3},{6,4},{7,5},{8,14},{9,15},{10,... | collective-permute-start | bytes 983048 | tf_op jit(solution)/shard_map/ppermute | solution.py:41
  95.7 13.3 %collective-permute-start.18 = (bf16[128,1280]{1,0:T(8,128)(2,1)}, bf16[128,1280]{1,0:T(8,128)(2,1)}, u32[]{:S(2)}, u32[]{:S(2)}) collective-permute-start(bf16[128,1280]{1,0:T(8,128)(2,1)} %add.331), channel_id=1, source_target_pairs={{0,2},{1,3},{2,4},{3,5},{4,6},{5,7},{6,0},{7,1},{8,10},{9,11},{10,... | collective-permute-start | bytes 983048 | tf_op jit(solution)/shard_map/ppermute | solution.py:41
  96.5 12.5 %collective-permute-start.19 = (bf16[128,1280]{1,0:T(8,128)(2,1)}, bf16[128,1280]{1,0:T(8,128)(2,1)}, u32[]{:S(2)}, u32[]{:S(2)}) collective-permute-start(bf16[128,1280]{1,0:T(8,128)(2,1)} %add.332), channel_id=1, source_target_pairs={{0,6},{1,7},{2,0},{3,1},{4,2},{5,3},{6,4},{7,5},{8,14},{9,15},{10,... | collective-permute-start | bytes 983048 | tf_op jit(solution)/shard_map/ppermute | solution.py:41
  113.7 19.8 %collective-permute-start.26 = (bf16[4,512,1024]{2,1,0:T(8,128)(2,1)}, bf16[4,512,1024]{2,1,0:T(8,128)(2,1)}, u32[]{:S(2)}, u32[]{:S(2)}) collective-permute-start(bf16[4,512,1024]{2,1,0:T(8,128)(2,1)} %bitcast.44), channel_id=1, source_target_pairs={{0,8},{1,9},{2,10},{3,11},{4,12},{5,13},{6,14},{7,15},{8,0},{9,1},... | collective-permute-start | bytes 12582920 | tf_op jit(solution)/shard_map/ppermute | solution.py:41
  138.1 16.6 %collective-permute-start.27 = (bf16[256,1024]{1,0:T(8,128)(2,1)}, bf16[256,1024]{1,0:T(8,128)(2,1)}, u32[]{:S(2)}, u32[]{:S(2)}) collective-permute-start(bf16[256,1024]{1,0:T(8,128)(2,1)} %get-tuple-element.80), channel_id=1, source_target_pairs={{0,16},{1,17},{2,18},{3,19},{4,20},{5,21},{6,22},{7,23},{8,24},{9,... | collective-permute-start | bytes 1572872 | tf_op jit(solution)/shard_map/ppermute | solution.py:41
  139.1 15.6 %collective-permute-start.28 = (bf16[256,1024]{1,0:T(8,128)(2,1)}, bf16[256,1024]{1,0:T(8,128)(2,1)}, u32[]{:S(2)}, u32[]{:S(2)}) collective-permute-start(bf16[256,1024]{1,0:T(8,128)(2,1)} %get-tuple-element.81), channel_id=1, source_target_pairs={{0,48},{1,49},{2,50},{3,51},{4,52},{5,53},{6,54},{7,55},{8,56},{9,... | collective-permute-start | bytes 1572872 | tf_op jit(solution)/shard_map/ppermute | solution.py:41
  145.2 20.0 %collective-permute-start.32 = (bf16[128,1024]{1,0:T(8,128)(2,1)S(1)}, bf16[128,1024]{1,0:T(8,128)(2,1)S(1)}, u32[]{:S(2)}, u32[]{:S(2)}) collective-permute-start(bf16[128,1024]{1,0:T(8,128)(2,1)S(1)} %get-tuple-element.94), channel_id=1, source_target_pairs={{0,16},{1,17},{2,18},{3,19},{4,20},{5,21},{6,22},{7,23},{8,24},{9,... | collective-permute-start | bytes 786440 | tf_op jit(solution)/shard_map/ppermute | solution.py:41
  147.8 17.4 %collective-permute-start.33 = (bf16[128,1024]{1,0:T(8,128)(2,1)S(1)}, bf16[128,1024]{1,0:T(8,128)(2,1)S(1)}, u32[]{:S(2)}, u32[]{:S(2)}) collective-permute-start(bf16[128,1024]{1,0:T(8,128)(2,1)S(1)} %get-tuple-element.95), channel_id=1, source_target_pairs={{0,48},{1,49},{2,50},{3,51},{4,52},{5,53},{6,54},{7,55},{8,56},{9,... | collective-permute-start | bytes 786440 | tf_op jit(solution)/shard_map/ppermute | solution.py:41
  161.5 14.3 %collective-permute-start.30 = (bf16[256,1024]{1,0:T(8,128)(2,1)}, bf16[256,1024]{1,0:T(8,128)(2,1)}, u32[]{:S(2)}, u32[]{:S(2)}) collective-permute-start(bf16[256,1024]{1,0:T(8,128)(2,1)} %add_dynamic-update-slice_fusion), channel_id=1, source_target_pairs={{0,48},{1,49},{2,50},{3,51},{4,52},{5,53},{6,54},{7,55},{8,56},{9,... | collective-permute-start | bytes 1572872 | tf_op jit(solution)/shard_map/ppermute | solution.py:41
  165.2 10.8 %collective-permute-start.29 = (bf16[256,1024]{1,0:T(8,128)(2,1)S(1)}, bf16[256,1024]{1,0:T(8,128)(2,1)}, u32[]{:S(2)}, u32[]{:S(2)}) collective-permute-start(bf16[256,1024]{1,0:T(8,128)(2,1)S(1)} %add_dynamic-update-slice_fusion.1), channel_id=1, source_target_pairs={{0,16},{1,17},{2,18},{3,19},{4,20},{5,21},{6,22},{7,23},{8,24},{9,... | collective-permute-start | bytes 1572872 | tf_op jit(solution)/shard_map/ppermute | solution.py:41
  177.7 14.3 %collective-permute-start.37 = (bf16[256,512]{1,0:T(8,128)(2,1)S(1)}, bf16[256,512]{1,0:T(8,128)(2,1)S(1)}, u32[]{:S(2)}, u32[]{:S(2)}) collective-permute-start(bf16[256,512]{1,0:T(8,128)(2,1)S(1)} %get-tuple-element.98), channel_id=1, source_target_pairs={{0,8},{1,24},{2,10},{3,26},{4,12},{5,28},{6,14},{7,30},{8,0},{9,16... | collective-permute-start | bytes 786440 | tf_op jit(solution)/shard_map/ppermute | solution.py:41
  185.4 12.5 %collective-permute-start.36 = (bf16[256,512]{1,0:T(8,128)(2,1)S(1)}, bf16[256,512]{1,0:T(8,128)(2,1)S(1)}, u32[]{:S(2)}, u32[]{:S(2)}) collective-permute-start(bf16[256,512]{1,0:T(8,128)(2,1)S(1)} %get-tuple-element.97), channel_id=1, source_target_pairs={{0,0},{1,16},{2,2},{3,18},{4,4},{5,20},{6,6},{7,22},{8,8},{9,24},{... | collective-permute-start | bytes 786440 | tf_op jit(solution)/shard_map/ppermute | solution.py:41
  (38 other events, 327.2 us)
Sparse Core Ops, SparseCore 0:
  20.1 58.1 all-gather.2

commit v19 on v18

--- a/solution.py
+++ b/solution.py
@@ -290,7 +290,7 @@
             out_specs=[pl.BlockSpec((size, 1024), lambda i, at: (0, 0))] * count,
         ),
         out_shape=[jax.ShapeDtypeStruct((size, 1024), jnp.bfloat16)] * count,
-        compiler_params=WIDE_GRANT if form == "joined" else GRANT,
+        compiler_params=WIDE_GRANT,
     )(at, *attended, near, other)
 
 

time: 207 us -> 206 us (level)
  local copies, waits for them, and re-layouts: 16.4 us -> 14.2 us
    unnamed x47 -> x49, local copies, waits for them, and re-layouts: 5.73 us -> 3.55 us
  transfers between devices with their start and end apart: 39 -> 39, of which waited for: 17 -> 17; matrix products, arithmetic and copies ran while one was open for 11% -> 11% of each run, Pallas kernels for 14% -> 15%
where the time goes in v19:
time: 206 us; the launch traced here: 205 us
  starting transfers between devices  62.4 us (30%)
  waiting for transfers between devices  61.8 us (30%)
  Pallas kernels  34.9 us (17%)
  other arithmetic  17.5 us (8%)
  between operations  14.6 us (7%)
  local copies, waits for them, and re-layouts  14.2 us (7%)
    ppermute x38, starting transfers between devices, send(): return lax.ppermute(value, AXES, pairs(change))  62.4 us
    ppermute x38, waiting for transfers between devices, send(): return lax.ppermute(value, AXES, pairs(change))  61.8 us
    pallas_call x3, Pallas kernels, products(): pl.pallas_call(lambda *refs: products_kernel(form, steps, *refs), grid_sp...  16.2 us
    pallas_call x3, Pallas kernels, project(): pl.pallas_call(project_kernel, grid_spec=pltpu.PrefetchScalarGridSpec(num...  9.87 us
    pallas_call x2, Pallas kernels, attention(): pl.pallas_call(attention_kernel, grid=(1,), in_specs=[pl.BlockSpec((v.sha...  5.48 us
  transfers between devices with their start and end apart: 39, of which 17 were waited for; matrix products, arithmetic and copies ran while one was open for 11% of the time, Pallas kernels for 15%

profile of v19, /device:TPU:3, one launch (start us, length us, event | category | flops | bytes accessed | tf_op | source)
XLA Modules:
  0.0 205.3 jit_solution(1198764472721084244)
XLA Ops:
  20.0 8.4 %collective-permute-start.3 = (bf16[256,1024]{1,0:T(8,128)(2,1)S(1)}, bf16[256,1024]{1,0:T(8,128)(2,1)S(1)}, u32[]{:S(2)}, u32[]{:S(2)}) collective-permute-start(bf16[256,1024]{1,0:T(8,128)(2,1)S(1)} %maximum_select_fusion), channel_id=1, source_target_pairs={{0,16},{1,17},{2,18},{3,19},{4,20},{5,21},{6,22},{7,23},{8,24},{9,... | collective-permute-start | bytes 1572872 | tf_op jit(solution)/shard_map/ppermute | solution.py:41
  28.3 3.7 %collective-permute-start.5 = (bf16[256,1024]{1,0:T(8,128)(2,1)S(1)}, bf16[256,1024]{1,0:T(8,128)(2,1)}, u32[]{:S(2)}, u32[]{:S(2)}) collective-permute-start(bf16[256,1024]{1,0:T(8,128)(2,1)S(1)} %maximum_select_fusion), channel_id=1, source_target_pairs={{0,64},{1,65},{2,66},{3,67},{4,68},{5,69},{6,70},{7,71},{8,72},{9,... | collective-permute-start | bytes 1572872 | tf_op jit(solution)/shard_map/ppermute | solution.py:41
  32.1 7.1 %collective-permute-done.3 = bf16[256,1024]{1,0:T(8,128)(2,1)S(1)} collective-permute-done((bf16[256,1024]{1,0:T(8,128)(2,1)S(1)}, bf16[256,1024]{1,0:T(8,128)(2,1)S(1)}, u32[]{:S(2)}, u32[]{:S(2)}) %collective-permute-start.3) | collective-permute-done | bytes 524320 | tf_op jit(solution)/shard_map/ppermute | solution.py:41
  43.8 3.3 %collective-permute-start.12 = (bf16[1024,640]{1,0:T(8,128)(2,1)}, bf16[1024,640]{1,0:T(8,128)(2,1)S(1)}, u32[]{:S(2)}, u32[]{:S(2)}) collective-permute-start(bf16[1024,640]{1,0:T(8,128)(2,1)} %pad_maximum_fusion), channel_id=1, source_target_pairs={{0,1},{1,0},{2,3},{3,2},{4,5},{5,4},{6,7},{7,6},{8,9},{9,8},{10,11... | collective-permute-start | bytes 3932168 | tf_op jit(solution)/shard_map/ppermute | solution.py:41
  48.9 10.7 %collective-permute-done.8 = bf16[256,1024]{1,0:T(8,128)(2,1)} collective-permute-done((bf16[256,1024]{1,0:T(8,128)(2,1)}, bf16[256,1024]{1,0:T(8,128)(2,1)}, u32[]{:S(2)}, u32[]{:S(2)}) %collective-permute-start.8) | collective-permute-done | bytes 524320 | tf_op jit(solution)/shard_map/ppermute | solution.py:41
  65.0 2.7 %collective-permute-start.11 = (bf16[128,1024]{1,0:T(8,128)(2,1)S(1)}, bf16[128,1024]{1,0:T(8,128)(2,1)S(1)}, u32[]{:S(2)}, u32[]{:S(2)}) collective-permute-start(bf16[128,1024]{1,0:T(8,128)(2,1)S(1)} %slice.41), channel_id=1, source_target_pairs={{0,48},{1,49},{2,50},{3,51},{4,52},{5,53},{6,54},{7,55},{8,56},{9,... | collective-permute-start | bytes 786440 | tf_op jit(solution)/shard_map/ppermute | solution.py:41
  67.8 6.3 %collective-permute-done.11 = bf16[128,1024]{1,0:T(8,128)(2,1)S(1)} collective-permute-done((bf16[128,1024]{1,0:T(8,128)(2,1)S(1)}, bf16[128,1024]{1,0:T(8,128)(2,1)S(1)}, u32[]{:S(2)}, u32[]{:S(2)}) %collective-permute-start.11) | collective-permute-done | bytes 262176 | tf_op jit(solution)/shard_map/ppermute | solution.py:41
  83.0 2.8 %collective-permute-start.15 = (bf16[128,1280]{1,0:T(8,128)(2,1)S(1)}, bf16[128,1280]{1,0:T(8,128)(2,1)S(1)}, u32[]{:S(2)}, u32[]{:S(2)}) collective-permute-start(bf16[128,1280]{1,0:T(8,128)(2,1)S(1)} %get-tuple-element.62), channel_id=1, source_target_pairs={{0,6},{1,7},{2,0},{3,1},{4,2},{5,3},{6,4},{7,5},{8,14},{9,15},{10,... | collective-permute-start | bytes 983048 | tf_op jit(solution)/shard_map/ppermute | solution.py:41
  85.8 5.2 %shard_map.65 = (bf16[128,1280]{1,0:T(8,128)(2,1)S(1)}, bf16[128,1280]{1,0:T(8,128)(2,1)S(1)}, bf16[128,1280]{1,0:T(8,128)(2,1)S(1)}, bf16[128,1280]{1,0:T(8,128)(2,1)S(1)}) custom-call(s32[4]{0:T(128)S(1)} %pad_add_fusion.4.at_ref, bf16[4,256,2048]{2,1,0:T(8,128)(2,1)S(1)} %bitcast_dynamic-update-slice_fusion.rows_ref, bf16[1024,512]{1,0:T(8,128)(2,1)S(1)} %copy-done, ...), custom_call_target="tpu_custom_call" | custom-call | tf_op jit(solution)/shard_map/pallas_call | solution.py:233
  91.1 2.7 %collective-permute-start.17 = (bf16[128,1280]{1,0:T(8,128)(2,1)S(1)}, bf16[128,1280]{1,0:T(8,128)(2,1)S(1)}, u32[]{:S(2)}, u32[]{:S(2)}) collective-permute-start(bf16[128,1280]{1,0:T(8,128)(2,1)S(1)} %get-tuple-element.70), channel_id=1, source_target_pairs={{0,6},{1,7},{2,0},{3,1},{4,2},{5,3},{6,4},{7,5},{8,14},{9,15},{10,... | collective-permute-start | bytes 983048 | tf_op jit(solution)/shard_map/ppermute | solution.py:41
  96.5 2.7 %collective-permute-start.19 = (bf16[128,1280]{1,0:T(8,128)(2,1)}, bf16[128,1280]{1,0:T(8,128)(2,1)}, u32[]{:S(2)}, u32[]{:S(2)}) collective-permute-start(bf16[128,1280]{1,0:T(8,128)(2,1)} %add.332), channel_id=1, source_target_pairs={{0,6},{1,7},{2,0},{3,1},{4,2},{5,3},{6,4},{7,5},{8,14},{9,15},{10,... | collective-permute-start | bytes 983048 | tf_op jit(solution)/shard_map/ppermute | solution.py:41
  115.0 2.7 %shard_map.68.refs_1_ = bf16[256,512]{1,0:T(8,128)(2,1)S(1)} custom-call(bf16[256,1280]{1,0:T(8,128)(2,1)S(1)} %copy-done.2, bf16[128,1280]{1,0:T(8,128)(2,1)} %collective-permute-done.18.refs_1_.refs_6_, bf16[128,1280]{1,0:T(8,128)(2,1)S(1)} %copy-done.5, bf16[128,1280]{1,0:T(8,128)(2,1)S(1)} %copy-done.7, ...), custom_call_target="tpu_custom_call" | custom-call | tf_op jit(solution)/shard_map/pallas_call | solution.py:184
  117.8 3.0 %collective-permute-start.24 = (bf16[256,512]{1,0:T(8,128)(2,1)S(1)}, bf16[256,512]{1,0:T(8,128)(2,1)S(1)}, u32[]{:S(2)}, u32[]{:S(2)}) collective-permute-start(bf16[256,512]{1,0:T(8,128)(2,1)S(1)} %shard_map.68.refs_1_), channel_id=1, source_target_pairs={{0,1},{1,0},{2,3},{3,2},{4,5},{5,4},{6,7},{7,6},{8,9},{9,8},{10,11... | collective-permute-start | bytes 786440 | tf_op jit(solution)/shard_map/ppermute | solution.py:41
  121.7 2.7 %shard_map.69.refs_2_ = bf16[256,512]{1,0:T(8,128)(2,1)S(1)} custom-call(bf16[256,1280]{1,0:T(8,128)(2,1)S(1)} %copy-done.2, bf16[128,1280]{1,0:T(8,128)(2,1)} %collective-permute-done.18.refs_1_.refs_6_, bf16[128,1280]{1,0:T(8,128)(2,1)S(1)} %copy-done.5, bf16[128,1280]{1,0:T(8,128)(2,1)S(1)} %copy-done.7, ...), custom_call_target="tpu_custom_call" | custom-call | tf_op jit(solution)/shard_map/pallas_call | solution.py:184
  127.1 6.4 %collective-permute-done.25.refs_4_ = bf16[256,512]{1,0:T(8,128)(2,1)S(1)} collective-permute-done((bf16[256,512]{1,0:T(8,128)(2,1)S(1)}, bf16[256,512]{1,0:T(8,128)(2,1)S(1)}, u32[]{:S(2)}, u32[]{:S(2)}) %collective-permute-start.25) | collective-permute-done | bytes 262176 | tf_op jit(solution)/shard_map/ppermute | solution.py:41
  133.5 4.6 %shard_map.71 = (bf16[256,1024]{1,0:T(8,128)(2,1)}, bf16[256,1024]{1,0:T(8,128)(2,1)}) custom-call(s32[4]{0:T(128)S(1)} %get-tuple-element.108.refs_0_, bf16[256,512]{1,0:T(8,128)(2,1)S(1)} %shard_map.68.refs_1_, bf16[256,512]{1,0:T(8,128)(2,1)S(1)} %shard_map.69.refs_2_, bf16[256,512]{1,0:T(8,128)(2,1)S(1)} %collective-permute-done.24.refs_3_, ...), custom_call_target="tpu_custom_call" | custom-call | tf_op jit(solution)/shard_map/pallas_call | solution.py:284
  139.9 4.3 %shard_map.72 = (bf16[128,1024]{1,0:T(8,128)(2,1)S(1)}, bf16[128,1024]{1,0:T(8,128)(2,1)S(1)}, bf16[128,1024]{1,0:T(8,128)(2,1)S(1)}, bf16[128,1024]{1,0:T(8,128)(2,1)S(1)}) custom-call(s32[4]{0:T(128)S(1)} %get-tuple-element.109.refs_0_, bf16[256,512]{1,0:T(8,128)(2,1)S(1)} %shard_map.68.refs_1_, bf16[256,512]{1,0:T(8,128)(2,1)S(1)} %shard_map.69.refs_2_, ...), custom_call_target="tpu_custom_call" | custom-call | tf_op jit(solution)/shard_map/pallas_call | solution.py:284
  147.4 7.3 %shard_map.70 = (bf16[256,1024]{1,0:T(8,128)(2,1)S(1)}, bf16[256,1024]{1,0:T(8,128)(2,1)}, bf16[256,1024]{1,0:T(8,128)(2,1)}, bf16[256,1024]{1,0:T(8,128)(2,1)}) custom-call(s32[8]{0:T(128)S(1)} %stack.102.refs_0_, bf16[256,512]{1,0:T(8,128)(2,1)S(1)} %shard_map.68.refs_1_, bf16[256,512]{1,0:T(8,128)(2,1)S(1)} %shard_map.69.refs_2_, ...), custom_call_target="tpu_custom_call" | custom-call | tf_op jit(solution)/shard_map/pallas_call | solution.py:284
  161.3 2.6 %collective-permute-start.30 = (bf16[256,1024]{1,0:T(8,128)(2,1)}, bf16[256,1024]{1,0:T(8,128)(2,1)}, u32[]{:S(2)}, u32[]{:S(2)}) collective-permute-start(bf16[256,1024]{1,0:T(8,128)(2,1)} %add_dynamic-update-slice_fusion), channel_id=1, source_target_pairs={{0,48},{1,49},{2,50},{3,51},{4,52},{5,53},{6,54},{7,55},{8,56},{9,... | collective-permute-start | bytes 1572872 | tf_op jit(solution)/shard_map/ppermute | solution.py:41
  167.0 8.6 %collective-permute-done.30 = bf16[256,1024]{1,0:T(8,128)(2,1)} collective-permute-done((bf16[256,1024]{1,0:T(8,128)(2,1)}, bf16[256,1024]{1,0:T(8,128)(2,1)}, u32[]{:S(2)}, u32[]{:S(2)}) %collective-permute-start.30) | collective-permute-done | bytes 524320 | tf_op jit(solution)/shard_map/ppermute | solution.py:41
  177.6 7.4 %collective-permute-start.37 = (bf16[256,512]{1,0:T(8,128)(2,1)S(1)}, bf16[256,512]{1,0:T(8,128)(2,1)S(1)}, u32[]{:S(2)}, u32[]{:S(2)}) collective-permute-start(bf16[256,512]{1,0:T(8,128)(2,1)S(1)} %get-tuple-element.98), channel_id=1, source_target_pairs={{0,8},{1,24},{2,10},{3,26},{4,12},{5,28},{6,14},{7,30},{8,0},{9,16... | collective-permute-start | bytes 786440 | tf_op jit(solution)/shard_map/ppermute | solution.py:41
  184.9 3.2 %collective-permute-start.36 = (bf16[256,512]{1,0:T(8,128)(2,1)S(1)}, bf16[256,512]{1,0:T(8,128)(2,1)S(1)}, u32[]{:S(2)}, u32[]{:S(2)}) collective-permute-start(bf16[256,512]{1,0:T(8,128)(2,1)S(1)} %get-tuple-element.97), channel_id=1, source_target_pairs={{0,0},{1,16},{2,2},{3,18},{4,4},{5,20},{6,6},{7,22},{8,8},{9,24},{... | collective-permute-start | bytes 786440 | tf_op jit(solution)/shard_map/ppermute | solution.py:41
  188.1 2.9 %collective-permute-done.37 = bf16[256,512]{1,0:T(8,128)(2,1)S(1)} collective-permute-done((bf16[256,512]{1,0:T(8,128)(2,1)S(1)}, bf16[256,512]{1,0:T(8,128)(2,1)S(1)}, u32[]{:S(2)}, u32[]{:S(2)}) %collective-permute-start.37) | collective-permute-done | bytes 262176 | tf_op jit(solution)/shard_map/ppermute | solution.py:41
  191.1 6.3 %collective-permute-done.36 = bf16[256,512]{1,0:T(8,128)(2,1)S(1)} collective-permute-done((bf16[256,512]{1,0:T(8,128)(2,1)S(1)}, bf16[256,512]{1,0:T(8,128)(2,1)S(1)}, u32[]{:S(2)}, u32[]{:S(2)}) %collective-permute-start.36) | collective-permute-done | bytes 262176 | tf_op jit(solution)/shard_map/ppermute | solution.py:41
  (163 shorter events, 73.0 us)
Async XLA Ops:
  6.5 107.2 %all-gather.3.cloned.1.call-start = ((), (), s32[]{:S(2)}) async-start(), calls=%async_computation | async-start | bytes 5242880 | tf_op jit(solution)/shard_map/all_gather | solution.py:377
  20.0 19.3 %collective-permute-start.3 = (bf16[256,1024]{1,0:T(8,128)(2,1)S(1)}, bf16[256,1024]{1,0:T(8,128)(2,1)S(1)}, u32[]{:S(2)}, u32[]{:S(2)}) collective-permute-start(bf16[256,1024]{1,0:T(8,128)(2,1)S(1)} %maximum_select_fusion), channel_id=1, source_target_pairs={{0,16},{1,17},{2,18},{3,19},{4,20},{5,21},{6,22},{7,23},{8,24},{9,... | collective-permute-start | bytes 1572872 | tf_op jit(solution)/shard_map/ppermute | solution.py:41
  28.3 12.9 %collective-permute-start.4 = (bf16[256,1024]{1,0:T(8,128)(2,1)S(1)}, bf16[256,1024]{1,0:T(8,128)(2,1)S(1)}, u32[]{:S(2)}, u32[]{:S(2)}) collective-permute-start(bf16[256,1024]{1,0:T(8,128)(2,1)S(1)} %maximum_select_fusion), channel_id=1, source_target_pairs={{0,48},{1,49},{2,50},{3,51},{4,52},{5,53},{6,54},{7,55},{8,56},{9,... | collective-permute-start | bytes 1572872 | tf_op jit(solution)/shard_map/ppermute | solution.py:41
  28.3 15.5 %collective-permute-start.5 = (bf16[256,1024]{1,0:T(8,128)(2,1)S(1)}, bf16[256,1024]{1,0:T(8,128)(2,1)}, u32[]{:S(2)}, u32[]{:S(2)}) collective-permute-start(bf16[256,1024]{1,0:T(8,128)(2,1)S(1)} %maximum_select_fusion), channel_id=1, source_target_pairs={{0,64},{1,65},{2,66},{3,67},{4,68},{5,69},{6,70},{7,71},{8,72},{9,... | collective-permute-start | bytes 1572872 | tf_op jit(solution)/shard_map/ppermute | solution.py:41
  43.8 31.4 %collective-permute-start.12 = (bf16[1024,640]{1,0:T(8,128)(2,1)}, bf16[1024,640]{1,0:T(8,128)(2,1)S(1)}, u32[]{:S(2)}, u32[]{:S(2)}) collective-permute-start(bf16[1024,640]{1,0:T(8,128)(2,1)} %pad_maximum_fusion), channel_id=1, source_target_pairs={{0,1},{1,0},{2,3},{3,2},{4,5},{5,4},{6,7},{7,6},{8,9},{9,8},{10,11... | collective-permute-start | bytes 3932168 | tf_op jit(solution)/shard_map/ppermute | solution.py:41
  47.1 12.5 %collective-permute-start.8 = (bf16[256,1024]{1,0:T(8,128)(2,1)}, bf16[256,1024]{1,0:T(8,128)(2,1)}, u32[]{:S(2)}, u32[]{:S(2)}) collective-permute-start(bf16[256,1024]{1,0:T(8,128)(2,1)} %collective-permute-done.5), channel_id=1, source_target_pairs={{0,16},{1,17},{2,18},{3,19},{4,20},{5,21},{6,22},{7,23},{8,24},{9,... | collective-permute-start | bytes 1572872 | tf_op jit(solution)/shard_map/ppermute | solution.py:41
  48.3 15.7 %collective-permute-start.9 = (bf16[256,1024]{1,0:T(8,128)(2,1)}, bf16[256,1024]{1,0:T(8,128)(2,1)}, u32[]{:S(2)}, u32[]{:S(2)}) collective-permute-start(bf16[256,1024]{1,0:T(8,128)(2,1)} %collective-permute-done.5), channel_id=1, source_target_pairs={{0,48},{1,49},{2,50},{3,51},{4,52},{5,53},{6,54},{7,55},{8,56},{9,... | collective-permute-start | bytes 1572872 | tf_op jit(solution)/shard_map/ppermute | solution.py:41
  61.8 16.4 %collective-permute-start.7 = (bf16[128,1024]{1,0:T(8,128)(2,1)S(1)}, bf16[128,1024]{1,0:T(8,128)(2,1)S(1)}, u32[]{:S(2)}, u32[]{:S(2)}) collective-permute-start(bf16[128,1024]{1,0:T(8,128)(2,1)S(1)} %slice.31), channel_id=1, source_target_pairs={{0,48},{1,49},{2,50},{3,51},{4,52},{5,53},{6,54},{7,55},{8,56},{9,... | collective-permute-start | bytes 786440 | tf_op jit(solution)/shard_map/ppermute | solution.py:41
  63.9 14.3 %collective-permute-start.6 = (bf16[128,1024]{1,0:T(8,128)(2,1)S(1)}, bf16[128,1024]{1,0:T(8,128)(2,1)S(1)}, u32[]{:S(2)}, u32[]{:S(2)}) collective-permute-start(bf16[128,1024]{1,0:T(8,128)(2,1)S(1)} %slice.30), channel_id=1, source_target_pairs={{0,16},{1,17},{2,18},{3,19},{4,20},{5,21},{6,22},{7,23},{8,24},{9,... | collective-permute-start | bytes 786440 | tf_op jit(solution)/shard_map/ppermute | solution.py:41
  82.9 12.0 %collective-permute-start.14 = (bf16[128,1280]{1,0:T(8,128)(2,1)S(1)}, bf16[128,1280]{1,0:T(8,128)(2,1)S(1)}, u32[]{:S(2)}, u32[]{:S(2)}) collective-permute-start(bf16[128,1280]{1,0:T(8,128)(2,1)S(1)} %get-tuple-element.61), channel_id=1, source_target_pairs={{0,2},{1,3},{2,4},{3,5},{4,6},{5,7},{6,0},{7,1},{8,10},{9,11},{10,... | collective-permute-start | bytes 983048 | tf_op jit(solution)/shard_map/ppermute | solution.py:41
  83.0 11.9 %collective-permute-start.15 = (bf16[128,1280]{1,0:T(8,128)(2,1)S(1)}, bf16[128,1280]{1,0:T(8,128)(2,1)S(1)}, u32[]{:S(2)}, u32[]{:S(2)}) collective-permute-start(bf16[128,1280]{1,0:T(8,128)(2,1)S(1)} %get-tuple-element.62), channel_id=1, source_target_pairs={{0,6},{1,7},{2,0},{3,1},{4,2},{5,3},{6,4},{7,5},{8,14},{9,15},{10,... | collective-permute-start | bytes 983048 | tf_op jit(solution)/shard_map/ppermute | solution.py:41
  91.0 10.1 %collective-permute-start.16 = (bf16[128,1280]{1,0:T(8,128)(2,1)S(1)}, bf16[128,1280]{1,0:T(8,128)(2,1)S(1)}, u32[]{:S(2)}, u32[]{:S(2)}) collective-permute-start(bf16[128,1280]{1,0:T(8,128)(2,1)S(1)} %get-tuple-element.69), channel_id=1, source_target_pairs={{0,2},{1,3},{2,4},{3,5},{4,6},{5,7},{6,0},{7,1},{8,10},{9,11},{10,... | collective-permute-start | bytes 983048 | tf_op jit(solution)/shard_map/ppermute | solution.py:41
  91.1 10.2 %collective-permute-start.17 = (bf16[128,1280]{1,0:T(8,128)(2,1)S(1)}, bf16[128,1280]{1,0:T(8,128)(2,1)S(1)}, u32[]{:S(2)}, u32[]{:S(2)}) collective-permute-start(bf16[128,1280]{1,0:T(8,128)(2,1)S(1)} %get-tuple-element.70), channel_id=1, source_target_pairs={{0,6},{1,7},{2,0},{3,1},{4,2},{5,3},{6,4},{7,5},{8,14},{9,15},{10,... | collective-permute-start | bytes 983048 | tf_op jit(solution)/shard_map/ppermute | solution.py:41
  95.7 13.4 %collective-permute-start.18 = (bf16[128,1280]{1,0:T(8,128)(2,1)}, bf16[128,1280]{1,0:T(8,128)(2,1)}, u32[]{:S(2)}, u32[]{:S(2)}) collective-permute-start(bf16[128,1280]{1,0:T(8,128)(2,1)} %add.331), channel_id=1, source_target_pairs={{0,2},{1,3},{2,4},{3,5},{4,6},{5,7},{6,0},{7,1},{8,10},{9,11},{10,... | collective-permute-start | bytes 983048 | tf_op jit(solution)/shard_map/ppermute | solution.py:41
  96.5 12.5 %collective-permute-start.19 = (bf16[128,1280]{1,0:T(8,128)(2,1)}, bf16[128,1280]{1,0:T(8,128)(2,1)}, u32[]{:S(2)}, u32[]{:S(2)}) collective-permute-start(bf16[128,1280]{1,0:T(8,128)(2,1)} %add.332), channel_id=1, source_target_pairs={{0,6},{1,7},{2,0},{3,1},{4,2},{5,3},{6,4},{7,5},{8,14},{9,15},{10,... | collective-permute-start | bytes 983048 | tf_op jit(solution)/shard_map/ppermute | solution.py:41
  113.7 19.8 %collective-permute-start.26 = (bf16[4,512,1024]{2,1,0:T(8,128)(2,1)}, bf16[4,512,1024]{2,1,0:T(8,128)(2,1)}, u32[]{:S(2)}, u32[]{:S(2)}) collective-permute-start(bf16[4,512,1024]{2,1,0:T(8,128)(2,1)} %bitcast.44), channel_id=1, source_target_pairs={{0,8},{1,9},{2,10},{3,11},{4,12},{5,13},{6,14},{7,15},{8,0},{9,1},... | collective-permute-start | bytes 12582920 | tf_op jit(solution)/shard_map/ppermute | solution.py:41
  138.2 16.5 %collective-permute-start.27 = (bf16[256,1024]{1,0:T(8,128)(2,1)}, bf16[256,1024]{1,0:T(8,128)(2,1)}, u32[]{:S(2)}, u32[]{:S(2)}) collective-permute-start(bf16[256,1024]{1,0:T(8,128)(2,1)} %get-tuple-element.80), channel_id=1, source_target_pairs={{0,16},{1,17},{2,18},{3,19},{4,20},{5,21},{6,22},{7,23},{8,24},{9,... | collective-permute-start | bytes 1572872 | tf_op jit(solution)/shard_map/ppermute | solution.py:41
  139.1 15.6 %collective-permute-start.28 = (bf16[256,1024]{1,0:T(8,128)(2,1)}, bf16[256,1024]{1,0:T(8,128)(2,1)}, u32[]{:S(2)}, u32[]{:S(2)}) collective-permute-start(bf16[256,1024]{1,0:T(8,128)(2,1)} %get-tuple-element.81), channel_id=1, source_target_pairs={{0,48},{1,49},{2,50},{3,51},{4,52},{5,53},{6,54},{7,55},{8,56},{9,... | collective-permute-start | bytes 1572872 | tf_op jit(solution)/shard_map/ppermute | solution.py:41
  144.2 20.8 %collective-permute-start.32 = (bf16[128,1024]{1,0:T(8,128)(2,1)S(1)}, bf16[128,1024]{1,0:T(8,128)(2,1)S(1)}, u32[]{:S(2)}, u32[]{:S(2)}) collective-permute-start(bf16[128,1024]{1,0:T(8,128)(2,1)S(1)} %get-tuple-element.94), channel_id=1, source_target_pairs={{0,16},{1,17},{2,18},{3,19},{4,20},{5,21},{6,22},{7,23},{8,24},{9,... | collective-permute-start | bytes 786440 | tf_op jit(solution)/shard_map/ppermute | solution.py:41
  146.6 18.5 %collective-permute-start.33 = (bf16[128,1024]{1,0:T(8,128)(2,1)S(1)}, bf16[128,1024]{1,0:T(8,128)(2,1)S(1)}, u32[]{:S(2)}, u32[]{:S(2)}) collective-permute-start(bf16[128,1024]{1,0:T(8,128)(2,1)S(1)} %get-tuple-element.95), channel_id=1, source_target_pairs={{0,48},{1,49},{2,50},{3,51},{4,52},{5,53},{6,54},{7,55},{8,56},{9,... | collective-permute-start | bytes 786440 | tf_op jit(solution)/shard_map/ppermute | solution.py:41
  161.3 14.3 %collective-permute-start.30 = (bf16[256,1024]{1,0:T(8,128)(2,1)}, bf16[256,1024]{1,0:T(8,128)(2,1)}, u32[]{:S(2)}, u32[]{:S(2)}) collective-permute-start(bf16[256,1024]{1,0:T(8,128)(2,1)} %add_dynamic-update-slice_fusion), channel_id=1, source_target_pairs={{0,48},{1,49},{2,50},{3,51},{4,52},{5,53},{6,54},{7,55},{8,56},{9,... | collective-permute-start | bytes 1572872 | tf_op jit(solution)/shard_map/ppermute | solution.py:41
  165.0 10.9 %collective-permute-start.29 = (bf16[256,1024]{1,0:T(8,128)(2,1)S(1)}, bf16[256,1024]{1,0:T(8,128)(2,1)}, u32[]{:S(2)}, u32[]{:S(2)}) collective-permute-start(bf16[256,1024]{1,0:T(8,128)(2,1)S(1)} %add_dynamic-update-slice_fusion.1), channel_id=1, source_target_pairs={{0,16},{1,17},{2,18},{3,19},{4,20},{5,21},{6,22},{7,23},{8,24},{9,... | collective-permute-start | bytes 1572872 | tf_op jit(solution)/shard_map/ppermute | solution.py:41
  177.6 13.5 %collective-permute-start.37 = (bf16[256,512]{1,0:T(8,128)(2,1)S(1)}, bf16[256,512]{1,0:T(8,128)(2,1)S(1)}, u32[]{:S(2)}, u32[]{:S(2)}) collective-permute-start(bf16[256,512]{1,0:T(8,128)(2,1)S(1)} %get-tuple-element.98), channel_id=1, source_target_pairs={{0,8},{1,24},{2,10},{3,26},{4,12},{5,28},{6,14},{7,30},{8,0},{9,16... | collective-permute-start | bytes 786440 | tf_op jit(solution)/shard_map/ppermute | solution.py:41
  184.9 12.5 %collective-permute-start.36 = (bf16[256,512]{1,0:T(8,128)(2,1)S(1)}, bf16[256,512]{1,0:T(8,128)(2,1)S(1)}, u32[]{:S(2)}, u32[]{:S(2)}) collective-permute-start(bf16[256,512]{1,0:T(8,128)(2,1)S(1)} %get-tuple-element.97), channel_id=1, source_target_pairs={{0,0},{1,16},{2,2},{3,18},{4,4},{5,20},{6,6},{7,22},{8,8},{9,24},{... | collective-permute-start | bytes 786440 | tf_op jit(solution)/shard_map/ppermute | solution.py:41
  (39 other events, 347.6 us)
Sparse Core Ops, SparseCore 0:
  20.1 58.1 all-gather.2
